TPU v7x, 32 devices: a whole 2x2x4 slice. The times are simulated.
32 devices in a mesh: tm: 2 (over x), clip: 16 (over z, y, core).
Axes of the slice: x: 2, y: 2, z: 4, core: 2. Of those that a mesh axis runs over, the one named last changes fastest.
Arguments:
- tokens: bfloat16 [48, 1536, 384], P('clip', 'tm'), may hold values from -6 to 6
- masked: int32 [48, 1152], P('clip'), may hold values from 0 to 1535, as said below
- groups: int32 [48], P('clip'), may hold values from 0 to 23
- cotangent: bfloat16 [48, 1536, 384], P('clip', 'tm'), may hold values from -6 to 6
- mask_token: bfloat16 [384], replicated, may hold values from -6 to 6
- gain_one: bfloat16 [384], replicated, may hold values from 0.099609375 to 1.8984375
- shift_one: bfloat16 [384], replicated, may hold values from -4 to 4
- w_qkv: bfloat16 [384, 1152], replicated, may hold values from -0.3125 to 0.3125
- q_bias: bfloat16 [384], replicated, may hold values from -4 to 4
- v_bias: bfloat16 [384], replicated, may hold values from -0.4375 to 0.4375
- w_proj: bfloat16 [384, 384], replicated, may hold values from -4 to 4
- b_proj: bfloat16 [384], replicated, may hold values from -4 to 4
- gain_two: bfloat16 [384], replicated, may hold values from 0.099609375 to 1.8984375
- shift_two: bfloat16 [384], replicated, may hold values from -4 to 4
- w_up: bfloat16 [384, 1536], replicated, may hold values from -0.3125 to 0.3125
- b_up: bfloat16 [1536], replicated, may hold values from -6 to 6
- w_down: bfloat16 [1536, 384], replicated, may hold values from -0.15625 to 0.15625
- b_down: bfloat16 [384], replicated, may hold values from -4 to 4
Outputs:
- block_out: bfloat16 [48, 1536, 384], P('clip', 'tm')
- grad_tokens: bfloat16 [48, 1536, 384], P('clip', 'tm')
- grad_mask_token: float32 [384], replicated
- grad_gain_one: float32 [384], replicated
- grad_shift_one: float32 [384], replicated
- grad_w_qkv: float32 [384, 1152], replicated
- grad_q_bias: float32 [384], replicated
- grad_v_bias: float32 [384], replicated
- grad_w_proj: float32 [384, 384], replicated
- grad_b_proj: float32 [384], replicated
- grad_gain_two: float32 [384], replicated
- grad_shift_two: float32 [384], replicated
- grad_w_up: float32 [384, 1536], replicated
- grad_b_up: float32 [1536], replicated
- grad_w_down: float32 [1536, 384], replicated
- grad_b_down: float32 [384], replicated
Inputs may be any that keep to these rules, and one draw needn't show every extreme that they name: `masked`: each row holds 1152 different positions of its copy.
All inputs are finite; a program needn't handle non-finite values.
Results may differ from a plain program's by a relative error of at most 0.04.
Values may be sent and summed in bfloat16 or wider, within the bound.
No kernel may reach another device: no remote copies, remote signals or barrier semaphores. Data moves between devices by JAX's collectives and lax.ppermute only.
A program may use at most 256 MiB of HBM per device.

v0:
```python
import jax
import jax.numpy as jnp
from jax import lax
from jax.sharding import PartitionSpec as P

HEADS = 6
HEAD_DIM = 64


EPSILON = 1e-06


def shortened(shard):

    def short(part):
        return part.astype(jnp.bfloat16) if part.dtype == jnp.float32 else part

    return jax.tree.map(short, shard)


def layer_norm(values, gain, shift):
    centre = jnp.mean(values, axis=-1, keepdims=True)
    centred = values - centre
    spread = jnp.mean(centred * centred, axis=-1, keepdims=True)
    return centred * lax.rsqrt(spread + EPSILON) * gain + shift


def gelu_exact(values):
    return jax.nn.gelu(values, approximate=False)


def contract_last(left, right):
    return lax.dot_general(
        left, right, (((1,), (1,)), ((), ())), preferred_element_type=jnp.float32
    )


def contract_rows(left, right):
    return lax.dot_general(
        left, right, (((0,), (0,)), ((), ())), preferred_element_type=jnp.float32
    )


def absorb_keys(queries, carry, piece):
    width = queries.shape[2]
    scale = HEAD_DIM ** (-0.5)

    def per_copy(item):
        query_rows, pair_rows, running_max, running_sum, running_acc = item
        maxima, totals, blocks = ([], [], [])
        for head_index in range(HEADS):
            first_col = head_index * HEAD_DIM
            query_head = query_rows[:, first_col : first_col + HEAD_DIM]
            key_head = pair_rows[:, first_col : first_col + HEAD_DIM]
            value_head = pair_rows[:, width + first_col : width + first_col + HEAD_DIM]
            scores = contract_last(query_head, key_head) * scale
            new_max = jnp.maximum(running_max[head_index], jnp.max(scores, axis=1))
            fading = jnp.exp(running_max[head_index] - new_max)
            expo = jnp.exp(scores - new_max[:, None])
            totals.append(running_sum[head_index] * fading + jnp.sum(expo, axis=1))
            blocks.append(
                running_acc[:, first_col : first_col + HEAD_DIM] * fading[:, None]
                + jnp.dot(expo.astype(jnp.bfloat16), value_head, preferred_element_type=jnp.float32)
            )
            maxima.append(new_max)
        return (jnp.stack(maxima), jnp.stack(totals), jnp.concatenate(blocks, axis=1))

    return lax.map(per_copy, (queries, piece) + tuple(carry))


def score_terms(query_head, grad_head, key_head, value_head, log_row, correction_row):
    scale = HEAD_DIM ** (-0.5)
    scores = contract_last(query_head, key_head) * scale
    probs = jnp.exp(scores - log_row[:, None])
    grad_probs = contract_last(grad_head, value_head)
    grad_scores = (probs * (grad_probs - correction_row[:, None])).astype(jnp.bfloat16)
    return (probs, grad_scores)


def attention_grads(item):
    query_rows, grad_rows, pair_rows, log_sums, corrections = item
    width = query_rows.shape[1]
    scale = HEAD_DIM ** (-0.5)
    query_parts, key_parts, value_parts = ([], [], [])
    for head_index in range(HEADS):
        first_col = head_index * HEAD_DIM
        query_head = query_rows[:, first_col : first_col + HEAD_DIM]
        grad_head = grad_rows[:, first_col : first_col + HEAD_DIM]
        key_head = pair_rows[:, first_col : first_col + HEAD_DIM]
        value_head = pair_rows[:, width + first_col : width + first_col + HEAD_DIM]
        probs, grad_scores = score_terms(
            query_head,
            grad_head,
            key_head,
            value_head,
            log_sums[head_index],
            corrections[head_index],
        )
        query_parts.append(
            jnp.dot(grad_scores, key_head, preferred_element_type=jnp.float32) * scale
        )
        key_parts.append(contract_rows(grad_scores, query_head) * scale)
        value_parts.append(contract_rows(probs.astype(jnp.bfloat16), grad_head))
    return (jnp.concatenate(query_parts, axis=1), jnp.concatenate(key_parts + value_parts, axis=1))


def body(
    tokens,
    masked,
    groups,
    cotangent,
    mask_token,
    gain_one,
    shift_one,
    w_qkv,
    q_bias,
    v_bias,
    w_proj,
    b_proj,
    gain_two,
    shift_two,
    w_up,
    b_up,
    w_down,
    b_down,
):
    copies, half_rows, width = tokens.shape
    total_rows = copies * half_rows
    offset = lax.axis_index("tm") * half_rows
    position = offset + lax.iota(jnp.int32, half_rows)
    masked_here = jnp.any(masked[:, :, None] == position[None, None, :], axis=1).reshape(
        total_rows, 1
    )
    group_total = lax.axis_size("clip") * copies // 2
    member = (groups[:, None] == lax.iota(jnp.int32, group_total)[None, :]).astype(jnp.float32)
    group_count = lax.psum(jnp.sum(member, axis=0), "clip")
    weighting = 1.0 / jnp.sum(member * group_count[None, :], axis=1)
    flat = tokens.reshape(total_rows, width).astype(jnp.float32)
    inputs = jnp.where(masked_here, mask_token.astype(jnp.float32)[None, :], flat)
    normed, norm_one_back = jax.vjp(
        layer_norm, inputs, gain_one.astype(jnp.float32), shift_one.astype(jnp.float32)
    )
    normed_low = normed.astype(jnp.bfloat16)
    mixed = jnp.dot(normed_low, w_qkv, preferred_element_type=jnp.float32)
    query = (mixed[:, :width] + q_bias.astype(jnp.float32)).astype(jnp.bfloat16)
    key_rows = mixed[:, width : 2 * width].astype(jnp.bfloat16)
    value = (mixed[:, 2 * width :] + v_bias.astype(jnp.float32)).astype(jnp.bfloat16)
    queries = query.reshape(copies, half_rows, width)
    pairs = jnp.concatenate([key_rows, value], axis=1).reshape(copies, half_rows, 2 * width)
    initial = (
        jnp.full((copies, HEADS, half_rows), -jnp.inf, jnp.float32),
        jnp.zeros((copies, HEADS, half_rows), jnp.float32),
        jnp.zeros((copies, half_rows, width), jnp.float32),
    )
    running_max, running_sum, running_acc = absorb_keys(
        queries, initial, lax.all_gather(pairs, "tm", axis=1, tiled=True)
    )
    gathered = None
    divisor = jnp.repeat(jnp.swapaxes(running_sum, 1, 2), HEAD_DIM, axis=2)
    attended = (running_acc / divisor).reshape(total_rows, width)
    log_sums = running_max + jnp.log(running_sum)
    attended_low = attended.astype(jnp.bfloat16)
    branch = jnp.dot(attended_low, w_proj, preferred_element_type=jnp.float32) + b_proj.astype(
        jnp.float32
    )
    middle = inputs + branch
    normed_two, norm_two_back = jax.vjp(
        layer_norm, middle, gain_two.astype(jnp.float32), shift_two.astype(jnp.float32)
    )
    normed_two_low = normed_two.astype(jnp.bfloat16)
    hidden = jnp.dot(normed_two_low, w_up, preferred_element_type=jnp.float32) + b_up.astype(
        jnp.float32
    )
    active, gelu_back = jax.vjp(gelu_exact, hidden)
    active_low = active.astype(jnp.bfloat16)
    result = jnp.dot(active_low, w_down, preferred_element_type=jnp.float32) + b_down.astype(
        jnp.float32
    )
    block_out = (middle + result).astype(jnp.bfloat16).reshape(copies, half_rows, width)
    upstream = (cotangent.astype(jnp.float32) * weighting[:, None, None]).reshape(total_rows, width)
    grad_result = upstream.astype(jnp.bfloat16)
    grad_w_down = contract_rows(active_low, grad_result)
    grad_b_down = jnp.sum(grad_result.astype(jnp.float32), axis=0)
    grad_active = contract_last(grad_result, w_down)
    grad_hidden = gelu_back(grad_active)[0].astype(jnp.bfloat16)
    grad_w_up = contract_rows(normed_two_low, grad_hidden)
    grad_b_up = jnp.sum(grad_hidden.astype(jnp.float32), axis=0)
    grad_normed_two = contract_last(grad_hidden, w_up)
    grad_mid_norm, grad_gain_two, grad_shift_two = norm_two_back(grad_normed_two)
    grad_middle = upstream + grad_mid_norm
    grad_branch = grad_middle.astype(jnp.bfloat16)
    grad_w_proj = contract_rows(attended_low, grad_branch)
    grad_b_proj = jnp.sum(grad_branch.astype(jnp.float32), axis=0)
    grad_attended = contract_last(grad_branch, w_proj).astype(jnp.bfloat16)
    corrections = jnp.swapaxes(
        jnp.sum(
            (grad_attended.astype(jnp.float32) * attended).reshape(
                copies, half_rows, HEADS, HEAD_DIM
            ),
            axis=3,
        ),
        1,
        2,
    )
    gathered = lax.all_gather(pairs, "tm", axis=1, tiled=True)
    grad_heads = grad_attended.reshape(copies, half_rows, width)
    query_grads, pair_terms = lax.map(
        attention_grads, (queries, grad_heads, gathered, log_sums, corrections)
    )
    pair_grads = jax.tree.map(
        lambda part: part.astype(jnp.float32),
        lax.psum_scatter(shortened(pair_terms), "tm", scatter_dimension=1, tiled=True),
    )
    grad_query = query_grads.reshape(total_rows, width).astype(jnp.bfloat16)
    grad_pairs = pair_grads.reshape(total_rows, 2 * width).astype(jnp.bfloat16)
    grad_mixed = jnp.concatenate([grad_query, grad_pairs], axis=1)
    grad_q_bias = jnp.sum(grad_query.astype(jnp.float32), axis=0)
    grad_v_bias = jnp.sum(grad_pairs[:, width:].astype(jnp.float32), axis=0)
    grad_w_qkv = contract_rows(normed_low, grad_mixed)
    grad_normed = contract_last(grad_mixed, w_qkv)
    grad_in_norm, grad_gain_one, grad_shift_one = norm_one_back(grad_normed)
    grad_inputs = grad_middle + grad_in_norm
    grad_tokens = (
        jnp.where(masked_here, 0.0, grad_inputs)
        .astype(jnp.bfloat16)
        .reshape(copies, half_rows, width)
    )
    grad_mask_token = jnp.sum(jnp.where(masked_here, grad_inputs, 0.0), axis=0)
    (
        grad_mask_token,
        grad_gain_one,
        grad_shift_one,
        grad_w_qkv,
        grad_q_bias,
        grad_v_bias,
        grad_w_proj,
        grad_b_proj,
        grad_gain_two,
        grad_shift_two,
        grad_w_up,
        grad_b_up,
        grad_w_down,
        grad_b_down,
    ) = lax.psum(
        (
            grad_mask_token,
            grad_gain_one,
            grad_shift_one,
            grad_w_qkv,
            grad_q_bias,
            grad_v_bias,
            grad_w_proj,
            grad_b_proj,
            grad_gain_two,
            grad_shift_two,
            grad_w_up,
            grad_b_up,
            grad_w_down,
            grad_b_down,
        ),
        ("tm", "clip"),
    )
    return (
        block_out,
        grad_tokens,
        grad_mask_token,
        grad_gain_one,
        grad_shift_one,
        grad_w_qkv,
        grad_q_bias,
        grad_v_bias,
        grad_w_proj,
        grad_b_proj,
        grad_gain_two,
        grad_shift_two,
        grad_w_up,
        grad_b_up,
        grad_w_down,
        grad_b_down,
    )


def solution(mesh):
    return jax.shard_map(
        body,
        mesh=mesh,
        in_specs=(
            P("clip", "tm", None),
            P("clip", None),
            P("clip"),
            P("clip", "tm", None),
            P(),
            P(),
            P(),
            P(),
            P(),
            P(),
            P(),
            P(),
            P(),
            P(),
            P(),
            P(),
            P(),
            P(),
        ),
        out_specs=(
            P("clip", "tm", None),
            P("clip", "tm", None),
            P(),
            P(),
            P(),
            P(),
            P(),
            P(),
            P(),
            P(),
            P(),
            P(),
            P(),
            P(),
            P(),
            P(),
        ),
        check_vma=False,
    )
```

profile of v0, /device:TPU:0, one launch (start us, length us, event | category | flops | bytes accessed | tf_op | source)
XLA Modules:
  0.0 723.6 jit_solution(17441699085733979757)
XLA Ops:
  15.2 3.2 add_convert_fusion.2
  26.4 34.9 %psum.105 = f32[24]{0:T(128)S(1)} all-reduce(f32[24]{0:T(128)S(1)} %convert_reduce_fusion.5), channel_id=1, replica_groups=mesh['tm'=2,'clip'=16] {'clip'}, use_global_device_ids=true, to_apply=%region_20.21 | all-reduce | flops 24 | bytes 192 | tf_op jit(solution)/shard_map/psum | solution.py:136
  67.7 50.1 %all-gather.2.cloned.1.call-done = bf16[3,1536,768]{2,1,0:T(8,128)(2,1)} async-done(((bf16[3,768,768]{2,1,0:T(8,128)(2,1)}), bf16[3,1536,768]{2,1,0:T(8,128)(2,1)}) %all-gather.2.cloned.1.call-update) | async-done | bytes 7077904 | tf_op jit(solution)/shard_map/all_gather | solution.py:156
  117.9 94.1 %while.26 = (s32[]{:T(128)}, f32[3,6,768]{2,1,0:T(8,128)S(1)}, f32[3,6,768]{2,1,0:T(8,128)S(1)}, f32[3,768,384]{1,2,0:T(8,128)}, bf16[3,768,384]{2,1,0:T(8,128)(2,1)}, /*index=5*/bf16[3,1536,768]{2,1,0:T(8,128)(2,1)}, s32[]{:T(128)}) while((s32[]{:T(128)}, f32[3,6,768]{2,1,0:T(8,128)S(1)}, f32[3,6,768]{2,1,0:T(8,128)S(1)}, ...), condition=%wide.region_16.17_spmd, body=%wide.region_3.16_spmd.sunk | while | flops 1868871168 | bytes 110112896 | solution.py:68
  120.2 3.2 dynamic-slice_bitcast_fusion.9
  151.4 3.2 dynamic-slice_bitcast_fusion.9
  182.6 3.2 dynamic-slice_bitcast_fusion.9
  212.0 4.1 bitcast_divide_fusion
  216.1 5.2 copy.44
  227.0 36.9 %multiply_convert_fusion.6 = (bf16[2304,1536]{1,0:T(8,128)(2,1)}, f32[2304,1536]{1,0:T(8,128)}, f32[2304,1536]{1,0:T(8,128)}) fusion(f32[1536]{0:T(1024)S(1)} %copy-done.49, bf16[384,1536]{1,0:T(8,128)(2,1)S(1)} %copy-done, f32[2304,384]{1,0:T(8,128)S(1)} %get-tuple-element.212, f32[384]{0:T(512)S(1)} %copy-done.51, f32[384]{0:T(512)S(1)} %copy-done.47, ...), kind=kOutput, calls=%fused_computation.218 | convolution fusion | flops 2955902976 | bytes 40135680 | tf_op jit(solution)/shard_map/dot_general | solution.py:171
  263.9 16.7 %convert_reduce_fusion = (f32[1536]{0:T(1024)}, bf16[2304,1536]{1,0:T(8,128)(2,1)}) fusion(f32[2304,1536]{1,0:T(8,128)} %get-tuple-element.181, f32[2304,1536]{1,0:T(8,128)} %get-tuple-element.213, bf16[2304,384]{1,0:T(8,128)(2,1)S(1)} %copy-done.23, bf16[1536,384]{1,0:T(8,128)(2,1)} %param.38), kind=kOutput, calls=%fused_computation.216 | convolution fusion | flops 2774530560 | bytes 38344704 | tf_op jit(solution)/shard_map/dot_general | solution.py:33
  280.6 8.3 %multiply_reduce_fusion.6 = (f32[384]{0:T(512)}, f32[2304]{0:T(1024)S(1)}, f32[384]{0:T(512)}, f32[2304,384]{1,0:T(8,128)S(1)}) fusion(f32[2304,384]{1,0:T(8,128)S(1)} %get-tuple-element.212, f32[2304]{0:T(1024)S(1)} %fusion.181, f32[2304]{0:T(1024)S(1)} %broadcast_multiply_fusion, f32[384]{0:T(512)S(1)} %copy-done.47, ...), kind=kOutput, calls=%fused_computation.256 | convolution fusion | flops 2724983808 | bytes 15367680 | tf_op jit(solution)/shard_map/dot_general | solution.py:33
  298.5 6.4 reshape.378
  304.9 3.6 reduce_sum.295
  308.5 142.0 %while.27 = (s32[]{:T(128)}, bf16[3,768,384]{2,1,0:T(8,128)(2,1)}, bf16[3,1536,768]{2,1,0:T(8,128)(2,1)}, bf16[3,768,384]{2,1,0:T(8,128)(2,1)}, bf16[3,1536,768]...) while((s32[]{:T(128)}, bf16[3,768,384]{2,1,0:T(8,128)(2,1)}, ...), condition=%wide.region_26.27_spmd, body=%wide.region_25.26_spmd.sunk | while | flops 4573200384 | bytes 173531504 | solution.py:207
  452.6 3.5 fusion.184
  456.2 9.3 %fusion.193 = f32[1536,384]{1,0:T(8,128)} fusion(bf16[2304,1536]{1,0:T(8,128)(2,1)} %get-tuple-element.180, bf16[2304,384]{1,0:T(8,128)(2,1)S(1)} %copy-done.24), kind=kOutput, calls=%fused_computation.299 | convolution fusion | flops 2717908992 | bytes 11206656 | tf_op jit(solution)/shard_map/dot_general | solution.py:39
  465.5 4.5 fusion.187
  470.0 66.3 %reduce-scatter.2.cloned.1.call-done = bf16[3,768,768]{2,1,0:T(8,128)(2,1)} async-done(((bf16[3,1536,768]{2,1,0:T(8,128)(2,1)}), bf16[3,768,768]{2,1,0:T(8,128)(2,1)}) %reduce-scatter.2.cloned.1.call-update) | async-done | bytes 3538960 | tf_op jit(solution)/shard_map/reduce_scatter | solution.py:212
  536.4 6.8 fusion.179
  545.1 9.8 %fusion.176 = bf16[2304,384]{1,0:T(8,128)(2,1)} fusion(f32[2304,384]{1,0:T(8,128)} %copy-done.7, bf16[2304,1536]{1,0:T(8,128)(2,1)} %get-tuple-element.180, bf16[1536,384]{1,0:T(8,128)(2,1)} %param.38, f32[384]{0:T(512)S(1)} %convert_element_type.193), kind=kOutput, calls=%fused_computation.241 | convolution fusion | flops 2720563200 | bytes 13567488 | tf_op jit(solution)/shard_map/dot_general | solution.py:176
  555.9 4.7 multiply_reduce_fusion.7
  566.1 41.3 %all-reduce = (f32[384]{0:T(512)}, f32[384]{0:T(512)}, f32[384]{0:T(512)}, f32[384]{0:T(512)}, f32[384]{0:T(512)}, /*index=5*/f32[384]{0:T(512)}, f32[384]{0:T(512)}, f32[384]{0:T(512)}, f32[1536]{0:T(1024)}, f32[384]{0:T(512)}) all-reduce(f32[384]{0:T(512)S(1)} %get-tuple-element.132, ...), channel_id=1, replica_groups=mesh['tm'=2,'clip'=16] {'tm','clip'}, use_global_device_ids=true, to_apply=%region_31.32 | all-reduce | flops 4992 | bytes 39936 | tf_op jit(solution)/shard_map/psum | solution.py:244
  607.4 102.8 %all-reduce.4.cloned.1.call-done = (f32[384,1152]{1,0:T(8,128)}, f32[384,384]{1,0:T(8,128)}, f32[384,1536]{1,0:T(8,128)}, f32[1536,384]{1,0:T(8,128)}) async-done(((f32[384,1152]{1,0:T(8,128)}, f32[384,384]{1,0:T(8,128)}, f32[384,1536]{1,0:T(8,128)}, f32[1536,384]{1,0:T(8,128)}), (f32[384,1152]{1,0:T(8,128)}, f32[384,384]{1,0:T(8,128)}, f32[384,1536]{1,0:T(8,128)}, ...) | async-done | bytes 7077904 | tf_op jit(solution)/shard_map/psum | solution.py:244
  (445 shorter events, 278.4 us)
Async XLA Ops:
  7.2 219.7 %copy-start = (bf16[384,1536]{1,0:T(8,128)(2,1)S(1)}, bf16[384,1536]{1,0:T(8,128)(2,1)}, u32[]{:S(2)}) copy-start(bf16[384,1536]{1,0:T(8,128)(2,1)} %param.36) | copy-start | bytes 3538948
  7.3 110.6 %all-gather.2.cloned.1.call-start = ((), (), s32[]{:S(2)}) async-start(), calls=%async_computation.1 | async-start | bytes 10616832 | tf_op jit(solution)/shard_map/all_gather | solution.py:156
  8.1 10.2 %copy-start.38 = (f32[384]{0:T(512)}, f32[384]{0:T(512)S(1)}, u32[]{:S(2)}) copy-start(f32[384]{0:T(512)S(1)} %convert_element_type.175) | copy-start | bytes 4612
  25.7 35.7 %copy-start.57 = (bf16[384]{0:T(512)(128)(2,1)S(1)}, bf16[384]{0:T(512)(128)(2,1)}, u32[]{:S(2)}) copy-start(bf16[384]{0:T(512)(128)(2,1)} %param.34) | copy-start | bytes 2308
  25.7 36.3 %copy-start.58 = (bf16[384]{0:T(512)(128)(2,1)S(1)}, bf16[384]{0:T(512)(128)(2,1)}, u32[]{:S(2)}) copy-start(bf16[384]{0:T(512)(128)(2,1)} %param.35) | copy-start | bytes 2308
  25.7 36.8 %copy-start.59 = (bf16[384]{0:T(512)(128)(2,1)S(1)}, bf16[384]{0:T(512)(128)(2,1)}, u32[]{:S(2)}) copy-start(bf16[384]{0:T(512)(128)(2,1)} %param.33) | copy-start | bytes 2308
  25.7 36.8 %copy-start.50 = (bf16[1536]{0:T(1024)(128)(2,1)S(1)}, bf16[1536]{0:T(1024)(128)(2,1)}, u32[]{:S(2)}) copy-start(bf16[1536]{0:T(1024)(128)(2,1)} %param.37) | copy-start | bytes 9220
  25.7 37.6 %copy-start.21 = (bf16[3,768,384]{2,1,0:T(8,128)(2,1)S(1)}, bf16[3,768,384]{2,1,0:T(8,128)(2,1)}, u32[]{:S(2)}) copy-start(bf16[3,768,384]{2,1,0:T(8,128)(2,1)} %param.25) | copy-start | bytes 5308420
  25.8 510.6 %reduce-scatter.2.cloned.1.call-start = ((), (), s32[]{:S(2)}) async-start(), calls=%async_computation.2 | async-start | bytes 10616832 | tf_op jit(solution)/shard_map/reduce_scatter | solution.py:212
  226.0 62.9 %copy-start.7 = (f32[2304,384]{1,0:T(8,128)}, f32[2304,384]{1,0:T(8,128)S(1)}, u32[]{:S(2)}) copy-start(f32[2304,384]{1,0:T(8,128)S(1)} %get-tuple-element.212) | copy-start | bytes 10616836
  226.1 62.8 %copy-start.30 = (f32[2304]{0:T(1024)}, f32[2304]{0:T(1024)S(1)}, u32[]{:S(2)}) copy-start(f32[2304]{0:T(1024)S(1)} %broadcast_multiply_fusion) | copy-start | bytes 27652
  226.9 62.0 %copy-start.42 = (f32[2304]{0:T(1024)}, f32[2304]{0:T(1024)S(1)}, u32[]{:S(2)}) copy-start(f32[2304]{0:T(1024)S(1)} %fusion.181) | copy-start | bytes 27652
  227.0 36.9 %copy-start.23 = (bf16[2304,384]{1,0:T(8,128)(2,1)S(1)}, bf16[2304,384]{1,0:T(8,128)(2,1)}, u32[]{:S(2)}) copy-start(bf16[2304,384]{1,0:T(8,128)(2,1)} %bitcast_convert_fusion) | copy-start | bytes 5308420
  311.4 9.9 %copy-start.3 = (bf16[768,384]{1,0:T(8,128)(2,1)}, bf16[768,384]{1,0:T(8,128)(2,1)S(1)}, u32[]{:S(2)}) copy-start(bf16[768,384]{1,0:T(8,128)(2,1)S(1)} %get-tuple-element.351) | copy-start | bytes 1769476 | tf_op jit(solution)/shard_map/while
  450.6 259.6 %all-reduce.4.cloned.1.call-start = ((), (), s32[]{:S(2)}) async-start(), calls=%async_computation.3 | async-start | bytes 14155776 | tf_op jit(solution)/shard_map/psum | solution.py:244
  452.6 12.9 %slice-start = ((s8[7077888]{0:T(1024)(128)(4,1)}), s8[4194304]{0:T(1024)(128)(4,1)S(1)}, s32[]{:S(2)}) async-start(s8[7077888]{0:T(1024)(128)(4,1)} %bitcast.152), calls=%async_computation.4 | async-start | bytes 8388608
  545.0 10.8 %copy-start.13 = (bf16[3,768,384]{2,1,0:T(8,128)(2,1)S(1)}, bf16[3,768,384]{2,1,0:T(8,128)(2,1)}, u32[]{:S(2)}) copy-start(bf16[3,768,384]{2,1,0:T(8,128)(2,1)} %param.22) | copy-start | bytes 5308420
  545.0 10.8 %copy-start.22 = (bf16[3,768,384]{2,1,0:T(8,128)(2,1)S(1)}, bf16[3,768,384]{2,1,0:T(8,128)(2,1)}, u32[]{:S(2)}) copy-start(bf16[3,768,384]{2,1,0:T(8,128)(2,1)} %get-tuple-element.96) | copy-start | bytes 5308420
  545.0 10.8 %copy-start.27 = (bf16[384,1152]{1,0:T(8,128)(2,1)S(1)}, bf16[384,1152]{1,0:T(8,128)(2,1)}, u32[]{:S(2)}) copy-start(bf16[384,1152]{1,0:T(8,128)(2,1)} %param.29) | copy-start | bytes 2654212
  545.0 10.8 %copy-start.35 = (f32[2304]{0:T(1024)S(1)}, f32[2304]{0:T(1024)}, u32[]{:S(2)}) copy-start(f32[2304]{0:T(1024)} %copy-done.34) | copy-start | bytes 27652
  545.0 10.8 %copy-start.37 = (f32[2304]{0:T(1024)S(1)}, f32[2304]{0:T(1024)}, u32[]{:S(2)}) copy-start(f32[2304]{0:T(1024)} %copy-done.36) | copy-start | bytes 27652
  545.0 10.8 %copy-start.39 = (f32[384]{0:T(512)S(1)}, f32[384]{0:T(512)}, u32[]{:S(2)}) copy-start(f32[384]{0:T(512)} %copy-done.38) | copy-start | bytes 4612
  545.0 10.8 %copy-start.41 = (pred[2304]{0:T(1024)(128)(4,1)S(1)}, pred[2304]{0:T(1024)(128)(4,1)}, u32[]{:S(2)}) copy-start(pred[2304]{0:T(1024)(128)(4,1)} %copy-done.40) | copy-start | bytes 6916
  545.1 10.8 %copy-start.45 = (f32[384]{0:T(512)S(1)}, f32[384]{0:T(512)}, u32[]{:S(2)}) copy-start(f32[384]{0:T(512)} %copy-done.44) | copy-start | bytes 4612
  (53 other events, 227.1 us)
Sparse Core Ops, SparseCore 0:
  25.9 91.9 all-gather.1
  450.7 85.5 reduce-scatter.1
  544.8 165.3 all-reduce.3
where the time goes:
time: 732 us; the launch traced here: 724 us
  matrix products  273 us (37%)
  waiting for transfers between devices  219 us (30%)
  local copies, waits for them, and re-layouts  79.6 us (11%)
  blocking collectives  76.2 us (10%)
  other arithmetic  58.1 us (8%)
  between operations  14.8 us (2%)
    dot_general x58, matrix products, contract_last(): lax.dot_general(left, right, (((1,), (1,)), ((), ())), preferred_element_...  106 us
    psum x1, waiting for transfers between devices, body(): lax.psum((grad_mask_token, grad_gain_one, grad_shift_one, grad_w_qkv, gra...  103 us
    dot_general x40, matrix products, contract_rows(): lax.dot_general(left, right, (((0,), (0,)), ((), ())), preferred_element_...  75.8 us
    reduce_scatter x1, waiting for transfers between devices, body(): lax.psum_scatter(shortened(pair_terms), 'tm', scatter_dimension=1, tiled=...  66.3 us
    all_gather x1, waiting for transfers between devices, body(): lax.all_gather(pairs, 'tm', axis=1, tiled=True)  50.1 us
    psum x1, blocking collectives, body(): lax.psum((grad_mask_token, grad_gain_one, grad_shift_one, grad_w_qkv, gra...  41.3 us
    dot_general x1, matrix products, body(): jnp.dot(normed_two_low, w_up, preferred_element_type=jnp.float32)  36.9 us
    psum x1, blocking collectives, body(): group_count = lax.psum(jnp.sum(member, axis=0), 'clip')  34.9 us
  transfers between devices with their start and end apart: 3, of which 3 were waited for; matrix products, arithmetic and copies ran while one was open for 6% of the time, Pallas kernels for 0%

commit v1 on v0

v1 whole, which is shorter than its diff:
```python
import functools
import math

import jax
import jax.numpy as jnp
from jax import lax
from jax.experimental import pallas as pl
from jax.experimental.pallas import tpu as pltpu
from jax.sharding import PartitionSpec as P

HEADS = 6
HEAD_DIM = 64
LANES = 128
EXTRA = 16
EPSILON = 1e-06

BF = jnp.bfloat16
F32 = jnp.float32
VMEM = pl.BlockSpec(memory_space=pltpu.VMEM)
SMEM = pl.BlockSpec(memory_space=pltpu.SMEM)


def dot(left, right):
    return jnp.dot(left, right, preferred_element_type=F32)


def dot_last(left, right):
    return lax.dot_general(left, right, (((1,), (1,)), ((), ())), preferred_element_type=F32)


def dot_rows(left, right):
    return lax.dot_general(left, right, (((0,), (0,)), ((), ())), preferred_element_type=F32)


def iota(shape, axis):
    return lax.broadcasted_iota(jnp.int32, shape, axis)


def ones_where(condition):
    return jnp.where(condition, 1.0, 0.0).astype(BF)


def column_sums(values):
    return jnp.sum(values, axis=0, keepdims=True)


def shape(*dims, kind=BF):
    return jax.ShapeDtypeStruct(dims, kind)


def plain(kernel, outs):
    return pl.pallas_call(kernel, out_shape=outs, compiler_params=pltpu.CompilerParams(vmem_limit_bytes=16 << 20))


def one_hots(masked_row):
    low = ones_where(iota((LANES, masked_row.shape[1]), 0) == (masked_row & (LANES - 1)))
    high = ones_where(iota((16, masked_row.shape[1]), 0) == (masked_row >> 7))
    return low, high


def ranks(masked_row, tm, half, unmasked):
    low, high = one_hots(masked_row)
    marks = dot_last(high, low)
    valid = iota((16, LANES), 0) < 2 * half // LANES
    free = jnp.where(valid, 1.0 - marks, 0.0).astype(BF)
    before = ones_where(iota((LANES, LANES), 0) < iota((LANES, LANES), 1))
    within = dot(free, before)
    totals = dot(free, jnp.ones((LANES, LANES), BF)).astype(BF)
    earlier = ones_where(iota((16, 16), 1) < iota((16, 16), 0))
    rank = within + dot(earlier, totals)
    rank = jnp.where(marks > 0.5, float(unmasked), rank).astype(jnp.int32)
    blocks = half // LANES
    return jnp.where(tm == 0, rank[:blocks], rank[blocks : 2 * blocks])


def ranks_down(masked_row, tm, half, unmasked):
    low, high = one_hots(masked_row)
    marks = dot_last(low, high)
    valid = iota((LANES, 16), 1) < 2 * half // LANES
    free = jnp.where(valid, 1.0 - marks, 0.0).astype(BF)
    before = ones_where(iota((LANES, LANES), 1) < iota((LANES, LANES), 0))
    within = dot(before, free)
    totals = dot(jnp.ones((LANES, LANES), BF), free).astype(BF)
    earlier = ones_where(iota((16, 16), 0) < iota((16, 16), 1))
    rank = within + dot(totals, earlier)
    rank = jnp.where(marks > 0.5, float(unmasked), rank).astype(jnp.int32)
    blocks = half // LANES
    return jnp.where(tm == 0, rank[:, :blocks], rank[:, blocks : 2 * blocks])


def picks(rank, labels):
    wide = jnp.broadcast_to(labels, (labels.shape[0], LANES))
    return jnp.concatenate([ones_where(wide == rank[b : b + 1, :]) for b in range(rank.shape[0])], axis=1)


def prep_tokens_kernel(unmasked, place_ref, masked_ref, tokens_ref, mine_ref, theirs_ref, shared_ref, rank_ref):
    tm = place_ref[0]
    half = tokens_ref.shape[1]
    rows = unmasked + EXTRA
    labels = iota((rows, 1), 0)
    for role, (copy, out_ref) in enumerate(((1 - tm, theirs_ref), (2, shared_ref), (tm, mine_ref))):
        rank = ranks(masked_ref[copy], tm, half, unmasked)
        rank_ref[role] = jnp.concatenate([rank, jnp.zeros((8 - rank.shape[0], LANES), jnp.int32)], axis=0)
        out_ref[...] = dot(picks(rank, labels), tokens_ref[copy]).astype(BF)


def prep_grads_kernel(unmasked, place_ref, masked_ref, rank_ref, cotangent_ref, keep_ref, send_ref, down_ref):
    tm = place_ref[0]
    half = cotangent_ref.shape[1]
    blocks = half // LANES
    rows = unmasked + EXTRA
    part = unmasked // 2
    labels = iota((rows, 1), 0)
    send_ref[:rows, :] = dot(picks(rank_ref[0, :blocks], labels), cotangent_ref[1 - tm]).astype(BF)
    rank = rank_ref[1, :blocks]
    small = iota((part + EXTRA, 1), 0)
    theirs = jnp.where(small < part, small + part * (1 - tm), -1)
    send_ref[rows:, :] = dot(picks(rank, theirs), cotangent_ref[2]).astype(BF)
    own = jnp.where(small < part, small + part * tm, small + part)
    keep_ref[rows:, :] = dot(picks(rank, own), cotangent_ref[2]).astype(BF)
    keep_ref[:rows, :] = dot(picks(rank_ref[2, :blocks], labels), cotangent_ref[tm]).astype(BF)
    for role, copy in enumerate((1 - tm, 2, tm)):
        down = ranks_down(masked_ref[copy], tm, half, unmasked)
        down_ref[role] = jnp.concatenate([down, jnp.zeros((LANES, 8 - blocks), jnp.int32)], axis=1)


def normalise(values):
    centred = values - jnp.mean(values, axis=-1, keepdims=True)
    scale = lax.rsqrt(jnp.mean(centred * centred, axis=-1, keepdims=True) + EPSILON)
    return centred * scale, scale


def attention_kernel(
    unmasked, count, split, place_ref, own_ref, got_ref, small_ref, w_ref,
    x_ref, q_ref, k_ref, v_ref, p_ref, att_ref, *rest
):
    rows, width = own_ref.shape
    at = iota((rows, width), 0)
    x = own_ref[...].astype(F32) + got_ref[...].astype(F32)
    x = jnp.where(at == unmasked, small_ref[0:1, :], x)
    hat, _ = normalise(x)
    normed = (hat * small_ref[1:2, :] + small_ref[2:3, :]).astype(BF)
    mixed = dot(normed, w_ref[...])
    query = ((mixed[:, :width] + small_ref[3:4, :]).astype(BF).astype(F32) * HEAD_DIM ** (-0.5)).astype(BF)
    key = mixed[:, width : 2 * width].astype(BF)
    value = (mixed[:, 2 * width :] + small_ref[4:5, :]).astype(BF)
    k_ref[...] = key
    v_ref[...] = value
    x = x.astype(BF)
    if split:
        tm = place_ref[0]
        part = unmasked // 2

        def take(values):
            chosen = jnp.where(tm == 0, values[:part].astype(F32), values[part:unmasked].astype(F32)).astype(BF)
            return jnp.concatenate([chosen, values[unmasked:]], axis=0)

        rest[0][...] = x
        x, query = take(x), take(query)
    x_ref[...] = x
    q_ref[...] = query
    across = iota((1, rows), 1)
    bias = jnp.where(across < unmasked, 0.0, jnp.where(across == unmasked, math.log(count), -1e30))
    first = iota((1, LANES), 1) < HEAD_DIM
    for pair in range(width // LANES):
        cols = slice(pair * LANES, (pair + 1) * LANES)
        q_pair, k_pair, v_pair = query[:, cols], key[:, cols], value[:, cols]
        parts = []
        for side in range(2):
            mine = first if side == 0 else jnp.logical_not(first)
            scores = dot_last(jnp.where(mine, q_pair, jnp.zeros_like(q_pair)), k_pair) + bias
            expo = jnp.exp(scores - jnp.max(scores, axis=1, keepdims=True))
            probs = (expo * (1.0 / jnp.sum(expo, axis=1, keepdims=True))).astype(BF)
            p_ref[2 * pair + side] = probs
            parts.append(dot(probs, v_pair))
        att_ref[:, cols] = jnp.where(first, parts[0], parts[1]).astype(BF)


def gelu_terms(hidden):
    size = jnp.abs(hidden) * (0.5**0.5)
    t = 1.0 / (1.0 + 0.3275911 * size)
    bell = jnp.exp(hidden * hidden * -0.5)
    tail = t * (0.254829592 + t * (-0.284496736 + t * (1.421413741 + t * (-1.453152027 + t * 1.061405429))))
    tail = 0.5 * tail * bell
    below = jnp.where(hidden >= 0.0, 1.0 - tail, tail)
    return hidden * below, below + hidden * bell * (1.0 / math.sqrt(2.0 * math.pi))


def stacked(refs):
    return jnp.concatenate([ref[...] for ref in refs], axis=0)


def scatter_chunks(me, stage_ref, keep_ref, send_ref):
    depth = keep_ref.shape[2]
    for rel in range(2 * 4 * keep_ref.shape[1]):
        first = pl.multiple_of((me ^ rel) * depth, 16)
        target = send_ref if rel & 1 else keep_ref
        target[(rel >> 1) & 3, rel >> 3] = stage_ref[pl.ds(first, depth), :]


def stage_weight(stage_ref, first, grad):
    depth = grad.shape[0]
    for block in range(grad.shape[1] // LANES):
        stage_ref[first + block * depth : first + (block + 1) * depth, :] = grad[
            :, block * LANES : (block + 1) * LANES
        ].astype(BF)
    return first + grad.shape[0] * (grad.shape[1] // LANES)


def stage_rows(stage_ref, first, vectors):
    pieces = [v[:, b * LANES : (b + 1) * LANES] for v in vectors for b in range(v.shape[1] // LANES)]
    missing = -len(pieces) % 16
    if missing:
        pieces.append(jnp.zeros((missing, LANES), F32))
    block = jnp.concatenate(pieces, axis=0).astype(BF)
    stage_ref[first : first + block.shape[0], :] = block
    return first + block.shape[0]


def clear_rest(stage_ref, first):
    if first < stage_ref.shape[0]:
        stage_ref[first:, :] = jnp.zeros((stage_ref.shape[0] - first, LANES), BF)


def up_kernel(
    place_ref, weight_ref, att_a, att_b, x_a, x_b, cot_own, cot_got, small_ref, bias_up_ref, w_proj_ref, w_up_ref,
    middle_ref, normed_ref, active_ref, slope_ref, upstream_ref, keep_ref, send_ref, stage_ref
):
    rows_a, width = x_a.shape
    total = rows_a + x_b.shape[0]
    attended = stacked((att_a, att_b))
    x = stacked((x_a, x_b)).astype(F32)
    middle = x + dot(attended, w_proj_ref[...]) + small_ref[5:6, :]
    middle_ref[...] = middle
    hat, _ = normalise(middle)
    normed = (hat * small_ref[6:7, :] + small_ref[7:8, :]).astype(BF)
    normed_ref[...] = normed
    weight = jnp.where(iota((total, 1), 0) < rows_a, weight_ref[0], weight_ref[1])
    upstream = (cot_own[...].astype(F32) + cot_got[...].astype(F32)) * weight
    upstream_ref[...] = upstream
    grad_result = upstream.astype(BF)
    hidden = dot(normed, w_up_ref[...]) + bias_up_ref[...]
    active, slope = gelu_terms(hidden)
    active = active.astype(BF)
    active_ref[...] = active
    slope_ref[...] = slope.astype(BF)
    end = stage_weight(stage_ref, 0, dot_rows(active, grad_result))
    clear_rest(stage_ref, end)
    scatter_chunks(place_ref[1], stage_ref, keep_ref, send_ref)


def norm_back(grad, hat, scale, gain):
    inner = grad * gain
    mean = jnp.mean(inner, axis=-1, keepdims=True)
    along = jnp.mean(inner * hat, axis=-1, keepdims=True)
    return scale * (inner - mean - hat * along)


def down_kernel(
    place_ref, middle_ref, normed_ref, active_ref, slope_ref, upstream_ref, att_a, att_b, small_ref,
    w_proj_ref, w_up_ref, w_down_ref,
    out_ref, grad_middle_ref, grad_att_ref, keep_ref, send_ref, stage_ref
):
    middle = middle_ref[...]
    out_ref[...] = (middle + dot(active_ref[...], w_down_ref[...]) + small_ref[8:9, :]).astype(BF)
    upstream = upstream_ref[...]
    grad_result = upstream.astype(BF)
    grad_hidden = (dot_last(grad_result, w_down_ref[...]) * slope_ref[...].astype(F32)).astype(BF)
    end = stage_weight(stage_ref, 0, dot_rows(normed_ref[...], grad_hidden))
    grad_normed = dot_last(grad_hidden, w_up_ref[...])
    hat, scale = normalise(middle)
    grad_middle = upstream + norm_back(grad_normed, hat, scale, small_ref[6:7, :])
    grad_middle_ref[...] = grad_middle
    grad_branch = grad_middle.astype(BF)
    grad_att_ref[...] = dot_last(grad_branch, w_proj_ref[...]).astype(BF)
    end = stage_weight(stage_ref, end, dot_rows(stacked((att_a, att_b)), grad_branch))
    vectors = (
        column_sums(grad_hidden.astype(F32)),
        column_sums(grad_normed * hat),
        column_sums(grad_normed),
        column_sums(grad_branch.astype(F32)),
        column_sums(grad_result.astype(F32)),
    )
    end = stage_rows(stage_ref, end, vectors)
    clear_rest(stage_ref, end)
    scatter_chunks(place_ref[1], stage_ref, keep_ref, send_ref)


def attention_back_kernel(row_from, g_ref, att_ref, q_ref, k_ref, v_ref, p_ref, dq_ref, dk_ref, dv_ref):
    width = q_ref.shape[1]
    rows = q_ref.shape[0]
    first = iota((1, LANES), 1) < HEAD_DIM
    for pair in range(width // LANES):
        cols = slice(pair * LANES, (pair + 1) * LANES)
        g_pair = g_ref[row_from : row_from + rows, cols]
        q_pair, k_pair, v_pair = q_ref[:, cols], k_ref[:, cols], v_ref[:, cols]
        agree = g_pair.astype(F32) * att_ref[:, cols].astype(F32)
        dq, dk, dv = [], [], []
        for side in range(2):
            mine = first if side == 0 else jnp.logical_not(first)
            correction = jnp.sum(jnp.where(mine, agree, 0.0), axis=1, keepdims=True)
            probs = p_ref[2 * pair + side]
            grad_probs = dot_last(jnp.where(mine, g_pair, jnp.zeros_like(g_pair)), v_pair)
            grad_scores = (probs.astype(F32) * (grad_probs - correction)).astype(BF)
            dq.append(dot(grad_scores, k_pair))
            dk.append(dot_rows(grad_scores, q_pair))
            dv.append(dot_rows(probs, g_pair))
        dq_ref[:, cols] = (jnp.where(first, dq[0], dq[1]) * HEAD_DIM ** (-0.5)).astype(BF)
        dk_ref[:, cols] = jnp.where(first, dk[0], dk[1]).astype(BF)
        dv_ref[:, cols] = jnp.where(first, dv[0], dv[1]).astype(BF)


def inputs_back_kernel(
    unmasked, place_ref, x_a, x_b, dq_a, dq_b, dk_a, dk_b, dv_a, dv_b, grad_middle_ref, small_ref, w_ref,
    grad_ref, keep_ref, send_ref, stage_ref
):
    rows, width = x_a.shape
    part = unmasked // 2
    tm = place_ref[0]

    def spread(block):
        wide = block.astype(F32)
        left = jnp.where(tm == 0, wide[:part], 0.0)
        right = jnp.where(tm == 0, 0.0, wide[:part])
        return jnp.concatenate([left, right, wide[part:]], axis=0)

    x = stacked((x_a, x_b)).astype(F32)
    hat, scale = normalise(x)
    gain = small_ref[1:2, :]
    normed = (hat * gain + small_ref[2:3, :]).astype(BF)
    dq = jnp.concatenate([dq_a[...], spread(dq_b[...]).astype(BF)], axis=0)
    mixed = jnp.concatenate([dq, stacked((dk_a, dk_b)), stacked((dv_a, dv_b))], axis=1)
    end = stage_weight(stage_ref, 0, dot_rows(normed, mixed))
    grad_normed = dot_last(mixed, w_ref[...])
    grad = norm_back(grad_normed, hat, scale, gain)
    grad = grad + jnp.concatenate([grad_middle_ref[:rows], spread(grad_middle_ref[rows:])], axis=0)
    grad_ref[:unmasked] = grad[:unmasked].astype(BF)
    grad_ref[unmasked:] = grad[rows : rows + unmasked].astype(BF)
    vectors = (
        column_sums(mixed[:, :width].astype(F32)),
        column_sums(mixed[:, 2 * width :].astype(F32)),
        column_sums(grad_normed * hat),
        column_sums(grad_normed),
        grad[unmasked : unmasked + 1] + grad[rows + unmasked : rows + unmasked + 1],
    )
    end = stage_rows(stage_ref, end, vectors)
    clear_rest(stage_ref, end)
    scatter_chunks(place_ref[1], stage_ref, keep_ref, send_ref)


def place_back(down, rows, half):
    labels = jnp.broadcast_to(iota((1, rows), 1), (LANES, rows))
    return jnp.concatenate([ones_where(labels == down[:, b : b + 1]) for b in range(half // LANES)], axis=0)


def outputs_kernel(unmasked, place_ref, down_ref, own_ref, got_ref, out_ref):
    tm = place_ref[0]
    half = out_ref.shape[1]
    rows = unmasked + EXTRA
    part = unmasked // 2
    out_ref[tm] = dot(place_back(down_ref[2], rows, half), own_ref[:rows]).astype(BF)
    out_ref[1 - tm] = dot(place_back(down_ref[0], rows, half), got_ref[:rows]).astype(BF)
    own = own_ref[rows:].astype(F32)
    got = got_ref[rows:].astype(F32)
    left = jnp.where(tm == 0, own[:part], got[:part])
    right = jnp.where(tm == 0, got[:part], own[:part])
    whole = jnp.concatenate([left, right, own[part:]], axis=0).astype(BF)
    out_ref[2] = dot(place_back(down_ref[1], rows, half), whole).astype(BF)


def grads_out_kernel(unmasked, place_ref, down_ref, own_ref, got_ref, out_ref):
    tm = place_ref[0]
    half = out_ref.shape[1]
    out_ref[tm] = dot(place_back(down_ref[2], unmasked, half), own_ref[:unmasked]).astype(BF)
    out_ref[1 - tm] = dot(place_back(down_ref[0], unmasked, half), got_ref[:unmasked]).astype(BF)
    whole = (own_ref[unmasked:].astype(F32) + got_ref[unmasked:].astype(F32)).astype(BF)
    out_ref[2] = dot(place_back(down_ref[1], unmasked, half), whole).astype(BF)


def fold_kernel(keep_ref, got_ref, *out_refs):
    for step, out_ref in enumerate(out_refs):
        out_ref[...] = (keep_ref[step].astype(F32) + got_ref[step].astype(F32)).astype(BF)


def fold_four_kernel(*refs):
    total = refs[0][...].astype(F32)
    for ref in refs[1:4]:
        total = total + ref[...].astype(F32)
    total = total.astype(BF)
    if len(refs) == 5:
        refs[4][...] = total
        return
    for step, out_ref in enumerate(refs[4:]):
        for slot in range(out_ref.shape[0]):
            out_ref[slot] = total[4 * slot + step]


def join_kernel(*refs):
    for step in range(len(refs) - 1):
        refs[-1][step] = refs[step][...]


def clip_swap(values, distance):
    size = lax.axis_size("clip")
    return lax.ppermute(values, "clip", [(i, i ^ distance) for i in range(size)])


def near_swap(values, step):
    size = lax.axis_size("clip")
    pairs = [
        (t * size + i, (t ^ (step & 1)) * size + (i ^ ((step >> 1) << 1))) for t in range(2) for i in range(size)
    ]
    return lax.ppermute(values, ("tm", "clip"), pairs)


def sum_over_devices(keep, send):
    far = []
    distance = 4
    while distance < lax.axis_size("clip"):
        far.append(distance)
        distance *= 4
    _, groups, depth, _ = keep.shape
    got = clip_swap(send, 1)
    pieces = plain(fold_kernel, [shape(groups, depth, LANES)] * 4)(keep, got)
    pieces = [pieces[0]] + [near_swap(pieces[step], step) for step in (1, 2, 3)]
    left = groups
    for distance in far:
        left //= 4
        pieces = plain(fold_four_kernel, [shape(left, depth, LANES)] * 4)(*pieces)
        pieces = [pieces[0]] + [clip_swap(pieces[step], step * distance) for step in (1, 2, 3)]
    total = plain(fold_four_kernel, shape(left, depth, LANES))(*pieces)
    for distance in reversed(far):
        pieces = [total] + [clip_swap(total, step * distance) for step in (1, 2, 3)]
        total = jnp.stack(pieces, axis=1).reshape(-1, depth, LANES)
    pieces = [total] + [near_swap(total, step) for step in (1, 2, 3)]
    total = jnp.stack(pieces)
    return total, clip_swap(total, 1)


def gather_chunks(me, own_ref, got_ref, stage_ref):
    depth = own_ref.shape[2]
    for rel in range(2 * 4 * own_ref.shape[1]):
        first = pl.multiple_of((me ^ rel) * depth, 16)
        source = got_ref if rel & 1 else own_ref
        stage_ref[pl.ds(first, depth), :] = source[(rel >> 1) & 3, rel >> 3]


def unstage_kernel(weights, vectors, place_ref, own_ref, got_ref, *refs):
    outs, stage_ref = refs[:-1], refs[-1]
    gather_chunks(place_ref[1], own_ref, got_ref, stage_ref)
    first = 0
    for out_ref in outs[:weights]:
        depth, width = out_ref.shape
        for block in range(width // LANES):
            out_ref[:, block * LANES : (block + 1) * LANES] = stage_ref[first : first + depth, :].astype(F32)
            first += depth
    if vectors:
        count = sum(ref.shape[0] // LANES for ref in outs[weights:])
        rows = stage_ref[first : first + count + -count % 16, :].astype(F32)
        at = 0
        for out_ref in outs[weights:]:
            blocks = out_ref.shape[0] // LANES
            for block in range(blocks):
                out_ref[block * LANES : (block + 1) * LANES] = rows[at + block]
            at += blocks


def chunk_rows(count, devices):
    return -(-count // (devices * 16)) * 16


def body(
    tokens,
    masked,
    groups,
    cotangent,
    mask_token,
    gain_one,
    shift_one,
    w_qkv,
    q_bias,
    v_bias,
    w_proj,
    b_proj,
    gain_two,
    shift_two,
    w_up,
    b_up,
    w_down,
    b_down,
):
    copies, half, width = tokens.shape
    hidden = w_up.shape[1]
    hide = masked.shape[1]
    unmasked = 2 * half - hide
    rows = unmasked + EXTRA
    some = unmasked // 2 + EXTRA
    total = rows + some
    tm, clip = lax.axis_index("tm"), lax.axis_index("clip")
    clips = lax.axis_size("clip")
    devices = 2 * clips
    me = (clip & 1) | (tm << 1) | ((clip >> 1) << 2)
    place = jnp.stack([tm, me]).astype(jnp.int32)
    smem = pl.BlockSpec(memory_space=pltpu.SMEM)
    swap = functools.partial(lax.ppermute, axis_name="tm", perm=[(0, 1), (1, 0)])

    def run(kernel, args, outs, scratch=(), scalars=1, limit=48, flops=0):
        moved = sum(math.prod(a.shape) * a.dtype.itemsize for a in list(args) + jax.tree.leaves(outs))
        return pl.pallas_call(
            kernel,
            out_shape=outs,
            in_specs=[smem] * scalars + [VMEM] * (len(args) - scalars),
            out_specs=jax.tree.map(lambda _: VMEM, outs),
            scratch_shapes=list(scratch),
            compiler_params=pltpu.CompilerParams(vmem_limit_bytes=limit << 20),
            cost_estimate=pl.CostEstimate(flops=flops, bytes_accessed=moved, transcendentals=0),
        )(*args)

    def chunked(count):
        depth = chunk_rows(count, devices)
        halves = [shape(4, devices // 8, depth, LANES)] * 2
        return halves, [pltpu.VMEM((devices * depth, LANES), BF)]

    masked = masked.reshape(copies, 1, hide)
    small = jnp.stack(
        [mask_token, gain_one, shift_one, q_bias, v_bias, b_proj, gain_two, shift_two, b_down]
    ).astype(F32)
    bias_up = b_up.astype(F32).reshape(1, hidden)

    everyone = groups
    distance = 1
    while distance < clips:
        everyone = jnp.concatenate([everyone] + [clip_swap(everyone, step * distance) for step in (1, 2, 3)])
        distance *= 4
    counts = jnp.sum((groups[:, None] == everyone[None, :]).astype(F32), axis=1)
    weighting = 1.0 / counts
    weighting = jnp.stack([jnp.where(tm == 0, weighting[0], weighting[1]), weighting[2]])

    block = shape(rows, width)
    mine, theirs, shared, rank = run(
        functools.partial(prep_tokens_kernel, unmasked),
        (place, masked, tokens),
        [block, block, block, shape(copies, 8, LANES, kind=jnp.int32)],
        flops=2 * copies * rows * half * width,
    )
    got_mine = swap(theirs)
    got_shared = swap(shared)
    cot_own, cot_send, down = run(
        functools.partial(prep_grads_kernel, unmasked),
        (place, masked, rank, cotangent),
        [shape(total, width), shape(total, width), shape(copies, LANES, 8, kind=jnp.int32)],
        flops=2 * copies * rows * half * width,
    )
    cot_got = swap(cot_send)

    def attend(own, got, split):
        queries = some if split else rows
        outs = [
            shape(queries, width), shape(queries, width), block, block,
            shape(HEADS, queries, rows), shape(queries, width),
        ]
        if split:
            outs.append(block)
        return run(
            functools.partial(attention_kernel, unmasked, hide, split),
            (place, own, got, small, w_qkv),
            outs,
            flops=6 * rows * width * width + 4 * queries * rows * width,
        )

    x_a, q_a, k_a, v_a, p_a, att_a = attend(mine, got_mine, False)
    x_b, q_b, k_b, v_b, p_b, att_b, x_whole = attend(shared, got_shared, True)

    halves, stage = chunked(width // LANES * hidden)
    middle, normed_two, active, slope, upstream, keep, send = run(
        up_kernel,
        (place, weighting, att_a, att_b, x_a, x_b, cot_own, cot_got, small, bias_up, w_proj, w_up),
        [
            shape(total, width, kind=F32), shape(total, width), shape(total, hidden), shape(total, hidden),
            shape(total, width, kind=F32),
        ]
        + halves,
        stage,
        scalars=2,
        flops=2 * total * width * (width + 2 * hidden),
    )
    down_sums = sum_over_devices(keep, send)

    halves, stage = chunked(hidden // LANES * width + width // LANES * width + 32)
    out_rows, grad_middle, grad_att, keep, send = run(
        down_kernel,
        (place, middle, normed_two, active, slope, upstream, att_a, att_b, small, w_proj, w_up, w_down),
        [shape(total, width), shape(total, width, kind=F32), shape(total, width)] + halves,
        stage,
        flops=2 * total * width * (2 * width + 4 * hidden),
    )
    up_sums = sum_over_devices(keep, send)
    out_got = swap(out_rows)

    def attend_back(row_from, att, q, k, v, p):
        return run(
            functools.partial(attention_back_kernel, row_from),
            (grad_att, att, q, k, v, p),
            [shape(q.shape[0], width), block, block],
            scalars=0,
            flops=8 * q.shape[0] * rows * width,
        )

    dq_a, dk_a, dv_a = attend_back(0, att_a, q_a, k_a, v_a, p_a)
    dq_b, dk_b, dv_b = attend_back(rows, att_b, q_b, k_b, v_b, p_b)
    halves, stage = chunked(3 * width // LANES * width + 16)
    grad_rows, keep, send = run(
        functools.partial(inputs_back_kernel, unmasked),
        (place, x_a, x_whole, dq_a, dq_b, dk_a, dk_b, dv_a, dv_b, grad_middle, small, w_qkv),
        [shape(2 * unmasked, width)] + halves,
        stage,
        flops=2 * 2 * rows * width * 6 * width,
    )
    in_sums = sum_over_devices(keep, send)
    grad_got = swap(grad_rows)

    block_out = run(
        functools.partial(outputs_kernel, unmasked), (place, down, out_rows, out_got), shape(*tokens.shape)
    )
    grad_tokens = run(
        functools.partial(grads_out_kernel, unmasked), (place, down, grad_rows, grad_got), shape(*tokens.shape)
    )

    def unstage(sums, weights, vectors):
        depth = sums[0].shape[2]
        outs = [shape(*dims, kind=F32) for dims in weights] + [shape(dim, kind=F32) for dim in vectors]
        return run(
            functools.partial(unstage_kernel, len(weights), len(vectors)),
            (place,) + tuple(sums),
            outs,
            [pltpu.VMEM((devices * depth, LANES), BF)],
        )

    (grad_w_down,) = unstage(down_sums, [(hidden, width)], [])
    grad_w_up, grad_w_proj, grad_b_up, grad_gain_two, grad_shift_two, grad_b_proj, grad_b_down = unstage(
        up_sums, [(width, hidden), (width, width)], [hidden, width, width, width, width]
    )
    grad_w_qkv, grad_q_bias, grad_v_bias, grad_gain_one, grad_shift_one, grad_mask_token = unstage(
        in_sums, [(width, 3 * width)], [width] * 5
    )
    return (
        block_out,
        grad_tokens,
        grad_mask_token,
        grad_gain_one,
        grad_shift_one,
        grad_w_qkv,
        grad_q_bias,
        grad_v_bias,
        grad_w_proj,
        grad_b_proj,
        grad_gain_two,
        grad_shift_two,
        grad_w_up,
        grad_b_up,
        grad_w_down,
        grad_b_down,
    )


def solution(mesh):
    return jax.shard_map(
        body,
        mesh=mesh,
        in_specs=(P("clip", "tm", None), P("clip", None), P("clip"), P("clip", "tm", None)) + (P(),) * 14,
        out_specs=(P("clip", "tm", None), P("clip", "tm", None)) + (P(),) * 14,
        check_vma=False,
    )
```

time: 732 us -> 179 us (0.24); the launches traced: 724 us -> 178 us
  matrix products: 273 us -> 0 us
  waiting for transfers between devices: 219 us -> 55.1 us
  blocking collectives: 76.2 us -> 0 us
  local copies, waits for them, and re-layouts: 79.6 us -> 6.56 us
  starting transfers between devices: 0.12 us -> 57.3 us
  other arithmetic: 58.1 us -> 1.39 us
  Pallas kernels: 0 us -> 55.3 us
  between operations: 14.8 us -> 2.53 us
    dot_general x138 -> x0, matrix products: 273 us -> none  [the longest x58 106 us: contract_last(): lax.dot_general(left, right, (((1,), (1,)), ((), ())), preferred_element_...]
    psum x1 -> x0, waiting for transfers between devices: 103 us -> none  [body(): lax.psum((grad_mask_token, grad_gain_one, grad_shift_one, grad_w_qkv, gra...]
    psum x2 -> x0, blocking collectives: 76.2 us -> none  [the longest x1 41.3 us: body(): lax.psum((grad_mask_token, grad_gain_one, grad_shift_one, grad_w_qkv, gra...]
    reduce_scatter x1 -> x0, waiting for transfers between devices: 66.3 us -> none  [body(): lax.psum_scatter(shortened(pair_terms), 'tm', scatter_dimension=1, tiled=...]
    ppermute x0 -> x53, starting transfers between devices: none -> 57.3 us  [the longest x30 31.2 us: clip_swap(): lax.ppermute(values, 'clip', [(i, i ^ distance) for i in range(size)])]
    pallas_call x0 -> x23, Pallas kernels: none -> 55.3 us  [the longest x14 54.5 us: run(): pl.pallas_call(kernel, out_shape=outs, in_specs=[smem] * scalars + [VMEM]...]
    ppermute x0 -> x53, waiting for transfers between devices: none -> 55.1 us  [the longest x18 23.6 us: near_swap(): return lax.ppermute(values, ('tm', 'clip'), pairs)]
    all_gather x1 -> x0, waiting for transfers between devices: 50.1 us -> none  [body(): lax.all_gather(pairs, 'tm', axis=1, tiled=True)]
  transfers between devices with their start and end apart: 3 -> 53, of which waited for: 3 -> 16; matrix products, arithmetic and copies ran while one was open for 6% -> 2% of each run, Pallas kernels for 0% -> 20%
where the time goes in v1:
time: 179 us; the launch traced here: 178 us
  starting transfers between devices  57.3 us (32%)
  Pallas kernels  55.3 us (31%)
  waiting for transfers between devices  55.1 us (31%)
  local copies, waits for them, and re-layouts  6.56 us (4%)
  between operations  2.53 us (1%)
    pallas_call x14, Pallas kernels, run(): pl.pallas_call(kernel, out_shape=outs, in_specs=[smem] * scalars + [VMEM]...  54.5 us
    ppermute x30, starting transfers between devices, clip_swap(): lax.ppermute(values, 'clip', [(i, i ^ distance) for i in range(size)])  31.2 us
    ppermute x18, waiting for transfers between devices, near_swap(): return lax.ppermute(values, ('tm', 'clip'), pairs)  23.6 us
    ppermute x30, waiting for transfers between devices, clip_swap(): lax.ppermute(values, 'clip', [(i, i ^ distance) for i in range(size)])  20.2 us
    ppermute x18, starting transfers between devices, near_swap(): return lax.ppermute(values, ('tm', 'clip'), pairs)  19.8 us
    ppermute x1, waiting for transfers between devices, body(): out_got = swap(out_rows)  11.3 us
    unnamed x52, local copies, waits for them, and re-layouts  5.04 us
  transfers between devices with their start and end apart: 53, of which 16 were waited for; matrix products, arithmetic and copies ran while one was open for 2% of the time, Pallas kernels for 20%

profile of v1, /device:TPU:0, one launch (start us, length us, event | category | flops | bytes accessed | tf_op | source)
XLA Modules:
  0.0 178.2 jit_solution(11144419782023608266)
XLA Ops:
  6.2 3.2 %shard_map.297 = (bf16[400,384]{1,0:T(8,128)(2,1)S(1)}, bf16[400,384]{1,0:T(8,128)(2,1)}, bf16[400,384]{1,0:T(8,128)(2,1)}, s32[3,8,128]{2,1,0:T(8,128)S(1)}) custom-call(s32[2]{0:T(128)S(1)} %pad_add_fusion.place_ref, s32[3,1,1152]{2,1,0:T(1,128)S(1)} %reshape.51.masked_ref, bf16[3,768,384]{2,1,0:T(8,128)(2,1)S(1)} %copy-done), custom_call_target="tpu_custom_call" | custom-call | flops 707788800 | bytes 2717192 | tf_op jit(solution)/shard_map/pallas_call | solution.py:509
  12.4 3.0 %shard_map.298 = (bf16[608,384]{1,0:T(8,128)(2,1)S(1)}, bf16[608,384]{1,0:T(8,128)(2,1)}, s32[3,128,8]{2,1,0:T(8,128)S(1)}) custom-call(s32[2]{0:T(128)S(1)} %pad_add_fusion.place_ref, s32[3,1,1152]{2,1,0:T(1,128)S(1)} %reshape.51.masked_ref, s32[3,8,128]{2,1,0:T(8,128)S(1)} %get-tuple-element.94.rank_ref, bf16[3,768,384]{2,1,0:T(8,128)(2,1)S(1)} %copy-done.1), custom_call_target="tpu_custom_call" | custom-call | flops 707788800 | bytes 2741768 | tf_op jit(solution)/shard_map/pallas_call | solution.py:509
  18.0 3.6 %collective-permute-start.5 = (s32[12]{0:T(128)S(1)}, s32[12]{0:T(128)S(1)}, u32[]{:S(2)}, u32[]{:S(2)}) collective-permute-start(s32[12]{0:T(128)S(1)} %pad_add_fusion.1), channel_id=1, source_target_pairs={{0,12},{1,13},{2,14},{3,15},{4,8},{5,9},{6,10},{7,11},{8,4},{9,5},... | collective-permute-start | bytes 152 | tf_op jit(solution)/shard_map/ppermute | solution.py:405
  23.3 2.7 %collective-permute-done.4 = s32[12]{0:T(128)S(1)} collective-permute-done((s32[12]{0:T(128)S(1)}, s32[12]{0:T(128)S(1)}, u32[]{:S(2)}, u32[]{:S(2)}) %collective-permute-start.4) | collective-permute-done | bytes 80 | tf_op jit(solution)/shard_map/ppermute | solution.py:405
  29.8 4.5 %shard_map.300 = (bf16[208,384]{1,0:T(8,128)(2,1)S(1)}, bf16[208,384]{1,0:T(8,128)(2,1)S(1)}, bf16[400,384]{1,0:T(8,128)(2,1)S(1)}, bf16[400,384]{1,0:T(8,128)(2...) custom-call(s32[2]{0:T(128)S(1)} %pad_add_fusion.place_ref, ...), custom_call_target="tpu_custom_call" | custom-call | flops 481689600 | bytes 3912200 | tf_op jit(solution)/shard_map/pallas_call | solution.py:509
  35.4 4.2 %shard_map.299 = (bf16[400,384]{1,0:T(8,128)(2,1)S(1)}, bf16[400,384]{1,0:T(8,128)(2,1)S(1)}, bf16[400,384]{1,0:T(8,128)(2,1)S(1)}, bf16[400,384]{1,0:T(8,128)(2...) custom-call(s32[2]{0:T(128)S(1)} %pad_add_fusion.place_ref, bf16[400,384]{1,0:T(8,128)(2,1)S(1)} %copy-done.11, ...), custom_call_target="tpu_custom_call" | custom-call | flops 599654400 | bytes 4968968 | tf_op jit(solution)/shard_map/pallas_call | solution.py:509
  39.6 8.6 %shard_map.301 = (f32[608,384]{1,0:T(8,128)S(1)}, bf16[608,384]{1,0:T(8,128)(2,1)S(1)}, bf16[608,1536]{1,0:T(8,128)(2,1)}, bf16[608,1536]{1,0:T(8,128)(2,1)}, f3...) custom-call(s32[2]{0:T(128)S(1)} %pad_add_fusion.place_ref, ...), custom_call_target="tpu_custom_call" | custom-call | flops 1613758464 | bytes 10612240 | tf_op jit(solution)/shard_map/pallas_call | solution.py:509
  49.1 8.9 %shard_map.302 = (bf16[608,384]{1,0:T(8,128)(2,1)S(1)}, f32[608,384]{1,0:T(8,128)S(1)}, bf16[608,384]{1,0:T(8,128)(2,1)S(1)}, bf16[4,4,192,128]{3,2,1,0:T(8,128)(2,1)S(1)}, bf16[4,4,192,128]{3,2,1,0:T(8,128)(2,1)}) custom-call(s32[2]{0:T(128)S(1)} %pad_add_fusion.place_ref, f32[608,384]{1,0:T(8,128)S(1)} %get-tuple-element.105.middle_ref, ...), custom_call_target="tpu_custom_call" | custom-call | flops 3227516928 | bytes 12645896 | tf_op jit(solution)/shard_map/pallas_call | solution.py:509
  60.9 3.4 %shard_map.304 = (bf16[400,384]{1,0:T(8,128)(2,1)S(1)}, bf16[400,384]{1,0:T(8,128)(2,1)S(1)}, bf16[400,384]{1,0:T(8,128)(2,1)S(1)}) custom-call(bf16[608,384]{1,0:T(8,128)(2,1)S(1)} %get-tuple-element.112.g_ref, bf16[400,384]{1,0:T(8,128)(2,1)S(1)} %get-tuple-element.98.att_a.att_ref, bf16[400,384]{1,0:T(8,128)(2,1)S(1)} %get-tuple-element.113.q_ref, ...), custom_call_target="tpu_custom_call" | custom-call | flops 491520000 | bytes 4537344 | tf_op jit(solution)/shard_map/pallas_call | solution.py:509
  64.3 3.7 %shard_map.306 = (bf16[768,384]{1,0:T(8,128)(2,1)S(1)}, bf16[4,4,112,128]{3,2,1,0:T(8,128)(2,1)S(1)}, bf16[4,4,112,128]{3,2,1,0:T(8,128)(2,1)S(1)}) custom-call(s32[2]{0:T(128)S(1)} %pad_add_fusion.place_ref, bf16[400,384]{1,0:T(8,128)(2,1)S(1)} %copy-done.13, bf16[400,384]{1,0:T(8,128)(2,1)S(1)} %copy-done.5, bf16[400,384]{1,0:T(8,128)(2,1)S(1)} %get-tuple-element.117.dq_a, ...), custom_call_target="tpu_custom_call" | custom-call | flops 1415577600 | bytes 5649928 | tf_op jit(solution)/shard_map/pallas_call | solution.py:509
  72.4 3.7 %collective-permute-done.26.refs_1_ = bf16[4,192,128]{2,1,0:T(8,128)(2,1)S(1)} collective-permute-done((bf16[4,192,128]{2,1,0:T(8,128)(2,1)S(1)}, bf16[4,192,128]{2,1,0:T(8,128)(2,1)S(1)}, u32[]{:S(2)}, u32[]{:S(2)}) %collective-permute-start.26) | collective-permute-done | bytes 196640 | tf_op jit(solution)/shard_map/ppermute | solution.py:413
  76.1 2.8 %collective-permute-done.27.refs_2_ = bf16[4,192,128]{2,1,0:T(8,128)(2,1)S(1)} collective-permute-done((bf16[4,192,128]{2,1,0:T(8,128)(2,1)S(1)}, bf16[4,192,128]{2,1,0:T(8,128)(2,1)S(1)}, u32[]{:S(2)}, u32[]{:S(2)}) %collective-permute-start.27) | collective-permute-done | bytes 196640 | tf_op jit(solution)/shard_map/ppermute | solution.py:413
  81.4 4.2 %collective-permute-start.30 = (bf16[1,192,128]{2,1,0:T(8,128)(2,1)S(1)}, bf16[1,192,128]{2,1,0:T(8,128)(2,1)S(1)}, u32[]{:S(2)}, u32[]{:S(2)}) collective-permute-start(bf16[1,192,128]{2,1,0:T(8,128)(2,1)S(1)} %get-tuple-element.153), channel_id=1, source_target_pairs={{0,8},{1,9},{2,10},{3,11},{4,12},{5,13},{6,14},{7,15},{8,0},{9,1},... | collective-permute-start | bytes 147464 | tf_op jit(solution)/shard_map/ppermute | solution.py:405
  92.9 5.0 %collective-permute-done.13.refs_2_ = bf16[4,112,128]{2,1,0:T(8,128)(2,1)S(1)} collective-permute-done((bf16[4,112,128]{2,1,0:T(8,128)(2,1)S(1)}, bf16[4,112,128]{2,1,0:T(8,128)(2,1)S(1)}, u32[]{:S(2)}, u32[]{:S(2)}) %collective-permute-start.13) | collective-permute-done | bytes 114720 | tf_op jit(solution)/shard_map/ppermute | solution.py:413
  97.8 3.5 %collective-permute-start.34 = (bf16[1,192,128]{2,1,0:T(8,128)(2,1)S(1)}, bf16[1,192,128]{2,1,0:T(8,128)(2,1)S(1)}, u32[]{:S(2)}, u32[]{:S(2)}) collective-permute-start(bf16[1,192,128]{2,1,0:T(8,128)(2,1)S(1)} %shard_map.314), channel_id=1, source_target_pairs={{0,12},{1,13},{2,14},{3,15},{4,8},{5,9},{6,10},{7,11},{8,4},{9,5},... | collective-permute-start | bytes 147464 | tf_op jit(solution)/shard_map/ppermute | solution.py:405
  103.6 2.9 %collective-permute-start.16 = (bf16[1,112,128]{2,1,0:T(8,128)(2,1)S(1)}, bf16[1,112,128]{2,1,0:T(8,128)(2,1)S(1)}, u32[]{:S(2)}, u32[]{:S(2)}) collective-permute-start(bf16[1,112,128]{2,1,0:T(8,128)(2,1)S(1)} %get-tuple-element.137), channel_id=1, source_target_pairs={{0,8},{1,9},{2,10},{3,11},{4,12},{5,13},{6,14},{7,15},{8,0},{9,1},... | collective-permute-start | bytes 86024 | tf_op jit(solution)/shard_map/ppermute | solution.py:405
  114.8 3.1 %collective-permute-start.48 = (bf16[1,144,128]{2,1,0:T(8,128)(2,1)S(1)}, bf16[1,144,128]{2,1,0:T(8,128)(2,1)S(1)}, u32[]{:S(2)}, u32[]{:S(2)}) collective-permute-start(bf16[1,144,128]{2,1,0:T(8,128)(2,1)S(1)} %shard_map.318), channel_id=1, source_target_pairs={{0,12},{1,13},{2,14},{3,15},{4,8},{5,9},{6,10},{7,11},{8,4},{9,5},... | collective-permute-start | bytes 110600 | tf_op jit(solution)/shard_map/ppermute | solution.py:405
  118.7 5.1 %collective-permute-done.17.refs_3_ = bf16[1,112,128]{2,1,0:T(8,128)(2,1)S(1)} collective-permute-done((bf16[1,112,128]{2,1,0:T(8,128)(2,1)S(1)}, bf16[1,112,128]{2,1,0:T(8,128)(2,1)S(1)}, u32[]{:S(2)}, u32[]{:S(2)}) %collective-permute-start.17) | collective-permute-done | bytes 28704 | tf_op jit(solution)/shard_map/ppermute | solution.py:405
  125.0 3.7 %collective-permute-done.47 = bf16[1,144,128]{2,1,0:T(8,128)(2,1)S(1)} collective-permute-done((bf16[1,144,128]{2,1,0:T(8,128)(2,1)S(1)}, bf16[1,144,128]{2,1,0:T(8,128)(2,1)S(1)}, u32[]{:S(2)}, u32[]{:S(2)}) %collective-permute-start.47) | collective-permute-done | bytes 36896 | tf_op jit(solution)/shard_map/ppermute | solution.py:405
  130.8 3.6 %collective-permute-done.20 = bf16[1,112,128]{2,1,0:T(8,128)(2,1)S(1)} collective-permute-done((bf16[1,112,128]{2,1,0:T(8,128)(2,1)S(1)}, bf16[1,112,128]{2,1,0:T(8,128)(2,1)S(1)}, u32[]{:S(2)}, u32[]{:S(2)}) %collective-permute-start.20) | collective-permute-done | bytes 28704 | tf_op jit(solution)/shard_map/ppermute | solution.py:405
  144.1 8.2 %collective-permute-done.23 = bf16[4,112,128]{2,1,0:T(8,128)(2,1)S(1)} collective-permute-done((bf16[4,112,128]{2,1,0:T(8,128)(2,1)S(1)}, bf16[4,112,128]{2,1,0:T(8,128)(2,1)S(1)}, u32[]{:S(2)}, u32[]{:S(2)}) %collective-permute-start.23) | collective-permute-done | bytes 114720 | tf_op jit(solution)/shard_map/ppermute | solution.py:413
  154.0 11.3 %collective-permute-done.9.got_ref = bf16[608,384]{1,0:T(8,128)(2,1)S(1)} collective-permute-done((bf16[608,384]{1,0:T(8,128)(2,1)S(1)}, bf16[608,384]{1,0:T(8,128)(2,1)S(1)}, u32[]{:S(2)}, u32[]{:S(2)}) %collective-permute-start.9) | collective-permute-done | bytes 466976 | tf_op jit(solution)/shard_map/ppermute | solution.py:598
  165.4 3.2 %shard_map.303 = bf16[3,768,384]{2,1,0:T(8,128)(2,1)} custom-call(s32[2]{0:T(128)S(1)} %pad_add_fusion.place_ref, s32[3,128,8]{2,1,0:T(8,128)S(1)} %get-tuple-element.95.down_ref, bf16[608,384]{1,0:T(8,128)(2,1)S(1)} %get-tuple-element.110.own_ref, bf16[608,384]{1,0:T(8,128)(2,1)S(1)} %collective-permute-done.9.got_ref), custom_call_target="tpu_custom_call" | custom-call | bytes 2715656 | tf_op jit(solution)/shard_map/pallas_call | solution.py:509
  168.6 3.1 %shard_map.307 = bf16[3,768,384]{2,1,0:T(8,128)(2,1)} custom-call(s32[2]{0:T(128)S(1)} %pad_add_fusion.place_ref, s32[3,128,8]{2,1,0:T(8,128)S(1)} %get-tuple-element.95.down_ref, bf16[768,384]{1,0:T(8,128)(2,1)S(1)} %get-tuple-element.128.own_ref, bf16[768,384]{1,0:T(8,128)(2,1)S(1)} %collective-permute-done.10.got_ref), custom_call_target="tpu_custom_call" | custom-call | bytes 2961416 | tf_op jit(solution)/shard_map/pallas_call | solution.py:509
  (183 shorter events, 66.6 us)
Async XLA Ops:
  0.8 15.4 %collective-permute-start.2 = (s32[3]{0:T(128)}, s32[3]{0:T(128)S(1)}, u32[]{:S(2)}, u32[]{:S(2)}) collective-permute-start(s32[3]{0:T(128)} %param.20), channel_id=1, source_target_pairs={{0,3},{1,2},{2,1},{3,0},{4,7},{5,6},{6,5},{7,4},{8,11},{9,10},{10,... | collective-permute-start | bytes 44 | tf_op jit(solution)/shard_map/ppermute | solution.py:405
  3.2 14.7 %collective-permute-start.1 = (s32[3]{0:T(128)}, s32[3]{0:T(128)S(1)}, u32[]{:S(2)}, u32[]{:S(2)}) collective-permute-start(s32[3]{0:T(128)} %param.20), channel_id=1, source_target_pairs={{0,2},{1,3},{2,0},{3,1},{4,6},{5,7},{6,4},{7,5},{8,10},{9,11},{10,... | collective-permute-start | bytes 44 | tf_op jit(solution)/shard_map/ppermute | solution.py:405
  3.9 14.0 %collective-permute-start = (s32[3]{0:T(128)}, s32[3]{0:T(128)S(1)}, u32[]{:S(2)}, u32[]{:S(2)}) collective-permute-start(s32[3]{0:T(128)} %param.20), channel_id=1, source_target_pairs={{0,1},{1,0},{2,3},{3,2},{4,5},{5,4},{6,7},{7,6},{8,9},{9,8},{10,11... | collective-permute-start | bytes 44 | tf_op jit(solution)/shard_map/ppermute | solution.py:405
  10.1 24.1 %collective-permute-start.6 = (bf16[400,384]{1,0:T(8,128)(2,1)}, bf16[400,384]{1,0:T(8,128)(2,1)}, u32[]{:S(2)}, u32[]{:S(2)}) collective-permute-start(bf16[400,384]{1,0:T(8,128)(2,1)} %get-tuple-element.97), channel_id=1, source_target_pairs={{0,16},{16,0},{1,17},{17,1},{2,18},{18,2},{3,19},{19,3},{4,20},{20... | collective-permute-start | bytes 921608 | tf_op jit(solution)/shard_map/ppermute | solution.py:546
  11.8 17.9 %collective-permute-start.7 = (bf16[400,384]{1,0:T(8,128)(2,1)}, bf16[400,384]{1,0:T(8,128)(2,1)}, u32[]{:S(2)}, u32[]{:S(2)}) collective-permute-start(bf16[400,384]{1,0:T(8,128)(2,1)} %get-tuple-element.99.own_ref), channel_id=1, source_target_pairs={{0,16},{16,0},{1,17},{17,1},{2,18},{18,2},{3,19},{19,3},{4,20},{20... | collective-permute-start | bytes 921608 | tf_op jit(solution)/shard_map/ppermute | solution.py:547
  16.2 23.4 %collective-permute-start.8 = (bf16[608,384]{1,0:T(8,128)(2,1)}, bf16[608,384]{1,0:T(8,128)(2,1)S(1)}, u32[]{:S(2)}, u32[]{:S(2)}) collective-permute-start(bf16[608,384]{1,0:T(8,128)(2,1)} %get-tuple-element.104), channel_id=1, source_target_pairs={{0,16},{16,0},{1,17},{17,1},{2,18},{18,2},{3,19},{19,3},{4,20},{20... | collective-permute-start | bytes 1400840 | tf_op jit(solution)/shard_map/ppermute | solution.py:554
  58.0 27.8 %collective-permute-start.39 = (bf16[4,4,144,128]{3,2,1,0:T(8,128)(2,1)}, bf16[4,4,144,128]{3,2,1,0:T(8,128)(2,1)S(1)}, u32[]{:S(2)}, u32[]{:S(2)}) collective-permute-start(bf16[4,4,144,128]{3,2,1,0:T(8,128)(2,1)} %get-tuple-element.162), channel_id=1, source_target_pairs={{0,1},{1,0},{2,3},{3,2},{4,5},{5,4},{6,7},{7,6},{8,9},{9,8},{10,11... | collective-permute-start | bytes 1769480 | tf_op jit(solution)/shard_map/ppermute | solution.py:405
  72.0 14.6 %collective-permute-start.12 = (bf16[4,112,128]{2,1,0:T(8,128)(2,1)S(1)}, bf16[4,112,128]{2,1,0:T(8,128)(2,1)S(1)}, u32[]{:S(2)}, u32[]{:S(2)}) collective-permute-start(bf16[4,112,128]{2,1,0:T(8,128)(2,1)S(1)} %get-tuple-element.132), channel_id=1, source_target_pairs={{0,16},{1,17},{2,18},{3,19},{4,20},{5,21},{6,22},{7,23},{8,24},{9,... | collective-permute-start | bytes 344072 | tf_op jit(solution)/shard_map/ppermute | solution.py:413
  86.0 15.4 %collective-permute-start.40 = (bf16[4,144,128]{2,1,0:T(8,128)(2,1)S(1)}, bf16[4,144,128]{2,1,0:T(8,128)(2,1)S(1)}, u32[]{:S(2)}, u32[]{:S(2)}) collective-permute-start(bf16[4,144,128]{2,1,0:T(8,128)(2,1)S(1)} %get-tuple-element.164), channel_id=1, source_target_pairs={{0,16},{1,17},{2,18},{3,19},{4,20},{5,21},{6,22},{7,23},{8,24},{9,... | collective-permute-start | bytes 442376 | tf_op jit(solution)/shard_map/ppermute | solution.py:413
  86.6 11.3 %collective-permute-start.13 = (bf16[4,112,128]{2,1,0:T(8,128)(2,1)S(1)}, bf16[4,112,128]{2,1,0:T(8,128)(2,1)S(1)}, u32[]{:S(2)}, u32[]{:S(2)}) collective-permute-start(bf16[4,112,128]{2,1,0:T(8,128)(2,1)S(1)} %get-tuple-element.133), channel_id=1, source_target_pairs={{0,2},{1,3},{2,0},{3,1},{4,6},{5,7},{6,4},{7,5},{8,10},{9,11},{10,... | collective-permute-start | bytes 344072 | tf_op jit(solution)/shard_map/ppermute | solution.py:413
  87.9 13.4 %collective-permute-start.14 = (bf16[4,112,128]{2,1,0:T(8,128)(2,1)S(1)}, bf16[4,112,128]{2,1,0:T(8,128)(2,1)S(1)}, u32[]{:S(2)}, u32[]{:S(2)}) collective-permute-start(bf16[4,112,128]{2,1,0:T(8,128)(2,1)S(1)} %get-tuple-element.134), channel_id=1, source_target_pairs={{0,18},{1,19},{2,16},{3,17},{4,22},{5,23},{6,20},{7,21},{8,26},{9,... | collective-permute-start | bytes 344072 | tf_op jit(solution)/shard_map/ppermute | solution.py:413
  89.5 12.8 %collective-permute-start.41 = (bf16[4,144,128]{2,1,0:T(8,128)(2,1)S(1)}, bf16[4,144,128]{2,1,0:T(8,128)(2,1)S(1)}, u32[]{:S(2)}, u32[]{:S(2)}) collective-permute-start(bf16[4,144,128]{2,1,0:T(8,128)(2,1)S(1)} %get-tuple-element.165), channel_id=1, source_target_pairs={{0,2},{1,3},{2,0},{3,1},{4,6},{5,7},{6,4},{7,5},{8,10},{9,11},{10,... | collective-permute-start | bytes 442376 | tf_op jit(solution)/shard_map/ppermute | solution.py:413
  91.5 12.1 %collective-permute-start.42 = (bf16[4,144,128]{2,1,0:T(8,128)(2,1)S(1)}, bf16[4,144,128]{2,1,0:T(8,128)(2,1)S(1)}, u32[]{:S(2)}, u32[]{:S(2)}) collective-permute-start(bf16[4,144,128]{2,1,0:T(8,128)(2,1)S(1)} %get-tuple-element.166), channel_id=1, source_target_pairs={{0,18},{1,19},{2,16},{3,17},{4,22},{5,23},{6,20},{7,21},{8,26},{9,... | collective-permute-start | bytes 442376 | tf_op jit(solution)/shard_map/ppermute | solution.py:413
  102.3 12.5 %collective-permute-start.15 = (bf16[1,112,128]{2,1,0:T(8,128)(2,1)S(1)}, bf16[1,112,128]{2,1,0:T(8,128)(2,1)S(1)}, u32[]{:S(2)}, u32[]{:S(2)}) collective-permute-start(bf16[1,112,128]{2,1,0:T(8,128)(2,1)S(1)} %get-tuple-element.136), channel_id=1, source_target_pairs={{0,4},{1,5},{2,6},{3,7},{4,0},{5,1},{6,2},{7,3},{8,12},{9,13},{10,... | collective-permute-start | bytes 86024 | tf_op jit(solution)/shard_map/ppermute | solution.py:405
  103.6 14.2 %collective-permute-start.16 = (bf16[1,112,128]{2,1,0:T(8,128)(2,1)S(1)}, bf16[1,112,128]{2,1,0:T(8,128)(2,1)S(1)}, u32[]{:S(2)}, u32[]{:S(2)}) collective-permute-start(bf16[1,112,128]{2,1,0:T(8,128)(2,1)S(1)} %get-tuple-element.137), channel_id=1, source_target_pairs={{0,8},{1,9},{2,10},{3,11},{4,12},{5,13},{6,14},{7,15},{8,0},{9,1},... | collective-permute-start | bytes 86024 | tf_op jit(solution)/shard_map/ppermute | solution.py:405
  111.1 23.3 %collective-permute-start.37 = (bf16[4,192,128]{2,1,0:T(8,128)(2,1)S(1)}, bf16[4,192,128]{2,1,0:T(8,128)(2,1)S(1)}, u32[]{:S(2)}, u32[]{:S(2)}) collective-permute-start(bf16[4,192,128]{2,1,0:T(8,128)(2,1)S(1)} %maximum_bitcast_fusion), channel_id=1, source_target_pairs={{0,18},{1,19},{2,16},{3,17},{4,22},{5,23},{6,20},{7,21},{8,26},{9,... | collective-permute-start | bytes 589832 | tf_op jit(solution)/shard_map/ppermute | solution.py:413
  112.6 23.0 %collective-permute-start.36 = (bf16[4,192,128]{2,1,0:T(8,128)(2,1)S(1)}, bf16[4,192,128]{2,1,0:T(8,128)(2,1)S(1)}, u32[]{:S(2)}, u32[]{:S(2)}) collective-permute-start(bf16[4,192,128]{2,1,0:T(8,128)(2,1)S(1)} %maximum_bitcast_fusion), channel_id=1, source_target_pairs={{0,2},{1,3},{2,0},{3,1},{4,6},{5,7},{6,4},{7,5},{8,10},{9,11},{10,... | collective-permute-start | bytes 589832 | tf_op jit(solution)/shard_map/ppermute | solution.py:413
  114.1 22.9 %collective-permute-start.35 = (bf16[4,192,128]{2,1,0:T(8,128)(2,1)S(1)}, bf16[4,192,128]{2,1,0:T(8,128)(2,1)S(1)}, u32[]{:S(2)}, u32[]{:S(2)}) collective-permute-start(bf16[4,192,128]{2,1,0:T(8,128)(2,1)S(1)} %maximum_bitcast_fusion), channel_id=1, source_target_pairs={{0,16},{1,17},{2,18},{3,19},{4,20},{5,21},{6,22},{7,23},{8,24},{9,... | collective-permute-start | bytes 589832 | tf_op jit(solution)/shard_map/ppermute | solution.py:413
  138.0 30.6 %collective-permute-start.10 = (bf16[768,384]{1,0:T(8,128)(2,1)S(1)}, bf16[768,384]{1,0:T(8,128)(2,1)S(1)}, u32[]{:S(2)}, u32[]{:S(2)}) collective-permute-start(bf16[768,384]{1,0:T(8,128)(2,1)S(1)} %get-tuple-element.128.own_ref), channel_id=1, source_target_pairs={{0,16},{16,0},{1,17},{17,1},{2,18},{18,2},{3,19},{19,3},{4,20},{20... | collective-permute-start | bytes 1769480 | tf_op jit(solution)/shard_map/ppermute | solution.py:620
  139.3 36.5 %collective-permute-start.38 = (bf16[4,4,192,128]{3,2,1,0:T(8,128)(2,1)S(1)}, bf16[4,4,192,128]{3,2,1,0:T(8,128)(2,1)S(1)}, u32[]{:S(2)}, u32[]{:S(2)}) collective-permute-start(bf16[4,4,192,128]{3,2,1,0:T(8,128)(2,1)S(1)} %pad_maximum_fusion.own_ref), channel_id=1, source_target_pairs={{0,1},{1,0},{2,3},{3,2},{4,5},{5,4},{6,7},{7,6},{8,9},{9,8},{10,11... | collective-permute-start | bytes 2359304 | tf_op jit(solution)/shard_map/ppermute | solution.py:405
  140.5 11.7 %collective-permute-start.23 = (bf16[4,112,128]{2,1,0:T(8,128)(2,1)S(1)}, bf16[4,112,128]{2,1,0:T(8,128)(2,1)S(1)}, u32[]{:S(2)}, u32[]{:S(2)}) collective-permute-start(bf16[4,112,128]{2,1,0:T(8,128)(2,1)S(1)} %maximum_bitcast_fusion.2), channel_id=1, source_target_pairs={{0,18},{1,19},{2,16},{3,17},{4,22},{5,23},{6,20},{7,21},{8,26},{9,... | collective-permute-start | bytes 344072 | tf_op jit(solution)/shard_map/ppermute | solution.py:413
  152.3 21.3 %collective-permute-start.52 = (bf16[4,4,144,128]{3,2,1,0:T(8,128)(2,1)S(1)}, bf16[4,4,144,128]{3,2,1,0:T(8,128)(2,1)S(1)}, u32[]{:S(2)}, u32[]{:S(2)}) collective-permute-start(bf16[4,4,144,128]{3,2,1,0:T(8,128)(2,1)S(1)} %pad_maximum_fusion.1.own_ref), channel_id=1, source_target_pairs={{0,1},{1,0},{2,3},{3,2},{4,5},{5,4},{6,7},{7,6},{8,9},{9,8},{10,11... | collective-permute-start | bytes 1769480 | tf_op jit(solution)/shard_map/ppermute | solution.py:405
  152.3 13.1 %collective-permute-start.9 = (bf16[608,384]{1,0:T(8,128)(2,1)S(1)}, bf16[608,384]{1,0:T(8,128)(2,1)S(1)}, u32[]{:S(2)}, u32[]{:S(2)}) collective-permute-start(bf16[608,384]{1,0:T(8,128)(2,1)S(1)} %get-tuple-element.110.own_ref), channel_id=1, source_target_pairs={{0,16},{16,0},{1,17},{17,1},{2,18},{18,2},{3,19},{19,3},{4,20},{20... | collective-permute-start | bytes 1400840 | tf_op jit(solution)/shard_map/ppermute | solution.py:598
  153.8 17.9 %collective-permute-start.24 = (bf16[4,4,112,128]{3,2,1,0:T(8,128)(2,1)S(1)}, bf16[4,4,112,128]{3,2,1,0:T(8,128)(2,1)S(1)}, u32[]{:S(2)}, u32[]{:S(2)}) collective-permute-start(bf16[4,4,112,128]{3,2,1,0:T(8,128)(2,1)S(1)} %pad_maximum_fusion.2.own_ref), channel_id=1, source_target_pairs={{0,1},{1,0},{2,3},{3,2},{4,5},{5,4},{6,7},{7,6},{8,9},{9,8},{10,11... | collective-permute-start | bytes 1376264 | tf_op jit(solution)/shard_map/ppermute | solution.py:405
  (55 other events, 407.0 us)

commit v2 on v1

--- a/solution.py
+++ b/solution.py
@@ -93,34 +93,47 @@
     return jnp.concatenate([ones_where(wide == rank[b : b + 1, :]) for b in range(rank.shape[0])], axis=1)
 
 
-def prep_tokens_kernel(unmasked, place_ref, masked_ref, tokens_ref, mine_ref, theirs_ref, shared_ref, rank_ref):
+def prep_theirs_kernel(unmasked, place_ref, masked_ref, tokens_ref, theirs_ref, rank_ref, half_ref, arrived):
+    copy = 1 - place_ref[0]
+    load = pltpu.make_async_copy(tokens_ref.at[copy], half_ref, arrived)
+    load.start()
+    half = tokens_ref.shape[1]
+    rank = ranks(masked_ref[pl.ds(copy, 1), :], place_ref[0], half, unmasked)
+    rank_ref[...] = jnp.concatenate([rank, jnp.zeros((8 - rank.shape[0], LANES), jnp.int32)], axis=0)
+    chosen = picks(rank, iota((unmasked + EXTRA, 1), 0))
+    load.wait()
+    theirs_ref[...] = dot(chosen, half_ref[...]).astype(BF)
+
+
+def prep_tokens_kernel(unmasked, place_ref, masked_ref, tokens_ref, shared_ref, mine_ref, rank_ref):
     tm = place_ref[0]
     half = tokens_ref.shape[1]
-    rows = unmasked + EXTRA
-    labels = iota((rows, 1), 0)
-    for role, (copy, out_ref) in enumerate(((1 - tm, theirs_ref), (2, shared_ref), (tm, mine_ref))):
-        rank = ranks(masked_ref[copy], tm, half, unmasked)
+    labels = iota((unmasked + EXTRA, 1), 0)
+    for role, (copy, out_ref) in enumerate(((2, shared_ref), (tm, mine_ref))):
+        rank = ranks(masked_ref[pl.ds(copy, 1), :], tm, half, unmasked)
         rank_ref[role] = jnp.concatenate([rank, jnp.zeros((8 - rank.shape[0], LANES), jnp.int32)], axis=0)
         out_ref[...] = dot(picks(rank, labels), tokens_ref[copy]).astype(BF)
 
 
-def prep_grads_kernel(unmasked, place_ref, masked_ref, rank_ref, cotangent_ref, keep_ref, send_ref, down_ref):
+def prep_grads_kernel(
+    unmasked, place_ref, masked_ref, rank_theirs_ref, rank_ref, cotangent_ref, keep_ref, send_ref, down_ref
+):
     tm = place_ref[0]
     half = cotangent_ref.shape[1]
     blocks = half // LANES
     rows = unmasked + EXTRA
     part = unmasked // 2
     labels = iota((rows, 1), 0)
-    send_ref[:rows, :] = dot(picks(rank_ref[0, :blocks], labels), cotangent_ref[1 - tm]).astype(BF)
-    rank = rank_ref[1, :blocks]
+    send_ref[:rows, :] = dot(picks(rank_theirs_ref[:blocks], labels), cotangent_ref[1 - tm]).astype(BF)
+    rank = rank_ref[0, :blocks]
     small = iota((part + EXTRA, 1), 0)
     theirs = jnp.where(small < part, small + part * (1 - tm), -1)
     send_ref[rows:, :] = dot(picks(rank, theirs), cotangent_ref[2]).astype(BF)
     own = jnp.where(small < part, small + part * tm, small + part)
     keep_ref[rows:, :] = dot(picks(rank, own), cotangent_ref[2]).astype(BF)
-    keep_ref[:rows, :] = dot(picks(rank_ref[2, :blocks], labels), cotangent_ref[tm]).astype(BF)
+    keep_ref[:rows, :] = dot(picks(rank_ref[1, :blocks], labels), cotangent_ref[tm]).astype(BF)
     for role, copy in enumerate((1 - tm, 2, tm)):
-        down = ranks_down(masked_ref[copy], tm, half, unmasked)
+        down = ranks_down(masked_ref[pl.ds(copy, 1), :], tm, half, unmasked)
         down_ref[role] = jnp.concatenate([down, jnp.zeros((LANES, 8 - blocks), jnp.int32)], axis=1)
 
 
@@ -190,12 +203,12 @@
     return jnp.concatenate([ref[...] for ref in refs], axis=0)
 
 
-def scatter_chunks(me, stage_ref, keep_ref, send_ref):
-    depth = keep_ref.shape[2]
+def scatter_chunks(me, stage_ref, keep_ref, send_ref, into=0):
+    depth = keep_ref.shape[2] - into
     for rel in range(2 * 4 * keep_ref.shape[1]):
         first = pl.multiple_of((me ^ rel) * depth, 16)
         target = send_ref if rel & 1 else keep_ref
-        target[(rel >> 1) & 3, rel >> 3] = stage_ref[pl.ds(first, depth), :]
+        target[(rel >> 1) & 3, rel >> 3, into:] = stage_ref[pl.ds(first, depth), :]
 
 
 def stage_weight(stage_ref, first, grad):
@@ -223,7 +236,7 @@
 
 
 def up_kernel(
-    place_ref, weight_ref, att_a, att_b, x_a, x_b, cot_own, cot_got, small_ref, bias_up_ref, w_proj_ref, w_up_ref,
+    place_ref, groups_ref, everyone_ref, att_a, att_b, x_a, x_b, cot_own, cot_got, small_ref, bias_up_ref, w_proj_ref, w_up_ref,
     middle_ref, normed_ref, active_ref, slope_ref, upstream_ref, keep_ref, send_ref, stage_ref
 ):
     rows_a, width = x_a.shape
@@ -235,7 +248,14 @@
     hat, _ = normalise(middle)
     normed = (hat * small_ref[6:7, :] + small_ref[7:8, :]).astype(BF)
     normed_ref[...] = normed
-    weight = jnp.where(iota((total, 1), 0) < rows_a, weight_ref[0], weight_ref[1])
+    everyone = everyone_ref[...]
+
+    def weight_of(group):
+        return 1.0 / jnp.sum(jnp.where(everyone == group, 1.0, 0.0), axis=1, keepdims=True)
+
+    weight = jnp.where(
+        iota((total, 1), 0) < rows_a, weight_of(groups_ref[place_ref[0]]), weight_of(groups_ref[2])
+    )
     upstream = (cot_own[...].astype(F32) + cot_got[...].astype(F32)) * weight
     upstream_ref[...] = upstream
     grad_result = upstream.astype(BF)
@@ -312,6 +332,7 @@
 
 def inputs_back_kernel(
     unmasked, place_ref, x_a, x_b, dq_a, dq_b, dk_a, dk_b, dv_a, dv_b, grad_middle_ref, small_ref, w_ref,
+    keep_one, send_one, keep_two, send_two,
     grad_ref, keep_ref, send_ref, stage_ref
 ):
     rows, width = x_a.shape
@@ -345,7 +366,12 @@
     )
     end = stage_rows(stage_ref, end, vectors)
     clear_rest(stage_ref, end)
-    scatter_chunks(place_ref[1], stage_ref, keep_ref, send_ref)
+    one, two = keep_one.shape[2], keep_two.shape[2]
+    keep_ref[:, :, :one] = keep_one[...]
+    send_ref[:, :, :one] = send_one[...]
+    keep_ref[:, :, one : one + two] = keep_two[...]
+    send_ref[:, :, one : one + two] = send_two[...]
+    scatter_chunks(place_ref[1], stage_ref, keep_ref, send_ref, one + two)
 
 
 def place_back(down, rows, half):
@@ -413,7 +439,7 @@
     return lax.ppermute(values, ("tm", "clip"), pairs)
 
 
-def sum_over_devices(keep, send):
+def sum_over_devices(keep, send, beside_near, send_far, beside_last):
     far = []
     distance = 4
     while distance < lax.axis_size("clip"):
@@ -423,38 +449,53 @@
     got = clip_swap(send, 1)
     pieces = plain(fold_kernel, [shape(groups, depth, LANES)] * 4)(keep, got)
     pieces = [pieces[0]] + [near_swap(pieces[step], step) for step in (1, 2, 3)]
+    first = beside_near()
+    *pieces, first = lax.optimization_barrier((*pieces, first))
     left = groups
+    sent = None
     for distance in far:
         left //= 4
         pieces = plain(fold_four_kernel, [shape(left, depth, LANES)] * 4)(*pieces)
+        if sent is None:
+            sent, pieces = send_far(pieces)
         pieces = [pieces[0]] + [clip_swap(pieces[step], step * distance) for step in (1, 2, 3)]
     total = plain(fold_four_kernel, shape(left, depth, LANES))(*pieces)
     for distance in reversed(far):
         pieces = [total] + [clip_swap(total, step * distance) for step in (1, 2, 3)]
         total = jnp.stack(pieces, axis=1).reshape(-1, depth, LANES)
+    total, sent = lax.optimization_barrier((total, sent))
     pieces = [total] + [near_swap(total, step) for step in (1, 2, 3)]
+    last = beside_last(sent)
+    *pieces, last = lax.optimization_barrier((*pieces, last))
     total = jnp.stack(pieces)
-    return total, clip_swap(total, 1)
-
-
-def gather_chunks(me, own_ref, got_ref, stage_ref):
-    depth = own_ref.shape[2]
+    return total, clip_swap(total, 1), first, last
+
+
+def gather_chunks(me, own_ref, got_ref, stage_ref, start, depth):
     for rel in range(2 * 4 * own_ref.shape[1]):
         first = pl.multiple_of((me ^ rel) * depth, 16)
         source = got_ref if rel & 1 else own_ref
-        stage_ref[pl.ds(first, depth), :] = source[(rel >> 1) & 3, rel >> 3]
-
-
-def unstage_kernel(weights, vectors, place_ref, own_ref, got_ref, *refs):
-    outs, stage_ref = refs[:-1], refs[-1]
-    gather_chunks(place_ref[1], own_ref, got_ref, stage_ref)
+        stage_ref[pl.ds(first, depth), :] = source[(rel >> 1) & 3, rel >> 3, start : start + depth]
+
+
+def unstage_kernel(units, place_ref, own_ref, got_ref, *refs):
+    stage_ref = refs[-1]
+    start = at = 0
+    for depth, weights, vectors in units:
+        gather_chunks(place_ref[1], own_ref, got_ref, stage_ref, start, depth)
+        unstage(weights, stage_ref, refs[at : at + weights + vectors])
+        start += depth
+        at += weights + vectors
+
+
+def unstage(weights, stage_ref, outs):
     first = 0
     for out_ref in outs[:weights]:
         depth, width = out_ref.shape
         for block in range(width // LANES):
             out_ref[:, block * LANES : (block + 1) * LANES] = stage_ref[first : first + depth, :].astype(F32)
             first += depth
-    if vectors:
+    if len(outs) > weights:
         count = sum(ref.shape[0] // LANES for ref in outs[weights:])
         rows = stage_ref[first : first + count + -count % 16, :].astype(F32)
         at = 0
@@ -504,53 +545,68 @@
     smem = pl.BlockSpec(memory_space=pltpu.SMEM)
     swap = functools.partial(lax.ppermute, axis_name="tm", perm=[(0, 1), (1, 0)])
 
-    def run(kernel, args, outs, scratch=(), scalars=1, limit=48, flops=0):
+    def run(kernel, args, outs, scratch=(), scalars=1, limit=48, flops=0, anywhere=()):
         moved = sum(math.prod(a.shape) * a.dtype.itemsize for a in list(args) + jax.tree.leaves(outs))
         return pl.pallas_call(
             kernel,
             out_shape=outs,
-            in_specs=[smem] * scalars + [VMEM] * (len(args) - scalars),
+            in_specs=[
+                smem if at < scalars else pl.BlockSpec(memory_space=pl.ANY) if at in anywhere else VMEM
+                for at in range(len(args))
+            ],
             out_specs=jax.tree.map(lambda _: VMEM, outs),
             scratch_shapes=list(scratch),
             compiler_params=pltpu.CompilerParams(vmem_limit_bytes=limit << 20),
             cost_estimate=pl.CostEstimate(flops=flops, bytes_accessed=moved, transcendentals=0),
         )(*args)
 
-    def chunked(count):
-        depth = chunk_rows(count, devices)
+    counts = (width // LANES * hidden, hidden // LANES * width + width // LANES * width + 32, 3 * width // LANES * width + 16)
+    depths = [chunk_rows(count, devices) for count in counts]
+
+    def chunked(unit, together=False):
+        depth = sum(depths) if together else depths[unit]
         halves = [shape(4, devices // 8, depth, LANES)] * 2
-        return halves, [pltpu.VMEM((devices * depth, LANES), BF)]
-
-    masked = masked.reshape(copies, 1, hide)
+        return halves, [pltpu.VMEM((devices * depths[unit], LANES), BF)]
+
     small = jnp.stack(
         [mask_token, gain_one, shift_one, q_bias, v_bias, b_proj, gain_two, shift_two, b_down]
     ).astype(F32)
     bias_up = b_up.astype(F32).reshape(1, hidden)
 
-    everyone = groups
-    distance = 1
-    while distance < clips:
-        everyone = jnp.concatenate([everyone] + [clip_swap(everyone, step * distance) for step in (1, 2, 3)])
-        distance *= 4
-    counts = jnp.sum((groups[:, None] == everyone[None, :]).astype(F32), axis=1)
-    weighting = 1.0 / counts
-    weighting = jnp.stack([jnp.where(tm == 0, weighting[0], weighting[1]), weighting[2]])
-
     block = shape(rows, width)
-    mine, theirs, shared, rank = run(
+    everyone = jnp.concatenate([groups, clip_swap(groups, 1)])
+    theirs, rank_theirs = run(
+        functools.partial(prep_theirs_kernel, unmasked),
+        (place, masked, tokens),
+        [block, shape(8, LANES, kind=jnp.int32)],
+        [pltpu.VMEM((half, width), BF), pltpu.SemaphoreType.DMA],
+        flops=2 * rows * half * width,
+        anywhere=(2,),
+    )
+    everyone, theirs = lax.optimization_barrier((everyone, theirs))
+    got_mine = swap(theirs)
+    shared, mine, rank = run(
         functools.partial(prep_tokens_kernel, unmasked),
         (place, masked, tokens),
-        [block, block, block, shape(copies, 8, LANES, kind=jnp.int32)],
-        flops=2 * copies * rows * half * width,
-    )
-    got_mine = swap(theirs)
+        [block, block, shape(2, 8, LANES, kind=jnp.int32)],
+        flops=4 * rows * half * width,
+    )
     got_shared = swap(shared)
+    everyone, shared = lax.optimization_barrier((everyone, shared))
+    everyone = jnp.concatenate([everyone, clip_swap(everyone, 2)])
     cot_own, cot_send, down = run(
         functools.partial(prep_grads_kernel, unmasked),
-        (place, masked, rank, cotangent),
+        (place, masked, rank_theirs, rank, cotangent),
         [shape(total, width), shape(total, width), shape(copies, LANES, 8, kind=jnp.int32)],
         flops=2 * copies * rows * half * width,
     )
+    everyone, cot_send = lax.optimization_barrier((everyone, cot_send))
+    everyone = jnp.concatenate([everyone, clip_swap(everyone, 4)])
+    everyone, got_mine = lax.optimization_barrier((everyone, got_mine))
+    distance = 8
+    while distance < clips:
+        everyone = jnp.concatenate([everyone, clip_swap(everyone, distance)])
+        distance *= 2
     cot_got = swap(cot_send)
 
     def attend(own, got, split):
@@ -571,10 +627,10 @@
     x_a, q_a, k_a, v_a, p_a, att_a = attend(mine, got_mine, False)
     x_b, q_b, k_b, v_b, p_b, att_b, x_whole = attend(shared, got_shared, True)
 
-    halves, stage = chunked(width // LANES * hidden)
-    middle, normed_two, active, slope, upstream, keep, send = run(
+    halves, stage = chunked(0)
+    middle, normed_two, active, slope, upstream, keep_one, send_one = run(
         up_kernel,
-        (place, weighting, att_a, att_b, x_a, x_b, cot_own, cot_got, small, bias_up, w_proj, w_up),
+        (place, groups, everyone.reshape(1, -1), att_a, att_b, x_a, x_b, cot_own, cot_got, small, bias_up, w_proj, w_up),
         [
             shape(total, width, kind=F32), shape(total, width), shape(total, hidden), shape(total, hidden),
             shape(total, width, kind=F32),
@@ -584,17 +640,15 @@
         scalars=2,
         flops=2 * total * width * (width + 2 * hidden),
     )
-    down_sums = sum_over_devices(keep, send)
-
-    halves, stage = chunked(hidden // LANES * width + width // LANES * width + 32)
-    out_rows, grad_middle, grad_att, keep, send = run(
+
+    halves, stage = chunked(1)
+    out_rows, grad_middle, grad_att, keep_two, send_two = run(
         down_kernel,
         (place, middle, normed_two, active, slope, upstream, att_a, att_b, small, w_proj, w_up, w_down),
         [shape(total, width), shape(total, width, kind=F32), shape(total, width)] + halves,
         stage,
         flops=2 * total * width * (2 * width + 4 * hidden),
     )
-    up_sums = sum_over_devices(keep, send)
     out_got = swap(out_rows)
 
     def attend_back(row_from, att, q, k, v, p):
@@ -608,40 +662,47 @@
 
     dq_a, dk_a, dv_a = attend_back(0, att_a, q_a, k_a, v_a, p_a)
     dq_b, dk_b, dv_b = attend_back(rows, att_b, q_b, k_b, v_b, p_b)
-    halves, stage = chunked(3 * width // LANES * width + 16)
+    halves, stage = chunked(2, True)
     grad_rows, keep, send = run(
         functools.partial(inputs_back_kernel, unmasked),
-        (place, x_a, x_whole, dq_a, dq_b, dk_a, dk_b, dv_a, dv_b, grad_middle, small, w_qkv),
+        (place, x_a, x_whole, dq_a, dq_b, dk_a, dk_b, dv_a, dv_b, grad_middle, small, w_qkv, keep_one, send_one, keep_two, send_two),
         [shape(2 * unmasked, width)] + halves,
         stage,
         flops=2 * 2 * rows * width * 6 * width,
     )
-    in_sums = sum_over_devices(keep, send)
-    grad_got = swap(grad_rows)
-
-    block_out = run(
-        functools.partial(outputs_kernel, unmasked), (place, down, out_rows, out_got), shape(*tokens.shape)
-    )
-    grad_tokens = run(
-        functools.partial(grads_out_kernel, unmasked), (place, down, grad_rows, grad_got), shape(*tokens.shape)
-    )
-
-    def unstage(sums, weights, vectors):
-        depth = sums[0].shape[2]
-        outs = [shape(*dims, kind=F32) for dims in weights] + [shape(dim, kind=F32) for dim in vectors]
-        return run(
-            functools.partial(unstage_kernel, len(weights), len(vectors)),
-            (place,) + tuple(sums),
-            outs,
-            [pltpu.VMEM((devices * depth, LANES), BF)],
-        )
-
-    (grad_w_down,) = unstage(down_sums, [(hidden, width)], [])
-    grad_w_up, grad_w_proj, grad_b_up, grad_gain_two, grad_shift_two, grad_b_proj, grad_b_down = unstage(
-        up_sums, [(width, hidden), (width, width)], [hidden, width, width, width, width]
-    )
-    grad_w_qkv, grad_q_bias, grad_v_bias, grad_gain_one, grad_shift_one, grad_mask_token = unstage(
-        in_sums, [(width, 3 * width)], [width] * 5
+    send, out_got = lax.optimization_barrier((send, out_got))
+
+    def place_outputs():
+        return run(functools.partial(outputs_kernel, unmasked), (place, down, out_rows, out_got), shape(*tokens.shape))
+
+    def send_grads(pieces):
+        *pieces, now = lax.optimization_barrier((*pieces, grad_rows))
+        return swap(now), pieces
+
+    def place_grads(got):
+        return run(functools.partial(grads_out_kernel, unmasked), (place, down, grad_rows, got), shape(*tokens.shape))
+
+    sums_own, sums_got, block_out, grad_tokens = sum_over_devices(
+        keep, send, place_outputs, send_grads, place_grads
+    )
+
+    vector = shape(width, kind=F32)
+    outs = [
+        shape(hidden, width, kind=F32),
+        shape(width, hidden, kind=F32), shape(width, width, kind=F32), shape(hidden, kind=F32),
+        vector, vector, vector, vector,
+        shape(width, 3 * width, kind=F32), vector, vector, vector, vector, vector,
+    ]
+    units = tuple(zip(depths, (1, 2, 1), (0, 5, 5)))
+    (
+        grad_w_down,
+        grad_w_up, grad_w_proj, grad_b_up, grad_gain_two, grad_shift_two, grad_b_proj, grad_b_down,
+        grad_w_qkv, grad_q_bias, grad_v_bias, grad_gain_one, grad_shift_one, grad_mask_token,
+    ) = run(
+        functools.partial(unstage_kernel, units),
+        (place, sums_own, sums_got),
+        outs,
+        [pltpu.VMEM((devices * max(depths), LANES), BF)],
     )
     return (
         block_out,

time: 179 us -> 156 us (0.87)
  starting transfers between devices: 57.3 us -> 29.2 us
  waiting for transfers between devices: 55.1 us -> 59.2 us
  local copies, waits for them, and re-layouts: 6.56 us -> 9.86 us
    ppermute x30 -> x12, starting transfers between devices: 31.2 us -> 15.7 us  [clip_swap(): lax.ppermute(values, 'clip', [(i, i ^ distance) for i in range(size)])]
    ppermute x18 -> x6, starting transfers between devices: 19.8 us -> 7.11 us  [near_swap(): return lax.ppermute(values, ('tm', 'clip'), pairs)]
    ppermute x1, waiting for transfers between devices: 11.3 us -> 0.01 us  [body(): out_got = swap(out_rows)]
    ppermute x18 -> x6, waiting for transfers between devices: 23.6 us -> 32.3 us  [near_swap(): return lax.ppermute(values, ('tm', 'clip'), pairs)]
    ppermute x30 -> x12, waiting for transfers between devices: 20.2 us -> 26.9 us  [clip_swap(): lax.ppermute(values, 'clip', [(i, i ^ distance) for i in range(size)])]
    unnamed x52, local copies, waits for them, and re-layouts: 5.04 us -> 9.75 us
    ppermute x1, starting transfers between devices: 0.31 us -> 2.58 us  [body(): got_shared = swap(shared)]
    pallas_call x14 -> x13, Pallas kernels: 54.5 us -> 55.4 us  [run(): pl.pallas_call(kernel, out_shape=outs, in_specs=[smem if at < scalars els...]
  transfers between devices with their start and end apart: 53 -> 23, of which waited for: 16 -> 12; matrix products, arithmetic and copies ran while one was open for 2% -> 0% of each run, Pallas kernels for 20% -> 22%
where the time goes in v2:
time: 156 us
  waiting for transfers between devices  59.2 us (38%)
  Pallas kernels  56.1 us (36%)
  starting transfers between devices  29.2 us (19%)
  local copies, waits for them, and re-layouts  9.86 us (6%)
    pallas_call x13, Pallas kernels, run(): pl.pallas_call(kernel, out_shape=outs, in_specs=[smem if at < scalars els...  55.4 us
    ppermute x6, waiting for transfers between devices, near_swap(): return lax.ppermute(values, ('tm', 'clip'), pairs)  32.3 us
    ppermute x12, waiting for transfers between devices, clip_swap(): lax.ppermute(values, 'clip', [(i, i ^ distance) for i in range(size)])  26.9 us
    ppermute x12, starting transfers between devices, clip_swap(): lax.ppermute(values, 'clip', [(i, i ^ distance) for i in range(size)])  15.7 us
    unnamed x52, local copies, waits for them, and re-layouts  9.75 us
    ppermute x6, starting transfers between devices, near_swap(): return lax.ppermute(values, ('tm', 'clip'), pairs)  7.11 us
  transfers between devices with their start and end apart: 23, of which 12 were waited for; matrix products, arithmetic and copies ran while one was open for 0% of the time, Pallas kernels for 22%

profile of v2, /device:TPU:0, one launch (start us, length us, event | category | flops | bytes accessed | tf_op | source)
XLA Modules:
  0.0 156.1 jit_solution(10068462216187630792)
XLA Ops:
  3.4 2.4 %shard_map.297 = (bf16[400,384]{1,0:T(8,128)(2,1)}, bf16[400,384]{1,0:T(8,128)(2,1)S(1)}, s32[2,8,128]{2,1,0:T(8,128)S(1)}) custom-call(s32[2]{0:T(128)S(1)} %pad_add_fusion.place_ref, s32[3,1152]{1,0:T(4,128)S(1)} %copy-done.4, bf16[3,768,384]{2,1,0:T(8,128)(2,1)S(1)} %copy-done), custom_call_target="tpu_custom_call" | custom-call | flops 471859200 | bytes 2405896 | tf_op jit(solution)/shard_map/pallas_call | solution.py:550
  6.7 2.6 %collective-permute-start.4 = (bf16[400,384]{1,0:T(8,128)(2,1)}, bf16[400,384]{1,0:T(8,128)(2,1)}, u32[]{:S(2)}, u32[]{:S(2)}) collective-permute-start(bf16[400,384]{1,0:T(8,128)(2,1)} %get-tuple-element.119.own_ref), channel_id=1, source_target_pairs={{0,16},{16,0},{1,17},{17,1},{2,18},{18,2},{3,19},{19,3},{4,20},{20... | collective-permute-start | bytes 921608 | tf_op jit(solution)/shard_map/ppermute | solution.py:594
  9.2 2.6 %shard_map.298 = (bf16[400,384]{1,0:T(8,128)(2,1)}, s32[8,128]{1,0:T(8,128)S(1)}) custom-call(s32[2]{0:T(128)S(1)} %pad_add_fusion.place_ref, s32[3,1152]{1,0:T(4,128)S(1)} %copy-done.4, bf16[3,768,384]{2,1,0:T(8,128)(2,1)S(1)} %copy-done), custom_call_target="tpu_custom_call" | custom-call | flops 235929600 | bytes 2094600 | tf_op jit(solution)/shard_map/pallas_call | solution.py:550
  11.9 2.9 %shard_map.299 = (bf16[608,384]{1,0:T(8,128)(2,1)S(1)}, bf16[608,384]{1,0:T(8,128)(2,1)S(1)}, s32[3,128,8]{2,1,0:T(8,128)S(1)}) custom-call(s32[2]{0:T(128)S(1)} %pad_add_fusion.place_ref, s32[3,1152]{1,0:T(4,128)S(1)} %copy-done.4, s32[8,128]{1,0:T(8,128)S(1)} %get-tuple-element.112.rank_theirs_ref, s32[2,8,128]{2,1,0:T(8,128)S(1)} %get-tuple-element.113.rank_ref, ...), custom_call_target="tpu_custom_call" | custom-call | flops 707788800 | bytes 2741768 | tf_op jit(solution)/shard_map/pallas_call | solution.py:550
  25.3 4.5 %shard_map.301 = (bf16[208,384]{1,0:T(8,128)(2,1)S(1)}, bf16[208,384]{1,0:T(8,128)(2,1)S(1)}, bf16[400,384]{1,0:T(8,128)(2,1)S(1)}, bf16[400,384]{1,0:T(8,128)(2...) custom-call(s32[2]{0:T(128)S(1)} %pad_add_fusion.place_ref, ...), custom_call_target="tpu_custom_call" | custom-call | flops 481689600 | bytes 3912200 | tf_op jit(solution)/shard_map/pallas_call | solution.py:550
  30.5 2.6 %collective-permute-start.5 = (s32[24]{0:T(128)S(1)}, s32[24]{0:T(128)S(1)}, u32[]{:S(2)}, u32[]{:S(2)}) collective-permute-start(s32[24]{0:T(128)S(1)} %pad_add_fusion.3), channel_id=1, source_target_pairs={{0,8},{1,9},{2,10},{3,11},{4,12},{5,13},{6,14},{7,15},{8,0},{9,1},... | collective-permute-start | bytes 296 | tf_op jit(solution)/shard_map/ppermute | solution.py:431
  35.0 3.7 %shard_map.300 = (bf16[400,384]{1,0:T(8,128)(2,1)S(1)}, bf16[400,384]{1,0:T(8,128)(2,1)S(1)}, bf16[400,384]{1,0:T(8,128)(2,1)S(1)}, bf16[400,384]{1,0:T(8,128)(2...) custom-call(s32[2]{0:T(128)S(1)} %pad_add_fusion.place_ref, bf16[400,384]{1,0:T(8,128)(2,1)S(1)} %copy-done.7, ...), custom_call_target="tpu_custom_call" | custom-call | flops 599654400 | bytes 4968968 | tf_op jit(solution)/shard_map/pallas_call | solution.py:550
  38.9 8.5 %shard_map.302 = (f32[608,384]{1,0:T(8,128)S(1)}, bf16[608,384]{1,0:T(8,128)(2,1)S(1)}, bf16[608,1536]{1,0:T(8,128)(2,1)}, bf16[608,1536]{1,0:T(8,128)(2,1)}, f3...) custom-call(s32[2]{0:T(128)S(1)} %pad_add_fusion.place_ref, ...), custom_call_target="tpu_custom_call" | custom-call | flops 1613758464 | bytes 10612436 | tf_op jit(solution)/shard_map/pallas_call | solution.py:550
  48.3 8.1 %shard_map.303 = (bf16[608,384]{1,0:T(8,128)(2,1)S(1)}, f32[608,384]{1,0:T(8,128)S(1)}, bf16[608,384]{1,0:T(8,128)(2,1)S(1)}, bf16[4,4,192,128]{3,2,1,0:T(8,128)(2,1)S(1)}, bf16[4,4,192,128]{3,2,1,0:T(8,128)(2,1)S(1)}) custom-call(s32[2]{0:T(128)S(1)} %pad_add_fusion.place_ref, f32[608,384]{1,0:T(8,128)S(1)} %get-tuple-element.127.middle_ref, ...), custom_call_target="tpu_custom_call" | custom-call | flops 3227516928 | bytes 12645896 | tf_op jit(solution)/shard_map/pallas_call | solution.py:550
  60.1 3.2 %shard_map.304 = (bf16[400,384]{1,0:T(8,128)(2,1)S(1)}, bf16[400,384]{1,0:T(8,128)(2,1)S(1)}, bf16[400,384]{1,0:T(8,128)(2,1)S(1)}) custom-call(bf16[608,384]{1,0:T(8,128)(2,1)S(1)} %get-tuple-element.132.g_ref, bf16[400,384]{1,0:T(8,128)(2,1)S(1)} %get-tuple-element.122.att_a.att_ref, bf16[400,384]{1,0:T(8,128)(2,1)S(1)} %get-tuple-element.133.q_ref, ...), custom_call_target="tpu_custom_call" | custom-call | flops 491520000 | bytes 4537344 | tf_op jit(solution)/shard_map/pallas_call | solution.py:550
  63.4 6.8 %shard_map.306 = (bf16[768,384]{1,0:T(8,128)(2,1)S(1)}, bf16[4,4,448,128]{3,2,1,0:T(8,128)(2,1)}, bf16[4,4,448,128]{3,2,1,0:T(8,128)(2,1)}) custom-call(s32[2]{0:T(128)S(1)} %pad_add_fusion.place_ref, bf16[400,384]{1,0:T(8,128)(2,1)S(1)} %get-tuple-element.118.x_a, bf16[400,384]{1,0:T(8,128)(2,1)S(1)} %get-tuple-element.120.x_b, ...), custom_call_target="tpu_custom_call" | custom-call | flops 1415577600 | bytes 11154952 | tf_op jit(solution)/shard_map/pallas_call | solution.py:550
  70.1 4.0 %collective-permute-done.8.got_ref = bf16[4,4,448,128]{3,2,1,0:T(8,128)(2,1)S(1)} collective-permute-done((bf16[4,4,448,128]{3,2,1,0:T(8,128)(2,1)}, bf16[4,4,448,128]{3,2,1,0:T(8,128)(2,1)S(1)}, u32[]{:S(2)}, u32[]{:S(2)}) %collective-permute-start.8) | collective-permute-done | bytes 1835040 | tf_op jit(solution)/shard_map/ppermute | solution.py:431
  79.6 3.2 %shard_map.308 = bf16[3,768,384]{2,1,0:T(8,128)(2,1)} custom-call(s32[2]{0:T(128)S(1)} %pad_add_fusion.place_ref, s32[3,128,8]{2,1,0:T(8,128)S(1)} %get-tuple-element.160.down_ref, bf16[608,384]{1,0:T(8,128)(2,1)S(1)} %get-tuple-element.154.own_ref, bf16[608,384]{1,0:T(8,128)(2,1)S(1)} %collective-permute-done.7.got_ref), custom_call_target="tpu_custom_call" | custom-call | bytes 2715656 | tf_op jit(solution)/shard_map/pallas_call | solution.py:550
  82.8 6.7 %collective-permute-done.9.refs_1_ = bf16[4,448,128]{2,1,0:T(8,128)(2,1)S(1)} collective-permute-done((bf16[4,448,128]{2,1,0:T(8,128)(2,1)S(1)}, bf16[4,448,128]{2,1,0:T(8,128)(2,1)S(1)}, u32[]{:S(2)}, u32[]{:S(2)}) %collective-permute-start.9) | collective-permute-done | bytes 458784 | tf_op jit(solution)/shard_map/ppermute | solution.py:439
  89.5 10.2 %collective-permute-done.10.refs_2_ = bf16[4,448,128]{2,1,0:T(8,128)(2,1)S(1)} collective-permute-done((bf16[4,448,128]{2,1,0:T(8,128)(2,1)S(1)}, bf16[4,448,128]{2,1,0:T(8,128)(2,1)S(1)}, u32[]{:S(2)}, u32[]{:S(2)}) %collective-permute-start.10) | collective-permute-done | bytes 458784 | tf_op jit(solution)/shard_map/ppermute | solution.py:439
  103.1 2.5 %collective-permute-start.14 = (bf16[1,448,128]{2,1,0:T(8,128)(2,1)S(1)}, bf16[1,448,128]{2,1,0:T(8,128)(2,1)S(1)}, u32[]{:S(2)}, u32[]{:S(2)}) collective-permute-start(bf16[1,448,128]{2,1,0:T(8,128)(2,1)S(1)} %get-tuple-element.175), channel_id=1, source_target_pairs={{0,12},{1,13},{2,14},{3,15},{4,8},{5,9},{6,10},{7,11},{8,4},{9,5},... | collective-permute-start | bytes 344072 | tf_op jit(solution)/shard_map/ppermute | solution.py:431
  107.0 6.3 %collective-permute-done.13.refs_2_ = bf16[1,448,128]{2,1,0:T(8,128)(2,1)S(1)} collective-permute-done((bf16[1,448,128]{2,1,0:T(8,128)(2,1)S(1)}, bf16[1,448,128]{2,1,0:T(8,128)(2,1)S(1)}, u32[]{:S(2)}, u32[]{:S(2)}) %collective-permute-start.13) | collective-permute-done | bytes 114720 | tf_op jit(solution)/shard_map/ppermute | solution.py:431
  117.9 3.4 %collective-permute-done.17 = bf16[1,448,128]{2,1,0:T(8,128)(2,1)S(1)} collective-permute-done((bf16[1,448,128]{2,1,0:T(8,128)(2,1)S(1)}, bf16[1,448,128]{2,1,0:T(8,128)(2,1)S(1)}, u32[]{:S(2)}, u32[]{:S(2)}) %collective-permute-start.17) | collective-permute-done | bytes 114720 | tf_op jit(solution)/shard_map/ppermute | solution.py:431
  121.3 4.5 %collective-permute-done.16 = bf16[1,448,128]{2,1,0:T(8,128)(2,1)S(1)} collective-permute-done((bf16[1,448,128]{2,1,0:T(8,128)(2,1)S(1)}, bf16[1,448,128]{2,1,0:T(8,128)(2,1)S(1)}, u32[]{:S(2)}, u32[]{:S(2)}) %collective-permute-start.16) | collective-permute-done | bytes 114720 | tf_op jit(solution)/shard_map/ppermute | solution.py:431
  129.4 3.1 %shard_map.311 = bf16[3,768,384]{2,1,0:T(8,128)(2,1)} custom-call(s32[2]{0:T(128)S(1)} %pad_add_fusion.place_ref, s32[3,128,8]{2,1,0:T(8,128)S(1)} %get-tuple-element.160.down_ref, bf16[768,384]{1,0:T(8,128)(2,1)S(1)} %get-tuple-element.176.own_ref, bf16[768,384]{1,0:T(8,128)(2,1)S(1)} %collective-permute-done.18.got_ref), custom_call_target="tpu_custom_call" | custom-call | bytes 2961416 | tf_op jit(solution)/shard_map/pallas_call | solution.py:550
  132.5 7.8 %collective-permute-done.21 = bf16[4,448,128]{2,1,0:T(8,128)(2,1)S(1)} collective-permute-done((bf16[4,448,128]{2,1,0:T(8,128)(2,1)S(1)}, bf16[4,448,128]{2,1,0:T(8,128)(2,1)S(1)}, u32[]{:S(2)}, u32[]{:S(2)}) %collective-permute-start.21) | collective-permute-done | bytes 458784 | tf_op jit(solution)/shard_map/ppermute | solution.py:439
  140.3 7.6 %collective-permute-done.20 = bf16[4,448,128]{2,1,0:T(8,128)(2,1)S(1)} collective-permute-done((bf16[4,448,128]{2,1,0:T(8,128)(2,1)S(1)}, bf16[4,448,128]{2,1,0:T(8,128)(2,1)S(1)}, u32[]{:S(2)}, u32[]{:S(2)}) %collective-permute-start.20) | collective-permute-done | bytes 458784 | tf_op jit(solution)/shard_map/ppermute | solution.py:439
  148.2 3.8 %collective-permute-done.22.got_ref = bf16[4,4,448,128]{3,2,1,0:T(8,128)(2,1)S(1)} collective-permute-done((bf16[4,4,448,128]{3,2,1,0:T(8,128)(2,1)S(1)}, bf16[4,4,448,128]{3,2,1,0:T(8,128)(2,1)S(1)}, u32[]{:S(2)}, u32[]{:S(2)}) %collective-permute-start.22) | collective-permute-done | bytes 1835040 | tf_op jit(solution)/shard_map/ppermute | solution.py:431
  151.9 4.1 %shard_map.312 = (f32[1536,384]{1,0:T(8,128)}, f32[384,1536]{1,0:T(8,128)}, f32[384,384]{1,0:T(8,128)}, f32[1536]{0:T(1024)}, f32[384]{0:T(512)}, /*index=5*/f32...) custom-call(s32[2]{0:T(128)S(1)} %pad_add_fusion.place_ref, ...), custom_call_target="tpu_custom_call" | custom-call | bytes 10767880 | tf_op jit(solution)/shard_map/pallas_call | solution.py:550
  (109 shorter events, 40.0 us)
Async XLA Ops:
  0.6 15.0 %collective-permute-start = (s32[3]{0:T(128)}, s32[3]{0:T(128)S(1)}, u32[]{:S(2)}, u32[]{:S(2)}) collective-permute-start(s32[3]{0:T(128)} %groups_ref.1), channel_id=1, source_target_pairs={{0,1},{1,0},{2,3},{3,2},{4,5},{5,4},{6,7},{7,6},{8,9},{9,8},{10,11... | collective-permute-start | bytes 44 | tf_op jit(solution)/shard_map/ppermute | solution.py:431
  6.6 18.7 %copy-start.3 = (bf16[384,1152]{1,0:T(8,128)(2,1)S(1)}, bf16[384,1152]{1,0:T(8,128)(2,1)}, u32[]{:S(2)}) copy-start(bf16[384,1152]{1,0:T(8,128)(2,1)} %w_ref.5) | copy-start | bytes 2654212
  6.7 18.6 %collective-permute-start.4 = (bf16[400,384]{1,0:T(8,128)(2,1)}, bf16[400,384]{1,0:T(8,128)(2,1)}, u32[]{:S(2)}, u32[]{:S(2)}) collective-permute-start(bf16[400,384]{1,0:T(8,128)(2,1)} %get-tuple-element.119.own_ref), channel_id=1, source_target_pairs={{0,16},{16,0},{1,17},{17,1},{2,18},{18,2},{3,19},{19,3},{4,20},{20... | collective-permute-start | bytes 921608 | tf_op jit(solution)/shard_map/ppermute | solution.py:594
  15.7 14.1 %collective-permute-start.3 = (bf16[400,384]{1,0:T(8,128)(2,1)}, bf16[400,384]{1,0:T(8,128)(2,1)S(1)}, u32[]{:S(2)}, u32[]{:S(2)}) collective-permute-start(bf16[400,384]{1,0:T(8,128)(2,1)} %get-tuple-element.116), channel_id=1, source_target_pairs={{0,16},{16,0},{1,17},{17,1},{2,18},{18,2},{3,19},{19,3},{4,20},{20... | collective-permute-start | bytes 921608 | tf_op jit(solution)/shard_map/ppermute | solution.py:587
  15.7 3.6 %collective-permute-start.1 = (s32[6]{0:T(128)S(1)}, s32[6]{0:T(128)S(1)}, u32[]{:S(2)}, u32[]{:S(2)}) collective-permute-start(s32[6]{0:T(128)S(1)} %pad_add_fusion.1), channel_id=1, source_target_pairs={{0,2},{1,3},{2,0},{3,1},{4,6},{5,7},{6,4},{7,5},{8,10},{9,11},{10,... | collective-permute-start | bytes 80 | tf_op jit(solution)/shard_map/ppermute | solution.py:431
  19.4 19.4 %collective-permute-start.6 = (bf16[608,384]{1,0:T(8,128)(2,1)S(1)}, bf16[608,384]{1,0:T(8,128)(2,1)}, u32[]{:S(2)}, u32[]{:S(2)}) collective-permute-start(bf16[608,384]{1,0:T(8,128)(2,1)S(1)} %get-tuple-element.126), channel_id=1, source_target_pairs={{0,16},{16,0},{1,17},{17,1},{2,18},{18,2},{3,19},{19,3},{4,20},{20... | collective-permute-start | bytes 1400840 | tf_op jit(solution)/shard_map/ppermute | solution.py:610
  21.6 3.6 %collective-permute-start.2 = (s32[12]{0:T(128)S(1)}, s32[12]{0:T(128)S(1)}, u32[]{:S(2)}, u32[]{:S(2)}) collective-permute-start(s32[12]{0:T(128)S(1)} %pad_add_fusion.2), channel_id=1, source_target_pairs={{0,4},{1,5},{2,6},{3,7},{4,0},{5,1},{6,2},{7,3},{8,12},{9,13},{10,... | collective-permute-start | bytes 152 | tf_op jit(solution)/shard_map/ppermute | solution.py:431
  30.5 8.2 %collective-permute-start.5 = (s32[24]{0:T(128)S(1)}, s32[24]{0:T(128)S(1)}, u32[]{:S(2)}, u32[]{:S(2)}) collective-permute-start(s32[24]{0:T(128)S(1)} %pad_add_fusion.3), channel_id=1, source_target_pairs={{0,8},{1,9},{2,10},{3,11},{4,12},{5,13},{6,14},{7,15},{8,0},{9,1},... | collective-permute-start | bytes 296 | tf_op jit(solution)/shard_map/ppermute | solution.py:431
  57.3 12.8 %collective-permute-start.7 = (bf16[608,384]{1,0:T(8,128)(2,1)S(1)}, bf16[608,384]{1,0:T(8,128)(2,1)S(1)}, u32[]{:S(2)}, u32[]{:S(2)}) collective-permute-start(bf16[608,384]{1,0:T(8,128)(2,1)S(1)} %get-tuple-element.154.own_ref), channel_id=1, source_target_pairs={{0,16},{16,0},{1,17},{17,1},{2,18},{18,2},{3,19},{19,3},{4,20},{20... | collective-permute-start | bytes 1400840 | tf_op jit(solution)/shard_map/ppermute | solution.py:652
  70.1 4.0 %collective-permute-start.8 = (bf16[4,4,448,128]{3,2,1,0:T(8,128)(2,1)}, bf16[4,4,448,128]{3,2,1,0:T(8,128)(2,1)S(1)}, u32[]{:S(2)}, u32[]{:S(2)}) collective-permute-start(bf16[4,4,448,128]{3,2,1,0:T(8,128)(2,1)} %get-tuple-element.155), channel_id=1, source_target_pairs={{0,1},{1,0},{2,3},{3,2},{4,5},{5,4},{6,7},{7,6},{8,9},{9,8},{10,11... | collective-permute-start | bytes 5505032 | tf_op jit(solution)/shard_map/ppermute | solution.py:431
  76.0 13.4 %collective-permute-start.9 = (bf16[4,448,128]{2,1,0:T(8,128)(2,1)S(1)}, bf16[4,448,128]{2,1,0:T(8,128)(2,1)S(1)}, u32[]{:S(2)}, u32[]{:S(2)}) collective-permute-start(bf16[4,448,128]{2,1,0:T(8,128)(2,1)S(1)} %get-tuple-element.157), channel_id=1, source_target_pairs={{0,16},{1,17},{2,18},{3,19},{4,20},{5,21},{6,22},{7,23},{8,24},{9,... | collective-permute-start | bytes 1376264 | tf_op jit(solution)/shard_map/ppermute | solution.py:439
  77.6 22.1 %collective-permute-start.10 = (bf16[4,448,128]{2,1,0:T(8,128)(2,1)S(1)}, bf16[4,448,128]{2,1,0:T(8,128)(2,1)S(1)}, u32[]{:S(2)}, u32[]{:S(2)}) collective-permute-start(bf16[4,448,128]{2,1,0:T(8,128)(2,1)S(1)} %get-tuple-element.158), channel_id=1, source_target_pairs={{0,2},{1,3},{2,0},{3,1},{4,6},{5,7},{6,4},{7,5},{8,10},{9,11},{10,... | collective-permute-start | bytes 1376264 | tf_op jit(solution)/shard_map/ppermute | solution.py:439
  79.1 20.6 %collective-permute-start.11 = (bf16[4,448,128]{2,1,0:T(8,128)(2,1)S(1)}, bf16[4,448,128]{2,1,0:T(8,128)(2,1)S(1)}, u32[]{:S(2)}, u32[]{:S(2)}) collective-permute-start(bf16[4,448,128]{2,1,0:T(8,128)(2,1)S(1)} %get-tuple-element.159), channel_id=1, source_target_pairs={{0,18},{1,19},{2,16},{3,17},{4,22},{5,23},{6,20},{7,21},{8,26},{9,... | collective-permute-start | bytes 1376264 | tf_op jit(solution)/shard_map/ppermute | solution.py:439
  99.9 25.9 %collective-permute-start.18 = (bf16[768,384]{1,0:T(8,128)(2,1)S(1)}, bf16[768,384]{1,0:T(8,128)(2,1)S(1)}, u32[]{:S(2)}, u32[]{:S(2)}) collective-permute-start(bf16[768,384]{1,0:T(8,128)(2,1)S(1)} %get-tuple-element.176.own_ref), channel_id=1, source_target_pairs={{0,16},{16,0},{1,17},{17,1},{2,18},{18,2},{3,19},{19,3},{4,20},{20... | collective-permute-start | bytes 1769480 | tf_op jit(solution)/shard_map/ppermute | solution.py:680
  101.2 5.7 %collective-permute-start.12 = (bf16[1,448,128]{2,1,0:T(8,128)(2,1)S(1)}, bf16[1,448,128]{2,1,0:T(8,128)(2,1)S(1)}, u32[]{:S(2)}, u32[]{:S(2)}) collective-permute-start(bf16[1,448,128]{2,1,0:T(8,128)(2,1)S(1)} %get-tuple-element.173), channel_id=1, source_target_pairs={{0,4},{1,5},{2,6},{3,7},{4,0},{5,1},{6,2},{7,3},{8,12},{9,13},{10,... | collective-permute-start | bytes 344072 | tf_op jit(solution)/shard_map/ppermute | solution.py:431
  102.8 10.5 %collective-permute-start.13 = (bf16[1,448,128]{2,1,0:T(8,128)(2,1)S(1)}, bf16[1,448,128]{2,1,0:T(8,128)(2,1)S(1)}, u32[]{:S(2)}, u32[]{:S(2)}) collective-permute-start(bf16[1,448,128]{2,1,0:T(8,128)(2,1)S(1)} %get-tuple-element.174), channel_id=1, source_target_pairs={{0,8},{1,9},{2,10},{3,11},{4,12},{5,13},{6,14},{7,15},{8,0},{9,1},... | collective-permute-start | bytes 344072 | tf_op jit(solution)/shard_map/ppermute | solution.py:431
  103.1 10.2 %collective-permute-start.14 = (bf16[1,448,128]{2,1,0:T(8,128)(2,1)S(1)}, bf16[1,448,128]{2,1,0:T(8,128)(2,1)S(1)}, u32[]{:S(2)}, u32[]{:S(2)}) collective-permute-start(bf16[1,448,128]{2,1,0:T(8,128)(2,1)S(1)} %get-tuple-element.175), channel_id=1, source_target_pairs={{0,12},{1,13},{2,14},{3,15},{4,8},{5,9},{6,10},{7,11},{8,4},{9,5},... | collective-permute-start | bytes 344072 | tf_op jit(solution)/shard_map/ppermute | solution.py:431
  113.4 7.9 %collective-permute-start.17 = (bf16[1,448,128]{2,1,0:T(8,128)(2,1)S(1)}, bf16[1,448,128]{2,1,0:T(8,128)(2,1)S(1)}, u32[]{:S(2)}, u32[]{:S(2)}) collective-permute-start(bf16[1,448,128]{2,1,0:T(8,128)(2,1)S(1)} %shard_map.310), channel_id=1, source_target_pairs={{0,12},{1,13},{2,14},{3,15},{4,8},{5,9},{6,10},{7,11},{8,4},{9,5},... | collective-permute-start | bytes 344072 | tf_op jit(solution)/shard_map/ppermute | solution.py:431
  114.9 10.8 %collective-permute-start.16 = (bf16[1,448,128]{2,1,0:T(8,128)(2,1)S(1)}, bf16[1,448,128]{2,1,0:T(8,128)(2,1)S(1)}, u32[]{:S(2)}, u32[]{:S(2)}) collective-permute-start(bf16[1,448,128]{2,1,0:T(8,128)(2,1)S(1)} %shard_map.310), channel_id=1, source_target_pairs={{0,8},{1,9},{2,10},{3,11},{4,12},{5,13},{6,14},{7,15},{8,0},{9,1},... | collective-permute-start | bytes 344072 | tf_op jit(solution)/shard_map/ppermute | solution.py:431
  116.9 8.8 %collective-permute-start.15 = (bf16[1,448,128]{2,1,0:T(8,128)(2,1)S(1)}, bf16[1,448,128]{2,1,0:T(8,128)(2,1)S(1)}, u32[]{:S(2)}, u32[]{:S(2)}) collective-permute-start(bf16[1,448,128]{2,1,0:T(8,128)(2,1)S(1)} %shard_map.310), channel_id=1, source_target_pairs={{0,4},{1,5},{2,6},{3,7},{4,0},{5,1},{6,2},{7,3},{8,12},{9,13},{10,... | collective-permute-start | bytes 344072 | tf_op jit(solution)/shard_map/ppermute | solution.py:431
  125.9 14.4 %collective-permute-start.21 = (bf16[4,448,128]{2,1,0:T(8,128)(2,1)S(1)}, bf16[4,448,128]{2,1,0:T(8,128)(2,1)S(1)}, u32[]{:S(2)}, u32[]{:S(2)}) collective-permute-start(bf16[4,448,128]{2,1,0:T(8,128)(2,1)S(1)} %maximum_bitcast_fusion), channel_id=1, source_target_pairs={{0,18},{1,19},{2,16},{3,17},{4,22},{5,23},{6,20},{7,21},{8,26},{9,... | collective-permute-start | bytes 1376264 | tf_op jit(solution)/shard_map/ppermute | solution.py:439
  126.6 21.3 %collective-permute-start.20 = (bf16[4,448,128]{2,1,0:T(8,128)(2,1)S(1)}, bf16[4,448,128]{2,1,0:T(8,128)(2,1)S(1)}, u32[]{:S(2)}, u32[]{:S(2)}) collective-permute-start(bf16[4,448,128]{2,1,0:T(8,128)(2,1)S(1)} %maximum_bitcast_fusion), channel_id=1, source_target_pairs={{0,2},{1,3},{2,0},{3,1},{4,6},{5,7},{6,4},{7,5},{8,10},{9,11},{10,... | collective-permute-start | bytes 1376264 | tf_op jit(solution)/shard_map/ppermute | solution.py:439
  127.8 20.0 %collective-permute-start.19 = (bf16[4,448,128]{2,1,0:T(8,128)(2,1)S(1)}, bf16[4,448,128]{2,1,0:T(8,128)(2,1)S(1)}, u32[]{:S(2)}, u32[]{:S(2)}) collective-permute-start(bf16[4,448,128]{2,1,0:T(8,128)(2,1)S(1)} %maximum_bitcast_fusion), channel_id=1, source_target_pairs={{0,16},{1,17},{2,18},{3,19},{4,20},{5,21},{6,22},{7,23},{8,24},{9,... | collective-permute-start | bytes 1376264 | tf_op jit(solution)/shard_map/ppermute | solution.py:439
  148.1 3.9 %collective-permute-start.22 = (bf16[4,4,448,128]{3,2,1,0:T(8,128)(2,1)S(1)}, bf16[4,4,448,128]{3,2,1,0:T(8,128)(2,1)S(1)}, u32[]{:S(2)}, u32[]{:S(2)}) collective-permute-start(bf16[4,4,448,128]{3,2,1,0:T(8,128)(2,1)S(1)} %pad_maximum_fusion.own_ref), channel_id=1, source_target_pairs={{0,1},{1,0},{2,3},{3,2},{4,5},{5,4},{6,7},{7,6},{8,9},{9,8},{10,11... | collective-permute-start | bytes 5505032 | tf_op jit(solution)/shard_map/ppermute | solution.py:431
  (25 other events, 212.3 us)

commit v3 on v2

v3 whole, which is shorter than its diff:
```python
import functools
import math

import jax
import jax.numpy as jnp
from jax import lax
from jax.experimental import pallas as pl
from jax.experimental.pallas import tpu as pltpu
from jax.sharding import PartitionSpec as P

HEADS = 6
HEAD_DIM = 64
LANES = 128
EXTRA = 16
EPSILON = 1e-06

BF = jnp.bfloat16
F32 = jnp.float32
VMEM = pl.BlockSpec(memory_space=pltpu.VMEM)
SMEM = pl.BlockSpec(memory_space=pltpu.SMEM)
HBM = pl.BlockSpec(memory_space=pltpu.HBM)


def dot(left, right):
    return jnp.dot(left, right, preferred_element_type=F32)


def dot_last(left, right):
    return lax.dot_general(left, right, (((1,), (1,)), ((), ())), preferred_element_type=F32)


def dot_rows(left, right):
    return lax.dot_general(left, right, (((0,), (0,)), ((), ())), preferred_element_type=F32)


def iota(shape, axis):
    return lax.broadcasted_iota(jnp.int32, shape, axis)


def ones_where(condition):
    return jnp.where(condition, 1.0, 0.0).astype(BF)


def column_sums(values):
    return jnp.sum(values, axis=0, keepdims=True)


def shape(*dims, kind=BF):
    return jax.ShapeDtypeStruct(dims, kind)


def plain(kernel, outs):
    return pl.pallas_call(kernel, out_shape=outs, compiler_params=pltpu.CompilerParams(vmem_limit_bytes=8 << 20))


def all_ranks(masked_ref, tm, half, unmasked):
    copies, hide = masked_ref.shape
    blocks = half // LANES
    marks = []
    for copy in range(copies):
        row = masked_ref[copy : copy + 1, :]
        low = ones_where(iota((LANES, hide), 0) == (row & (LANES - 1)))
        high = ones_where(iota((16, hide), 0) == (row >> 7))
        marks.append(dot_last(high, low))
    marks = jnp.concatenate(marks, axis=0)
    count = 16 * copies
    block = iota((count, LANES), 0)
    free = jnp.where((block & 15) < 2 * blocks, 1.0 - marks, 0.0).astype(BF)
    before = ones_where(iota((LANES, LANES), 0) < iota((LANES, LANES), 1))
    within = dot(free, before)
    totals = dot(free, jnp.ones((LANES, LANES), BF)).astype(BF)
    row, column = iota((count, count), 0), iota((count, count), 1)
    earlier = ones_where(jnp.logical_and(column < row, (column >> 4) == (row >> 4)))
    rank = within + dot(earlier, totals)
    rank = jnp.where(marks > 0.5, float(unmasked), rank)
    rank = jnp.concatenate([rank, jnp.zeros((LANES - count, LANES), F32)], axis=0)
    down = jnp.transpose(rank).astype(jnp.int32)
    rank = rank.astype(jnp.int32)
    across = []
    for copy in range(copies):
        first = rank[16 * copy : 16 * copy + blocks]
        second = rank[16 * copy + blocks : 16 * copy + 2 * blocks]
        across.append(jnp.concatenate([jnp.where(tm == 0, first, second), rank[:8-blocks]], axis=0))
    return across, down


def picks(rank, labels):
    wide = jnp.broadcast_to(labels, (labels.shape[0], LANES))
    return jnp.concatenate([ones_where(wide == rank[b : b + 1, :]) for b in range(rank.shape[0])], axis=1)


def load_halves(copies, half_refs, arrived, source_ref):
    loads = [
        pltpu.make_async_copy(source_ref.at[copy], half_refs.at[at], arrived.at[at]) for at, copy in enumerate(copies)
    ]
    for load in loads:
        load.start()
    return loads


def prep_theirs_kernel(unmasked, place_ref, masked_ref, tokens_ref, theirs_ref, rank_ref, down_ref, half_refs, arrived):
    tm = place_ref[0]
    half = tokens_ref.shape[1]
    blocks = half // LANES
    (load,) = load_halves((1 - tm,), half_refs, arrived, tokens_ref)
    across, down = all_ranks(masked_ref, tm, half, unmasked)
    for copy, rank in enumerate(across):
        rank_ref[copy] = rank
    for copy in range(len(across)):
        first = 16 * copy
        down_ref[copy] = jnp.where(tm == 0, down[:, first : first + 8], down[:, first + blocks : first + blocks + 8])
    chosen = picks(rank_ref[1 - tm, :blocks], iota((unmasked + EXTRA, 1), 0))
    load.wait()
    theirs_ref[...] = dot(chosen, half_refs[0]).astype(BF)


def prep_tokens_kernel(unmasked, place_ref, rank_ref, tokens_ref, shared_ref, mine_ref, half_refs, arrived):
    tm = place_ref[0]
    copies = (2, tm)
    loads = load_halves(copies, half_refs, arrived, tokens_ref)
    labels = iota((unmasked + EXTRA, 1), 0)
    for role, out_ref in enumerate((shared_ref, mine_ref)):
        chosen = picks(rank_ref[copies[role], : tokens_ref.shape[1] // LANES], labels)
        loads[role].wait()
        out_ref[...] = dot(chosen, half_refs[role]).astype(BF)


def prep_grads_kernel(unmasked, place_ref, rank_ref, cotangent_ref, keep_ref, send_ref, half_refs, arrived):
    tm = place_ref[0]
    blocks = cotangent_ref.shape[1] // LANES
    rows = unmasked + EXTRA
    part = unmasked // 2
    loads = load_halves((1 - tm, 2, tm), half_refs, arrived, cotangent_ref)
    labels = iota((rows, 1), 0)
    chosen = picks(rank_ref[1 - tm, :blocks], labels)
    loads[0].wait()
    send_ref[:rows, :] = dot(chosen, half_refs[0]).astype(BF)
    small = iota((part + EXTRA, 1), 0)
    theirs = jnp.where(small < part, small + part * (1 - tm), -1)
    own = jnp.where(small < part, small + part * tm, small + part)
    chosen = picks(rank_ref[2, :blocks], jnp.concatenate([theirs, own], axis=0))
    loads[1].wait()
    both = dot(chosen, half_refs[1]).astype(BF)
    send_ref[rows:, :] = both[: part + EXTRA]
    keep_ref[rows:, :] = both[part + EXTRA :]
    chosen = picks(rank_ref[tm, :blocks], labels)
    loads[2].wait()
    keep_ref[:rows, :] = dot(chosen, half_refs[2]).astype(BF)


def normalise(values):
    centred = values - jnp.mean(values, axis=-1, keepdims=True)
    scale = lax.rsqrt(jnp.mean(centred * centred, axis=-1, keepdims=True) + EPSILON)
    return centred * scale, scale


def attention_kernel(
    unmasked, count, split, place_ref, own_ref, got_ref, small_ref, w_ref,
    x_ref, q_ref, k_ref, v_ref, p_ref, att_ref, *rest
):
    rows, width = own_ref.shape
    at = iota((rows, width), 0)
    x = own_ref[...].astype(F32) + got_ref[...].astype(F32)
    x = jnp.where(at == unmasked, small_ref[0:1, :], x)
    hat, _ = normalise(x)
    normed = (hat * small_ref[1:2, :] + small_ref[2:3, :]).astype(BF)
    mixed = dot(normed, w_ref[...])
    query = ((mixed[:, :width] + small_ref[3:4, :]).astype(BF).astype(F32) * HEAD_DIM ** (-0.5)).astype(BF)
    key = mixed[:, width : 2 * width].astype(BF)
    value = (mixed[:, 2 * width :] + small_ref[4:5, :]).astype(BF)
    k_ref[...] = key
    v_ref[...] = value
    x = x.astype(BF)
    if split:
        tm = place_ref[0]
        part = unmasked // 2

        def take(values):
            chosen = jnp.where(tm == 0, values[:part].astype(F32), values[part:unmasked].astype(F32)).astype(BF)
            return jnp.concatenate([chosen, values[unmasked:]], axis=0)

        rest[0][...] = x
        x, query = take(x), take(query)
    x_ref[...] = x
    q_ref[...] = query
    across = iota((1, rows), 1)
    bias = jnp.where(across < unmasked, 0.0, jnp.where(across == unmasked, math.log(count), -1e30))
    first = iota((1, LANES), 1) < HEAD_DIM
    for pair in range(width // LANES):
        cols = slice(pair * LANES, (pair + 1) * LANES)
        q_pair, k_pair, v_pair = query[:, cols], key[:, cols], value[:, cols]
        parts = []
        for side in range(2):
            mine = first if side == 0 else jnp.logical_not(first)
            scores = dot_last(jnp.where(mine, q_pair, jnp.zeros_like(q_pair)), k_pair) + bias
            expo = jnp.exp(scores - jnp.max(scores, axis=1, keepdims=True))
            probs = (expo * (1.0 / jnp.sum(expo, axis=1, keepdims=True))).astype(BF)
            p_ref[2 * pair + side] = probs
            parts.append(dot(probs, v_pair))
        att_ref[:, cols] = jnp.where(first, parts[0], parts[1]).astype(BF)


def gelu_terms(hidden):
    size = jnp.abs(hidden) * (0.5**0.5)
    t = 1.0 / (1.0 + 0.3275911 * size)
    bell = jnp.exp(hidden * hidden * -0.5)
    tail = t * (0.254829592 + t * (-0.284496736 + t * (1.421413741 + t * (-1.453152027 + t * 1.061405429))))
    tail = 0.5 * tail * bell
    below = jnp.where(hidden >= 0.0, 1.0 - tail, tail)
    return hidden * below, below + hidden * bell * (1.0 / math.sqrt(2.0 * math.pi))


def stacked(refs):
    return jnp.concatenate([ref[...] for ref in refs], axis=0)


def scatter_chunks(me, stage_ref, keep_ref, send_ref):
    depth = keep_ref.shape[2]
    for rel in range(2 * 4 * keep_ref.shape[1]):
        first = pl.multiple_of((me ^ rel) * depth, 16)
        target = send_ref if rel & 1 else keep_ref
        target[(rel >> 1) & 3, rel >> 3] = stage_ref[pl.ds(first, depth), :]


def stage_weight(stage_ref, first, grad, apart=None):
    depth = grad.shape[0]
    apart = apart or depth
    for block in range(grad.shape[1] // LANES):
        at = first + block * apart
        stage_ref[at : at + depth, :] = grad[:, block * LANES : (block + 1) * LANES].astype(BF)
    return first + apart * (grad.shape[1] // LANES)


def stage_rows(stage_ref, first, vectors):
    pieces = [v[:, b * LANES : (b + 1) * LANES] for v in vectors for b in range(v.shape[1] // LANES)]
    missing = -len(pieces) % 16
    if missing:
        pieces.append(jnp.zeros((missing, LANES), F32))
    block = jnp.concatenate(pieces, axis=0).astype(BF)
    stage_ref[first : first + block.shape[0], :] = block
    return first + block.shape[0]


def clear_rest(stage_ref, first):
    if first < stage_ref.shape[0]:
        stage_ref[first:, :] = jnp.zeros((stage_ref.shape[0] - first, LANES), BF)


def forward_kernel(
    att_a, att_b, x_a, x_b, small_ref, bias_up_ref, w_proj_ref, w_up_ref, w_down_ref,
    out_ref, middle_ref, normed_ref, active_ref, slope_ref
):
    attended = stacked((att_a, att_b))
    x = stacked((x_a, x_b)).astype(F32)
    middle = x + dot(attended, w_proj_ref[...]) + small_ref[5:6, :]
    middle_ref[...] = middle
    hat, _ = normalise(middle)
    normed = (hat * small_ref[6:7, :] + small_ref[7:8, :]).astype(BF)
    normed_ref[...] = normed
    result = middle + small_ref[8:9, :]
    step = 512
    for first in range(0, w_up_ref.shape[1], step):
        cols = slice(first, first + step)
        active, slope = gelu_terms(dot(normed, w_up_ref[:, cols]) + bias_up_ref[:, cols])
        active = active.astype(BF)
        active_ref[:, cols] = active
        slope_ref[:, cols] = slope.astype(BF)
        result = result + dot(active, w_down_ref[cols, :])
    out_ref[...] = result.astype(BF)


def norm_back(grad, hat, scale, gain):
    inner = grad * gain
    mean = jnp.mean(inner, axis=-1, keepdims=True)
    along = jnp.mean(inner * hat, axis=-1, keepdims=True)
    return scale * (inner - mean - hat * along)


def backward_kernel(
    place_ref, groups_ref, everyone_ref, cot_own, cot_got, middle_ref, normed_ref, active_ref, slope_ref, att_a, att_b,
    small_ref, w_proj_ref, w_up_ref, w_down_ref,
    grad_middle_ref, grad_att_ref, keep_ref, send_ref, stage_ref
):
    rows_a, total = att_a.shape[0], cot_own.shape[0]
    everyone = everyone_ref[...]

    def weight_of(group):
        return 1.0 / jnp.sum(jnp.where(everyone == group, 1.0, 0.0), axis=1, keepdims=True)

    weight = jnp.where(
        iota((total, 1), 0) < rows_a, weight_of(groups_ref[place_ref[0]]), weight_of(groups_ref[2])
    )
    upstream = (cot_own[...].astype(F32) + cot_got[...].astype(F32)) * weight
    grad_result = upstream.astype(BF)
    normed = normed_ref[...]
    hidden, step = active_ref.shape[1], 512
    grad_normed = None
    sums = []
    parts = []
    for first in range(0, hidden, step):
        cols = slice(first, first + step)
        grad_hidden = (dot_last(grad_result, w_down_ref[cols, :]) * slope_ref[:, cols].astype(F32)).astype(BF)
        stage_weight(stage_ref, first, dot_rows(active_ref[:, cols], grad_result), hidden)
        part = dot_last(grad_hidden, w_up_ref[:, cols])
        grad_normed = part if grad_normed is None else grad_normed + part
        sums.append(column_sums(grad_hidden.astype(F32)))
        parts.append(dot_rows(normed, grad_hidden))
    end = hidden * (grad_result.shape[1] // LANES)
    for part in parts:
        end = stage_weight(stage_ref, end, part)
    hat, scale = normalise(middle_ref[...])
    grad_middle = upstream + norm_back(grad_normed, hat, scale, small_ref[6:7, :])
    grad_middle_ref[...] = grad_middle
    grad_branch = grad_middle.astype(BF)
    grad_att_ref[...] = dot_last(grad_branch, w_proj_ref[...]).astype(BF)
    end = stage_weight(stage_ref, end, dot_rows(stacked((att_a, att_b)), grad_branch))
    vectors = sums + [
        column_sums(grad_normed * hat),
        column_sums(grad_normed),
        column_sums(grad_branch.astype(F32)),
        column_sums(grad_result.astype(F32)),
    ]
    end = stage_rows(stage_ref, end, vectors)
    clear_rest(stage_ref, end)
    scatter_chunks(place_ref[1], stage_ref, keep_ref, send_ref)


def attention_back_kernel(row_from, g_ref, att_ref, q_ref, k_ref, v_ref, p_ref, dq_ref, dk_ref, dv_ref):
    width = q_ref.shape[1]
    rows = q_ref.shape[0]
    first = iota((1, LANES), 1) < HEAD_DIM
    for pair in range(width // LANES):
        cols = slice(pair * LANES, (pair + 1) * LANES)
        g_pair = g_ref[row_from : row_from + rows, cols]
        q_pair, k_pair, v_pair = q_ref[:, cols], k_ref[:, cols], v_ref[:, cols]
        agree = g_pair.astype(F32) * att_ref[:, cols].astype(F32)
        dq, dk, dv = [], [], []
        for side in range(2):
            mine = first if side == 0 else jnp.logical_not(first)
            correction = jnp.sum(jnp.where(mine, agree, 0.0), axis=1, keepdims=True)
            probs = p_ref[2 * pair + side]
            grad_probs = dot_last(jnp.where(mine, g_pair, jnp.zeros_like(g_pair)), v_pair)
            grad_scores = (probs.astype(F32) * (grad_probs - correction)).astype(BF)
            dq.append(dot(grad_scores, k_pair))
            dk.append(dot_rows(grad_scores, q_pair))
            dv.append(dot_rows(probs, g_pair))
        dq_ref[:, cols] = (jnp.where(first, dq[0], dq[1]) * HEAD_DIM ** (-0.5)).astype(BF)
        dk_ref[:, cols] = jnp.where(first, dk[0], dk[1]).astype(BF)
        dv_ref[:, cols] = jnp.where(first, dv[0], dv[1]).astype(BF)


def inputs_back_kernel(
    unmasked, place_ref, x_a, x_b, dq_a, dq_b, dk_a, dk_b, dv_a, dv_b, grad_middle_ref, small_ref, w_ref,
    grad_ref, keep_ref, send_ref, stage_ref
):
    rows, width = x_a.shape
    part = unmasked // 2
    tm = place_ref[0]

    def spread(block):
        wide = block.astype(F32)
        left = jnp.where(tm == 0, wide[:part], 0.0)
        right = jnp.where(tm == 0, 0.0, wide[:part])
        return jnp.concatenate([left, right, wide[part:]], axis=0)

    x = stacked((x_a, x_b)).astype(F32)
    hat, scale = normalise(x)
    gain = small_ref[1:2, :]
    normed = (hat * gain + small_ref[2:3, :]).astype(BF)
    dq = jnp.concatenate([dq_a[...], spread(dq_b[...]).astype(BF)], axis=0)
    mixed = jnp.concatenate([dq, stacked((dk_a, dk_b)), stacked((dv_a, dv_b))], axis=1)
    end = stage_weight(stage_ref, 0, dot_rows(normed, mixed))
    grad_normed = dot_last(mixed, w_ref[...])
    grad = norm_back(grad_normed, hat, scale, gain)
    grad = grad + jnp.concatenate([grad_middle_ref[:rows], spread(grad_middle_ref[rows:])], axis=0)
    grad_ref[:unmasked] = grad[:unmasked].astype(BF)
    grad_ref[unmasked:] = grad[rows : rows + unmasked].astype(BF)
    vectors = (
        column_sums(mixed[:, :width].astype(F32)),
        column_sums(mixed[:, 2 * width :].astype(F32)),
        column_sums(grad_normed * hat),
        column_sums(grad_normed),
        grad[unmasked : unmasked + 1] + grad[rows + unmasked : rows + unmasked + 1],
    )
    end = stage_rows(stage_ref, end, vectors)
    clear_rest(stage_ref, end)
    scatter_chunks(place_ref[1], stage_ref, keep_ref, send_ref)


def place_back(down, rows, half):
    labels = jnp.broadcast_to(iota((1, rows), 1), (LANES, rows))
    return jnp.concatenate([ones_where(labels == down[:, b : b + 1]) for b in range(half // LANES)], axis=0)


def outputs_kernel(unmasked, place_ref, down_ref, own_ref, got_ref, out_ref):
    tm = place_ref[0]
    half = out_ref.shape[1]
    rows = unmasked + EXTRA
    part = unmasked // 2
    out_ref[tm] = dot(place_back(down_ref[tm], rows, half), own_ref[:rows]).astype(BF)
    out_ref[1 - tm] = dot(place_back(down_ref[1 - tm], rows, half), got_ref[:rows]).astype(BF)
    own = own_ref[rows:].astype(F32)
    got = got_ref[rows:].astype(F32)
    left = jnp.where(tm == 0, own[:part], got[:part])
    right = jnp.where(tm == 0, got[:part], own[:part])
    whole = jnp.concatenate([left, right, own[part:]], axis=0).astype(BF)
    out_ref[2] = dot(place_back(down_ref[2], rows, half), whole).astype(BF)


def grads_out_kernel(unmasked, place_ref, down_ref, own_ref, got_ref, out_ref):
    tm = place_ref[0]
    half = out_ref.shape[1]
    out_ref[tm] = dot(place_back(down_ref[tm], unmasked, half), own_ref[:unmasked]).astype(BF)
    out_ref[1 - tm] = dot(place_back(down_ref[1 - tm], unmasked, half), got_ref[:unmasked]).astype(BF)
    whole = (own_ref[unmasked:].astype(F32) + got_ref[unmasked:].astype(F32)).astype(BF)
    out_ref[2] = dot(place_back(down_ref[2], unmasked, half), whole).astype(BF)


def fold_kernel(keep_ref, got_ref, *out_refs):
    for step, out_ref in enumerate(out_refs):
        out_ref[...] = (keep_ref[step].astype(F32) + got_ref[step].astype(F32)).astype(BF)


def fold_four_kernel(units, *refs):
    outs = refs[4 * units :]
    first = 0
    for unit in range(units):
        total = refs[4 * unit][...].astype(F32)
        for ref in refs[4 * unit + 1 : 4 * unit + 4]:
            total = total + ref[...].astype(F32)
        total = total.astype(BF)
        rows = slice(first, first + total.shape[1])
        first += total.shape[1]
        if len(outs) == 1:
            outs[0][:, rows] = total
        else:
            for step, out_ref in enumerate(outs):
                for slot in range(out_ref.shape[0]):
                    out_ref[slot, rows] = total[4 * slot + step]


def clip_swap(values, distance):
    size = lax.axis_size("clip")
    return lax.ppermute(values, "clip", [(i, i ^ distance) for i in range(size)])


def near_swap(values, step):
    size = lax.axis_size("clip")
    pairs = [
        (t * size + i, (t ^ (step & 1)) * size + (i ^ ((step >> 1) << 1))) for t in range(2) for i in range(size)
    ]
    return lax.ppermute(values, ("tm", "clip"), pairs)


def sum_nearby(keep, send, after, before=()):
    _, groups, depth, _ = keep.shape
    got, after = lax.optimization_barrier((clip_swap(send, 1), after))
    pieces = plain(fold_kernel, [shape(groups, depth, LANES)] * 4)(keep, got)
    *pieces, before = lax.optimization_barrier((*pieces, before))
    return [pieces[0]] + [near_swap(pieces[step], step) for step in (1, 2, 3)], before


def sum_over_devices(first_pieces, second_pieces, send_far, beside_last):
    far = []
    distance = 4
    while distance < lax.axis_size("clip"):
        far.append(distance)
        distance *= 4
    pieces = [*first_pieces, *second_pieces]
    groups = pieces[0].shape[0]
    depth = pieces[0].shape[1] + pieces[4].shape[1]
    left = groups
    sent = None
    for distance in far:
        left //= 4
        fold = functools.partial(fold_four_kernel, len(pieces) // 4)
        pieces = plain(fold, [shape(left, depth, LANES)] * 4)(*pieces)
        if sent is None:
            sent, pieces = send_far(pieces)
        pieces = [pieces[0]] + [clip_swap(pieces[step], step * distance) for step in (1, 2, 3)]
    total = plain(functools.partial(fold_four_kernel, 1), shape(left, depth, LANES))(*pieces)
    for distance in reversed(far):
        pieces = [total] + [clip_swap(total, step * distance) for step in (1, 2, 3)]
        total = jnp.stack(pieces, axis=1).reshape(-1, depth, LANES)
    total, sent = lax.optimization_barrier((total, sent))
    pieces = [total] + [near_swap(total, step) for step in (1, 2, 3)]
    last = beside_last(sent)
    *pieces, last = lax.optimization_barrier((*pieces, last))
    total = jnp.stack(pieces)
    return total, clip_swap(total, 1), last


def gather_chunks(me, own_ref, got_ref, stage_ref, start, depth):
    for rel in range(2 * 4 * own_ref.shape[1]):
        first = pl.multiple_of((me ^ rel) * depth, 16)
        source = got_ref if rel & 1 else own_ref
        stage_ref[pl.ds(first, depth), :] = source[(rel >> 1) & 3, rel >> 3, start : start + depth]


def unstage_kernel(units, place_ref, own_ref, got_ref, *refs):
    stage_ref = refs[-1]
    start = at = 0
    for depth, weights, vectors in units:
        gather_chunks(place_ref[1], own_ref, got_ref, stage_ref, start, depth)
        unstage(weights, stage_ref, refs[at : at + weights + vectors])
        start += depth
        at += weights + vectors


def unstage(weights, stage_ref, outs):
    first = 0
    for out_ref in outs[:weights]:
        depth, width = out_ref.shape
        for block in range(width // LANES):
            out_ref[:, block * LANES : (block + 1) * LANES] = stage_ref[first : first + depth, :].astype(F32)
            first += depth
    if len(outs) > weights:
        count = sum(ref.shape[0] // LANES for ref in outs[weights:])
        rows = stage_ref[first : first + count + -count % 16, :].astype(F32)
        at = 0
        for out_ref in outs[weights:]:
            blocks = out_ref.shape[0] // LANES
            for block in range(blocks):
                out_ref[block * LANES : (block + 1) * LANES] = rows[at + block]
            at += blocks


def chunk_rows(count, devices):
    return -(-count // (devices * 16)) * 16


def body(
    tokens,
    masked,
    groups,
    cotangent,
    mask_token,
    gain_one,
    shift_one,
    w_qkv,
    q_bias,
    v_bias,
    w_proj,
    b_proj,
    gain_two,
    shift_two,
    w_up,
    b_up,
    w_down,
    b_down,
):
    copies, half, width = tokens.shape
    hidden = w_up.shape[1]
    hide = masked.shape[1]
    unmasked = 2 * half - hide
    rows = unmasked + EXTRA
    some = unmasked // 2 + EXTRA
    total = rows + some
    tm, clip = lax.axis_index("tm"), lax.axis_index("clip")
    clips = lax.axis_size("clip")
    devices = 2 * clips
    me = (clip & 1) | (tm << 1) | ((clip >> 1) << 2)
    place = jnp.stack([tm, me]).astype(jnp.int32)
    swap = functools.partial(lax.ppermute, axis_name="tm", perm=[(0, 1), (1, 0)])

    def run(kernel, args, outs, scratch=(), scalars=1, limit=20, flops=0, in_hbm=(), hides=True):
        moved = sum(math.prod(a.shape) * a.dtype.itemsize for a in list(args) + jax.tree.leaves(outs))
        return pl.pallas_call(
            kernel,
            out_shape=outs,
            in_specs=[
                SMEM if at < scalars else HBM if at in in_hbm else VMEM
                for at in range(len(args))
            ],
            out_specs=jax.tree.map(lambda _: VMEM, outs),
            scratch_shapes=list(scratch),
            compiler_params=pltpu.CompilerParams(vmem_limit_bytes=limit << 20),
            cost_estimate=pl.CostEstimate(
                flops=flops if hides else 1, bytes_accessed=moved if hides else 1, transcendentals=0
            ),
        )(*args)

    counts = (2 * width // LANES * hidden + width // LANES * width + 32, 3 * width // LANES * width + 16)
    depths = [chunk_rows(count, devices) for count in counts]

    def chunked(unit):
        halves = [shape(4, devices // 8, depths[unit], LANES)] * 2
        return halves, [pltpu.VMEM((devices * depths[unit], LANES), BF)]

    small = jnp.stack(
        [mask_token, gain_one, shift_one, q_bias, v_bias, b_proj, gain_two, shift_two, b_down]
    ).astype(F32)
    bias_up = b_up.astype(F32).reshape(1, hidden)

    block = shape(rows, width)
    def loads(count):
        return [pltpu.VMEM((count, half, width), BF), pltpu.SemaphoreType.DMA((count,))]

    everyone = jnp.concatenate([groups, clip_swap(groups, 1)])
    theirs, rank, down = run(
        functools.partial(prep_theirs_kernel, unmasked),
        (place, masked, tokens),
        [block, shape(copies, 8, LANES, kind=jnp.int32), shape(copies, LANES, 8, kind=jnp.int32)],
        loads(1),
        limit=60,
        flops=2 * rows * half * width,
        in_hbm=(2,),
    )
    got_mine = swap(theirs)
    everyone, theirs, rank = lax.optimization_barrier((everyone, theirs, rank))
    everyone = jnp.concatenate([everyone, clip_swap(everyone, 2)])
    shared, mine = run(
        functools.partial(prep_tokens_kernel, unmasked),
        (place, rank, tokens),
        [block, block],
        loads(2),
        limit=60,
        flops=4 * rows * half * width,
        in_hbm=(2,),
    )
    got_shared = swap(shared)
    everyone, shared, rank = lax.optimization_barrier((everyone, shared, rank))
    everyone = jnp.concatenate([everyone, clip_swap(everyone, 4)])
    cot_own, cot_send = run(
        functools.partial(prep_grads_kernel, unmasked),
        (place, rank, cotangent),
        [shape(total, width), shape(total, width)],
        loads(3),
        limit=60,
        flops=2 * copies * rows * half * width,
        in_hbm=(2,),
    )
    everyone, cot_send = lax.optimization_barrier((everyone, cot_send))
    distance = 8
    while distance < clips:
        everyone = jnp.concatenate([everyone, clip_swap(everyone, distance)])
        distance *= 2
    cot_got = swap(cot_send)

    def attend(own, got, split):
        queries = some if split else rows
        outs = [
            shape(queries, width), shape(queries, width), block, block,
            shape(HEADS, queries, rows), shape(queries, width),
        ]
        if split:
            outs.append(block)
        return run(
            functools.partial(attention_kernel, unmasked, hide, split),
            (place, own, got, small, w_qkv),
            outs,
            flops=6 * rows * width * width + 4 * queries * rows * width,
        )

    x_a, q_a, k_a, v_a, p_a, att_a = attend(mine, got_mine, False)
    x_b, q_b, k_b, v_b, p_b, att_b, x_whole = attend(shared, got_shared, True)

    out_rows, middle, normed_two, active, slope = run(
        forward_kernel,
        (att_a, att_b, x_a, x_b, small, bias_up, w_proj, w_up, w_down),
        [
            shape(total, width), shape(total, width, kind=F32), shape(total, width), shape(total, hidden),
            shape(total, hidden),
        ],
        scalars=0,
        flops=2 * total * width * (width + 2 * hidden),
    )
    halves, stage = chunked(0)
    grad_middle, grad_att, keep, send = run(
        backward_kernel,
        (
            place, groups, everyone.reshape(1, -1), cot_own, cot_got, middle, normed_two, active, slope, att_a, att_b,
            small, w_proj, w_up, w_down,
        ),
        [shape(total, width, kind=F32), shape(total, width)] + halves,
        stage,
        scalars=2,
        hides=False,
    )

    def attend_back(row_from, grads, att, q, k, v, p):
        return run(
            functools.partial(attention_back_kernel, row_from),
            (grads, att, q, k, v, p),
            [shape(q.shape[0], width), block, block],
            scalars=0,
            hides=False,
        )

    dq_b, dk_b, dv_b = attend_back(rows, grad_att, att_b, q_b, k_b, v_b, p_b)
    first_pieces, grad_att = sum_nearby(keep, send, dq_b, grad_att)
    dq_a, dk_a, dv_a = attend_back(0, grad_att, att_a, q_a, k_a, v_a, p_a)
    halves, stage = chunked(1)
    grad_rows, keep, send = run(
        functools.partial(inputs_back_kernel, unmasked),
        (place, x_a, x_whole, dq_a, dq_b, dk_a, dk_b, dv_a, dv_b, grad_middle, small, w_qkv),
        [shape(2 * unmasked, width)] + halves,
        stage,
        hides=False,
    )
    send, first_pieces = lax.optimization_barrier((send, first_pieces))
    second_pieces, _ = sum_nearby(keep, send, ())

    def send_rows(pieces):
        *pieces, grads, outs = lax.optimization_barrier((*pieces, grad_rows, out_rows))
        return (swap(grads), swap(outs)), pieces

    def place_rows(got):
        grads_got, out_got = got
        return (
            run(functools.partial(outputs_kernel, unmasked), (place, down, out_rows, out_got), shape(*tokens.shape)),
            run(functools.partial(grads_out_kernel, unmasked), (place, down, grad_rows, grads_got), shape(*tokens.shape)),
        )

    sums_own, sums_got, (block_out, grad_tokens) = sum_over_devices(first_pieces, second_pieces, send_rows, place_rows)

    vector = shape(width, kind=F32)
    outs = [
        shape(hidden, width, kind=F32), shape(width, hidden, kind=F32), shape(width, width, kind=F32), shape(hidden, kind=F32),
        vector, vector, vector, vector,
        shape(width, 3 * width, kind=F32), vector, vector, vector, vector, vector,
    ]
    units = tuple(zip(depths, (3, 1), (5, 5)))
    (
        grad_w_down, grad_w_up, grad_w_proj, grad_b_up, grad_gain_two, grad_shift_two, grad_b_proj, grad_b_down,
        grad_w_qkv, grad_q_bias, grad_v_bias, grad_gain_one, grad_shift_one, grad_mask_token,
    ) = run(
        functools.partial(unstage_kernel, units),
        (place, sums_own, sums_got),
        outs,
        [pltpu.VMEM((devices * max(depths), LANES), BF)],
    )
    return (
        block_out,
        grad_tokens,
        grad_mask_token,
        grad_gain_one,
        grad_shift_one,
        grad_w_qkv,
        grad_q_bias,
        grad_v_bias,
        grad_w_proj,
        grad_b_proj,
        grad_gain_two,
        grad_shift_two,
        grad_w_up,
        grad_b_up,
        grad_w_down,
        grad_b_down,
    )


def solution(mesh):
    return jax.shard_map(
        body,
        mesh=mesh,
        in_specs=(P("clip", "tm", None), P("clip", None), P("clip"), P("clip", "tm", None)) + (P(),) * 14,
        out_specs=(P("clip", "tm", None), P("clip", "tm", None)) + (P(),) * 14,
        check_vma=False,
    )
```

time: 156 us -> 132 us (0.85)
  waiting for transfers between devices: 59.2 us -> 44.6 us
  local copies, waits for them, and re-layouts: 9.86 us -> 0.22 us
  Pallas kernels: 56.1 us -> 50.3 us
  starting transfers between devices: 29.2 us -> 33 us
    unnamed x52 -> x40, local copies, waits for them, and re-layouts: 9.75 us -> 0.11 us
    ppermute x6 -> x9, waiting for transfers between devices: 32.3 us -> 22.7 us  [near_swap(): return lax.ppermute(values, ('tm', 'clip'), pairs)]
    pallas_call x16 -> x17, Pallas kernels: 56.1 us -> 50.3 us  [the longest x13 49.6 us: run(): pl.pallas_call(kernel, out_shape=outs, in_specs=[SMEM if at < scalars els...]
    ppermute x12 -> x13, waiting for transfers between devices: 26.9 us -> 21.9 us  [clip_swap(): lax.ppermute(values, 'clip', [(i, i ^ distance) for i in range(size)])]
    ppermute x6 -> x9, starting transfers between devices: 7.11 us -> 10.7 us  [near_swap(): return lax.ppermute(values, ('tm', 'clip'), pairs)]
    ppermute x1, starting transfers between devices: 0.02 us -> 2.57 us  [body(): got_mine = swap(theirs)]
    ppermute x1, starting transfers between devices: 2.58 us -> 0.6 us  [body(): got_shared = swap(shared)]
    ppermute x12 -> x13, starting transfers between devices: 15.7 us -> 15.6 us  [clip_swap(): lax.ppermute(values, 'clip', [(i, i ^ distance) for i in range(size)])]
  transfers between devices with their start and end apart: 23 -> 27, of which waited for: 12 -> 14; matrix products, arithmetic and copies ran while one was open for 0% -> 1% of each run, Pallas kernels for 22% -> 30%
where the time goes in v3:
time: 132 us; the launch traced here: 131 us
  Pallas kernels  50.3 us (38%)
  waiting for transfers between devices  44.6 us (34%)
  starting transfers between devices  33 us (25%)
  other arithmetic  1.83 us (1%)
    pallas_call x13, Pallas kernels, run(): pl.pallas_call(kernel, out_shape=outs, in_specs=[SMEM if at < scalars els...  49.6 us
    ppermute x9, waiting for transfers between devices, near_swap(): return lax.ppermute(values, ('tm', 'clip'), pairs)  22.7 us
    ppermute x13, waiting for transfers between devices, clip_swap(): lax.ppermute(values, 'clip', [(i, i ^ distance) for i in range(size)])  21.9 us
    ppermute x13, starting transfers between devices, clip_swap(): lax.ppermute(values, 'clip', [(i, i ^ distance) for i in range(size)])  15.6 us
    ppermute x9, starting transfers between devices, near_swap(): return lax.ppermute(values, ('tm', 'clip'), pairs)  10.7 us
  transfers between devices with their start and end apart: 27, of which 14 were waited for; matrix products, arithmetic and copies ran while one was open for 1% of the time, Pallas kernels for 30%

profile of v3, /device:TPU:0, one launch (start us, length us, event | category | flops | bytes accessed | tf_op | source)
XLA Modules:
  0.0 131.0 jit_solution(6393070728707304543)
XLA Ops:
  1.7 3.1 %shard_map.297 = (bf16[400,384]{1,0:T(8,128)(2,1)}, s32[3,8,128]{2,1,0:T(8,128)}, s32[3,128,8]{2,1,0:T(8,128)}) custom-call(s32[2]{0:T(128)} %pad_add_fusion.place_ref, s32[3,1152]{1,0:T(4,128)} %masked_ref.1, bf16[3,768,384]{2,1,0:T(8,128)(2,1)} %tokens_ref.3), custom_call_target="tpu_custom_call" | custom-call | flops 235929600 | bytes 2115080 | tf_op jit(solution)/shard_map/pallas_call | solution.py:568
  4.8 2.6 %collective-permute-start.1 = (bf16[400,384]{1,0:T(8,128)(2,1)}, bf16[400,384]{1,0:T(8,128)(2,1)S(1)}, u32[]{:S(2)}, u32[]{:S(2)}) collective-permute-start(bf16[400,384]{1,0:T(8,128)(2,1)} %get-tuple-element.113), channel_id=1, source_target_pairs={{0,16},{16,0},{1,17},{17,1},{2,18},{18,2},{3,19},{19,3},{4,20},{20... | collective-permute-start | bytes 921608 | tf_op jit(solution)/shard_map/ppermute | solution.py:609
  9.8 3.6 %shard_map.298 = (bf16[400,384]{1,0:T(8,128)(2,1)}, bf16[400,384]{1,0:T(8,128)(2,1)}) custom-call(s32[2]{0:T(128)} %pad_add_fusion.place_ref, s32[3,8,128]{2,1,0:T(8,128)} %get-tuple-element.123.rank_ref, bf16[3,768,384]{2,1,0:T(8,128)(2,1)} %tokens_ref.3), custom_call_target="tpu_custom_call" | custom-call | flops 471859200 | bytes 2396168 | tf_op jit(solution)/shard_map/pallas_call | solution.py:568
  15.7 4.2 %shard_map.301 = (bf16[608,384]{1,0:T(8,128)(2,1)}, bf16[608,384]{1,0:T(8,128)(2,1)}) custom-call(s32[2]{0:T(128)} %pad_add_fusion.place_ref, s32[3,8,128]{2,1,0:T(8,128)} %get-tuple-element.123.rank_ref, bf16[3,768,384]{2,1,0:T(8,128)(2,1)} %cotangent_ref.1), custom_call_target="tpu_custom_call" | custom-call | flops 707788800 | bytes 2715656 | tf_op jit(solution)/shard_map/pallas_call | solution.py:568
  21.7 2.6 %collective-permute-start.5 = (s32[24]{0:T(128)S(1)}, s32[24]{0:T(128)S(1)}, u32[]{:S(2)}, u32[]{:S(2)}) collective-permute-start(s32[24]{0:T(128)S(1)} %pad_add_fusion.3), channel_id=1, source_target_pairs={{0,8},{1,9},{2,10},{3,11},{4,12},{5,13},{6,14},{7,15},{8,0},{9,1},... | collective-permute-start | bytes 296 | tf_op jit(solution)/shard_map/ppermute | solution.py:444
  26.3 3.7 %shard_map.299 = (bf16[400,384]{1,0:T(8,128)(2,1)S(1)}, bf16[400,384]{1,0:T(8,128)(2,1)S(1)}, bf16[400,384]{1,0:T(8,128)(2,1)S(1)}, bf16[400,384]{1,0:T(8,128)(2...) custom-call(s32[2]{0:T(128)S(1)} %copy-done.6, bf16[400,384]{1,0:T(8,128)(2,1)S(1)} %copy-done.9, ...), custom_call_target="tpu_custom_call" | custom-call | flops 599654400 | bytes 4968968 | tf_op jit(solution)/shard_map/pallas_call | solution.py:568
  30.1 3.9 %shard_map.300 = (bf16[208,384]{1,0:T(8,128)(2,1)S(1)}, bf16[208,384]{1,0:T(8,128)(2,1)S(1)}, bf16[400,384]{1,0:T(8,128)(2,1)S(1)}, bf16[400,384]{1,0:T(8,128)(2...) custom-call(s32[2]{0:T(128)S(1)} %copy-done.6, ...), custom_call_target="tpu_custom_call" | custom-call | flops 481689600 | bytes 3912200 | tf_op jit(solution)/shard_map/pallas_call | solution.py:568
  34.0 5.6 %shard_map.302 = (bf16[608,384]{1,0:T(8,128)(2,1)S(1)}, f32[608,384]{1,0:T(8,128)S(1)}, bf16[608,384]{1,0:T(8,128)(2,1)S(1)}, bf16[608,1536]{1,0:T(8,128)(2,1)S(1)}, bf16[608,1536]{1,0:T(8,128)(2,1)S(1)}) custom-call(bf16[400,384]{1,0:T(8,128)(2,1)S(1)} %get-tuple-element.128.att_a.att_ref, bf16[208,384]{1,0:T(8,128)(2,1)S(1)} %get-tuple-element.129.att_b.att_ref, ...), custom_call_target="tpu_custom_call" | custom-call | flops 1613758464 | bytes 9211392 | tf_op jit(solution)/shard_map/pallas_call | solution.py:568
  39.7 5.8 %shard_map.303 = (f32[608,384]{1,0:T(8,128)S(1)}, bf16[608,384]{1,0:T(8,128)(2,1)S(1)}, bf16[4,4,336,128]{3,2,1,0:T(8,128)(2,1)S(1)}, bf16[4,4,336,128]{3,2,1,0:T(8,128)(2,1)S(1)}) custom-call(s32[2]{0:T(128)S(1)} %copy-done.6, s32[3]{0:T(128)S(1)} %copy-done.7, s32[1,48]{1,0:T(1,128)S(1)} %add_bitcast_fusion.everyone_ref, bf16[608,384]{1,0:T(8,128)(2,1)S(1)} %copy-done.4, ...), custom_call_target="tpu_custom_call" | custom-call | flops 1 | bytes 1 | tf_op jit(solution)/shard_map/pallas_call | solution.py:568
  52.5 3.4 %shard_map.306 = (bf16[400,384]{1,0:T(8,128)(2,1)S(1)}, bf16[400,384]{1,0:T(8,128)(2,1)S(1)}, bf16[400,384]{1,0:T(8,128)(2,1)S(1)}) custom-call(bf16[608,384]{1,0:T(8,128)(2,1)S(1)} %get-tuple-element.148.g_ref, bf16[400,384]{1,0:T(8,128)(2,1)S(1)} %get-tuple-element.128.att_a.att_ref, bf16[400,384]{1,0:T(8,128)(2,1)S(1)} %get-tuple-element.149.q_ref, ...), custom_call_target="tpu_custom_call" | custom-call | flops 1 | bytes 1 | tf_op jit(solution)/shard_map/pallas_call | solution.py:568
  56.0 3.8 %shard_map.307 = (bf16[768,384]{1,0:T(8,128)(2,1)S(1)}, bf16[4,4,112,128]{3,2,1,0:T(8,128)(2,1)S(1)}, bf16[4,4,112,128]{3,2,1,0:T(8,128)(2,1)S(1)}) custom-call(s32[2]{0:T(128)S(1)} %copy-done.6, bf16[400,384]{1,0:T(8,128)(2,1)S(1)} %get-tuple-element.117.x_a, bf16[400,384]{1,0:T(8,128)(2,1)S(1)} %get-tuple-element.121.x_b, ...), custom_call_target="tpu_custom_call" | custom-call | flops 1 | bytes 1 | tf_op jit(solution)/shard_map/pallas_call | solution.py:568
  60.0 6.8 %collective-permute-done.9.refs_2_ = bf16[4,336,128]{2,1,0:T(8,128)(2,1)S(1)} collective-permute-done((bf16[4,336,128]{2,1,0:T(8,128)(2,1)S(1)}, bf16[4,336,128]{2,1,0:T(8,128)(2,1)S(1)}, u32[]{:S(2)}, u32[]{:S(2)}) %collective-permute-start.9) | collective-permute-done | bytes 344096 | tf_op jit(solution)/shard_map/ppermute | solution.py:452
  74.0 3.7 %collective-permute-done.13.refs_6_ = bf16[4,112,128]{2,1,0:T(8,128)(2,1)S(1)} collective-permute-done((bf16[4,112,128]{2,1,0:T(8,128)(2,1)S(1)}, bf16[4,112,128]{2,1,0:T(8,128)(2,1)S(1)}, u32[]{:S(2)}, u32[]{:S(2)}) %collective-permute-start.13) | collective-permute-done | bytes 114720 | tf_op jit(solution)/shard_map/ppermute | solution.py:452
  80.4 2.6 %collective-permute-start.16 = (bf16[1,448,128]{2,1,0:T(8,128)(2,1)S(1)}, bf16[1,448,128]{2,1,0:T(8,128)(2,1)S(1)}, u32[]{:S(2)}, u32[]{:S(2)}) collective-permute-start(bf16[1,448,128]{2,1,0:T(8,128)(2,1)S(1)} %get-tuple-element.182), channel_id=1, source_target_pairs={{0,8},{1,9},{2,10},{3,11},{4,12},{5,13},{6,14},{7,15},{8,0},{9,1},... | collective-permute-start | bytes 344072 | tf_op jit(solution)/shard_map/ppermute | solution.py:444
  84.8 6.6 %collective-permute-done.16.refs_2_ = bf16[1,448,128]{2,1,0:T(8,128)(2,1)S(1)} collective-permute-done((bf16[1,448,128]{2,1,0:T(8,128)(2,1)S(1)}, bf16[1,448,128]{2,1,0:T(8,128)(2,1)S(1)}, u32[]{:S(2)}, u32[]{:S(2)}) %collective-permute-start.16) | collective-permute-done | bytes 114720 | tf_op jit(solution)/shard_map/ppermute | solution.py:444
  91.5 2.6 %collective-permute-start.20 = (bf16[1,448,128]{2,1,0:T(8,128)(2,1)S(1)}, bf16[1,448,128]{2,1,0:T(8,128)(2,1)S(1)}, u32[]{:S(2)}, u32[]{:S(2)}) collective-permute-start(bf16[1,448,128]{2,1,0:T(8,128)(2,1)S(1)} %shard_map.310), channel_id=1, source_target_pairs={{0,12},{1,13},{2,14},{3,15},{4,8},{5,9},{6,10},{7,11},{8,4},{9,5},... | collective-permute-start | bytes 344072 | tf_op jit(solution)/shard_map/ppermute | solution.py:444
  96.2 3.1 %collective-permute-done.20 = bf16[1,448,128]{2,1,0:T(8,128)(2,1)S(1)} collective-permute-done((bf16[1,448,128]{2,1,0:T(8,128)(2,1)S(1)}, bf16[1,448,128]{2,1,0:T(8,128)(2,1)S(1)}, u32[]{:S(2)}, u32[]{:S(2)}) %collective-permute-start.20) | collective-permute-done | bytes 114720 | tf_op jit(solution)/shard_map/ppermute | solution.py:444
  99.3 3.5 %collective-permute-done.19 = bf16[1,448,128]{2,1,0:T(8,128)(2,1)S(1)} collective-permute-done((bf16[1,448,128]{2,1,0:T(8,128)(2,1)S(1)}, bf16[1,448,128]{2,1,0:T(8,128)(2,1)S(1)}, u32[]{:S(2)}, u32[]{:S(2)}) %collective-permute-start.19) | collective-permute-done | bytes 114720 | tf_op jit(solution)/shard_map/ppermute | solution.py:444
  106.4 3.2 %shard_map.311 = bf16[3,768,384]{2,1,0:T(8,128)(2,1)} custom-call(s32[2]{0:T(128)S(1)} %copy-done.6, s32[3,128,8]{2,1,0:T(8,128)S(1)} %copy-done.3, bf16[608,384]{1,0:T(8,128)(2,1)S(1)} %get-tuple-element.185.own_ref, bf16[608,384]{1,0:T(8,128)(2,1)S(1)} %collective-permute-done.22.got_ref), custom_call_target="tpu_custom_call" | custom-call | bytes 2715656 | tf_op jit(solution)/shard_map/pallas_call | solution.py:568
  109.6 3.1 %shard_map.312 = bf16[3,768,384]{2,1,0:T(8,128)(2,1)} custom-call(s32[2]{0:T(128)S(1)} %copy-done.6, s32[3,128,8]{2,1,0:T(8,128)S(1)} %copy-done.3, bf16[768,384]{1,0:T(8,128)(2,1)S(1)} %get-tuple-element.184.own_ref, bf16[768,384]{1,0:T(8,128)(2,1)S(1)} %collective-permute-done.21.got_ref), custom_call_target="tpu_custom_call" | custom-call | bytes 2961416 | tf_op jit(solution)/shard_map/pallas_call | solution.py:568
  112.7 4.6 %collective-permute-done.25 = bf16[4,448,128]{2,1,0:T(8,128)(2,1)S(1)} collective-permute-done((bf16[4,448,128]{2,1,0:T(8,128)(2,1)S(1)}, bf16[4,448,128]{2,1,0:T(8,128)(2,1)S(1)}, u32[]{:S(2)}, u32[]{:S(2)}) %collective-permute-start.25) | collective-permute-done | bytes 458784 | tf_op jit(solution)/shard_map/ppermute | solution.py:452
  117.3 5.7 %collective-permute-done.24 = bf16[4,448,128]{2,1,0:T(8,128)(2,1)S(1)} collective-permute-done((bf16[4,448,128]{2,1,0:T(8,128)(2,1)S(1)}, bf16[4,448,128]{2,1,0:T(8,128)(2,1)S(1)}, u32[]{:S(2)}, u32[]{:S(2)}) %collective-permute-start.24) | collective-permute-done | bytes 458784 | tf_op jit(solution)/shard_map/ppermute | solution.py:452
  123.3 3.8 %collective-permute-done.26.got_ref = bf16[4,4,448,128]{3,2,1,0:T(8,128)(2,1)S(1)} collective-permute-done((bf16[4,4,448,128]{3,2,1,0:T(8,128)(2,1)S(1)}, bf16[4,4,448,128]{3,2,1,0:T(8,128)(2,1)S(1)}, u32[]{:S(2)}, u32[]{:S(2)}) %collective-permute-start.26) | collective-permute-done | bytes 1835040 | tf_op jit(solution)/shard_map/ppermute | solution.py:444
  127.0 4.0 %shard_map.313 = (f32[1536,384]{1,0:T(8,128)}, f32[384,1536]{1,0:T(8,128)}, f32[384,384]{1,0:T(8,128)}, f32[1536]{0:T(1024)}, f32[384]{0:T(512)}, /*index=5*/f32...) custom-call(s32[2]{0:T(128)S(1)} %copy-done.6, ...), custom_call_target="tpu_custom_call" | custom-call | bytes 10767880 | tf_op jit(solution)/shard_map/pallas_call | solution.py:568
  (106 shorter events, 34.5 us)
Async XLA Ops:
  0.6 6.8 %collective-permute-start = (s32[3]{0:T(128)}, s32[3]{0:T(128)S(1)}, u32[]{:S(2)}, u32[]{:S(2)}) collective-permute-start(s32[3]{0:T(128)} %groups_ref.1), channel_id=1, source_target_pairs={{0,1},{1,0},{2,3},{3,2},{4,5},{5,4},{6,7},{7,6},{8,9},{9,8},{10,11... | collective-permute-start | bytes 44 | tf_op jit(solution)/shard_map/ppermute | solution.py:444
  4.8 21.5 %collective-permute-start.1 = (bf16[400,384]{1,0:T(8,128)(2,1)}, bf16[400,384]{1,0:T(8,128)(2,1)S(1)}, u32[]{:S(2)}, u32[]{:S(2)}) collective-permute-start(bf16[400,384]{1,0:T(8,128)(2,1)} %get-tuple-element.113), channel_id=1, source_target_pairs={{0,16},{16,0},{1,17},{17,1},{2,18},{18,2},{3,19},{19,3},{4,20},{20... | collective-permute-start | bytes 921608 | tf_op jit(solution)/shard_map/ppermute | solution.py:609
  8.3 5.8 %collective-permute-start.2 = (s32[6]{0:T(128)S(1)}, s32[6]{0:T(128)S(1)}, u32[]{:S(2)}, u32[]{:S(2)}) collective-permute-start(s32[6]{0:T(128)S(1)} %pad_add_fusion.1), channel_id=1, source_target_pairs={{0,2},{1,3},{2,0},{3,1},{4,6},{5,7},{6,4},{7,5},{8,10},{9,11},{10,... | collective-permute-start | bytes 80 | tf_op jit(solution)/shard_map/ppermute | solution.py:444
  13.4 16.6 %collective-permute-start.3 = (bf16[400,384]{1,0:T(8,128)(2,1)}, bf16[400,384]{1,0:T(8,128)(2,1)S(1)}, u32[]{:S(2)}, u32[]{:S(2)}) collective-permute-start(bf16[400,384]{1,0:T(8,128)(2,1)} %get-tuple-element.120.own_ref), channel_id=1, source_target_pairs={{0,16},{16,0},{1,17},{17,1},{2,18},{18,2},{3,19},{19,3},{4,20},{20... | collective-permute-start | bytes 921608 | tf_op jit(solution)/shard_map/ppermute | solution.py:621
  14.1 5.8 %collective-permute-start.4 = (s32[12]{0:T(128)S(1)}, s32[12]{0:T(128)S(1)}, u32[]{:S(2)}, u32[]{:S(2)}) collective-permute-start(s32[12]{0:T(128)S(1)} %pad_add_fusion.2), channel_id=1, source_target_pairs={{0,4},{1,5},{2,6},{3,7},{4,0},{5,1},{6,2},{7,3},{8,12},{9,13},{10,... | collective-permute-start | bytes 152 | tf_op jit(solution)/shard_map/ppermute | solution.py:444
  20.0 19.7 %collective-permute-start.6 = (bf16[608,384]{1,0:T(8,128)(2,1)}, bf16[608,384]{1,0:T(8,128)(2,1)S(1)}, u32[]{:S(2)}, u32[]{:S(2)}) collective-permute-start(bf16[608,384]{1,0:T(8,128)(2,1)} %get-tuple-element.127), channel_id=1, source_target_pairs={{0,16},{16,0},{1,17},{17,1},{2,18},{18,2},{3,19},{19,3},{4,20},{20... | collective-permute-start | bytes 1400840 | tf_op jit(solution)/shard_map/ppermute | solution.py:638
  21.7 4.5 %collective-permute-start.5 = (s32[24]{0:T(128)S(1)}, s32[24]{0:T(128)S(1)}, u32[]{:S(2)}, u32[]{:S(2)}) collective-permute-start(s32[24]{0:T(128)S(1)} %pad_add_fusion.3), channel_id=1, source_target_pairs={{0,8},{1,9},{2,10},{3,11},{4,12},{5,13},{6,14},{7,15},{8,0},{9,1},... | collective-permute-start | bytes 296 | tf_op jit(solution)/shard_map/ppermute | solution.py:444
  49.0 11.0 %collective-permute-start.8 = (bf16[4,336,128]{2,1,0:T(8,128)(2,1)S(1)}, bf16[4,336,128]{2,1,0:T(8,128)(2,1)S(1)}, u32[]{:S(2)}, u32[]{:S(2)}) collective-permute-start(bf16[4,336,128]{2,1,0:T(8,128)(2,1)S(1)} %get-tuple-element.161), channel_id=1, source_target_pairs={{0,16},{1,17},{2,18},{3,19},{4,20},{5,21},{6,22},{7,23},{8,24},{9,... | collective-permute-start | bytes 1032200 | tf_op jit(solution)/shard_map/ppermute | solution.py:452
  49.6 17.2 %collective-permute-start.9 = (bf16[4,336,128]{2,1,0:T(8,128)(2,1)S(1)}, bf16[4,336,128]{2,1,0:T(8,128)(2,1)S(1)}, u32[]{:S(2)}, u32[]{:S(2)}) collective-permute-start(bf16[4,336,128]{2,1,0:T(8,128)(2,1)S(1)} %get-tuple-element.162), channel_id=1, source_target_pairs={{0,2},{1,3},{2,0},{3,1},{4,6},{5,7},{6,4},{7,5},{8,10},{9,11},{10,... | collective-permute-start | bytes 1032200 | tf_op jit(solution)/shard_map/ppermute | solution.py:452
  50.1 16.7 %collective-permute-start.10 = (bf16[4,336,128]{2,1,0:T(8,128)(2,1)S(1)}, bf16[4,336,128]{2,1,0:T(8,128)(2,1)S(1)}, u32[]{:S(2)}, u32[]{:S(2)}) collective-permute-start(bf16[4,336,128]{2,1,0:T(8,128)(2,1)S(1)} %get-tuple-element.163), channel_id=1, source_target_pairs={{0,18},{1,19},{2,16},{3,17},{4,22},{5,23},{6,20},{7,21},{8,26},{9,... | collective-permute-start | bytes 1032200 | tf_op jit(solution)/shard_map/ppermute | solution.py:452
  68.7 5.3 %collective-permute-start.12 = (bf16[4,112,128]{2,1,0:T(8,128)(2,1)S(1)}, bf16[4,112,128]{2,1,0:T(8,128)(2,1)S(1)}, u32[]{:S(2)}, u32[]{:S(2)}) collective-permute-start(bf16[4,112,128]{2,1,0:T(8,128)(2,1)S(1)} %get-tuple-element.171), channel_id=1, source_target_pairs={{0,16},{1,17},{2,18},{3,19},{4,20},{5,21},{6,22},{7,23},{8,24},{9,... | collective-permute-start | bytes 344072 | tf_op jit(solution)/shard_map/ppermute | solution.py:452
  70.3 7.4 %collective-permute-start.13 = (bf16[4,112,128]{2,1,0:T(8,128)(2,1)S(1)}, bf16[4,112,128]{2,1,0:T(8,128)(2,1)S(1)}, u32[]{:S(2)}, u32[]{:S(2)}) collective-permute-start(bf16[4,112,128]{2,1,0:T(8,128)(2,1)S(1)} %get-tuple-element.172), channel_id=1, source_target_pairs={{0,2},{1,3},{2,0},{3,1},{4,6},{5,7},{6,4},{7,5},{8,10},{9,11},{10,... | collective-permute-start | bytes 344072 | tf_op jit(solution)/shard_map/ppermute | solution.py:452
  70.8 6.9 %collective-permute-start.14 = (bf16[4,112,128]{2,1,0:T(8,128)(2,1)S(1)}, bf16[4,112,128]{2,1,0:T(8,128)(2,1)S(1)}, u32[]{:S(2)}, u32[]{:S(2)}) collective-permute-start(bf16[4,112,128]{2,1,0:T(8,128)(2,1)S(1)} %get-tuple-element.173), channel_id=1, source_target_pairs={{0,18},{1,19},{2,16},{3,17},{4,22},{5,23},{6,20},{7,21},{8,26},{9,... | collective-permute-start | bytes 344072 | tf_op jit(solution)/shard_map/ppermute | solution.py:452
  77.9 25.0 %collective-permute-start.21 = (bf16[768,384]{1,0:T(8,128)(2,1)S(1)}, bf16[768,384]{1,0:T(8,128)(2,1)S(1)}, u32[]{:S(2)}, u32[]{:S(2)}) collective-permute-start(bf16[768,384]{1,0:T(8,128)(2,1)S(1)} %get-tuple-element.184.own_ref), channel_id=1, source_target_pairs={{0,16},{16,0},{1,17},{17,1},{2,18},{18,2},{3,19},{19,3},{4,20},{20... | collective-permute-start | bytes 1769480 | tf_op jit(solution)/shard_map/ppermute | solution.py:706
  78.5 24.4 %collective-permute-start.22 = (bf16[608,384]{1,0:T(8,128)(2,1)S(1)}, bf16[608,384]{1,0:T(8,128)(2,1)S(1)}, u32[]{:S(2)}, u32[]{:S(2)}) collective-permute-start(bf16[608,384]{1,0:T(8,128)(2,1)S(1)} %get-tuple-element.185.own_ref), channel_id=1, source_target_pairs={{0,16},{16,0},{1,17},{17,1},{2,18},{18,2},{3,19},{19,3},{4,20},{20... | collective-permute-start | bytes 1400840 | tf_op jit(solution)/shard_map/ppermute | solution.py:706
  80.0 4.8 %collective-permute-start.15 = (bf16[1,448,128]{2,1,0:T(8,128)(2,1)S(1)}, bf16[1,448,128]{2,1,0:T(8,128)(2,1)S(1)}, u32[]{:S(2)}, u32[]{:S(2)}) collective-permute-start(bf16[1,448,128]{2,1,0:T(8,128)(2,1)S(1)} %get-tuple-element.181), channel_id=1, source_target_pairs={{0,4},{1,5},{2,6},{3,7},{4,0},{5,1},{6,2},{7,3},{8,12},{9,13},{10,... | collective-permute-start | bytes 344072 | tf_op jit(solution)/shard_map/ppermute | solution.py:444
  80.4 11.0 %collective-permute-start.16 = (bf16[1,448,128]{2,1,0:T(8,128)(2,1)S(1)}, bf16[1,448,128]{2,1,0:T(8,128)(2,1)S(1)}, u32[]{:S(2)}, u32[]{:S(2)}) collective-permute-start(bf16[1,448,128]{2,1,0:T(8,128)(2,1)S(1)} %get-tuple-element.182), channel_id=1, source_target_pairs={{0,8},{1,9},{2,10},{3,11},{4,12},{5,13},{6,14},{7,15},{8,0},{9,1},... | collective-permute-start | bytes 344072 | tf_op jit(solution)/shard_map/ppermute | solution.py:444
  83.0 8.4 %collective-permute-start.17 = (bf16[1,448,128]{2,1,0:T(8,128)(2,1)S(1)}, bf16[1,448,128]{2,1,0:T(8,128)(2,1)S(1)}, u32[]{:S(2)}, u32[]{:S(2)}) collective-permute-start(bf16[1,448,128]{2,1,0:T(8,128)(2,1)S(1)} %get-tuple-element.183), channel_id=1, source_target_pairs={{0,12},{1,13},{2,14},{3,15},{4,8},{5,9},{6,10},{7,11},{8,4},{9,5},... | collective-permute-start | bytes 344072 | tf_op jit(solution)/shard_map/ppermute | solution.py:444
  91.5 7.9 %collective-permute-start.20 = (bf16[1,448,128]{2,1,0:T(8,128)(2,1)S(1)}, bf16[1,448,128]{2,1,0:T(8,128)(2,1)S(1)}, u32[]{:S(2)}, u32[]{:S(2)}) collective-permute-start(bf16[1,448,128]{2,1,0:T(8,128)(2,1)S(1)} %shard_map.310), channel_id=1, source_target_pairs={{0,12},{1,13},{2,14},{3,15},{4,8},{5,9},{6,10},{7,11},{8,4},{9,5},... | collective-permute-start | bytes 344072 | tf_op jit(solution)/shard_map/ppermute | solution.py:444
  94.1 8.7 %collective-permute-start.19 = (bf16[1,448,128]{2,1,0:T(8,128)(2,1)S(1)}, bf16[1,448,128]{2,1,0:T(8,128)(2,1)S(1)}, u32[]{:S(2)}, u32[]{:S(2)}) collective-permute-start(bf16[1,448,128]{2,1,0:T(8,128)(2,1)S(1)} %shard_map.310), channel_id=1, source_target_pairs={{0,8},{1,9},{2,10},{3,11},{4,12},{5,13},{6,14},{7,15},{8,0},{9,1},... | collective-permute-start | bytes 344072 | tf_op jit(solution)/shard_map/ppermute | solution.py:444
  96.0 6.8 %collective-permute-start.18 = (bf16[1,448,128]{2,1,0:T(8,128)(2,1)S(1)}, bf16[1,448,128]{2,1,0:T(8,128)(2,1)S(1)}, u32[]{:S(2)}, u32[]{:S(2)}) collective-permute-start(bf16[1,448,128]{2,1,0:T(8,128)(2,1)S(1)} %shard_map.310), channel_id=1, source_target_pairs={{0,4},{1,5},{2,6},{3,7},{4,0},{5,1},{6,2},{7,3},{8,12},{9,13},{10,... | collective-permute-start | bytes 344072 | tf_op jit(solution)/shard_map/ppermute | solution.py:444
  102.9 14.4 %collective-permute-start.25 = (bf16[4,448,128]{2,1,0:T(8,128)(2,1)S(1)}, bf16[4,448,128]{2,1,0:T(8,128)(2,1)S(1)}, u32[]{:S(2)}, u32[]{:S(2)}) collective-permute-start(bf16[4,448,128]{2,1,0:T(8,128)(2,1)S(1)} %maximum_bitcast_fusion), channel_id=1, source_target_pairs={{0,18},{1,19},{2,16},{3,17},{4,22},{5,23},{6,20},{7,21},{8,26},{9,... | collective-permute-start | bytes 1376264 | tf_op jit(solution)/shard_map/ppermute | solution.py:452
  104.7 18.2 %collective-permute-start.24 = (bf16[4,448,128]{2,1,0:T(8,128)(2,1)S(1)}, bf16[4,448,128]{2,1,0:T(8,128)(2,1)S(1)}, u32[]{:S(2)}, u32[]{:S(2)}) collective-permute-start(bf16[4,448,128]{2,1,0:T(8,128)(2,1)S(1)} %maximum_bitcast_fusion), channel_id=1, source_target_pairs={{0,2},{1,3},{2,0},{3,1},{4,6},{5,7},{6,4},{7,5},{8,10},{9,11},{10,... | collective-permute-start | bytes 1376264 | tf_op jit(solution)/shard_map/ppermute | solution.py:452
  104.9 18.1 %collective-permute-start.23 = (bf16[4,448,128]{2,1,0:T(8,128)(2,1)S(1)}, bf16[4,448,128]{2,1,0:T(8,128)(2,1)S(1)}, u32[]{:S(2)}, u32[]{:S(2)}) collective-permute-start(bf16[4,448,128]{2,1,0:T(8,128)(2,1)S(1)} %maximum_bitcast_fusion), channel_id=1, source_target_pairs={{0,16},{1,17},{2,18},{3,19},{4,20},{5,21},{6,22},{7,23},{8,24},{9,... | collective-permute-start | bytes 1376264 | tf_op jit(solution)/shard_map/ppermute | solution.py:452
  (23 other events, 279.5 us)

commit v4 on v3

--- a/solution.py
+++ b/solution.py
@@ -3,6 +3,7 @@
 
 import jax
 import jax.numpy as jnp
+import numpy as np
 from jax import lax
 from jax.experimental import pallas as pl
 from jax.experimental.pallas import tpu as pltpu
@@ -73,79 +74,55 @@
     earlier = ones_where(jnp.logical_and(column < row, (column >> 4) == (row >> 4)))
     rank = within + dot(earlier, totals)
     rank = jnp.where(marks > 0.5, float(unmasked), rank)
-    rank = jnp.concatenate([rank, jnp.zeros((LANES - count, LANES), F32)], axis=0)
-    down = jnp.transpose(rank).astype(jnp.int32)
-    rank = rank.astype(jnp.int32)
     across = []
-    for copy in range(copies):
-        first = rank[16 * copy : 16 * copy + blocks]
-        second = rank[16 * copy + blocks : 16 * copy + 2 * blocks]
-        across.append(jnp.concatenate([jnp.where(tm == 0, first, second), rank[:8-blocks]], axis=0))
-    return across, down
+    for first in range(0, count, 16):
+        mine = jnp.where(tm == 0, rank[first : first + blocks], rank[first + blocks : first + 2 * blocks])
+        across.append(jnp.concatenate([mine, jnp.zeros((16 - blocks, LANES), F32)], axis=0))
+    return jnp.concatenate(across, axis=0)
 
 
 def picks(rank, labels):
-    wide = jnp.broadcast_to(labels, (labels.shape[0], LANES))
+    wide = jnp.broadcast_to(labels.astype(F32), (labels.shape[0], LANES))
     return jnp.concatenate([ones_where(wide == rank[b : b + 1, :]) for b in range(rank.shape[0])], axis=1)
 
 
-def load_halves(copies, half_refs, arrived, source_ref):
-    loads = [
-        pltpu.make_async_copy(source_ref.at[copy], half_refs.at[at], arrived.at[at]) for at, copy in enumerate(copies)
-    ]
-    for load in loads:
-        load.start()
-    return loads
-
-
-def prep_theirs_kernel(unmasked, place_ref, masked_ref, tokens_ref, theirs_ref, rank_ref, down_ref, half_refs, arrived):
+def ranks_of(rank_ref, copy, half):
+    return rank_ref[pl.ds(pl.multiple_of(16 * copy, 16), 16), :][: half // LANES]
+
+
+def prep_theirs_kernel(
+    unmasked, place_ref, masked_ref, tokens_ref, theirs_ref, rank_ref, half_ref, arrived
+):
     tm = place_ref[0]
     half = tokens_ref.shape[1]
-    blocks = half // LANES
-    (load,) = load_halves((1 - tm,), half_refs, arrived, tokens_ref)
-    across, down = all_ranks(masked_ref, tm, half, unmasked)
-    for copy, rank in enumerate(across):
-        rank_ref[copy] = rank
-    for copy in range(len(across)):
-        first = 16 * copy
-        down_ref[copy] = jnp.where(tm == 0, down[:, first : first + 8], down[:, first + blocks : first + blocks + 8])
-    chosen = picks(rank_ref[1 - tm, :blocks], iota((unmasked + EXTRA, 1), 0))
+    load = pltpu.make_async_copy(tokens_ref.at[1 - tm], half_ref, arrived)
+    load.start()
+    rank_ref[...] = all_ranks(masked_ref, tm, half, unmasked)
+    chosen = picks(ranks_of(rank_ref, 1 - tm, half), iota((unmasked + EXTRA, 1), 0))
     load.wait()
-    theirs_ref[...] = dot(chosen, half_refs[0]).astype(BF)
-
-
-def prep_tokens_kernel(unmasked, place_ref, rank_ref, tokens_ref, shared_ref, mine_ref, half_refs, arrived):
+    theirs_ref[...] = dot(chosen, half_ref[...]).astype(BF)
+
+
+def prep_shared_kernel(unmasked, rank_ref, tokens_ref, shared_ref):
+    chosen = picks(ranks_of(rank_ref, 2, tokens_ref.shape[1]), iota((unmasked + EXTRA, 1), 0))
+    shared_ref[...] = dot(chosen, tokens_ref[2]).astype(BF)
+
+
+def prep_grads_kernel(unmasked, place_ref, rank_ref, cotangent_ref, keep_ref, send_ref):
     tm = place_ref[0]
-    copies = (2, tm)
-    loads = load_halves(copies, half_refs, arrived, tokens_ref)
-    labels = iota((unmasked + EXTRA, 1), 0)
-    for role, out_ref in enumerate((shared_ref, mine_ref)):
-        chosen = picks(rank_ref[copies[role], : tokens_ref.shape[1] // LANES], labels)
-        loads[role].wait()
-        out_ref[...] = dot(chosen, half_refs[role]).astype(BF)
-
-
-def prep_grads_kernel(unmasked, place_ref, rank_ref, cotangent_ref, keep_ref, send_ref, half_refs, arrived):
-    tm = place_ref[0]
-    blocks = cotangent_ref.shape[1] // LANES
+    half = cotangent_ref.shape[1]
     rows = unmasked + EXTRA
     part = unmasked // 2
-    loads = load_halves((1 - tm, 2, tm), half_refs, arrived, cotangent_ref)
     labels = iota((rows, 1), 0)
-    chosen = picks(rank_ref[1 - tm, :blocks], labels)
-    loads[0].wait()
-    send_ref[:rows, :] = dot(chosen, half_refs[0]).astype(BF)
     small = iota((part + EXTRA, 1), 0)
     theirs = jnp.where(small < part, small + part * (1 - tm), -1)
     own = jnp.where(small < part, small + part * tm, small + part)
-    chosen = picks(rank_ref[2, :blocks], jnp.concatenate([theirs, own], axis=0))
-    loads[1].wait()
-    both = dot(chosen, half_refs[1]).astype(BF)
+    send_ref[:rows, :] = dot(picks(ranks_of(rank_ref, 1 - tm, half), labels), cotangent_ref[1 - tm]).astype(BF)
+    chosen = picks(ranks_of(rank_ref, 2, half), jnp.concatenate([theirs, own], axis=0))
+    both = dot(chosen, cotangent_ref[2]).astype(BF)
     send_ref[rows:, :] = both[: part + EXTRA]
     keep_ref[rows:, :] = both[part + EXTRA :]
-    chosen = picks(rank_ref[tm, :blocks], labels)
-    loads[2].wait()
-    keep_ref[:rows, :] = dot(chosen, half_refs[2]).astype(BF)
+    keep_ref[:rows, :] = dot(picks(ranks_of(rank_ref, tm, half), labels), cotangent_ref[tm]).astype(BF)
 
 
 def normalise(values):
@@ -154,14 +131,26 @@
     return centred * scale, scale
 
 
-def attention_kernel(
-    unmasked, count, split, place_ref, own_ref, got_ref, small_ref, w_ref,
-    x_ref, q_ref, k_ref, v_ref, p_ref, att_ref, *rest
-):
-    rows, width = own_ref.shape
-    at = iota((rows, width), 0)
-    x = own_ref[...].astype(F32) + got_ref[...].astype(F32)
-    x = jnp.where(at == unmasked, small_ref[0:1, :], x)
+def bias_terms(count):
+    terms, rest = [], math.log(count)
+    for _ in range(3):
+        terms.append(float(np.asarray(rest).astype(jnp.bfloat16)))
+        rest -= terms[-1]
+    return terms
+
+
+def attention_kernel(unmasked, count, split, place_ref, *refs):
+    tm = place_ref[0]
+    if split:
+        own_ref, got_ref, small_ref, w_ref, x_ref, q_ref, k_ref, v_ref, e_ref, inverse_ref, att_ref, whole_ref = refs
+        own = own_ref[...].astype(F32)
+    else:
+        rank_ref, tokens_ref, got_ref, small_ref, w_ref, x_ref, q_ref, k_ref, v_ref, e_ref, inverse_ref, att_ref = refs
+        chosen = picks(ranks_of(rank_ref, tm, tokens_ref.shape[1]), iota((unmasked + EXTRA, 1), 0))
+        own = dot(chosen, tokens_ref[tm])
+    rows, width = got_ref.shape
+    x = own + got_ref[...].astype(F32)
+    x = jnp.where(iota((rows, width), 0) == unmasked, small_ref[0:1, :], x)
     hat, _ = normalise(x)
     normed = (hat * small_ref[1:2, :] + small_ref[2:3, :]).astype(BF)
     mixed = dot(normed, w_ref[...])
@@ -172,32 +161,41 @@
     v_ref[...] = value
     x = x.astype(BF)
     if split:
-        tm = place_ref[0]
         part = unmasked // 2
 
         def take(values):
             chosen = jnp.where(tm == 0, values[:part].astype(F32), values[part:unmasked].astype(F32)).astype(BF)
             return jnp.concatenate([chosen, values[unmasked:]], axis=0)
 
-        rest[0][...] = x
+        whole_ref[...] = x
         x, query = take(x), take(query)
     x_ref[...] = x
     q_ref[...] = query
-    across = iota((1, rows), 1)
-    bias = jnp.where(across < unmasked, 0.0, jnp.where(across == unmasked, math.log(count), -1e30))
-    first = iota((1, LANES), 1) < HEAD_DIM
+    lane = iota((1, LANES), 1)
+    first = lane < HEAD_DIM
+    at = iota((rows, LANES), 0)
+    place = iota((rows, LANES), 1) & (HEAD_DIM - 1)
+    log_count = jnp.zeros((rows, LANES), F32)
+    for which, term in enumerate(bias_terms(count)):
+        log_count = jnp.where(place == which, term, log_count)
+    bias = jnp.where(at < unmasked, 0.0, jnp.where(at == unmasked, log_count, jnp.where(place == 0, -1e30, 0.0)))
+    bias = bias.astype(BF)
+    ones = jnp.where((lane & (HEAD_DIM - 1)) < 3, 1.0, 0.0).astype(BF)
+    all_ones = jnp.ones((rows, LANES), BF)
     for pair in range(width // LANES):
         cols = slice(pair * LANES, (pair + 1) * LANES)
         q_pair, k_pair, v_pair = query[:, cols], key[:, cols], value[:, cols]
+        v_wide = jnp.concatenate([v_pair, all_ones], axis=1)
         parts = []
         for side in range(2):
             mine = first if side == 0 else jnp.logical_not(first)
-            scores = dot_last(jnp.where(mine, q_pair, jnp.zeros_like(q_pair)), k_pair) + bias
-            expo = jnp.exp(scores - jnp.max(scores, axis=1, keepdims=True))
-            probs = (expo * (1.0 / jnp.sum(expo, axis=1, keepdims=True))).astype(BF)
-            p_ref[2 * pair + side] = probs
-            parts.append(dot(probs, v_pair))
-        att_ref[:, cols] = jnp.where(first, parts[0], parts[1]).astype(BF)
+            scores = dot_last(jnp.where(mine, q_pair, ones), jnp.where(mine, k_pair, bias))
+            expo = jnp.exp(scores - jnp.max(scores, axis=1, keepdims=True)).astype(BF)
+            e_ref[2 * pair + side] = expo
+            parts.append(dot(expo, v_wide))
+        inverse = 1.0 / jnp.where(first, parts[0][:, LANES:], parts[1][:, LANES:])
+        inverse_ref[:, cols] = inverse
+        att_ref[:, cols] = (jnp.where(first, parts[0][:, :LANES], parts[1][:, :LANES]) * inverse).astype(BF)
 
 
 def gelu_terms(hidden):
@@ -214,12 +212,17 @@
     return jnp.concatenate([ref[...] for ref in refs], axis=0)
 
 
-def scatter_chunks(me, stage_ref, keep_ref, send_ref):
+def scatter_chunks(me, stage_ref, keep_ref, send_refs):
     depth = keep_ref.shape[2]
     for rel in range(2 * 4 * keep_ref.shape[1]):
         first = pl.multiple_of((me ^ rel) * depth, 16)
-        target = send_ref if rel & 1 else keep_ref
-        target[(rel >> 1) & 3, rel >> 3] = stage_ref[pl.ds(first, depth), :]
+        near, far = (rel >> 1) & 3, rel >> 3
+        chunk = stage_ref[pl.ds(first, depth), :]
+        if rel & 1 == 0:
+            keep_ref[near, far] = chunk
+        else:
+            each = send_refs[0].shape[0]
+            send_refs[near // each][near % each, far] = chunk
 
 
 def stage_weight(stage_ref, first, grad, apart=None):
@@ -279,8 +282,9 @@
 def backward_kernel(
     place_ref, groups_ref, everyone_ref, cot_own, cot_got, middle_ref, normed_ref, active_ref, slope_ref, att_a, att_b,
     small_ref, w_proj_ref, w_up_ref, w_down_ref,
-    grad_middle_ref, grad_att_ref, keep_ref, send_ref, stage_ref
+    grad_middle_ref, grad_att_ref, keep_ref, *send_refs
 ):
+    *send_refs, stage_ref = send_refs
     rows_a, total = att_a.shape[0], cot_own.shape[0]
     everyone = everyone_ref[...]
 
@@ -322,28 +326,27 @@
     ]
     end = stage_rows(stage_ref, end, vectors)
     clear_rest(stage_ref, end)
-    scatter_chunks(place_ref[1], stage_ref, keep_ref, send_ref)
-
-
-def attention_back_kernel(row_from, g_ref, att_ref, q_ref, k_ref, v_ref, p_ref, dq_ref, dk_ref, dv_ref):
-    width = q_ref.shape[1]
-    rows = q_ref.shape[0]
+    scatter_chunks(place_ref[1], stage_ref, keep_ref, send_refs)
+
+
+def attention_back_kernel(row_from, g_ref, att_ref, q_ref, k_ref, v_ref, e_ref, inverse_ref, dq_ref, dk_ref, dv_ref):
+    rows, width = q_ref.shape
     first = iota((1, LANES), 1) < HEAD_DIM
     for pair in range(width // LANES):
         cols = slice(pair * LANES, (pair + 1) * LANES)
-        g_pair = g_ref[row_from : row_from + rows, cols]
         q_pair, k_pair, v_pair = q_ref[:, cols], k_ref[:, cols], v_ref[:, cols]
+        g_pair = (g_ref[row_from : row_from + rows, cols].astype(F32) * inverse_ref[:, cols]).astype(BF)
         agree = g_pair.astype(F32) * att_ref[:, cols].astype(F32)
         dq, dk, dv = [], [], []
         for side in range(2):
             mine = first if side == 0 else jnp.logical_not(first)
             correction = jnp.sum(jnp.where(mine, agree, 0.0), axis=1, keepdims=True)
-            probs = p_ref[2 * pair + side]
+            expo = e_ref[2 * pair + side]
             grad_probs = dot_last(jnp.where(mine, g_pair, jnp.zeros_like(g_pair)), v_pair)
-            grad_scores = (probs.astype(F32) * (grad_probs - correction)).astype(BF)
+            grad_scores = expo * (grad_probs - correction).astype(BF)
             dq.append(dot(grad_scores, k_pair))
             dk.append(dot_rows(grad_scores, q_pair))
-            dv.append(dot_rows(probs, g_pair))
+            dv.append(dot_rows(expo, g_pair))
         dq_ref[:, cols] = (jnp.where(first, dq[0], dq[1]) * HEAD_DIM ** (-0.5)).astype(BF)
         dk_ref[:, cols] = jnp.where(first, dk[0], dk[1]).astype(BF)
         dv_ref[:, cols] = jnp.where(first, dv[0], dv[1]).astype(BF)
@@ -351,8 +354,9 @@
 
 def inputs_back_kernel(
     unmasked, place_ref, x_a, x_b, dq_a, dq_b, dk_a, dk_b, dv_a, dv_b, grad_middle_ref, small_ref, w_ref,
-    grad_ref, keep_ref, send_ref, stage_ref
+    grad_ref, keep_ref, *send_refs
 ):
+    *send_refs, stage_ref = send_refs
     rows, width = x_a.shape
     part = unmasked // 2
     tm = place_ref[0]
@@ -384,41 +388,45 @@
     )
     end = stage_rows(stage_ref, end, vectors)
     clear_rest(stage_ref, end)
-    scatter_chunks(place_ref[1], stage_ref, keep_ref, send_ref)
-
-
-def place_back(down, rows, half):
-    labels = jnp.broadcast_to(iota((1, rows), 1), (LANES, rows))
+    scatter_chunks(place_ref[1], stage_ref, keep_ref, send_refs)
+
+
+def place_back(rank_ref, copy, rows, half):
+    down = jnp.transpose(ranks_of(rank_ref, copy, 16 * LANES))
+    labels = jnp.broadcast_to(iota((1, rows), 1).astype(F32), (LANES, rows))
     return jnp.concatenate([ones_where(labels == down[:, b : b + 1]) for b in range(half // LANES)], axis=0)
 
 
-def outputs_kernel(unmasked, place_ref, down_ref, own_ref, got_ref, out_ref):
+def outputs_kernel(unmasked, place_ref, rank_ref, own_ref, got_ref, out_ref):
     tm = place_ref[0]
     half = out_ref.shape[1]
     rows = unmasked + EXTRA
     part = unmasked // 2
-    out_ref[tm] = dot(place_back(down_ref[tm], rows, half), own_ref[:rows]).astype(BF)
-    out_ref[1 - tm] = dot(place_back(down_ref[1 - tm], rows, half), got_ref[:rows]).astype(BF)
+    out_ref[tm] = dot(place_back(rank_ref, tm, rows, half), own_ref[:rows]).astype(BF)
+    out_ref[1 - tm] = dot(place_back(rank_ref, 1 - tm, rows, half), got_ref[:rows]).astype(BF)
     own = own_ref[rows:].astype(F32)
     got = got_ref[rows:].astype(F32)
     left = jnp.where(tm == 0, own[:part], got[:part])
     right = jnp.where(tm == 0, got[:part], own[:part])
     whole = jnp.concatenate([left, right, own[part:]], axis=0).astype(BF)
-    out_ref[2] = dot(place_back(down_ref[2], rows, half), whole).astype(BF)
-
-
-def grads_out_kernel(unmasked, place_ref, down_ref, own_ref, got_ref, out_ref):
+    out_ref[2] = dot(place_back(rank_ref, 2, rows, half), whole).astype(BF)
+
+
+def grads_out_kernel(unmasked, place_ref, rank_ref, own_ref, got_ref, out_ref):
     tm = place_ref[0]
     half = out_ref.shape[1]
-    out_ref[tm] = dot(place_back(down_ref[tm], unmasked, half), own_ref[:unmasked]).astype(BF)
-    out_ref[1 - tm] = dot(place_back(down_ref[1 - tm], unmasked, half), got_ref[:unmasked]).astype(BF)
+    out_ref[tm] = dot(place_back(rank_ref, tm, unmasked, half), own_ref[:unmasked]).astype(BF)
+    out_ref[1 - tm] = dot(place_back(rank_ref, 1 - tm, unmasked, half), got_ref[:unmasked]).astype(BF)
     whole = (own_ref[unmasked:].astype(F32) + got_ref[unmasked:].astype(F32)).astype(BF)
-    out_ref[2] = dot(place_back(down_ref[2], unmasked, half), whole).astype(BF)
-
-
-def fold_kernel(keep_ref, got_ref, *out_refs):
+    out_ref[2] = dot(place_back(rank_ref, 2, unmasked, half), whole).astype(BF)
+
+
+def fold_kernel(keep_ref, *refs):
+    got_refs, out_refs = refs[:-4], refs[-4:]
+    each = got_refs[0].shape[0]
     for step, out_ref in enumerate(out_refs):
-        out_ref[...] = (keep_ref[step].astype(F32) + got_ref[step].astype(F32)).astype(BF)
+        got = got_refs[step // each][step % each]
+        out_ref[...] = (keep_ref[step].astype(F32) + got.astype(F32)).astype(BF)
 
 
 def fold_four_kernel(units, *refs):
@@ -452,12 +460,14 @@
     return lax.ppermute(values, ("tm", "clip"), pairs)
 
 
-def sum_nearby(keep, send, after, before=()):
+def sum_cores(keep, send, after):
     _, groups, depth, _ = keep.shape
-    got, after = lax.optimization_barrier((clip_swap(send, 1), after))
-    pieces = plain(fold_kernel, [shape(groups, depth, LANES)] * 4)(keep, got)
-    *pieces, before = lax.optimization_barrier((*pieces, before))
-    return [pieces[0]] + [near_swap(pieces[step], step) for step in (1, 2, 3)], before
+    got, after = lax.optimization_barrier(([clip_swap(part, 1) for part in send], after))
+    return plain(fold_kernel, [shape(groups, depth, LANES)] * 4)(keep, *got)
+
+
+def spread_near(pieces):
+    return [pieces[0]] + [near_swap(pieces[step], step) for step in (1, 2, 3)]
 
 
 def sum_over_devices(first_pieces, second_pieces, send_far, beside_last):
@@ -483,46 +493,57 @@
         pieces = [total] + [clip_swap(total, step * distance) for step in (1, 2, 3)]
         total = jnp.stack(pieces, axis=1).reshape(-1, depth, LANES)
     total, sent = lax.optimization_barrier((total, sent))
-    pieces = [total] + [near_swap(total, step) for step in (1, 2, 3)]
+    pieces = spread_near([total] * 4)
     last = beside_last(sent)
     *pieces, last = lax.optimization_barrier((*pieces, last))
-    total = jnp.stack(pieces)
-    return total, clip_swap(total, 1), last
-
-
-def gather_chunks(me, own_ref, got_ref, stage_ref, start, depth):
-    for rel in range(2 * 4 * own_ref.shape[1]):
+    return pieces, [clip_swap(piece, 1) for piece in pieces], last
+
+
+def gather_chunks(me, refs, stage_ref, start, depth):
+    for rel in range(8 * refs[0].shape[0]):
         first = pl.multiple_of((me ^ rel) * depth, 16)
-        source = got_ref if rel & 1 else own_ref
-        stage_ref[pl.ds(first, depth), :] = source[(rel >> 1) & 3, rel >> 3, start : start + depth]
-
-
-def unstage_kernel(units, place_ref, own_ref, got_ref, *refs):
-    stage_ref = refs[-1]
-    start = at = 0
+        source = refs[4 * (rel & 1) + ((rel >> 1) & 3)]
+        stage_ref[pl.ds(first, depth), :] = source[rel >> 3, start : start + depth]
+
+
+def unstage_kernel(units, place_ref, *refs):
+    weights = sum(count for _, count, _ in units)
+    vectors = sum(count for _, _, count in units)
+    pieces, outs, vector_outs = refs[:8], refs[8 : 8 + weights], refs[8 + weights : 8 + weights + vectors]
+    stage_ref, done, *wide_refs = refs[8 + weights + vectors :]
+    stores = []
+    start = at = vector_at = 0
     for depth, weights, vectors in units:
-        gather_chunks(place_ref[1], own_ref, got_ref, stage_ref, start, depth)
-        unstage(weights, stage_ref, refs[at : at + weights + vectors])
-        start += depth
-        at += weights + vectors
-
-
-def unstage(weights, stage_ref, outs):
-    first = 0
-    for out_ref in outs[:weights]:
-        depth, width = out_ref.shape
-        for block in range(width // LANES):
-            out_ref[:, block * LANES : (block + 1) * LANES] = stage_ref[first : first + depth, :].astype(F32)
-            first += depth
-    if len(outs) > weights:
-        count = sum(ref.shape[0] // LANES for ref in outs[weights:])
-        rows = stage_ref[first : first + count + -count % 16, :].astype(F32)
-        at = 0
-        for out_ref in outs[weights:]:
-            blocks = out_ref.shape[0] // LANES
-            for block in range(blocks):
-                out_ref[block * LANES : (block + 1) * LANES] = rows[at + block]
-            at += blocks
+        gather_chunks(place_ref[1], pieces, stage_ref, start, depth)
+        first = 0
+        for each in range(at, at + weights):
+            first = widen(stage_ref, first, wide_refs[each], outs[each], done, stores)
+        widen_vectors(stage_ref, first, vector_outs[vector_at : vector_at + vectors])
+        start, at, vector_at = start + depth, at + weights, vector_at + vectors
+    for store in stores:
+        store.wait()
+
+
+def widen(stage_ref, first, wide_ref, out_ref, done, stores):
+    depth, width = out_ref.shape
+    for block in range(width // LANES):
+        columns = slice(block * LANES, (block + 1) * LANES)
+        wide_ref[:, columns] = stage_ref[first : first + depth, :].astype(F32)
+        stores.append(pltpu.make_async_copy(wide_ref.at[:, columns], out_ref.at[:, columns], done.at[len(stores)]))
+        stores[-1].start()
+        first += depth
+    return first
+
+
+def widen_vectors(stage_ref, first, outs):
+    count = sum(ref.shape[0] // LANES for ref in outs)
+    rows = stage_ref[first : first + count + -count % 16, :].astype(F32)
+    at = 0
+    for out_ref in outs:
+        blocks = out_ref.shape[0] // LANES
+        for block in range(blocks):
+            out_ref[block * LANES : (block + 1) * LANES] = rows[at + block]
+        at += blocks
 
 
 def chunk_rows(count, devices):
@@ -563,7 +584,7 @@
     place = jnp.stack([tm, me]).astype(jnp.int32)
     swap = functools.partial(lax.ppermute, axis_name="tm", perm=[(0, 1), (1, 0)])
 
-    def run(kernel, args, outs, scratch=(), scalars=1, limit=20, flops=0, in_hbm=(), hides=True):
+    def run(kernel, args, outs, scratch=(), scalars=1, limit=20, flops=0, in_hbm=(), out_hbm=(), hides=True):
         moved = sum(math.prod(a.shape) * a.dtype.itemsize for a in list(args) + jax.tree.leaves(outs))
         return pl.pallas_call(
             kernel,
@@ -572,7 +593,7 @@
                 SMEM if at < scalars else HBM if at in in_hbm else VMEM
                 for at in range(len(args))
             ],
-            out_specs=jax.tree.map(lambda _: VMEM, outs),
+            out_specs=[HBM if at in out_hbm else VMEM for at in range(len(outs))] if isinstance(outs, list) else VMEM,
             scratch_shapes=list(scratch),
             compiler_params=pltpu.CompilerParams(vmem_limit_bytes=limit << 20),
             cost_estimate=pl.CostEstimate(
@@ -583,8 +604,8 @@
     counts = (2 * width // LANES * hidden + width // LANES * width + 32, 3 * width // LANES * width + 16)
     depths = [chunk_rows(count, devices) for count in counts]
 
-    def chunked(unit):
-        halves = [shape(4, devices // 8, depths[unit], LANES)] * 2
+    def chunked(unit, parts):
+        halves = [shape(near, devices // 8, depths[unit], LANES) for near in [4] + [4 // parts] * parts]
         return halves, [pltpu.VMEM((devices * depths[unit], LANES), BF)]
 
     small = jnp.stack(
@@ -593,30 +614,24 @@
     bias_up = b_up.astype(F32).reshape(1, hidden)
 
     block = shape(rows, width)
-    def loads(count):
-        return [pltpu.VMEM((count, half, width), BF), pltpu.SemaphoreType.DMA((count,))]
-
     everyone = jnp.concatenate([groups, clip_swap(groups, 1)])
-    theirs, rank, down = run(
+    theirs, rank = run(
         functools.partial(prep_theirs_kernel, unmasked),
-        (place, masked, tokens),
-        [block, shape(copies, 8, LANES, kind=jnp.int32), shape(copies, LANES, 8, kind=jnp.int32)],
-        loads(1),
-        limit=60,
+        (place, masked, pltpu.with_memory_space_constraint(tokens, pltpu.HBM)),
+        [block, shape(16 * copies, LANES, kind=F32)],
+        [pltpu.VMEM((half, width), BF), pltpu.SemaphoreType.DMA],
         flops=2 * rows * half * width,
         in_hbm=(2,),
     )
     got_mine = swap(theirs)
     everyone, theirs, rank = lax.optimization_barrier((everyone, theirs, rank))
     everyone = jnp.concatenate([everyone, clip_swap(everyone, 2)])
-    shared, mine = run(
-        functools.partial(prep_tokens_kernel, unmasked),
-        (place, rank, tokens),
-        [block, block],
-        loads(2),
-        limit=60,
-        flops=4 * rows * half * width,
-        in_hbm=(2,),
+    shared = run(
+        functools.partial(prep_shared_kernel, unmasked),
+        (rank, tokens),
+        block,
+        scalars=0,
+        flops=2 * rows * half * width,
     )
     got_shared = swap(shared)
     everyone, shared, rank = lax.optimization_barrier((everyone, shared, rank))
@@ -625,35 +640,33 @@
         functools.partial(prep_grads_kernel, unmasked),
         (place, rank, cotangent),
         [shape(total, width), shape(total, width)],
-        loads(3),
-        limit=60,
         flops=2 * copies * rows * half * width,
-        in_hbm=(2,),
-    )
-    everyone, cot_send = lax.optimization_barrier((everyone, cot_send))
-    distance = 8
-    while distance < clips:
-        everyone = jnp.concatenate([everyone, clip_swap(everyone, distance)])
-        distance *= 2
+    )
+    everyone, cot_own, cot_send = lax.optimization_barrier((everyone, cot_own, cot_send))
     cot_got = swap(cot_send)
 
-    def attend(own, got, split):
+    def attend(sources, got, split):
         queries = some if split else rows
         outs = [
             shape(queries, width), shape(queries, width), block, block,
-            shape(HEADS, queries, rows), shape(queries, width),
+            shape(HEADS, queries, rows), shape(queries, width, kind=F32), shape(queries, width),
         ]
         if split:
             outs.append(block)
         return run(
             functools.partial(attention_kernel, unmasked, hide, split),
-            (place, own, got, small, w_qkv),
+            (place, *sources, got, small, w_qkv),
             outs,
             flops=6 * rows * width * width + 4 * queries * rows * width,
         )
 
-    x_a, q_a, k_a, v_a, p_a, att_a = attend(mine, got_mine, False)
-    x_b, q_b, k_b, v_b, p_b, att_b, x_whole = attend(shared, got_shared, True)
+    x_a, q_a, k_a, v_a, e_a, inverse_a, att_a = attend((rank, tokens), got_mine, False)
+    everyone, att_a = lax.optimization_barrier((everyone, att_a))
+    distance = 8
+    while distance < clips:
+        everyone = jnp.concatenate([everyone, clip_swap(everyone, distance)])
+        distance *= 2
+    x_b, q_b, k_b, v_b, e_b, inverse_b, att_b, x_whole = attend((shared,), got_shared, True)
 
     out_rows, middle, normed_two, active, slope = run(
         forward_kernel,
@@ -665,8 +678,9 @@
         scalars=0,
         flops=2 * total * width * (width + 2 * hidden),
     )
-    halves, stage = chunked(0)
-    grad_middle, grad_att, keep, send = run(
+    out_got = swap(out_rows)
+    halves, stage = chunked(0, 4)
+    grad_middle, grad_att, keep, *send = run(
         backward_kernel,
         (
             place, groups, everyone.reshape(1, -1), cot_own, cot_got, middle, normed_two, active, slope, att_a, att_b,
@@ -678,57 +692,55 @@
         hides=False,
     )
 
-    def attend_back(row_from, grads, att, q, k, v, p):
+    def attend_back(row_from, grads, att, q, k, v, e, inverse):
         return run(
             functools.partial(attention_back_kernel, row_from),
-            (grads, att, q, k, v, p),
+            (grads, att, q, k, v, e, inverse),
             [shape(q.shape[0], width), block, block],
             scalars=0,
             hides=False,
         )
 
-    dq_b, dk_b, dv_b = attend_back(rows, grad_att, att_b, q_b, k_b, v_b, p_b)
-    first_pieces, grad_att = sum_nearby(keep, send, dq_b, grad_att)
-    dq_a, dk_a, dv_a = attend_back(0, grad_att, att_a, q_a, k_a, v_a, p_a)
-    halves, stage = chunked(1)
-    grad_rows, keep, send = run(
+    dq_b, dk_b, dv_b = attend_back(rows, grad_att, att_b, q_b, k_b, v_b, e_b, inverse_b)
+    pieces, grad_att = lax.optimization_barrier((sum_cores(keep, send, dq_b), grad_att))
+    first_pieces = spread_near(pieces)
+    dq_a, dk_a, dv_a = attend_back(0, grad_att, att_a, q_a, k_a, v_a, e_a, inverse_a)
+    dq_a, out_got = lax.optimization_barrier((dq_a, out_got))
+    halves, stage = chunked(1, 2)
+    grad_rows, keep, *send = run(
         functools.partial(inputs_back_kernel, unmasked),
         (place, x_a, x_whole, dq_a, dq_b, dk_a, dk_b, dv_a, dv_b, grad_middle, small, w_qkv),
         [shape(2 * unmasked, width)] + halves,
         stage,
         hides=False,
     )
-    send, first_pieces = lax.optimization_barrier((send, first_pieces))
-    second_pieces, _ = sum_nearby(keep, send, ())
+    pieces, first_pieces = lax.optimization_barrier((sum_cores(keep, send, ()), first_pieces))
+    second_pieces = spread_near(pieces)
 
     def send_rows(pieces):
-        *pieces, grads, outs = lax.optimization_barrier((*pieces, grad_rows, out_rows))
-        return (swap(grads), swap(outs)), pieces
+        *pieces, grads = lax.optimization_barrier((*pieces, grad_rows))
+        return swap(grads), pieces
 
     def place_rows(got):
-        grads_got, out_got = got
         return (
-            run(functools.partial(outputs_kernel, unmasked), (place, down, out_rows, out_got), shape(*tokens.shape)),
-            run(functools.partial(grads_out_kernel, unmasked), (place, down, grad_rows, grads_got), shape(*tokens.shape)),
+            run(functools.partial(outputs_kernel, unmasked), (place, rank, out_rows, out_got), shape(*tokens.shape)),
+            run(functools.partial(grads_out_kernel, unmasked), (place, rank, grad_rows, got), shape(*tokens.shape)),
         )
 
-    sums_own, sums_got, (block_out, grad_tokens) = sum_over_devices(first_pieces, second_pieces, send_rows, place_rows)
-
-    vector = shape(width, kind=F32)
-    outs = [
-        shape(hidden, width, kind=F32), shape(width, hidden, kind=F32), shape(width, width, kind=F32), shape(hidden, kind=F32),
-        vector, vector, vector, vector,
-        shape(width, 3 * width, kind=F32), vector, vector, vector, vector, vector,
-    ]
-    units = tuple(zip(depths, (3, 1), (5, 5)))
+    own, got, (block_out, grad_tokens) = sum_over_devices(first_pieces, second_pieces, send_rows, place_rows)
+    weights = [(hidden, width), (width, hidden), (width, width), (width, 3 * width)]
+    vectors = [hidden] + [width] * 9
     (
-        grad_w_down, grad_w_up, grad_w_proj, grad_b_up, grad_gain_two, grad_shift_two, grad_b_proj, grad_b_down,
-        grad_w_qkv, grad_q_bias, grad_v_bias, grad_gain_one, grad_shift_one, grad_mask_token,
+        grad_w_down, grad_w_up, grad_w_proj, grad_w_qkv,
+        grad_b_up, grad_gain_two, grad_shift_two, grad_b_proj, grad_b_down,
+        grad_q_bias, grad_v_bias, grad_gain_one, grad_shift_one, grad_mask_token,
     ) = run(
-        functools.partial(unstage_kernel, units),
-        (place, sums_own, sums_got),
-        outs,
-        [pltpu.VMEM((devices * max(depths), LANES), BF)],
+        functools.partial(unstage_kernel, tuple(zip(depths, (3, 1), (5, 5)))),
+        (place, *own, *got),
+        [shape(*dims, kind=F32) for dims in weights] + [shape(dim, kind=F32) for dim in vectors],
+        [pltpu.VMEM((devices * max(depths), LANES), BF), pltpu.SemaphoreType.DMA((sum(dims[1] for dims in weights) // LANES,))]
+        + [pltpu.VMEM(dims, F32) for dims in weights],
+        out_hbm=(0, 1, 2, 3),
     )
     return (
         block_out,

time: 132 us -> 122 us (0.924)
  waiting for transfers between devices: 44.6 us -> 37.3 us
  Pallas kernels: 50.3 us -> 46 us
  starting transfers between devices: 33 us -> 36 us
  other arithmetic: 1.83 us -> 0.44 us
    ppermute x13 -> x20, waiting for transfers between devices: 21.9 us -> 16.9 us  [clip_swap(): lax.ppermute(values, 'clip', [(i, i ^ distance) for i in range(size)])]
    pallas_call x13, Pallas kernels: 49.6 us -> 45.3 us  [run(): pl.pallas_call(kernel, out_shape=outs, in_specs=[SMEM if at < scalars els...]
    ppermute x13 -> x20, starting transfers between devices: 15.6 us -> 18.2 us  [clip_swap(): lax.ppermute(values, 'clip', [(i, i ^ distance) for i in range(size)])]
    ppermute x9, waiting for transfers between devices: 22.7 us -> 20.4 us  [near_swap(): return lax.ppermute(values, ('tm', 'clip'), pairs)]
  transfers between devices with their start and end apart: 27 -> 34, of which waited for: 14 -> 19; matrix products, arithmetic and copies ran while one was open for 1% -> 0% of each run, Pallas kernels for 30% -> 34%
where the time goes in v4:
time: 122 us
  Pallas kernels  46 us (38%)
  waiting for transfers between devices  37.3 us (31%)
  starting transfers between devices  36 us (30%)
  between operations  1.26 us (1%)
    pallas_call x13, Pallas kernels, run(): pl.pallas_call(kernel, out_shape=outs, in_specs=[SMEM if at < scalars els...  45.3 us
    ppermute x9, waiting for transfers between devices, near_swap(): return lax.ppermute(values, ('tm', 'clip'), pairs)  20.4 us
    ppermute x20, starting transfers between devices, clip_swap(): lax.ppermute(values, 'clip', [(i, i ^ distance) for i in range(size)])  18.2 us
    ppermute x20, waiting for transfers between devices, clip_swap(): lax.ppermute(values, 'clip', [(i, i ^ distance) for i in range(size)])  16.9 us
    ppermute x9, starting transfers between devices, near_swap(): return lax.ppermute(values, ('tm', 'clip'), pairs)  10.6 us
    ppermute x1, starting transfers between devices, body(): got_mine = swap(theirs)  2.7 us
  transfers between devices with their start and end apart: 34, of which 19 were waited for; matrix products, arithmetic and copies ran while one was open for 0% of the time, Pallas kernels for 34%

profile of v4, /device:TPU:0, one launch (start us, length us, event | category | flops | bytes accessed | tf_op | source)
XLA Modules:
  0.0 121.9 jit_solution(1861597062690132198)
XLA Ops:
  2.0 3.0 %shard_map.297 = (bf16[400,384]{1,0:T(8,128)(2,1)}, f32[48,128]{1,0:T(8,128)S(1)}) custom-call(s32[2]{0:T(128)S(1)} %pad_add_fusion.place_ref, s32[3,1152]{1,0:T(4,128)S(1)} %copy-done.5, bf16[3,768,384]{2,1,0:T(8,128)(2,1)} %refs_1_.1), custom_call_target="tpu_custom_call" | custom-call | flops 235929600 | bytes 2115080 | tf_op jit(solution)/shard_map/pallas_call | solution.py:589
  5.0 2.7 %collective-permute-start.2 = (bf16[400,384]{1,0:T(8,128)(2,1)}, bf16[400,384]{1,0:T(8,128)(2,1)S(1)}, u32[]{:S(2)}, u32[]{:S(2)}) collective-permute-start(bf16[400,384]{1,0:T(8,128)(2,1)} %get-tuple-element.127), channel_id=1, source_target_pairs={{0,16},{16,0},{1,17},{17,1},{2,18},{18,2},{3,19},{19,3},{4,20},{20... | collective-permute-start | bytes 921608 | tf_op jit(solution)/shard_map/ppermute | solution.py:626
  13.0 2.1 %shard_map.301 = (bf16[608,384]{1,0:T(8,128)(2,1)S(1)}, bf16[608,384]{1,0:T(8,128)(2,1)}) custom-call(s32[2]{0:T(128)S(1)} %pad_add_fusion.place_ref, f32[48,128]{1,0:T(8,128)S(1)} %get-tuple-element.131.rank_ref.refs_0_, bf16[3,768,384]{2,1,0:T(8,128)(2,1)S(1)} %copy-done.7), custom_call_target="tpu_custom_call" | custom-call | flops 707788800 | bytes 2727944 | tf_op jit(solution)/shard_map/pallas_call | solution.py:589
  16.8 3.6 %shard_map.299 = (bf16[400,384]{1,0:T(8,128)(2,1)S(1)}, bf16[400,384]{1,0:T(8,128)(2,1)S(1)}, bf16[400,384]{1,0:T(8,128)(2,1)S(1)}, bf16[400,384]{1,0:T(8,128)(2...) custom-call(s32[2]{0:T(128)S(1)} %pad_add_fusion.place_ref, ...), custom_call_target="tpu_custom_call" | custom-call | flops 599654400 | bytes 7070216 | tf_op jit(solution)/shard_map/pallas_call | solution.py:589
  20.4 2.6 %collective-permute-start.5 = (s32[24]{0:T(128)S(1)}, s32[24]{0:T(128)S(1)}, u32[]{:S(2)}, u32[]{:S(2)}) collective-permute-start(s32[24]{0:T(128)S(1)} %pad_add_fusion.3), channel_id=1, source_target_pairs={{0,8},{1,9},{2,10},{3,11},{4,12},{5,13},{6,14},{7,15},{8,0},{9,1},... | collective-permute-start | bytes 296 | tf_op jit(solution)/shard_map/ppermute | solution.py:452
  23.0 3.0 %shard_map.300 = (bf16[208,384]{1,0:T(8,128)(2,1)S(1)}, bf16[208,384]{1,0:T(8,128)(2,1)S(1)}, bf16[400,384]{1,0:T(8,128)(2,1)S(1)}, bf16[400,384]{1,0:T(8,128)(2...) custom-call(s32[2]{0:T(128)S(1)} %pad_add_fusion.place_ref, ...), custom_call_target="tpu_custom_call" | custom-call | flops 481689600 | bytes 4231688 | tf_op jit(solution)/shard_map/pallas_call | solution.py:589
  26.0 5.6 %shard_map.302 = (bf16[608,384]{1,0:T(8,128)(2,1)S(1)}, f32[608,384]{1,0:T(8,128)S(1)}, bf16[608,384]{1,0:T(8,128)(2,1)S(1)}, bf16[608,1536]{1,0:T(8,128)(2,1)S(1)}, bf16[608,1536]{1,0:T(8,128)(2,1)S(1)}) custom-call(bf16[400,384]{1,0:T(8,128)(2,1)S(1)} %get-tuple-element.143.att_a.att_ref, bf16[208,384]{1,0:T(8,128)(2,1)S(1)} %get-tuple-element.144.att_b.att_ref, ...), custom_call_target="tpu_custom_call" | custom-call | flops 1613758464 | bytes 9211392 | tf_op jit(solution)/shard_map/pallas_call | solution.py:589
  33.4 6.3 %shard_map.303 = (f32[608,384]{1,0:T(8,128)S(1)}, bf16[608,384]{1,0:T(8,128)(2,1)S(1)}, bf16[4,4,336,128]{3,2,1,0:T(8,128)(2,1)S(1)}, bf16[1,4,336,128]{3,2,1,0:...) custom-call(s32[2]{0:T(128)S(1)} %pad_add_fusion.place_ref, ...), custom_call_target="tpu_custom_call" | custom-call | flops 1 | bytes 1 | tf_op jit(solution)/shard_map/pallas_call | solution.py:589
  40.8 2.3 %shard_map.304 = (bf16[208,384]{1,0:T(8,128)(2,1)S(1)}, bf16[400,384]{1,0:T(8,128)(2,1)S(1)}, bf16[400,384]{1,0:T(8,128)(2,1)S(1)}) custom-call(bf16[608,384]{1,0:T(8,128)(2,1)S(1)} %get-tuple-element.170.g_ref, bf16[208,384]{1,0:T(8,128)(2,1)S(1)} %get-tuple-element.144.att_b.att_ref, bf16[208,384]{1,0:T(8,128)(2,1)S(1)} %get-tuple-element.156.q_ref, ...), custom_call_target="tpu_custom_call" | custom-call | flops 1 | bytes 1 | tf_op jit(solution)/shard_map/pallas_call | solution.py:589
  47.0 3.2 %shard_map.306 = (bf16[400,384]{1,0:T(8,128)(2,1)S(1)}, bf16[400,384]{1,0:T(8,128)(2,1)S(1)}, bf16[400,384]{1,0:T(8,128)(2,1)S(1)}) custom-call(bf16[608,384]{1,0:T(8,128)(2,1)S(1)} %get-tuple-element.170.g_ref, bf16[400,384]{1,0:T(8,128)(2,1)S(1)} %get-tuple-element.143.att_a.att_ref, bf16[400,384]{1,0:T(8,128)(2,1)S(1)} %get-tuple-element.171.q_ref, ...), custom_call_target="tpu_custom_call" | custom-call | flops 1 | bytes 1 | tf_op jit(solution)/shard_map/pallas_call | solution.py:589
  50.2 4.0 %shard_map.307 = (bf16[768,384]{1,0:T(8,128)(2,1)S(1)}, bf16[4,4,112,128]{3,2,1,0:T(8,128)(2,1)S(1)}, bf16[2,4,112,128]{3,2,1,0:T(8,128)(2,1)S(1)}, bf16[2,4,112,128]{3,2,1,0:T(8,128)(2,1)S(1)}) custom-call(s32[2]{0:T(128)S(1)} %pad_add_fusion.place_ref, bf16[400,384]{1,0:T(8,128)(2,1)S(1)} %get-tuple-element.132.x_a, ...), custom_call_target="tpu_custom_call" | custom-call | flops 1 | bytes 1 | tf_op jit(solution)/shard_map/pallas_call | solution.py:589
  56.2 4.3 %collective-permute-done.15.refs_2_ = bf16[4,336,128]{2,1,0:T(8,128)(2,1)S(1)} collective-permute-done((bf16[4,336,128]{2,1,0:T(8,128)(2,1)S(1)}, bf16[4,336,128]{2,1,0:T(8,128)(2,1)S(1)}, u32[]{:S(2)}, u32[]{:S(2)}) %collective-permute-start.15) | collective-permute-done | bytes 344096 | tf_op jit(solution)/shard_map/ppermute | solution.py:460
  65.4 2.4 %collective-permute-done.17.refs_5_ = bf16[4,112,128]{2,1,0:T(8,128)(2,1)S(1)} collective-permute-done((bf16[4,112,128]{2,1,0:T(8,128)(2,1)S(1)}, bf16[4,112,128]{2,1,0:T(8,128)(2,1)S(1)}, u32[]{:S(2)}, u32[]{:S(2)}) %collective-permute-start.17) | collective-permute-done | bytes 114720 | tf_op jit(solution)/shard_map/ppermute | solution.py:460
  72.5 2.6 %collective-permute-start.21 = (bf16[1,448,128]{2,1,0:T(8,128)(2,1)S(1)}, bf16[1,448,128]{2,1,0:T(8,128)(2,1)S(1)}, u32[]{:S(2)}, u32[]{:S(2)}) collective-permute-start(bf16[1,448,128]{2,1,0:T(8,128)(2,1)S(1)} %get-tuple-element.212), channel_id=1, source_target_pairs={{0,8},{1,9},{2,10},{3,11},{4,12},{5,13},{6,14},{7,15},{8,0},{9,1},... | collective-permute-start | bytes 344072 | tf_op jit(solution)/shard_map/ppermute | solution.py:452
  76.1 5.7 %collective-permute-done.21.refs_2_ = bf16[1,448,128]{2,1,0:T(8,128)(2,1)S(1)} collective-permute-done((bf16[1,448,128]{2,1,0:T(8,128)(2,1)S(1)}, bf16[1,448,128]{2,1,0:T(8,128)(2,1)S(1)}, u32[]{:S(2)}, u32[]{:S(2)}) %collective-permute-start.21) | collective-permute-done | bytes 114720 | tf_op jit(solution)/shard_map/ppermute | solution.py:452
  81.9 2.6 %collective-permute-start.25 = (bf16[1,448,128]{2,1,0:T(8,128)(2,1)S(1)}, bf16[1,448,128]{2,1,0:T(8,128)(2,1)S(1)}, u32[]{:S(2)}, u32[]{:S(2)}) collective-permute-start(bf16[1,448,128]{2,1,0:T(8,128)(2,1)S(1)} %shard_map.310), channel_id=1, source_target_pairs={{0,12},{1,13},{2,14},{3,15},{4,8},{5,9},{6,10},{7,11},{8,4},{9,5},... | collective-permute-start | bytes 344072 | tf_op jit(solution)/shard_map/ppermute | solution.py:452
  86.8 3.0 %collective-permute-done.25 = bf16[1,448,128]{2,1,0:T(8,128)(2,1)S(1)} collective-permute-done((bf16[1,448,128]{2,1,0:T(8,128)(2,1)S(1)}, bf16[1,448,128]{2,1,0:T(8,128)(2,1)S(1)}, u32[]{:S(2)}, u32[]{:S(2)}) %collective-permute-start.25) | collective-permute-done | bytes 114720 | tf_op jit(solution)/shard_map/ppermute | solution.py:452
  89.8 3.2 %collective-permute-done.24 = bf16[1,448,128]{2,1,0:T(8,128)(2,1)S(1)} collective-permute-done((bf16[1,448,128]{2,1,0:T(8,128)(2,1)S(1)}, bf16[1,448,128]{2,1,0:T(8,128)(2,1)S(1)}, u32[]{:S(2)}, u32[]{:S(2)}) %collective-permute-start.24) | collective-permute-done | bytes 114720 | tf_op jit(solution)/shard_map/ppermute | solution.py:452
  93.0 2.3 %collective-permute-start.29 = (bf16[4,448,128]{2,1,0:T(8,128)(2,1)S(1)}, bf16[4,448,128]{2,1,0:T(8,128)(2,1)S(1)}, u32[]{:S(2)}, u32[]{:S(2)}) collective-permute-start(bf16[4,448,128]{2,1,0:T(8,128)(2,1)S(1)} %maximum_bitcast_fusion.refs_0_), channel_id=1, source_target_pairs={{0,18},{1,19},{2,16},{3,17},{4,22},{5,23},{6,20},{7,21},{8,26},{9,... | collective-permute-start | bytes 1376264 | tf_op jit(solution)/shard_map/ppermute | solution.py:460
  96.6 3.4 %shard_map.311 = bf16[3,768,384]{2,1,0:T(8,128)(2,1)} custom-call(s32[2]{0:T(128)S(1)} %pad_add_fusion.place_ref, f32[48,128]{1,0:T(8,128)S(1)} %get-tuple-element.131.rank_ref.refs_0_, bf16[608,384]{1,0:T(8,128)(2,1)S(1)} %get-tuple-element.177.own_ref, bf16[608,384]{1,0:T(8,128)(2,1)S(1)} %collective-permute-done.11.got_ref), custom_call_target="tpu_custom_call" | custom-call | bytes 2727944 | tf_op jit(solution)/shard_map/pallas_call | solution.py:589
  100.0 3.3 %shard_map.312 = bf16[3,768,384]{2,1,0:T(8,128)(2,1)} custom-call(s32[2]{0:T(128)S(1)} %pad_add_fusion.place_ref, f32[48,128]{1,0:T(8,128)S(1)} %get-tuple-element.131.rank_ref.refs_0_, bf16[768,384]{1,0:T(8,128)(2,1)S(1)} %get-tuple-element.214.own_ref, bf16[768,384]{1,0:T(8,128)(2,1)S(1)} %collective-permute-done.26.got_ref), custom_call_target="tpu_custom_call" | custom-call | bytes 2973704 | tf_op jit(solution)/shard_map/pallas_call | solution.py:589
  103.2 4.2 %collective-permute-done.29.refs_3_ = bf16[4,448,128]{2,1,0:T(8,128)(2,1)S(1)} collective-permute-done((bf16[4,448,128]{2,1,0:T(8,128)(2,1)S(1)}, bf16[4,448,128]{2,1,0:T(8,128)(2,1)S(1)}, u32[]{:S(2)}, u32[]{:S(2)}) %collective-permute-start.29) | collective-permute-done | bytes 458784 | tf_op jit(solution)/shard_map/ppermute | solution.py:460
  107.5 5.5 %collective-permute-done.28.refs_2_ = bf16[4,448,128]{2,1,0:T(8,128)(2,1)S(1)} collective-permute-done((bf16[4,448,128]{2,1,0:T(8,128)(2,1)S(1)}, bf16[4,448,128]{2,1,0:T(8,128)(2,1)S(1)}, u32[]{:S(2)}, u32[]{:S(2)}) %collective-permute-start.28) | collective-permute-done | bytes 458784 | tf_op jit(solution)/shard_map/ppermute | solution.py:460
  117.3 4.5 %shard_map.313 = (f32[1536,384]{1,0:T(8,128)}, f32[384,1536]{1,0:T(8,128)}, f32[384,384]{1,0:T(8,128)}, f32[384,1152]{1,0:T(8,128)}, f32[1536]{0:T(1024)}, /*ind...) custom-call(s32[2]{0:T(128)S(1)} %pad_add_fusion.place_ref, ...), custom_call_target="tpu_custom_call" | custom-call | bytes 10767880 | tf_op jit(solution)/shard_map/pallas_call | solution.py:589
  (115 shorter events, 35.4 us)
Async XLA Ops:
  0.7 7.0 %collective-permute-start = (s32[3]{0:T(128)}, s32[3]{0:T(128)S(1)}, u32[]{:S(2)}, u32[]{:S(2)}) collective-permute-start(s32[3]{0:T(128)} %groups_ref.1), channel_id=1, source_target_pairs={{0,1},{1,0},{2,3},{3,2},{4,5},{5,4},{6,7},{7,6},{8,9},{9,8},{10,11... | collective-permute-start | bytes 44 | tf_op jit(solution)/shard_map/ppermute | solution.py:452
  5.0 11.8 %collective-permute-start.2 = (bf16[400,384]{1,0:T(8,128)(2,1)}, bf16[400,384]{1,0:T(8,128)(2,1)S(1)}, u32[]{:S(2)}, u32[]{:S(2)}) collective-permute-start(bf16[400,384]{1,0:T(8,128)(2,1)} %get-tuple-element.127), channel_id=1, source_target_pairs={{0,16},{16,0},{1,17},{17,1},{2,18},{18,2},{3,19},{19,3},{4,20},{20... | collective-permute-start | bytes 921608 | tf_op jit(solution)/shard_map/ppermute | solution.py:626
  7.8 3.5 %collective-permute-start.1 = (s32[6]{0:T(128)S(1)}, s32[6]{0:T(128)S(1)}, u32[]{:S(2)}, u32[]{:S(2)}) collective-permute-start(s32[6]{0:T(128)S(1)} %pad_add_fusion.1), channel_id=1, source_target_pairs={{0,2},{1,3},{2,0},{3,1},{4,6},{5,7},{6,4},{7,5},{8,10},{9,11},{10,... | collective-permute-start | bytes 80 | tf_op jit(solution)/shard_map/ppermute | solution.py:452
  10.6 12.4 %collective-permute-start.3 = (bf16[400,384]{1,0:T(8,128)(2,1)}, bf16[400,384]{1,0:T(8,128)(2,1)}, u32[]{:S(2)}, u32[]{:S(2)}) collective-permute-start(bf16[400,384]{1,0:T(8,128)(2,1)} %shard_map.298.refs_0_), channel_id=1, source_target_pairs={{0,16},{16,0},{1,17},{17,1},{2,18},{18,2},{3,19},{19,3},{4,20},{20... | collective-permute-start | bytes 921608 | tf_op jit(solution)/shard_map/ppermute | solution.py:636
  11.4 3.7 %collective-permute-start.4 = (s32[12]{0:T(128)S(1)}, s32[12]{0:T(128)S(1)}, u32[]{:S(2)}, u32[]{:S(2)}) collective-permute-start(s32[12]{0:T(128)S(1)} %pad_add_fusion.2), channel_id=1, source_target_pairs={{0,4},{1,5},{2,6},{3,7},{4,0},{5,1},{6,2},{7,3},{8,12},{9,13},{10,... | collective-permute-start | bytes 152 | tf_op jit(solution)/shard_map/ppermute | solution.py:452
  15.1 18.3 %collective-permute-start.6 = (bf16[608,384]{1,0:T(8,128)(2,1)}, bf16[608,384]{1,0:T(8,128)(2,1)}, u32[]{:S(2)}, u32[]{:S(2)}) collective-permute-start(bf16[608,384]{1,0:T(8,128)(2,1)} %get-tuple-element.142), channel_id=1, source_target_pairs={{0,16},{16,0},{1,17},{17,1},{2,18},{18,2},{3,19},{19,3},{4,20},{20... | collective-permute-start | bytes 1400840 | tf_op jit(solution)/shard_map/ppermute | solution.py:646
  20.4 12.9 %collective-permute-start.5 = (s32[24]{0:T(128)S(1)}, s32[24]{0:T(128)S(1)}, u32[]{:S(2)}, u32[]{:S(2)}) collective-permute-start(s32[24]{0:T(128)S(1)} %pad_add_fusion.3), channel_id=1, source_target_pairs={{0,8},{1,9},{2,10},{3,11},{4,12},{5,13},{6,14},{7,15},{8,0},{9,1},... | collective-permute-start | bytes 296 | tf_op jit(solution)/shard_map/ppermute | solution.py:452
  31.6 18.6 %collective-permute-start.11 = (bf16[608,384]{1,0:T(8,128)(2,1)S(1)}, bf16[608,384]{1,0:T(8,128)(2,1)S(1)}, u32[]{:S(2)}, u32[]{:S(2)}) collective-permute-start(bf16[608,384]{1,0:T(8,128)(2,1)S(1)} %get-tuple-element.177.own_ref), channel_id=1, source_target_pairs={{0,16},{16,0},{1,17},{17,1},{2,18},{18,2},{3,19},{19,3},{4,20},{20... | collective-permute-start | bytes 1400840 | tf_op jit(solution)/shard_map/ppermute | solution.py:681
  43.5 12.7 %collective-permute-start.14 = (bf16[4,336,128]{2,1,0:T(8,128)(2,1)S(1)}, bf16[4,336,128]{2,1,0:T(8,128)(2,1)S(1)}, u32[]{:S(2)}, u32[]{:S(2)}) collective-permute-start(bf16[4,336,128]{2,1,0:T(8,128)(2,1)S(1)} %get-tuple-element.194), channel_id=1, source_target_pairs={{0,16},{1,17},{2,18},{3,19},{4,20},{5,21},{6,22},{7,23},{8,24},{9,... | collective-permute-start | bytes 1032200 | tf_op jit(solution)/shard_map/ppermute | solution.py:460
  44.3 16.2 %collective-permute-start.15 = (bf16[4,336,128]{2,1,0:T(8,128)(2,1)S(1)}, bf16[4,336,128]{2,1,0:T(8,128)(2,1)S(1)}, u32[]{:S(2)}, u32[]{:S(2)}) collective-permute-start(bf16[4,336,128]{2,1,0:T(8,128)(2,1)S(1)} %get-tuple-element.195), channel_id=1, source_target_pairs={{0,2},{1,3},{2,0},{3,1},{4,6},{5,7},{6,4},{7,5},{8,10},{9,11},{10,... | collective-permute-start | bytes 1032200 | tf_op jit(solution)/shard_map/ppermute | solution.py:460
  45.8 16.1 %collective-permute-start.16 = (bf16[4,336,128]{2,1,0:T(8,128)(2,1)S(1)}, bf16[4,336,128]{2,1,0:T(8,128)(2,1)S(1)}, u32[]{:S(2)}, u32[]{:S(2)}) collective-permute-start(bf16[4,336,128]{2,1,0:T(8,128)(2,1)S(1)} %get-tuple-element.196), channel_id=1, source_target_pairs={{0,18},{1,19},{2,16},{3,17},{4,22},{5,23},{6,20},{7,21},{8,26},{9,... | collective-permute-start | bytes 1032200 | tf_op jit(solution)/shard_map/ppermute | solution.py:460
  61.9 5.9 %collective-permute-start.17 = (bf16[4,112,128]{2,1,0:T(8,128)(2,1)S(1)}, bf16[4,112,128]{2,1,0:T(8,128)(2,1)S(1)}, u32[]{:S(2)}, u32[]{:S(2)}) collective-permute-start(bf16[4,112,128]{2,1,0:T(8,128)(2,1)S(1)} %get-tuple-element.202), channel_id=1, source_target_pairs={{0,16},{1,17},{2,18},{3,19},{4,20},{5,21},{6,22},{7,23},{8,24},{9,... | collective-permute-start | bytes 344072 | tf_op jit(solution)/shard_map/ppermute | solution.py:460
  62.7 5.8 %collective-permute-start.18 = (bf16[4,112,128]{2,1,0:T(8,128)(2,1)S(1)}, bf16[4,112,128]{2,1,0:T(8,128)(2,1)S(1)}, u32[]{:S(2)}, u32[]{:S(2)}) collective-permute-start(bf16[4,112,128]{2,1,0:T(8,128)(2,1)S(1)} %get-tuple-element.203), channel_id=1, source_target_pairs={{0,2},{1,3},{2,0},{3,1},{4,6},{5,7},{6,4},{7,5},{8,10},{9,11},{10,... | collective-permute-start | bytes 344072 | tf_op jit(solution)/shard_map/ppermute | solution.py:460
  64.2 5.7 %collective-permute-start.19 = (bf16[4,112,128]{2,1,0:T(8,128)(2,1)S(1)}, bf16[4,112,128]{2,1,0:T(8,128)(2,1)S(1)}, u32[]{:S(2)}, u32[]{:S(2)}) collective-permute-start(bf16[4,112,128]{2,1,0:T(8,128)(2,1)S(1)} %get-tuple-element.204), channel_id=1, source_target_pairs={{0,18},{1,19},{2,16},{3,17},{4,22},{5,23},{6,20},{7,21},{8,26},{9,... | collective-permute-start | bytes 344072 | tf_op jit(solution)/shard_map/ppermute | solution.py:460
  70.1 22.9 %collective-permute-start.26 = (bf16[768,384]{1,0:T(8,128)(2,1)S(1)}, bf16[768,384]{1,0:T(8,128)(2,1)S(1)}, u32[]{:S(2)}, u32[]{:S(2)}) collective-permute-start(bf16[768,384]{1,0:T(8,128)(2,1)S(1)} %get-tuple-element.214.own_ref), channel_id=1, source_target_pairs={{0,16},{16,0},{1,17},{17,1},{2,18},{18,2},{3,19},{19,3},{4,20},{20... | collective-permute-start | bytes 1769480 | tf_op jit(solution)/shard_map/ppermute | solution.py:722
  70.9 5.1 %collective-permute-start.20 = (bf16[1,448,128]{2,1,0:T(8,128)(2,1)S(1)}, bf16[1,448,128]{2,1,0:T(8,128)(2,1)S(1)}, u32[]{:S(2)}, u32[]{:S(2)}) collective-permute-start(bf16[1,448,128]{2,1,0:T(8,128)(2,1)S(1)} %get-tuple-element.211), channel_id=1, source_target_pairs={{0,4},{1,5},{2,6},{3,7},{4,0},{5,1},{6,2},{7,3},{8,12},{9,13},{10,... | collective-permute-start | bytes 344072 | tf_op jit(solution)/shard_map/ppermute | solution.py:452
  72.5 9.3 %collective-permute-start.21 = (bf16[1,448,128]{2,1,0:T(8,128)(2,1)S(1)}, bf16[1,448,128]{2,1,0:T(8,128)(2,1)S(1)}, u32[]{:S(2)}, u32[]{:S(2)}) collective-permute-start(bf16[1,448,128]{2,1,0:T(8,128)(2,1)S(1)} %get-tuple-element.212), channel_id=1, source_target_pairs={{0,8},{1,9},{2,10},{3,11},{4,12},{5,13},{6,14},{7,15},{8,0},{9,1},... | collective-permute-start | bytes 344072 | tf_op jit(solution)/shard_map/ppermute | solution.py:452
  75.1 6.7 %collective-permute-start.22 = (bf16[1,448,128]{2,1,0:T(8,128)(2,1)S(1)}, bf16[1,448,128]{2,1,0:T(8,128)(2,1)S(1)}, u32[]{:S(2)}, u32[]{:S(2)}) collective-permute-start(bf16[1,448,128]{2,1,0:T(8,128)(2,1)S(1)} %get-tuple-element.213), channel_id=1, source_target_pairs={{0,12},{1,13},{2,14},{3,15},{4,8},{5,9},{6,10},{7,11},{8,4},{9,5},... | collective-permute-start | bytes 344072 | tf_op jit(solution)/shard_map/ppermute | solution.py:452
  81.9 7.9 %collective-permute-start.25 = (bf16[1,448,128]{2,1,0:T(8,128)(2,1)S(1)}, bf16[1,448,128]{2,1,0:T(8,128)(2,1)S(1)}, u32[]{:S(2)}, u32[]{:S(2)}) collective-permute-start(bf16[1,448,128]{2,1,0:T(8,128)(2,1)S(1)} %shard_map.310), channel_id=1, source_target_pairs={{0,12},{1,13},{2,14},{3,15},{4,8},{5,9},{6,10},{7,11},{8,4},{9,5},... | collective-permute-start | bytes 344072 | tf_op jit(solution)/shard_map/ppermute | solution.py:452
  84.5 8.5 %collective-permute-start.24 = (bf16[1,448,128]{2,1,0:T(8,128)(2,1)S(1)}, bf16[1,448,128]{2,1,0:T(8,128)(2,1)S(1)}, u32[]{:S(2)}, u32[]{:S(2)}) collective-permute-start(bf16[1,448,128]{2,1,0:T(8,128)(2,1)S(1)} %shard_map.310), channel_id=1, source_target_pairs={{0,8},{1,9},{2,10},{3,11},{4,12},{5,13},{6,14},{7,15},{8,0},{9,1},... | collective-permute-start | bytes 344072 | tf_op jit(solution)/shard_map/ppermute | solution.py:452
  86.3 6.7 %collective-permute-start.23 = (bf16[1,448,128]{2,1,0:T(8,128)(2,1)S(1)}, bf16[1,448,128]{2,1,0:T(8,128)(2,1)S(1)}, u32[]{:S(2)}, u32[]{:S(2)}) collective-permute-start(bf16[1,448,128]{2,1,0:T(8,128)(2,1)S(1)} %shard_map.310), channel_id=1, source_target_pairs={{0,4},{1,5},{2,6},{3,7},{4,0},{5,1},{6,2},{7,3},{8,12},{9,13},{10,... | collective-permute-start | bytes 344072 | tf_op jit(solution)/shard_map/ppermute | solution.py:452
  93.0 14.4 %collective-permute-start.29 = (bf16[4,448,128]{2,1,0:T(8,128)(2,1)S(1)}, bf16[4,448,128]{2,1,0:T(8,128)(2,1)S(1)}, u32[]{:S(2)}, u32[]{:S(2)}) collective-permute-start(bf16[4,448,128]{2,1,0:T(8,128)(2,1)S(1)} %maximum_bitcast_fusion.refs_0_), channel_id=1, source_target_pairs={{0,18},{1,19},{2,16},{3,17},{4,22},{5,23},{6,20},{7,21},{8,26},{9,... | collective-permute-start | bytes 1376264 | tf_op jit(solution)/shard_map/ppermute | solution.py:460
  95.4 17.6 %collective-permute-start.28 = (bf16[4,448,128]{2,1,0:T(8,128)(2,1)S(1)}, bf16[4,448,128]{2,1,0:T(8,128)(2,1)S(1)}, u32[]{:S(2)}, u32[]{:S(2)}) collective-permute-start(bf16[4,448,128]{2,1,0:T(8,128)(2,1)S(1)} %maximum_bitcast_fusion.refs_0_), channel_id=1, source_target_pairs={{0,2},{1,3},{2,0},{3,1},{4,6},{5,7},{6,4},{7,5},{8,10},{9,11},{10,... | collective-permute-start | bytes 1376264 | tf_op jit(solution)/shard_map/ppermute | solution.py:460
  95.4 18.1 %collective-permute-start.27 = (bf16[4,448,128]{2,1,0:T(8,128)(2,1)S(1)}, bf16[4,448,128]{2,1,0:T(8,128)(2,1)S(1)}, u32[]{:S(2)}, u32[]{:S(2)}) collective-permute-start(bf16[4,448,128]{2,1,0:T(8,128)(2,1)S(1)} %maximum_bitcast_fusion.refs_0_), channel_id=1, source_target_pairs={{0,16},{1,17},{2,18},{3,19},{4,20},{5,21},{6,22},{7,23},{8,24},{9,... | collective-permute-start | bytes 1376264 | tf_op jit(solution)/shard_map/ppermute | solution.py:460
  (28 other events, 146.5 us)

commit v5 on v4

--- a/solution.py
+++ b/solution.py
@@ -91,20 +91,23 @@
 
 
 def prep_theirs_kernel(
-    unmasked, place_ref, masked_ref, tokens_ref, theirs_ref, rank_ref, half_ref, arrived
+    unmasked, place_ref, masked_ref, tokens_ref, theirs_ref, rank_ref, marks_ref, half_ref, arrived
 ):
     tm = place_ref[0]
     half = tokens_ref.shape[1]
-    load = pltpu.make_async_copy(tokens_ref.at[1 - tm], half_ref, arrived)
+    load_marks = pltpu.make_async_copy(masked_ref, marks_ref, arrived.at[0])
+    load_marks.start()
+    load = pltpu.make_async_copy(tokens_ref.at[1 - tm], half_ref, arrived.at[1])
     load.start()
-    rank_ref[...] = all_ranks(masked_ref, tm, half, unmasked)
-    chosen = picks(ranks_of(rank_ref, 1 - tm, half), iota((unmasked + EXTRA, 1), 0))
+    load_marks.wait()
+    rank_ref[...] = all_ranks(marks_ref, tm, half, unmasked)
+    chosen = picks(ranks_of(rank_ref, 1 - tm, half), iota((unmasked, 1), 0))
     load.wait()
     theirs_ref[...] = dot(chosen, half_ref[...]).astype(BF)
 
 
 def prep_shared_kernel(unmasked, rank_ref, tokens_ref, shared_ref):
-    chosen = picks(ranks_of(rank_ref, 2, tokens_ref.shape[1]), iota((unmasked + EXTRA, 1), 0))
+    chosen = picks(ranks_of(rank_ref, 2, tokens_ref.shape[1]), iota((unmasked, 1), 0))
     shared_ref[...] = dot(chosen, tokens_ref[2]).astype(BF)
 
 
@@ -115,13 +118,13 @@
     part = unmasked // 2
     labels = iota((rows, 1), 0)
     small = iota((part + EXTRA, 1), 0)
-    theirs = jnp.where(small < part, small + part * (1 - tm), -1)
+    theirs = iota((part, 1), 0) + part * (1 - tm)
     own = jnp.where(small < part, small + part * tm, small + part)
     send_ref[:rows, :] = dot(picks(ranks_of(rank_ref, 1 - tm, half), labels), cotangent_ref[1 - tm]).astype(BF)
     chosen = picks(ranks_of(rank_ref, 2, half), jnp.concatenate([theirs, own], axis=0))
     both = dot(chosen, cotangent_ref[2]).astype(BF)
-    send_ref[rows:, :] = both[: part + EXTRA]
-    keep_ref[rows:, :] = both[part + EXTRA :]
+    send_ref[rows:, :] = both[:part]
+    keep_ref[rows:, :] = both[part:]
     keep_ref[:rows, :] = dot(picks(ranks_of(rank_ref, tm, half), labels), cotangent_ref[tm]).astype(BF)
 
 
@@ -146,11 +149,11 @@
         own = own_ref[...].astype(F32)
     else:
         rank_ref, tokens_ref, got_ref, small_ref, w_ref, x_ref, q_ref, k_ref, v_ref, e_ref, inverse_ref, att_ref = refs
-        chosen = picks(ranks_of(rank_ref, tm, tokens_ref.shape[1]), iota((unmasked + EXTRA, 1), 0))
+        chosen = picks(ranks_of(rank_ref, tm, tokens_ref.shape[1]), iota((unmasked, 1), 0))
         own = dot(chosen, tokens_ref[tm])
-    rows, width = got_ref.shape
-    x = own + got_ref[...].astype(F32)
-    x = jnp.where(iota((rows, width), 0) == unmasked, small_ref[0:1, :], x)
+    rows, width = k_ref.shape
+    extra = jnp.where(iota((EXTRA, width), 0) == 0, small_ref[0:1, :], 0.0)
+    x = jnp.concatenate([own + got_ref[...].astype(F32), extra], axis=0)
     hat, _ = normalise(x)
     normed = (hat * small_ref[1:2, :] + small_ref[2:3, :]).astype(BF)
     mixed = dot(normed, w_ref[...])
@@ -199,12 +202,8 @@
 
 
 def gelu_terms(hidden):
-    size = jnp.abs(hidden) * (0.5**0.5)
-    t = 1.0 / (1.0 + 0.3275911 * size)
-    bell = jnp.exp(hidden * hidden * -0.5)
-    tail = t * (0.254829592 + t * (-0.284496736 + t * (1.421413741 + t * (-1.453152027 + t * 1.061405429))))
-    tail = 0.5 * tail * bell
-    below = jnp.where(hidden >= 0.0, 1.0 - tail, tail)
+    below = 0.5 * lax.erf(hidden * 0.5**0.5) + 0.5
+    bell = jnp.exp2(hidden * hidden * (-0.5 * math.log2(math.e)))
     return hidden * below, below + hidden * bell * (1.0 / math.sqrt(2.0 * math.pi))
 
 
@@ -212,41 +211,62 @@
     return jnp.concatenate([ref[...] for ref in refs], axis=0)
 
 
-def scatter_chunks(me, stage_ref, keep_ref, send_refs):
-    depth = keep_ref.shape[2]
-    for rel in range(2 * 4 * keep_ref.shape[1]):
-        first = pl.multiple_of((me ^ rel) * depth, 16)
-        near, far = (rel >> 1) & 3, rel >> 3
-        chunk = stage_ref[pl.ds(first, depth), :]
-        if rel & 1 == 0:
-            keep_ref[near, far] = chunk
-        else:
-            each = send_refs[0].shape[0]
-            send_refs[near // each][near % each, far] = chunk
-
-
-def stage_weight(stage_ref, first, grad, apart=None):
-    depth = grad.shape[0]
-    apart = apart or depth
+def eighth_at(place_ref, near, side):
+    me = place_ref[1]
+    return ((near ^ ((me >> 1) & 3)) << 1) | (side ^ (me & 1))
+
+
+def chunk_rows_at(place_ref, far, depth):
+    return pl.ds(pl.multiple_of((far ^ (place_ref[1] >> 3)) * depth, 16), depth)
+
+
+def scatter_chunks(place_ref, stage_ref, keep_ref, send_refs):
+    near_places, far_places, depth, _ = keep_ref.shape
+    each = send_refs[0].shape[0]
+    for near in range(near_places):
+        for side in range(2):
+            eighth = eighth_at(place_ref, near, side)
+            for far in range(far_places):
+                chunk = stage_ref[eighth, chunk_rows_at(place_ref, far, depth), :]
+                if side:
+                    send_refs[near // each][near % each, far] = chunk
+                else:
+                    keep_ref[near, far] = chunk
+
+
+def stage_rows(stage_ref, base, grad, total, first=0):
+    slab = total // 8
+    step = math.gcd(slab, grad.shape[0])
+    grad = grad.astype(BF)
+    for row in range(0, grad.shape[0], step):
+        eighth, offset = divmod(first + row, slab)
+        for block in range(grad.shape[1] // LANES):
+            at = base + block * slab + offset
+            stage_ref[eighth, at : at + step, :] = grad[row : row + step, block * LANES : (block + 1) * LANES]
+
+
+def stage_columns(stage_ref, base, grad, total, first):
+    slab = grad.shape[0] // 2
+    grad = grad.astype(BF)
     for block in range(grad.shape[1] // LANES):
-        at = first + block * apart
-        stage_ref[at : at + depth, :] = grad[:, block * LANES : (block + 1) * LANES].astype(BF)
-    return first + apart * (grad.shape[1] // LANES)
-
-
-def stage_rows(stage_ref, first, vectors):
+        quarter, offset = divmod(first // LANES + block, total // 4 // LANES)
+        at = base + offset * slab
+        for half in range(2):
+            stage_ref[2 * quarter + half, at : at + slab, :] = grad[
+                half * slab : (half + 1) * slab, block * LANES : (block + 1) * LANES
+            ]
+
+
+def stage_vectors(stage_ref, base, vectors):
     pieces = [v[:, b * LANES : (b + 1) * LANES] for v in vectors for b in range(v.shape[1] // LANES)]
-    missing = -len(pieces) % 16
-    if missing:
-        pieces.append(jnp.zeros((missing, LANES), F32))
-    block = jnp.concatenate(pieces, axis=0).astype(BF)
-    stage_ref[first : first + block.shape[0], :] = block
-    return first + block.shape[0]
-
-
-def clear_rest(stage_ref, first):
-    if first < stage_ref.shape[0]:
-        stage_ref[first:, :] = jnp.zeros((stage_ref.shape[0] - first, LANES), BF)
+    each = -(-len(pieces) // 8)
+    for eighth in range(8):
+        rows = pieces[eighth * each : (eighth + 1) * each]
+        rows = rows + [jnp.zeros((16 - len(rows), LANES), F32)]
+        stage_ref[eighth, base : base + 16, :] = jnp.concatenate(rows, axis=0).astype(BF)
+        rest = stage_ref.shape[1] - base - 16
+        if rest:
+            stage_ref[eighth, base + 16 :, :] = jnp.zeros((rest, LANES), BF)
 
 
 def forward_kernel(
@@ -261,10 +281,14 @@
     normed = (hat * small_ref[6:7, :] + small_ref[7:8, :]).astype(BF)
     normed_ref[...] = normed
     result = middle + small_ref[8:9, :]
-    step = 512
-    for first in range(0, w_up_ref.shape[1], step):
+    width, step = w_up_ref.shape[1], 512
+    ahead = dot(normed, w_up_ref[:, :step])
+    for first in range(0, width, step):
         cols = slice(first, first + step)
-        active, slope = gelu_terms(dot(normed, w_up_ref[:, cols]) + bias_up_ref[:, cols])
+        hidden = ahead + bias_up_ref[:, cols]
+        if first + step < width:
+            ahead = dot(normed, w_up_ref[:, first + step : first + 2 * step])
+        active, slope = gelu_terms(hidden)
         active = active.astype(BF)
         active_ref[:, cols] = active
         slope_ref[:, cols] = slope.astype(BF)
@@ -294,39 +318,37 @@
     weight = jnp.where(
         iota((total, 1), 0) < rows_a, weight_of(groups_ref[place_ref[0]]), weight_of(groups_ref[2])
     )
-    upstream = (cot_own[...].astype(F32) + cot_got[...].astype(F32)) * weight
+    got = jnp.concatenate([cot_got[...].astype(F32), jnp.zeros((EXTRA, cot_got.shape[1]), F32)], axis=0)
+    upstream = (cot_own[...].astype(F32) + got) * weight
     grad_result = upstream.astype(BF)
     normed = normed_ref[...]
     hidden, step = active_ref.shape[1], 512
     grad_normed = None
     sums = []
-    parts = []
+    slab = hidden // 8 * (grad_result.shape[1] // LANES)
     for first in range(0, hidden, step):
         cols = slice(first, first + step)
         grad_hidden = (dot_last(grad_result, w_down_ref[cols, :]) * slope_ref[:, cols].astype(F32)).astype(BF)
-        stage_weight(stage_ref, first, dot_rows(active_ref[:, cols], grad_result), hidden)
+        stage_rows(stage_ref, 0, dot_rows(active_ref[:, cols], grad_result), hidden, first)
         part = dot_last(grad_hidden, w_up_ref[:, cols])
         grad_normed = part if grad_normed is None else grad_normed + part
         sums.append(column_sums(grad_hidden.astype(F32)))
-        parts.append(dot_rows(normed, grad_hidden))
-    end = hidden * (grad_result.shape[1] // LANES)
-    for part in parts:
-        end = stage_weight(stage_ref, end, part)
+        stage_columns(stage_ref, slab, dot_rows(normed, grad_hidden), hidden, first)
     hat, scale = normalise(middle_ref[...])
     grad_middle = upstream + norm_back(grad_normed, hat, scale, small_ref[6:7, :])
     grad_middle_ref[...] = grad_middle
     grad_branch = grad_middle.astype(BF)
     grad_att_ref[...] = dot_last(grad_branch, w_proj_ref[...]).astype(BF)
-    end = stage_weight(stage_ref, end, dot_rows(stacked((att_a, att_b)), grad_branch))
+    width = grad_branch.shape[1]
+    stage_rows(stage_ref, 2 * slab, dot_rows(stacked((att_a, att_b)), grad_branch), width)
     vectors = sums + [
         column_sums(grad_normed * hat),
         column_sums(grad_normed),
         column_sums(grad_branch.astype(F32)),
         column_sums(grad_result.astype(F32)),
     ]
-    end = stage_rows(stage_ref, end, vectors)
-    clear_rest(stage_ref, end)
-    scatter_chunks(place_ref[1], stage_ref, keep_ref, send_refs)
+    stage_vectors(stage_ref, 2 * slab + width // 8 * (width // LANES), vectors)
+    scatter_chunks(place_ref, stage_ref, keep_ref, send_refs)
 
 
 def attention_back_kernel(row_from, g_ref, att_ref, q_ref, k_ref, v_ref, e_ref, inverse_ref, dq_ref, dk_ref, dv_ref):
@@ -373,7 +395,7 @@
     normed = (hat * gain + small_ref[2:3, :]).astype(BF)
     dq = jnp.concatenate([dq_a[...], spread(dq_b[...]).astype(BF)], axis=0)
     mixed = jnp.concatenate([dq, stacked((dk_a, dk_b)), stacked((dv_a, dv_b))], axis=1)
-    end = stage_weight(stage_ref, 0, dot_rows(normed, mixed))
+    stage_rows(stage_ref, 0, dot_rows(normed, mixed), width)
     grad_normed = dot_last(mixed, w_ref[...])
     grad = norm_back(grad_normed, hat, scale, gain)
     grad = grad + jnp.concatenate([grad_middle_ref[:rows], spread(grad_middle_ref[rows:])], axis=0)
@@ -386,9 +408,8 @@
         column_sums(grad_normed),
         grad[unmasked : unmasked + 1] + grad[rows + unmasked : rows + unmasked + 1],
     )
-    end = stage_rows(stage_ref, end, vectors)
-    clear_rest(stage_ref, end)
-    scatter_chunks(place_ref[1], stage_ref, keep_ref, send_refs)
+    stage_vectors(stage_ref, width // 8 * (mixed.shape[1] // LANES), vectors)
+    scatter_chunks(place_ref, stage_ref, keep_ref, send_refs)
 
 
 def place_back(rank_ref, copy, rows, half):
@@ -470,7 +491,7 @@
     return [pieces[0]] + [near_swap(pieces[step], step) for step in (1, 2, 3)]
 
 
-def sum_over_devices(first_pieces, second_pieces, send_far, beside_last):
+def sum_over_devices(first_pieces, second_pieces, send_far, beside_last, finish):
     far = []
     distance = 4
     while distance < lax.axis_size("clip"):
@@ -491,59 +512,70 @@
     total = plain(functools.partial(fold_four_kernel, 1), shape(left, depth, LANES))(*pieces)
     for distance in reversed(far):
         pieces = [total] + [clip_swap(total, step * distance) for step in (1, 2, 3)]
-        total = jnp.stack(pieces, axis=1).reshape(-1, depth, LANES)
+        total = plain(join_kernel, shape(4 * total.shape[0], *total.shape[1:]))(*pieces)
     total, sent = lax.optimization_barrier((total, sent))
     pieces = spread_near([total] * 4)
     last = beside_last(sent)
     *pieces, last = lax.optimization_barrier((*pieces, last))
-    return pieces, [clip_swap(piece, 1) for piece in pieces], last
-
-
-def gather_chunks(me, refs, stage_ref, start, depth):
-    for rel in range(8 * refs[0].shape[0]):
-        first = pl.multiple_of((me ^ rel) * depth, 16)
-        source = refs[4 * (rel & 1) + ((rel >> 1) & 3)]
-        stage_ref[pl.ds(first, depth), :] = source[rel >> 3, start : start + depth]
-
-
-def unstage_kernel(units, place_ref, *refs):
-    weights = sum(count for _, count, _ in units)
-    vectors = sum(count for _, _, count in units)
-    pieces, outs, vector_outs = refs[:8], refs[8 : 8 + weights], refs[8 + weights : 8 + weights + vectors]
-    stage_ref, done, *wide_refs = refs[8 + weights + vectors :]
+    got = [clip_swap(piece, 1) for piece in pieces]
+    return finish(1, got, finish(0, pieces, ())), last
+
+
+def join_kernel(*refs):
+    for step in range(4):
+        for slot in range(refs[step].shape[0]):
+            refs[4][4 * slot + step] = refs[step][slot]
+
+
+def finish_kernel(side, depths, counts, place_ref, *refs):
+    sources, refs = refs[:4], refs[4:]
+    if side:
+        first_kept_ref, refs = refs[4], refs[5:]
+        outs, vectors, refs = refs[:4], refs[4 : 4 + sum(counts)], refs[4 + sum(counts) :]
+        kept_ref, *refs = refs
+    else:
+        outs, kept_ref, refs = refs[:4], refs[4], refs[5:]
+    stage_a, stage_b, done, *wides = refs
+    far_places = sources[0].shape[0]
     stores = []
-    start = at = vector_at = 0
-    for depth, weights, vectors in units:
-        gather_chunks(place_ref[1], pieces, stage_ref, start, depth)
-        first = 0
-        for each in range(at, at + weights):
-            first = widen(stage_ref, first, wide_refs[each], outs[each], done, stores)
-        widen_vectors(stage_ref, first, vector_outs[vector_at : vector_at + vectors])
-        start, at, vector_at = start + depth, at + weights, vector_at + vectors
+    for near in range(4):
+        eighth = eighth_at(place_ref, near, side)
+        for far in range(far_places):
+            stage_a[chunk_rows_at(place_ref, far, depths[0]), :] = sources[near][far, : depths[0]]
+            stage_b[chunk_rows_at(place_ref, far, depths[1]), :] = sources[near][far, depths[0] :]
+        for unit, stage_ref in enumerate((stage_a, stage_b)):
+            first = 0
+            for at in ((0, 1, 2), (3,))[unit]:
+                wide_ref = wides[at].at[near]
+                depth, width = wide_ref.shape
+                for block in range(width // LANES):
+                    wide_ref[:, block * LANES : (block + 1) * LANES] = stage_ref[first : first + depth, :].astype(F32)
+                    first += depth
+                if at == 1:
+                    rows = pl.ds(pl.multiple_of((eighth & 1) * depth, 16), depth)
+                    target = outs[at].at[rows, pl.ds(pl.multiple_of((eighth >> 1) * width, LANES), width)]
+                else:
+                    target = outs[at].at[pl.ds(pl.multiple_of(eighth * depth, 16), depth), :]
+                stores.append(pltpu.make_async_copy(wide_ref, target, done.at[len(stores)]))
+                stores[-1].start()
+            kept_ref[eighth, 16 * unit : 16 * unit + 16] = stage_ref[first : first + 16, :].astype(F32)
+    if side:
+        for near in range(4):
+            eighth = eighth_at(place_ref, near, 0)
+            kept_ref[eighth] = first_kept_ref[eighth]
+        at = 0
+        for unit, count in enumerate(counts):
+            blocks = [(ref, block) for ref in vectors[at : at + count] for block in range(ref.shape[0] // LANES)]
+            at += count
+            each = -(-len(blocks) // 8)
+            for number, (ref, block) in enumerate(blocks):
+                eighth, row = divmod(number, each)
+                ref[block * LANES : (block + 1) * LANES] = kept_ref[eighth, 16 * unit + row]
+    else:
+        for near in range(4):
+            kept_ref[eighth_at(place_ref, near, 1)] = jnp.zeros(kept_ref.shape[1:], F32)
     for store in stores:
         store.wait()
-
-
-def widen(stage_ref, first, wide_ref, out_ref, done, stores):
-    depth, width = out_ref.shape
-    for block in range(width // LANES):
-        columns = slice(block * LANES, (block + 1) * LANES)
-        wide_ref[:, columns] = stage_ref[first : first + depth, :].astype(F32)
-        stores.append(pltpu.make_async_copy(wide_ref.at[:, columns], out_ref.at[:, columns], done.at[len(stores)]))
-        stores[-1].start()
-        first += depth
-    return first
-
-
-def widen_vectors(stage_ref, first, outs):
-    count = sum(ref.shape[0] // LANES for ref in outs)
-    rows = stage_ref[first : first + count + -count % 16, :].astype(F32)
-    at = 0
-    for out_ref in outs:
-        blocks = out_ref.shape[0] // LANES
-        for block in range(blocks):
-            out_ref[block * LANES : (block + 1) * LANES] = rows[at + block]
-        at += blocks
 
 
 def chunk_rows(count, devices):
@@ -584,7 +616,7 @@
     place = jnp.stack([tm, me]).astype(jnp.int32)
     swap = functools.partial(lax.ppermute, axis_name="tm", perm=[(0, 1), (1, 0)])
 
-    def run(kernel, args, outs, scratch=(), scalars=1, limit=20, flops=0, in_hbm=(), out_hbm=(), hides=True):
+    def run(kernel, args, outs, scratch=(), scalars=1, limit=20, flops=0, in_hbm=(), out_hbm=(), aliases=None, hides=True):
         moved = sum(math.prod(a.shape) * a.dtype.itemsize for a in list(args) + jax.tree.leaves(outs))
         return pl.pallas_call(
             kernel,
@@ -595,18 +627,20 @@
             ],
             out_specs=[HBM if at in out_hbm else VMEM for at in range(len(outs))] if isinstance(outs, list) else VMEM,
             scratch_shapes=list(scratch),
+            input_output_aliases=aliases or {},
             compiler_params=pltpu.CompilerParams(vmem_limit_bytes=limit << 20),
             cost_estimate=pl.CostEstimate(
                 flops=flops if hides else 1, bytes_accessed=moved if hides else 1, transcendentals=0
             ),
         )(*args)
 
-    counts = (2 * width // LANES * hidden + width // LANES * width + 32, 3 * width // LANES * width + 16)
-    depths = [chunk_rows(count, devices) for count in counts]
+    blocks = width // LANES
+    counts = ((2 * hidden + width) // 8 * blocks + 16, 3 * width // 8 * blocks + 16)
+    depths = [chunk_rows(count, devices // 8) for count in counts]
 
     def chunked(unit, parts):
         halves = [shape(near, devices // 8, depths[unit], LANES) for near in [4] + [4 // parts] * parts]
-        return halves, [pltpu.VMEM((devices * depths[unit], LANES), BF)]
+        return halves, [pltpu.VMEM((8, devices // 8 * depths[unit], LANES), BF)]
 
     small = jnp.stack(
         [mask_token, gain_one, shift_one, q_bias, v_bias, b_proj, gain_two, shift_two, b_down]
@@ -617,11 +651,11 @@
     everyone = jnp.concatenate([groups, clip_swap(groups, 1)])
     theirs, rank = run(
         functools.partial(prep_theirs_kernel, unmasked),
-        (place, masked, pltpu.with_memory_space_constraint(tokens, pltpu.HBM)),
-        [block, shape(16 * copies, LANES, kind=F32)],
-        [pltpu.VMEM((half, width), BF), pltpu.SemaphoreType.DMA],
+        (place, *(pltpu.with_memory_space_constraint(each, pltpu.HBM) for each in (masked, tokens))),
+        [shape(unmasked, width), shape(16 * copies, LANES, kind=F32)],
+        [pltpu.VMEM(masked.shape, jnp.int32), pltpu.VMEM((half, width), BF), pltpu.SemaphoreType.DMA((2,))],
         flops=2 * rows * half * width,
-        in_hbm=(2,),
+        in_hbm=(1, 2),
     )
     got_mine = swap(theirs)
     everyone, theirs, rank = lax.optimization_barrier((everyone, theirs, rank))
@@ -629,7 +663,7 @@
     shared = run(
         functools.partial(prep_shared_kernel, unmasked),
         (rank, tokens),
-        block,
+        shape(unmasked, width),
         scalars=0,
         flops=2 * rows * half * width,
     )
@@ -639,7 +673,7 @@
     cot_own, cot_send = run(
         functools.partial(prep_grads_kernel, unmasked),
         (place, rank, cotangent),
-        [shape(total, width), shape(total, width)],
+        [shape(total, width), shape(total - EXTRA, width)],
         flops=2 * copies * rows * half * width,
     )
     everyone, cot_own, cot_send = lax.optimization_barrier((everyone, cot_own, cot_send))
@@ -727,21 +761,34 @@
             run(functools.partial(grads_out_kernel, unmasked), (place, rank, grad_rows, got), shape(*tokens.shape)),
         )
 
-    own, got, (block_out, grad_tokens) = sum_over_devices(first_pieces, second_pieces, send_rows, place_rows)
     weights = [(hidden, width), (width, hidden), (width, width), (width, 3 * width)]
-    vectors = [hidden] + [width] * 9
+    slabs = [(hidden // 8, width), (width // 2, hidden // 4), (width // 8, width), (width // 8, 3 * width)]
+    vectors = [shape(dim, kind=F32) for dim in [hidden] + [width] * 9]
+
+    def finish(side, sources, earlier):
+        kept = pltpu.VMEM((8, 32, LANES), F32)
+        return run(
+            functools.partial(finish_kernel, side, depths, (5, 5)),
+            (place, *sources, *earlier),
+            [shape(*dims, kind=F32) for dims in weights] + (vectors if side else [shape(8, 32, LANES, kind=F32)]),
+            [kept] * side
+            + [pltpu.VMEM((devices // 8 * depth, LANES), BF) for depth in depths]
+            + [pltpu.SemaphoreType.DMA((16,))]
+            + [pltpu.VMEM((4, *dims), F32) for dims in slabs],
+            in_hbm=range(1 + len(sources), 5 + len(sources)) if side else (),
+            out_hbm=range(4),
+            aliases={1 + len(sources) + at: at for at in range(4)} if side else {},
+            hides=False,
+        )
+
     (
-        grad_w_down, grad_w_up, grad_w_proj, grad_w_qkv,
-        grad_b_up, grad_gain_two, grad_shift_two, grad_b_proj, grad_b_down,
-        grad_q_bias, grad_v_bias, grad_gain_one, grad_shift_one, grad_mask_token,
-    ) = run(
-        functools.partial(unstage_kernel, tuple(zip(depths, (3, 1), (5, 5)))),
-        (place, *own, *got),
-        [shape(*dims, kind=F32) for dims in weights] + [shape(dim, kind=F32) for dim in vectors],
-        [pltpu.VMEM((devices * max(depths), LANES), BF), pltpu.SemaphoreType.DMA((sum(dims[1] for dims in weights) // LANES,))]
-        + [pltpu.VMEM(dims, F32) for dims in weights],
-        out_hbm=(0, 1, 2, 3),
-    )
+        (
+            grad_w_down, grad_w_up, grad_w_proj, grad_w_qkv,
+            grad_b_up, grad_gain_two, grad_shift_two, grad_b_proj, grad_b_down,
+            grad_q_bias, grad_v_bias, grad_gain_one, grad_shift_one, grad_mask_token,
+        ),
+        (block_out, grad_tokens),
+    ) = sum_over_devices(first_pieces, second_pieces, send_rows, place_rows, finish)
     return (
         block_out,
         grad_tokens,

time: 122 us -> 120 us (0.984)
  waiting for transfers between devices: 37.3 us -> 34.1 us
  starting transfers between devices: 36 us -> 38.5 us
    ppermute x20, waiting for transfers between devices: 16.9 us -> 13.1 us  [clip_swap(): lax.ppermute(values, 'clip', [(i, i ^ distance) for i in range(size)])]
    ppermute x20, starting transfers between devices: 18.2 us -> 20 us  [clip_swap(): lax.ppermute(values, 'clip', [(i, i ^ distance) for i in range(size)])]
    pallas_call x13 -> x14, Pallas kernels: 45.3 us -> 44.5 us  [run(): pl.pallas_call(kernel, out_shape=outs, in_specs=[SMEM if at < scalars els...]
  transfers between devices with their start and end apart: 34 -> 34, of which waited for: 19 -> 18; matrix products, arithmetic and copies ran while one was open for 0% -> 0% of each run, Pallas kernels for 34% -> 35%
where the time goes in v5:
time: 120 us
  Pallas kernels  45.3 us (38%)
  starting transfers between devices  38.5 us (32%)
  waiting for transfers between devices  34.1 us (28%)
  between operations  1.3 us (1%)
    pallas_call x14, Pallas kernels, run(): pl.pallas_call(kernel, out_shape=outs, in_specs=[SMEM if at < scalars els...  44.5 us
    ppermute x9, waiting for transfers between devices, near_swap(): return lax.ppermute(values, ('tm', 'clip'), pairs)  20.1 us
    ppermute x20, starting transfers between devices, clip_swap(): lax.ppermute(values, 'clip', [(i, i ^ distance) for i in range(size)])  20 us
    ppermute x20, waiting for transfers between devices, clip_swap(): lax.ppermute(values, 'clip', [(i, i ^ distance) for i in range(size)])  13.1 us
    ppermute x9, starting transfers between devices, near_swap(): return lax.ppermute(values, ('tm', 'clip'), pairs)  10.7 us
    ppermute x1, starting transfers between devices, body(): got_mine = swap(theirs)  2.93 us
  transfers between devices with their start and end apart: 34, of which 18 were waited for; matrix products, arithmetic and copies ran while one was open for 0% of the time, Pallas kernels for 35%

profile of v5, /device:TPU:0, one launch (start us, length us, event | category | flops | bytes accessed | tf_op | source)
XLA Modules:
  0.0 119.8 jit_solution(17826585093228953714)
XLA Ops:
  1.3 3.2 %shard_map.297 = (bf16[384,384]{1,0:T(8,128)(2,1)}, f32[48,128]{1,0:T(8,128)S(1)}) custom-call(s32[2]{0:T(128)S(1)} %pad_add_fusion.place_ref, s32[3,1152]{1,0:T(4,128)} %masked_ref.1, bf16[3,768,384]{2,1,0:T(8,128)(2,1)} %refs_1_.1), custom_call_target="tpu_custom_call" | custom-call | flops 235929600 | bytes 2102792 | tf_op jit(solution)/shard_map/pallas_call | solution.py:621
  4.5 2.9 %collective-permute-start.2 = (bf16[384,384]{1,0:T(8,128)(2,1)}, bf16[384,384]{1,0:T(8,128)(2,1)S(1)}, u32[]{:S(2)}, u32[]{:S(2)}) collective-permute-start(bf16[384,384]{1,0:T(8,128)(2,1)} %get-tuple-element.132), channel_id=1, source_target_pairs={{0,16},{16,0},{1,17},{17,1},{2,18},{18,2},{3,19},{19,3},{4,20},{20... | collective-permute-start | bytes 884744 | tf_op jit(solution)/shard_map/ppermute | solution.py:660
  12.7 2.1 %shard_map.301 = (bf16[608,384]{1,0:T(8,128)(2,1)S(1)}, bf16[592,384]{1,0:T(8,128)(2,1)}) custom-call(s32[2]{0:T(128)S(1)} %pad_add_fusion.place_ref, f32[48,128]{1,0:T(8,128)S(1)} %get-tuple-element.136.rank_ref.refs_0_, bf16[3,768,384]{2,1,0:T(8,128)(2,1)S(1)} %copy-done.6), custom_call_target="tpu_custom_call" | custom-call | flops 707788800 | bytes 2715656 | tf_op jit(solution)/shard_map/pallas_call | solution.py:621
  16.5 3.6 %shard_map.299 = (bf16[400,384]{1,0:T(8,128)(2,1)S(1)}, bf16[400,384]{1,0:T(8,128)(2,1)S(1)}, bf16[400,384]{1,0:T(8,128)(2,1)S(1)}, bf16[400,384]{1,0:T(8,128)(2...) custom-call(s32[2]{0:T(128)S(1)} %pad_add_fusion.place_ref, ...), custom_call_target="tpu_custom_call" | custom-call | flops 599654400 | bytes 7057928 | tf_op jit(solution)/shard_map/pallas_call | solution.py:621
  20.1 2.7 %collective-permute-start.5 = (s32[24]{0:T(128)S(1)}, s32[24]{0:T(128)S(1)}, u32[]{:S(2)}, u32[]{:S(2)}) collective-permute-start(s32[24]{0:T(128)S(1)} %pad_add_fusion.3), channel_id=1, source_target_pairs={{0,8},{1,9},{2,10},{3,11},{4,12},{5,13},{6,14},{7,15},{8,0},{9,1},... | collective-permute-start | bytes 296 | tf_op jit(solution)/shard_map/ppermute | solution.py:473
  22.8 3.0 %shard_map.300 = (bf16[208,384]{1,0:T(8,128)(2,1)S(1)}, bf16[208,384]{1,0:T(8,128)(2,1)S(1)}, bf16[400,384]{1,0:T(8,128)(2,1)S(1)}, bf16[400,384]{1,0:T(8,128)(2...) custom-call(s32[2]{0:T(128)S(1)} %pad_add_fusion.place_ref, ...), custom_call_target="tpu_custom_call" | custom-call | flops 481689600 | bytes 4207112 | tf_op jit(solution)/shard_map/pallas_call | solution.py:621
  25.8 3.6 %shard_map.302 = (bf16[608,384]{1,0:T(8,128)(2,1)S(1)}, f32[608,384]{1,0:T(8,128)S(1)}, bf16[608,384]{1,0:T(8,128)(2,1)S(1)}, bf16[608,1536]{1,0:T(8,128)(2,1)S(1)}, bf16[608,1536]{1,0:T(8,128)(2,1)S(1)}) custom-call(bf16[400,384]{1,0:T(8,128)(2,1)S(1)} %get-tuple-element.148.att_a.att_ref, bf16[208,384]{1,0:T(8,128)(2,1)S(1)} %get-tuple-element.149.att_b.att_ref, ...), custom_call_target="tpu_custom_call" | custom-call | flops 1613758464 | bytes 9211392 | tf_op jit(solution)/shard_map/pallas_call | solution.py:621
  31.6 6.4 %shard_map.303 = (f32[608,384]{1,0:T(8,128)S(1)}, bf16[608,384]{1,0:T(8,128)(2,1)S(1)}, bf16[4,4,336,128]{3,2,1,0:T(8,128)(2,1)S(1)}, bf16[1,4,336,128]{3,2,1,0:...) custom-call(s32[2]{0:T(128)S(1)} %pad_add_fusion.place_ref, ...), custom_call_target="tpu_custom_call" | custom-call | flops 1 | bytes 1 | tf_op jit(solution)/shard_map/pallas_call | solution.py:621
  39.1 2.3 %shard_map.304 = (bf16[208,384]{1,0:T(8,128)(2,1)S(1)}, bf16[400,384]{1,0:T(8,128)(2,1)S(1)}, bf16[400,384]{1,0:T(8,128)(2,1)S(1)}) custom-call(bf16[608,384]{1,0:T(8,128)(2,1)S(1)} %get-tuple-element.175.g_ref, bf16[208,384]{1,0:T(8,128)(2,1)S(1)} %get-tuple-element.149.att_b.att_ref, bf16[208,384]{1,0:T(8,128)(2,1)S(1)} %get-tuple-element.161.q_ref, ...), custom_call_target="tpu_custom_call" | custom-call | flops 1 | bytes 1 | tf_op jit(solution)/shard_map/pallas_call | solution.py:621
  41.8 2.1 %collective-permute-start.14 = (bf16[4,336,128]{2,1,0:T(8,128)(2,1)S(1)}, bf16[4,336,128]{2,1,0:T(8,128)(2,1)S(1)}, u32[]{:S(2)}, u32[]{:S(2)}) collective-permute-start(bf16[4,336,128]{2,1,0:T(8,128)(2,1)S(1)} %get-tuple-element.199), channel_id=1, source_target_pairs={{0,16},{1,17},{2,18},{3,19},{4,20},{5,21},{6,22},{7,23},{8,24},{9,... | collective-permute-start | bytes 1032200 | tf_op jit(solution)/shard_map/ppermute | solution.py:481
  45.5 3.2 %shard_map.306 = (bf16[400,384]{1,0:T(8,128)(2,1)S(1)}, bf16[400,384]{1,0:T(8,128)(2,1)S(1)}, bf16[400,384]{1,0:T(8,128)(2,1)S(1)}) custom-call(bf16[608,384]{1,0:T(8,128)(2,1)S(1)} %get-tuple-element.175.g_ref, bf16[400,384]{1,0:T(8,128)(2,1)S(1)} %get-tuple-element.148.att_a.att_ref, bf16[400,384]{1,0:T(8,128)(2,1)S(1)} %get-tuple-element.176.q_ref, ...), custom_call_target="tpu_custom_call" | custom-call | flops 1 | bytes 1 | tf_op jit(solution)/shard_map/pallas_call | solution.py:621
  48.7 3.7 %shard_map.307 = (bf16[768,384]{1,0:T(8,128)(2,1)S(1)}, bf16[4,4,112,128]{3,2,1,0:T(8,128)(2,1)S(1)}, bf16[2,4,112,128]{3,2,1,0:T(8,128)(2,1)S(1)}, bf16[2,4,112,128]{3,2,1,0:T(8,128)(2,1)S(1)}) custom-call(s32[2]{0:T(128)S(1)} %pad_add_fusion.place_ref, bf16[400,384]{1,0:T(8,128)(2,1)S(1)} %get-tuple-element.137.x_a, ...), custom_call_target="tpu_custom_call" | custom-call | flops 1 | bytes 1 | tf_op jit(solution)/shard_map/pallas_call | solution.py:621
  54.4 6.6 %collective-permute-done.15.refs_2_ = bf16[4,336,128]{2,1,0:T(8,128)(2,1)S(1)} collective-permute-done((bf16[4,336,128]{2,1,0:T(8,128)(2,1)S(1)}, bf16[4,336,128]{2,1,0:T(8,128)(2,1)S(1)}, u32[]{:S(2)}, u32[]{:S(2)}) %collective-permute-start.15) | collective-permute-done | bytes 344096 | tf_op jit(solution)/shard_map/ppermute | solution.py:481
  64.6 2.2 %collective-permute-done.17.refs_5_ = bf16[4,112,128]{2,1,0:T(8,128)(2,1)S(1)} collective-permute-done((bf16[4,112,128]{2,1,0:T(8,128)(2,1)S(1)}, bf16[4,112,128]{2,1,0:T(8,128)(2,1)S(1)}, u32[]{:S(2)}, u32[]{:S(2)}) %collective-permute-start.17) | collective-permute-done | bytes 114720 | tf_op jit(solution)/shard_map/ppermute | solution.py:481
  72.4 2.6 %collective-permute-start.21 = (bf16[1,448,128]{2,1,0:T(8,128)(2,1)S(1)}, bf16[1,448,128]{2,1,0:T(8,128)(2,1)S(1)}, u32[]{:S(2)}, u32[]{:S(2)}) collective-permute-start(bf16[1,448,128]{2,1,0:T(8,128)(2,1)S(1)} %get-tuple-element.217), channel_id=1, source_target_pairs={{0,8},{1,9},{2,10},{3,11},{4,12},{5,13},{6,14},{7,15},{8,0},{9,1},... | collective-permute-start | bytes 344072 | tf_op jit(solution)/shard_map/ppermute | solution.py:473
  76.8 3.0 %collective-permute-done.21.refs_2_ = bf16[1,448,128]{2,1,0:T(8,128)(2,1)S(1)} collective-permute-done((bf16[1,448,128]{2,1,0:T(8,128)(2,1)S(1)}, bf16[1,448,128]{2,1,0:T(8,128)(2,1)S(1)}, u32[]{:S(2)}, u32[]{:S(2)}) %collective-permute-start.21) | collective-permute-done | bytes 114720 | tf_op jit(solution)/shard_map/ppermute | solution.py:473
  81.9 4.6 %collective-permute-start.25 = (bf16[1,448,128]{2,1,0:T(8,128)(2,1)S(1)}, bf16[1,448,128]{2,1,0:T(8,128)(2,1)S(1)}, u32[]{:S(2)}, u32[]{:S(2)}) collective-permute-start(bf16[1,448,128]{2,1,0:T(8,128)(2,1)S(1)} %shard_map.310.refs_0_), channel_id=1, source_target_pairs={{0,12},{1,13},{2,14},{3,15},{4,8},{5,9},{6,10},{7,11},{8,4},{9,5},... | collective-permute-start | bytes 344072 | tf_op jit(solution)/shard_map/ppermute | solution.py:473
  89.2 3.0 %collective-permute-done.24.refs_2_ = bf16[1,448,128]{2,1,0:T(8,128)(2,1)S(1)} collective-permute-done((bf16[1,448,128]{2,1,0:T(8,128)(2,1)S(1)}, bf16[1,448,128]{2,1,0:T(8,128)(2,1)S(1)}, u32[]{:S(2)}, u32[]{:S(2)}) %collective-permute-start.24) | collective-permute-done | bytes 114720 | tf_op jit(solution)/shard_map/ppermute | solution.py:473
  97.0 3.4 %shard_map.312 = bf16[3,768,384]{2,1,0:T(8,128)(2,1)} custom-call(s32[2]{0:T(128)S(1)} %pad_add_fusion.place_ref, f32[48,128]{1,0:T(8,128)S(1)} %get-tuple-element.136.rank_ref.refs_0_, bf16[608,384]{1,0:T(8,128)(2,1)S(1)} %get-tuple-element.182.own_ref, bf16[608,384]{1,0:T(8,128)(2,1)S(1)} %collective-permute-done.11.got_ref), custom_call_target="tpu_custom_call" | custom-call | bytes 2727944 | tf_op jit(solution)/shard_map/pallas_call | solution.py:621
  100.4 3.3 %shard_map.313 = bf16[3,768,384]{2,1,0:T(8,128)(2,1)} custom-call(s32[2]{0:T(128)S(1)} %pad_add_fusion.place_ref, f32[48,128]{1,0:T(8,128)S(1)} %get-tuple-element.136.rank_ref.refs_0_, bf16[768,384]{1,0:T(8,128)(2,1)S(1)} %get-tuple-element.219.own_ref, bf16[768,384]{1,0:T(8,128)(2,1)S(1)} %collective-permute-done.26.got_ref), custom_call_target="tpu_custom_call" | custom-call | bytes 2973704 | tf_op jit(solution)/shard_map/pallas_call | solution.py:621
  103.6 3.7 %collective-permute-done.29.refs_3_ = bf16[4,448,128]{2,1,0:T(8,128)(2,1)S(1)} collective-permute-done((bf16[4,448,128]{2,1,0:T(8,128)(2,1)S(1)}, bf16[4,448,128]{2,1,0:T(8,128)(2,1)S(1)}, u32[]{:S(2)}, u32[]{:S(2)}) %collective-permute-start.29) | collective-permute-done | bytes 458784 | tf_op jit(solution)/shard_map/ppermute | solution.py:481
  107.3 4.8 %collective-permute-done.28.refs_2_ = bf16[4,448,128]{2,1,0:T(8,128)(2,1)S(1)} collective-permute-done((bf16[4,448,128]{2,1,0:T(8,128)(2,1)S(1)}, bf16[4,448,128]{2,1,0:T(8,128)(2,1)S(1)}, u32[]{:S(2)}, u32[]{:S(2)}) %collective-permute-start.28) | collective-permute-done | bytes 458784 | tf_op jit(solution)/shard_map/ppermute | solution.py:481
  113.7 2.5 %shard_map.314 = (f32[1536,384]{1,0:T(8,128)}, f32[384,1536]{1,0:T(8,128)}, f32[384,384]{1,0:T(8,128)}, f32[384,1152]{1,0:T(8,128)}, f32[8,32,128]{2,1,0:T(8,128)S(1)}) custom-call(s32[2]{0:T(128)S(1)} %pad_add_fusion.place_ref, bf16[4,448,128]{2,1,0:T(8,128)(2,1)S(1)} %shard_map.311.refs_0_, bf16[4,448,128]{2,1,0:T(8,128)(2,1)S(1)} %collective-permute-done.27.refs_1_, ...), custom_call_target="tpu_custom_call" | custom-call | flops 1 | bytes 1 | tf_op jit(solution)/shard_map/pallas_call | solution.py:621
  116.5 3.1 %shard_map.315 = (f32[1536,384]{1,0:T(8,128)}, f32[384,1536]{1,0:T(8,128)}, f32[384,384]{1,0:T(8,128)}, f32[384,1152]{1,0:T(8,128)}, f32[1536]{0:T(1024)}, /*ind...) custom-call(s32[2]{0:T(128)S(1)} %pad_add_fusion.place_ref, ...), custom_call_target="tpu_custom_call", output_to_operand_aliasing={{0}: (5, {}), {1}: (6, {}), {2}: (7, {}), {3}: (8, {})} | custom-call | flops 1 | bytes 1 | tf_op jit(solution)/shard_map/pallas_call | solution.py:621
  (114 shorter events, 37.0 us)
Async XLA Ops:
  0.7 6.8 %collective-permute-start = (s32[3]{0:T(128)}, s32[3]{0:T(128)S(1)}, u32[]{:S(2)}, u32[]{:S(2)}) collective-permute-start(s32[3]{0:T(128)} %groups_ref.1), channel_id=1, source_target_pairs={{0,1},{1,0},{2,3},{3,2},{4,5},{5,4},{6,7},{7,6},{8,9},{9,8},{10,11... | collective-permute-start | bytes 44 | tf_op jit(solution)/shard_map/ppermute | solution.py:473
  4.5 12.0 %collective-permute-start.2 = (bf16[384,384]{1,0:T(8,128)(2,1)}, bf16[384,384]{1,0:T(8,128)(2,1)S(1)}, u32[]{:S(2)}, u32[]{:S(2)}) collective-permute-start(bf16[384,384]{1,0:T(8,128)(2,1)} %get-tuple-element.132), channel_id=1, source_target_pairs={{0,16},{16,0},{1,17},{17,1},{2,18},{18,2},{3,19},{19,3},{4,20},{20... | collective-permute-start | bytes 884744 | tf_op jit(solution)/shard_map/ppermute | solution.py:660
  10.3 12.4 %collective-permute-start.3 = (bf16[384,384]{1,0:T(8,128)(2,1)}, bf16[384,384]{1,0:T(8,128)(2,1)}, u32[]{:S(2)}, u32[]{:S(2)}) collective-permute-start(bf16[384,384]{1,0:T(8,128)(2,1)} %shard_map.298.refs_0_), channel_id=1, source_target_pairs={{0,16},{16,0},{1,17},{17,1},{2,18},{18,2},{3,19},{19,3},{4,20},{20... | collective-permute-start | bytes 884744 | tf_op jit(solution)/shard_map/ppermute | solution.py:670
  11.1 3.6 %collective-permute-start.4 = (s32[12]{0:T(128)S(1)}, s32[12]{0:T(128)S(1)}, u32[]{:S(2)}, u32[]{:S(2)}) collective-permute-start(s32[12]{0:T(128)S(1)} %pad_add_fusion.2), channel_id=1, source_target_pairs={{0,4},{1,5},{2,6},{3,7},{4,0},{5,1},{6,2},{7,3},{8,12},{9,13},{10,... | collective-permute-start | bytes 152 | tf_op jit(solution)/shard_map/ppermute | solution.py:473
  14.9 16.8 %collective-permute-start.6 = (bf16[592,384]{1,0:T(8,128)(2,1)}, bf16[592,384]{1,0:T(8,128)(2,1)}, u32[]{:S(2)}, u32[]{:S(2)}) collective-permute-start(bf16[592,384]{1,0:T(8,128)(2,1)} %get-tuple-element.147), channel_id=1, source_target_pairs={{0,16},{16,0},{1,17},{17,1},{2,18},{18,2},{3,19},{19,3},{4,20},{20... | collective-permute-start | bytes 1363976 | tf_op jit(solution)/shard_map/ppermute | solution.py:680
  20.1 10.5 %collective-permute-start.5 = (s32[24]{0:T(128)S(1)}, s32[24]{0:T(128)S(1)}, u32[]{:S(2)}, u32[]{:S(2)}) collective-permute-start(s32[24]{0:T(128)S(1)} %pad_add_fusion.3), channel_id=1, source_target_pairs={{0,8},{1,9},{2,10},{3,11},{4,12},{5,13},{6,14},{7,15},{8,0},{9,1},... | collective-permute-start | bytes 296 | tf_op jit(solution)/shard_map/ppermute | solution.py:473
  29.4 19.3 %collective-permute-start.11 = (bf16[608,384]{1,0:T(8,128)(2,1)S(1)}, bf16[608,384]{1,0:T(8,128)(2,1)S(1)}, u32[]{:S(2)}, u32[]{:S(2)}) collective-permute-start(bf16[608,384]{1,0:T(8,128)(2,1)S(1)} %get-tuple-element.182.own_ref), channel_id=1, source_target_pairs={{0,16},{16,0},{1,17},{17,1},{2,18},{18,2},{3,19},{19,3},{4,20},{20... | collective-permute-start | bytes 1400840 | tf_op jit(solution)/shard_map/ppermute | solution.py:715
  41.8 12.6 %collective-permute-start.14 = (bf16[4,336,128]{2,1,0:T(8,128)(2,1)S(1)}, bf16[4,336,128]{2,1,0:T(8,128)(2,1)S(1)}, u32[]{:S(2)}, u32[]{:S(2)}) collective-permute-start(bf16[4,336,128]{2,1,0:T(8,128)(2,1)S(1)} %get-tuple-element.199), channel_id=1, source_target_pairs={{0,16},{1,17},{2,18},{3,19},{4,20},{5,21},{6,22},{7,23},{8,24},{9,... | collective-permute-start | bytes 1032200 | tf_op jit(solution)/shard_map/ppermute | solution.py:481
  43.9 17.1 %collective-permute-start.15 = (bf16[4,336,128]{2,1,0:T(8,128)(2,1)S(1)}, bf16[4,336,128]{2,1,0:T(8,128)(2,1)S(1)}, u32[]{:S(2)}, u32[]{:S(2)}) collective-permute-start(bf16[4,336,128]{2,1,0:T(8,128)(2,1)S(1)} %get-tuple-element.200), channel_id=1, source_target_pairs={{0,2},{1,3},{2,0},{3,1},{4,6},{5,7},{6,4},{7,5},{8,10},{9,11},{10,... | collective-permute-start | bytes 1032200 | tf_op jit(solution)/shard_map/ppermute | solution.py:481
  45.4 15.6 %collective-permute-start.16 = (bf16[4,336,128]{2,1,0:T(8,128)(2,1)S(1)}, bf16[4,336,128]{2,1,0:T(8,128)(2,1)S(1)}, u32[]{:S(2)}, u32[]{:S(2)}) collective-permute-start(bf16[4,336,128]{2,1,0:T(8,128)(2,1)S(1)} %get-tuple-element.201), channel_id=1, source_target_pairs={{0,18},{1,19},{2,16},{3,17},{4,22},{5,23},{6,20},{7,21},{8,26},{9,... | collective-permute-start | bytes 1032200 | tf_op jit(solution)/shard_map/ppermute | solution.py:481
  61.1 5.7 %collective-permute-start.17 = (bf16[4,112,128]{2,1,0:T(8,128)(2,1)S(1)}, bf16[4,112,128]{2,1,0:T(8,128)(2,1)S(1)}, u32[]{:S(2)}, u32[]{:S(2)}) collective-permute-start(bf16[4,112,128]{2,1,0:T(8,128)(2,1)S(1)} %get-tuple-element.207), channel_id=1, source_target_pairs={{0,16},{1,17},{2,18},{3,19},{4,20},{5,21},{6,22},{7,23},{8,24},{9,... | collective-permute-start | bytes 344072 | tf_op jit(solution)/shard_map/ppermute | solution.py:481
  62.3 5.4 %collective-permute-start.18 = (bf16[4,112,128]{2,1,0:T(8,128)(2,1)S(1)}, bf16[4,112,128]{2,1,0:T(8,128)(2,1)S(1)}, u32[]{:S(2)}, u32[]{:S(2)}) collective-permute-start(bf16[4,112,128]{2,1,0:T(8,128)(2,1)S(1)} %get-tuple-element.208), channel_id=1, source_target_pairs={{0,2},{1,3},{2,0},{3,1},{4,6},{5,7},{6,4},{7,5},{8,10},{9,11},{10,... | collective-permute-start | bytes 344072 | tf_op jit(solution)/shard_map/ppermute | solution.py:481
  63.1 5.8 %collective-permute-start.19 = (bf16[4,112,128]{2,1,0:T(8,128)(2,1)S(1)}, bf16[4,112,128]{2,1,0:T(8,128)(2,1)S(1)}, u32[]{:S(2)}, u32[]{:S(2)}) collective-permute-start(bf16[4,112,128]{2,1,0:T(8,128)(2,1)S(1)} %get-tuple-element.209), channel_id=1, source_target_pairs={{0,18},{1,19},{2,16},{3,17},{4,22},{5,23},{6,20},{7,21},{8,26},{9,... | collective-permute-start | bytes 344072 | tf_op jit(solution)/shard_map/ppermute | solution.py:481
  69.1 24.3 %collective-permute-start.26 = (bf16[768,384]{1,0:T(8,128)(2,1)S(1)}, bf16[768,384]{1,0:T(8,128)(2,1)S(1)}, u32[]{:S(2)}, u32[]{:S(2)}) collective-permute-start(bf16[768,384]{1,0:T(8,128)(2,1)S(1)} %get-tuple-element.219.own_ref), channel_id=1, source_target_pairs={{0,16},{16,0},{1,17},{17,1},{2,18},{18,2},{3,19},{19,3},{4,20},{20... | collective-permute-start | bytes 1769480 | tf_op jit(solution)/shard_map/ppermute | solution.py:756
  70.8 6.0 %collective-permute-start.20 = (bf16[1,448,128]{2,1,0:T(8,128)(2,1)S(1)}, bf16[1,448,128]{2,1,0:T(8,128)(2,1)S(1)}, u32[]{:S(2)}, u32[]{:S(2)}) collective-permute-start(bf16[1,448,128]{2,1,0:T(8,128)(2,1)S(1)} %get-tuple-element.216), channel_id=1, source_target_pairs={{0,4},{1,5},{2,6},{3,7},{4,0},{5,1},{6,2},{7,3},{8,12},{9,13},{10,... | collective-permute-start | bytes 344072 | tf_op jit(solution)/shard_map/ppermute | solution.py:473
  72.4 7.4 %collective-permute-start.21 = (bf16[1,448,128]{2,1,0:T(8,128)(2,1)S(1)}, bf16[1,448,128]{2,1,0:T(8,128)(2,1)S(1)}, u32[]{:S(2)}, u32[]{:S(2)}) collective-permute-start(bf16[1,448,128]{2,1,0:T(8,128)(2,1)S(1)} %get-tuple-element.217), channel_id=1, source_target_pairs={{0,8},{1,9},{2,10},{3,11},{4,12},{5,13},{6,14},{7,15},{8,0},{9,1},... | collective-permute-start | bytes 344072 | tf_op jit(solution)/shard_map/ppermute | solution.py:473
  75.0 6.8 %collective-permute-start.22 = (bf16[1,448,128]{2,1,0:T(8,128)(2,1)S(1)}, bf16[1,448,128]{2,1,0:T(8,128)(2,1)S(1)}, u32[]{:S(2)}, u32[]{:S(2)}) collective-permute-start(bf16[1,448,128]{2,1,0:T(8,128)(2,1)S(1)} %get-tuple-element.218), channel_id=1, source_target_pairs={{0,12},{1,13},{2,14},{3,15},{4,8},{5,9},{6,10},{7,11},{8,4},{9,5},... | collective-permute-start | bytes 344072 | tf_op jit(solution)/shard_map/ppermute | solution.py:473
  81.9 7.3 %collective-permute-start.25 = (bf16[1,448,128]{2,1,0:T(8,128)(2,1)S(1)}, bf16[1,448,128]{2,1,0:T(8,128)(2,1)S(1)}, u32[]{:S(2)}, u32[]{:S(2)}) collective-permute-start(bf16[1,448,128]{2,1,0:T(8,128)(2,1)S(1)} %shard_map.310.refs_0_), channel_id=1, source_target_pairs={{0,12},{1,13},{2,14},{3,15},{4,8},{5,9},{6,10},{7,11},{8,4},{9,5},... | collective-permute-start | bytes 344072 | tf_op jit(solution)/shard_map/ppermute | solution.py:473
  86.5 5.7 %collective-permute-start.24 = (bf16[1,448,128]{2,1,0:T(8,128)(2,1)S(1)}, bf16[1,448,128]{2,1,0:T(8,128)(2,1)S(1)}, u32[]{:S(2)}, u32[]{:S(2)}) collective-permute-start(bf16[1,448,128]{2,1,0:T(8,128)(2,1)S(1)} %shard_map.310.refs_0_), channel_id=1, source_target_pairs={{0,8},{1,9},{2,10},{3,11},{4,12},{5,13},{6,14},{7,15},{8,0},{9,1},... | collective-permute-start | bytes 344072 | tf_op jit(solution)/shard_map/ppermute | solution.py:473
  88.1 5.3 %collective-permute-start.23 = (bf16[1,448,128]{2,1,0:T(8,128)(2,1)S(1)}, bf16[1,448,128]{2,1,0:T(8,128)(2,1)S(1)}, u32[]{:S(2)}, u32[]{:S(2)}) collective-permute-start(bf16[1,448,128]{2,1,0:T(8,128)(2,1)S(1)} %shard_map.310.refs_0_), channel_id=1, source_target_pairs={{0,4},{1,5},{2,6},{3,7},{4,0},{5,1},{6,2},{7,3},{8,12},{9,13},{10,... | collective-permute-start | bytes 344072 | tf_op jit(solution)/shard_map/ppermute | solution.py:473
  93.4 13.9 %collective-permute-start.29 = (bf16[4,448,128]{2,1,0:T(8,128)(2,1)S(1)}, bf16[4,448,128]{2,1,0:T(8,128)(2,1)S(1)}, u32[]{:S(2)}, u32[]{:S(2)}) collective-permute-start(bf16[4,448,128]{2,1,0:T(8,128)(2,1)S(1)} %shard_map.311.refs_0_), channel_id=1, source_target_pairs={{0,18},{1,19},{2,16},{3,17},{4,22},{5,23},{6,20},{7,21},{8,26},{9,... | collective-permute-start | bytes 1376264 | tf_op jit(solution)/shard_map/ppermute | solution.py:481
  94.9 17.2 %collective-permute-start.28 = (bf16[4,448,128]{2,1,0:T(8,128)(2,1)S(1)}, bf16[4,448,128]{2,1,0:T(8,128)(2,1)S(1)}, u32[]{:S(2)}, u32[]{:S(2)}) collective-permute-start(bf16[4,448,128]{2,1,0:T(8,128)(2,1)S(1)} %shard_map.311.refs_0_), channel_id=1, source_target_pairs={{0,2},{1,3},{2,0},{3,1},{4,6},{5,7},{6,4},{7,5},{8,10},{9,11},{10,... | collective-permute-start | bytes 1376264 | tf_op jit(solution)/shard_map/ppermute | solution.py:481
  95.4 17.3 %collective-permute-start.27 = (bf16[4,448,128]{2,1,0:T(8,128)(2,1)S(1)}, bf16[4,448,128]{2,1,0:T(8,128)(2,1)S(1)}, u32[]{:S(2)}, u32[]{:S(2)}) collective-permute-start(bf16[4,448,128]{2,1,0:T(8,128)(2,1)S(1)} %shard_map.311.refs_0_), channel_id=1, source_target_pairs={{0,16},{1,17},{2,18},{3,19},{4,20},{5,21},{6,22},{7,23},{8,24},{9,... | collective-permute-start | bytes 1376264 | tf_op jit(solution)/shard_map/ppermute | solution.py:481
  112.7 3.6 %collective-permute-start.31 = (bf16[4,448,128]{2,1,0:T(8,128)(2,1)S(1)}, bf16[4,448,128]{2,1,0:T(8,128)(2,1)S(1)}, u32[]{:S(2)}, u32[]{:S(2)}) collective-permute-start(bf16[4,448,128]{2,1,0:T(8,128)(2,1)S(1)} %collective-permute-done.27.refs_1_), channel_id=1, source_target_pairs={{0,1},{1,0},{2,3},{3,2},{4,5},{5,4},{6,7},{7,6},{8,9},{9,8},{10,11... | collective-permute-start | bytes 1376264 | tf_op jit(solution)/shard_map/ppermute | solution.py:473
  (27 other events, 150.2 us)

commit v6 on v5

--- a/solution.py
+++ b/solution.py
@@ -516,9 +516,14 @@
     total, sent = lax.optimization_barrier((total, sent))
     pieces = spread_near([total] * 4)
     last = beside_last(sent)
-    *pieces, last = lax.optimization_barrier((*pieces, last))
-    got = [clip_swap(piece, 1) for piece in pieces]
-    return finish(1, got, finish(0, pieces, ())), last
+    early, last = lax.optimization_barrier((total, last))
+    middle = total.shape[1] // 32 * 16
+    parts = [early[:, :middle], early[:, middle:]]
+    done = finish(((0, 0), (0, 1)), [parts, [clip_swap(part, 1) for part in parts]], ())
+    *pieces, done = lax.optimization_barrier((*pieces, done))
+    got = [clip_swap(piece, 1) for piece in pieces[1:]]
+    done = finish(((1, 0), (2, 0), (3, 0)), [[piece] for piece in pieces[1:]], done)
+    return finish(((1, 1), (2, 1), (3, 1)), [[piece] for piece in got], done), last
 
 
 def join_kernel(*refs):
@@ -527,26 +532,33 @@
             refs[4][4 * slot + step] = refs[step][slot]
 
 
-def finish_kernel(side, depths, counts, place_ref, *refs):
-    sources, refs = refs[:4], refs[4:]
-    if side:
-        first_kept_ref, refs = refs[4], refs[5:]
-        outs, vectors, refs = refs[:4], refs[4 : 4 + sum(counts)], refs[4 + sum(counts) :]
-        kept_ref, *refs = refs
-    else:
-        outs, kept_ref, refs = refs[:4], refs[4], refs[5:]
-    stage_a, stage_b, done, *wides = refs
-    far_places = sources[0].shape[0]
+def finish_kernel(jobs, first_call, depths, counts, place_ref, *refs):
+    parts = len(jobs) if not first_call else 2 * len(jobs)
+    sources, refs = refs[:parts], refs[parts:]
+    if not first_call:
+        earlier_ref, refs = refs[4], refs[5:]
+    outs, refs = refs[:4], refs[4:]
+    vectors, refs = refs[: sum(counts)], refs[sum(counts) :]
+    kept_ref, stage_a, stage_b, done, *wides = refs
+    kept_ref[...] = jnp.zeros(kept_ref.shape, F32) if first_call else earlier_ref[...]
     stores = []
-    for near in range(4):
+    each = parts // len(jobs)
+    for job, (near, side) in enumerate(jobs):
         eighth = eighth_at(place_ref, near, side)
-        for far in range(far_places):
-            stage_a[chunk_rows_at(place_ref, far, depths[0]), :] = sources[near][far, : depths[0]]
-            stage_b[chunk_rows_at(place_ref, far, depths[1]), :] = sources[near][far, depths[0] :]
+        for far in range(sources[0].shape[0]):
+            start = 0
+            for source in sources[job * each : (job + 1) * each]:
+                stop = start + source.shape[1]
+                for stage_ref, low, depth in ((stage_a, 0, depths[0]), (stage_b, depths[0], depths[1])):
+                    top, end = max(start, low), min(stop, low + depth)
+                    if top < end:
+                        first = pl.multiple_of((far ^ (place_ref[1] >> 3)) * depth + (top - low), 16)
+                        stage_ref[pl.ds(first, end - top), :] = source[far, top - start : end - start]
+                start = stop
         for unit, stage_ref in enumerate((stage_a, stage_b)):
             first = 0
             for at in ((0, 1, 2), (3,))[unit]:
-                wide_ref = wides[at].at[near]
+                wide_ref = wides[at].at[job]
                 depth, width = wide_ref.shape
                 for block in range(width // LANES):
                     wide_ref[:, block * LANES : (block + 1) * LANES] = stage_ref[first : first + depth, :].astype(F32)
@@ -559,21 +571,14 @@
                 stores.append(pltpu.make_async_copy(wide_ref, target, done.at[len(stores)]))
                 stores[-1].start()
             kept_ref[eighth, 16 * unit : 16 * unit + 16] = stage_ref[first : first + 16, :].astype(F32)
-    if side:
-        for near in range(4):
-            eighth = eighth_at(place_ref, near, 0)
-            kept_ref[eighth] = first_kept_ref[eighth]
-        at = 0
-        for unit, count in enumerate(counts):
-            blocks = [(ref, block) for ref in vectors[at : at + count] for block in range(ref.shape[0] // LANES)]
-            at += count
-            each = -(-len(blocks) // 8)
-            for number, (ref, block) in enumerate(blocks):
-                eighth, row = divmod(number, each)
-                ref[block * LANES : (block + 1) * LANES] = kept_ref[eighth, 16 * unit + row]
-    else:
-        for near in range(4):
-            kept_ref[eighth_at(place_ref, near, 1)] = jnp.zeros(kept_ref.shape[1:], F32)
+    at = 0
+    for unit, count in enumerate(counts):
+        blocks = [(ref, block) for ref in vectors[at : at + count] for block in range(ref.shape[0] // LANES)]
+        at += count
+        each = -(-len(blocks) // 8)
+        for number, (ref, block) in enumerate(blocks):
+            eighth, row = divmod(number, each)
+            ref[block * LANES : (block + 1) * LANES] = kept_ref[eighth, 16 * unit + row]
     for store in stores:
         store.wait()
 
@@ -757,27 +762,29 @@
 
     def place_rows(got):
         return (
-            run(functools.partial(outputs_kernel, unmasked), (place, rank, out_rows, out_got), shape(*tokens.shape)),
-            run(functools.partial(grads_out_kernel, unmasked), (place, rank, grad_rows, got), shape(*tokens.shape)),
+            run(functools.partial(outputs_kernel, unmasked), (place, rank, out_rows, out_got), shape(*tokens.shape), hides=False),
+            run(functools.partial(grads_out_kernel, unmasked), (place, rank, grad_rows, got), shape(*tokens.shape), hides=False),
         )
 
     weights = [(hidden, width), (width, hidden), (width, width), (width, 3 * width)]
     slabs = [(hidden // 8, width), (width // 2, hidden // 4), (width // 8, width), (width // 8, 3 * width)]
     vectors = [shape(dim, kind=F32) for dim in [hidden] + [width] * 9]
 
-    def finish(side, sources, earlier):
-        kept = pltpu.VMEM((8, 32, LANES), F32)
+    def finish(jobs, sources, earlier):
+        sources = [part for parts in sources for part in parts]
+        last = bool(earlier) and jobs[0][1] == 1
+        kept = (8, 32, LANES)
         return run(
-            functools.partial(finish_kernel, side, depths, (5, 5)),
+            functools.partial(finish_kernel, jobs, not earlier, depths, (5, 5) if last else ()),
             (place, *sources, *earlier),
-            [shape(*dims, kind=F32) for dims in weights] + (vectors if side else [shape(8, 32, LANES, kind=F32)]),
-            [kept] * side
+            [shape(*dims, kind=F32) for dims in weights] + (vectors if last else [shape(*kept, kind=F32)]),
+            [pltpu.VMEM(kept, F32)] * last
             + [pltpu.VMEM((devices // 8 * depth, LANES), BF) for depth in depths]
-            + [pltpu.SemaphoreType.DMA((16,))]
-            + [pltpu.VMEM((4, *dims), F32) for dims in slabs],
-            in_hbm=range(1 + len(sources), 5 + len(sources)) if side else (),
+            + [pltpu.SemaphoreType.DMA((4 * len(jobs),))]
+            + [pltpu.VMEM((len(jobs), *dims), F32) for dims in slabs],
+            in_hbm=range(1 + len(sources), 5 + len(sources)) if earlier else (),
             out_hbm=range(4),
-            aliases={1 + len(sources) + at: at for at in range(4)} if side else {},
+            aliases={1 + len(sources) + at: at for at in range(4)} if earlier else {},
             hides=False,
         )
 

time: 120 us -> 119 us (level)
  waiting for transfers between devices: 34.1 us -> 31.8 us
  Pallas kernels: 45.3 us -> 46.5 us
    ppermute x20 -> x21, waiting for transfers between devices: 13.1 us -> 11.2 us  [clip_swap(): lax.ppermute(values, 'clip', [(i, i ^ distance) for i in range(size)])]
    pallas_call x14 -> x15, Pallas kernels: 44.5 us -> 45.8 us  [run(): pl.pallas_call(kernel, out_shape=outs, in_specs=[SMEM if at < scalars els...]
    ppermute x20 -> x21, starting transfers between devices: 20 us -> 20.1 us  [clip_swap(): lax.ppermute(values, 'clip', [(i, i ^ distance) for i in range(size)])]
  transfers between devices with their start and end apart: 34 -> 35, of which waited for: 18 -> 19; matrix products, arithmetic and copies ran while one was open for 0% -> 0% of each run, Pallas kernels for 35% -> 37%
where the time goes in v6:
time: 119 us
  Pallas kernels  46.5 us (39%)
  starting transfers between devices  38.6 us (32%)
  waiting for transfers between devices  31.8 us (27%)
  between operations  1.31 us (1%)
    pallas_call x15, Pallas kernels, run(): pl.pallas_call(kernel, out_shape=outs, in_specs=[SMEM if at < scalars els...  45.8 us
    ppermute x21, starting transfers between devices, clip_swap(): lax.ppermute(values, 'clip', [(i, i ^ distance) for i in range(size)])  20.1 us
    ppermute x9, waiting for transfers between devices, near_swap(): return lax.ppermute(values, ('tm', 'clip'), pairs)  19.6 us
    ppermute x21, waiting for transfers between devices, clip_swap(): lax.ppermute(values, 'clip', [(i, i ^ distance) for i in range(size)])  11.2 us
    ppermute x9, starting transfers between devices, near_swap(): return lax.ppermute(values, ('tm', 'clip'), pairs)  10.7 us
    ppermute x1, starting transfers between devices, body(): got_mine = swap(theirs)  2.93 us
  transfers between devices with their start and end apart: 35, of which 19 were waited for; matrix products, arithmetic and copies ran while one was open for 0% of the time, Pallas kernels for 37%

profile of v6, /device:TPU:0, one launch (start us, length us, event | category | flops | bytes accessed | tf_op | source)
XLA Modules:
  0.0 118.8 jit_solution(16956966721928298889)
XLA Ops:
  1.3 3.2 %shard_map.297 = (bf16[384,384]{1,0:T(8,128)(2,1)}, f32[48,128]{1,0:T(8,128)S(1)}) custom-call(s32[2]{0:T(128)S(1)} %pad_add_fusion.place_ref, s32[3,1152]{1,0:T(4,128)} %masked_ref.1, bf16[3,768,384]{2,1,0:T(8,128)(2,1)} %refs_1_.1), custom_call_target="tpu_custom_call" | custom-call | flops 235929600 | bytes 2102792 | tf_op jit(solution)/shard_map/pallas_call | solution.py:626
  4.5 2.9 %collective-permute-start.2 = (bf16[384,384]{1,0:T(8,128)(2,1)}, bf16[384,384]{1,0:T(8,128)(2,1)S(1)}, u32[]{:S(2)}, u32[]{:S(2)}) collective-permute-start(bf16[384,384]{1,0:T(8,128)(2,1)} %get-tuple-element.142), channel_id=1, source_target_pairs={{0,16},{16,0},{1,17},{17,1},{2,18},{18,2},{3,19},{19,3},{4,20},{20... | collective-permute-start | bytes 884744 | tf_op jit(solution)/shard_map/ppermute | solution.py:665
  12.7 2.1 %shard_map.301 = (bf16[608,384]{1,0:T(8,128)(2,1)S(1)}, bf16[592,384]{1,0:T(8,128)(2,1)}) custom-call(s32[2]{0:T(128)S(1)} %pad_add_fusion.place_ref, f32[48,128]{1,0:T(8,128)S(1)} %get-tuple-element.146.rank_ref.refs_0_, bf16[3,768,384]{2,1,0:T(8,128)(2,1)S(1)} %copy-done.6), custom_call_target="tpu_custom_call" | custom-call | flops 707788800 | bytes 2715656 | tf_op jit(solution)/shard_map/pallas_call | solution.py:626
  16.5 3.6 %shard_map.299 = (bf16[400,384]{1,0:T(8,128)(2,1)S(1)}, bf16[400,384]{1,0:T(8,128)(2,1)S(1)}, bf16[400,384]{1,0:T(8,128)(2,1)S(1)}, bf16[400,384]{1,0:T(8,128)(2...) custom-call(s32[2]{0:T(128)S(1)} %pad_add_fusion.place_ref, ...), custom_call_target="tpu_custom_call" | custom-call | flops 599654400 | bytes 7057928 | tf_op jit(solution)/shard_map/pallas_call | solution.py:626
  20.1 2.7 %collective-permute-start.5 = (s32[24]{0:T(128)S(1)}, s32[24]{0:T(128)S(1)}, u32[]{:S(2)}, u32[]{:S(2)}) collective-permute-start(s32[24]{0:T(128)S(1)} %pad_add_fusion.3), channel_id=1, source_target_pairs={{0,8},{1,9},{2,10},{3,11},{4,12},{5,13},{6,14},{7,15},{8,0},{9,1},... | collective-permute-start | bytes 296 | tf_op jit(solution)/shard_map/ppermute | solution.py:473
  22.8 3.0 %shard_map.300 = (bf16[208,384]{1,0:T(8,128)(2,1)S(1)}, bf16[208,384]{1,0:T(8,128)(2,1)S(1)}, bf16[400,384]{1,0:T(8,128)(2,1)S(1)}, bf16[400,384]{1,0:T(8,128)(2...) custom-call(s32[2]{0:T(128)S(1)} %pad_add_fusion.place_ref, ...), custom_call_target="tpu_custom_call" | custom-call | flops 481689600 | bytes 4207112 | tf_op jit(solution)/shard_map/pallas_call | solution.py:626
  25.8 3.6 %shard_map.302 = (bf16[608,384]{1,0:T(8,128)(2,1)S(1)}, f32[608,384]{1,0:T(8,128)S(1)}, bf16[608,384]{1,0:T(8,128)(2,1)S(1)}, bf16[608,1536]{1,0:T(8,128)(2,1)S(1)}, bf16[608,1536]{1,0:T(8,128)(2,1)S(1)}) custom-call(bf16[400,384]{1,0:T(8,128)(2,1)S(1)} %get-tuple-element.158.att_a.att_ref, bf16[208,384]{1,0:T(8,128)(2,1)S(1)} %get-tuple-element.159.att_b.att_ref, ...), custom_call_target="tpu_custom_call" | custom-call | flops 1613758464 | bytes 9211392 | tf_op jit(solution)/shard_map/pallas_call | solution.py:626
  31.6 6.4 %shard_map.303 = (f32[608,384]{1,0:T(8,128)S(1)}, bf16[608,384]{1,0:T(8,128)(2,1)S(1)}, bf16[4,4,336,128]{3,2,1,0:T(8,128)(2,1)S(1)}, bf16[1,4,336,128]{3,2,1,0:...) custom-call(s32[2]{0:T(128)S(1)} %pad_add_fusion.place_ref, ...), custom_call_target="tpu_custom_call" | custom-call | flops 1 | bytes 1 | tf_op jit(solution)/shard_map/pallas_call | solution.py:626
  39.1 2.3 %shard_map.304 = (bf16[208,384]{1,0:T(8,128)(2,1)S(1)}, bf16[400,384]{1,0:T(8,128)(2,1)S(1)}, bf16[400,384]{1,0:T(8,128)(2,1)S(1)}) custom-call(bf16[608,384]{1,0:T(8,128)(2,1)S(1)} %get-tuple-element.185.g_ref, bf16[208,384]{1,0:T(8,128)(2,1)S(1)} %get-tuple-element.159.att_b.att_ref, bf16[208,384]{1,0:T(8,128)(2,1)S(1)} %get-tuple-element.171.q_ref, ...), custom_call_target="tpu_custom_call" | custom-call | flops 1 | bytes 1 | tf_op jit(solution)/shard_map/pallas_call | solution.py:626
  41.8 2.1 %collective-permute-start.14 = (bf16[4,336,128]{2,1,0:T(8,128)(2,1)S(1)}, bf16[4,336,128]{2,1,0:T(8,128)(2,1)S(1)}, u32[]{:S(2)}, u32[]{:S(2)}) collective-permute-start(bf16[4,336,128]{2,1,0:T(8,128)(2,1)S(1)} %get-tuple-element.209), channel_id=1, source_target_pairs={{0,16},{1,17},{2,18},{3,19},{4,20},{5,21},{6,22},{7,23},{8,24},{9,... | collective-permute-start | bytes 1032200 | tf_op jit(solution)/shard_map/ppermute | solution.py:481
  45.5 3.2 %shard_map.306 = (bf16[400,384]{1,0:T(8,128)(2,1)S(1)}, bf16[400,384]{1,0:T(8,128)(2,1)S(1)}, bf16[400,384]{1,0:T(8,128)(2,1)S(1)}) custom-call(bf16[608,384]{1,0:T(8,128)(2,1)S(1)} %get-tuple-element.185.g_ref, bf16[400,384]{1,0:T(8,128)(2,1)S(1)} %get-tuple-element.158.att_a.att_ref, bf16[400,384]{1,0:T(8,128)(2,1)S(1)} %get-tuple-element.186.q_ref, ...), custom_call_target="tpu_custom_call" | custom-call | flops 1 | bytes 1 | tf_op jit(solution)/shard_map/pallas_call | solution.py:626
  48.7 3.7 %shard_map.307 = (bf16[768,384]{1,0:T(8,128)(2,1)S(1)}, bf16[4,4,112,128]{3,2,1,0:T(8,128)(2,1)S(1)}, bf16[2,4,112,128]{3,2,1,0:T(8,128)(2,1)S(1)}, bf16[2,4,112,128]{3,2,1,0:T(8,128)(2,1)S(1)}) custom-call(s32[2]{0:T(128)S(1)} %pad_add_fusion.place_ref, bf16[400,384]{1,0:T(8,128)(2,1)S(1)} %get-tuple-element.147.x_a, ...), custom_call_target="tpu_custom_call" | custom-call | flops 1 | bytes 1 | tf_op jit(solution)/shard_map/pallas_call | solution.py:626
  54.4 6.6 %collective-permute-done.15.refs_2_ = bf16[4,336,128]{2,1,0:T(8,128)(2,1)S(1)} collective-permute-done((bf16[4,336,128]{2,1,0:T(8,128)(2,1)S(1)}, bf16[4,336,128]{2,1,0:T(8,128)(2,1)S(1)}, u32[]{:S(2)}, u32[]{:S(2)}) %collective-permute-start.15) | collective-permute-done | bytes 344096 | tf_op jit(solution)/shard_map/ppermute | solution.py:481
  64.6 2.2 %collective-permute-done.17.refs_5_ = bf16[4,112,128]{2,1,0:T(8,128)(2,1)S(1)} collective-permute-done((bf16[4,112,128]{2,1,0:T(8,128)(2,1)S(1)}, bf16[4,112,128]{2,1,0:T(8,128)(2,1)S(1)}, u32[]{:S(2)}, u32[]{:S(2)}) %collective-permute-start.17) | collective-permute-done | bytes 114720 | tf_op jit(solution)/shard_map/ppermute | solution.py:481
  72.4 2.6 %collective-permute-start.21 = (bf16[1,448,128]{2,1,0:T(8,128)(2,1)S(1)}, bf16[1,448,128]{2,1,0:T(8,128)(2,1)S(1)}, u32[]{:S(2)}, u32[]{:S(2)}) collective-permute-start(bf16[1,448,128]{2,1,0:T(8,128)(2,1)S(1)} %get-tuple-element.227), channel_id=1, source_target_pairs={{0,8},{1,9},{2,10},{3,11},{4,12},{5,13},{6,14},{7,15},{8,0},{9,1},... | collective-permute-start | bytes 344072 | tf_op jit(solution)/shard_map/ppermute | solution.py:473
  76.8 3.0 %collective-permute-done.21.refs_2_ = bf16[1,448,128]{2,1,0:T(8,128)(2,1)S(1)} collective-permute-done((bf16[1,448,128]{2,1,0:T(8,128)(2,1)S(1)}, bf16[1,448,128]{2,1,0:T(8,128)(2,1)S(1)}, u32[]{:S(2)}, u32[]{:S(2)}) %collective-permute-start.21) | collective-permute-done | bytes 114720 | tf_op jit(solution)/shard_map/ppermute | solution.py:473
  79.8 2.0 %collective-permute-done.22.refs_3_ = bf16[1,448,128]{2,1,0:T(8,128)(2,1)S(1)} collective-permute-done((bf16[1,448,128]{2,1,0:T(8,128)(2,1)S(1)}, bf16[1,448,128]{2,1,0:T(8,128)(2,1)S(1)}, u32[]{:S(2)}, u32[]{:S(2)}) %collective-permute-start.22) | collective-permute-done | bytes 114720 | tf_op jit(solution)/shard_map/ppermute | solution.py:473
  81.9 4.6 %collective-permute-start.25 = (bf16[1,448,128]{2,1,0:T(8,128)(2,1)S(1)}, bf16[1,448,128]{2,1,0:T(8,128)(2,1)S(1)}, u32[]{:S(2)}, u32[]{:S(2)}) collective-permute-start(bf16[1,448,128]{2,1,0:T(8,128)(2,1)S(1)} %shard_map.310.refs_0_), channel_id=1, source_target_pairs={{0,12},{1,13},{2,14},{3,15},{4,8},{5,9},{6,10},{7,11},{8,4},{9,5},... | collective-permute-start | bytes 344072 | tf_op jit(solution)/shard_map/ppermute | solution.py:473
  88.6 3.4 %shard_map.312 = bf16[3,768,384]{2,1,0:T(8,128)(2,1)} custom-call(s32[2]{0:T(128)S(1)} %pad_add_fusion.place_ref, f32[48,128]{1,0:T(8,128)S(1)} %get-tuple-element.146.rank_ref.refs_0_, bf16[608,384]{1,0:T(8,128)(2,1)S(1)} %get-tuple-element.192.own_ref, bf16[608,384]{1,0:T(8,128)(2,1)S(1)} %collective-permute-done.11.got_ref), custom_call_target="tpu_custom_call" | custom-call | flops 1 | bytes 1 | tf_op jit(solution)/shard_map/pallas_call | solution.py:626
  97.0 3.3 %shard_map.313 = bf16[3,768,384]{2,1,0:T(8,128)(2,1)} custom-call(s32[2]{0:T(128)S(1)} %pad_add_fusion.place_ref, f32[48,128]{1,0:T(8,128)S(1)} %get-tuple-element.146.rank_ref.refs_0_, bf16[768,384]{1,0:T(8,128)(2,1)S(1)} %get-tuple-element.229.own_ref, bf16[768,384]{1,0:T(8,128)(2,1)S(1)} %collective-permute-done.26.got_ref), custom_call_target="tpu_custom_call" | custom-call | flops 1 | bytes 1 | tf_op jit(solution)/shard_map/pallas_call | solution.py:626
  104.0 3.3 %collective-permute-done.29.refs_2_ = bf16[4,448,128]{2,1,0:T(8,128)(2,1)S(1)} collective-permute-done((bf16[4,448,128]{2,1,0:T(8,128)(2,1)S(1)}, bf16[4,448,128]{2,1,0:T(8,128)(2,1)S(1)}, u32[]{:S(2)}, u32[]{:S(2)}) %collective-permute-start.29) | collective-permute-done | bytes 458784 | tf_op jit(solution)/shard_map/ppermute | solution.py:481
  107.3 4.8 %collective-permute-done.28.refs_1_ = bf16[4,448,128]{2,1,0:T(8,128)(2,1)S(1)} collective-permute-done((bf16[4,448,128]{2,1,0:T(8,128)(2,1)S(1)}, bf16[4,448,128]{2,1,0:T(8,128)(2,1)S(1)}, u32[]{:S(2)}, u32[]{:S(2)}) %collective-permute-start.28) | collective-permute-done | bytes 458784 | tf_op jit(solution)/shard_map/ppermute | solution.py:481
  113.2 2.2 %shard_map.315 = (f32[1536,384]{1,0:T(8,128)}, f32[384,1536]{1,0:T(8,128)}, f32[384,384]{1,0:T(8,128)}, f32[384,1152]{1,0:T(8,128)}, f32[8,32,128]{2,1,0:T(8,128)S(1)}) custom-call(s32[2]{0:T(128)S(1)} %pad_add_fusion.place_ref, ...), custom_call_target="tpu_custom_call", output_to_operand_aliasing={{0}: (4, {}), {1}: (5, {}), {2}: (6, {}), {3}: (7, {})} | custom-call | flops 1 | bytes 1 | tf_op jit(solution)/shard_map/pallas_call | solution.py:626
  115.8 2.8 %shard_map.316 = (f32[1536,384]{1,0:T(8,128)}, f32[384,1536]{1,0:T(8,128)}, f32[384,384]{1,0:T(8,128)}, f32[384,1152]{1,0:T(8,128)}, f32[1536]{0:T(1024)}, /*ind...) custom-call(s32[2]{0:T(128)S(1)} %pad_add_fusion.place_ref, ...), custom_call_target="tpu_custom_call", output_to_operand_aliasing={{0}: (4, {}), {1}: (5, {}), {2}: (6, {}), {3}: (7, {})} | custom-call | flops 1 | bytes 1 | tf_op jit(solution)/shard_map/pallas_call | solution.py:626
  (118 shorter events, 38.0 us)
Async XLA Ops:
  0.7 6.8 %collective-permute-start = (s32[3]{0:T(128)}, s32[3]{0:T(128)S(1)}, u32[]{:S(2)}, u32[]{:S(2)}) collective-permute-start(s32[3]{0:T(128)} %groups_ref.1), channel_id=1, source_target_pairs={{0,1},{1,0},{2,3},{3,2},{4,5},{5,4},{6,7},{7,6},{8,9},{9,8},{10,11... | collective-permute-start | bytes 44 | tf_op jit(solution)/shard_map/ppermute | solution.py:473
  4.5 12.0 %collective-permute-start.2 = (bf16[384,384]{1,0:T(8,128)(2,1)}, bf16[384,384]{1,0:T(8,128)(2,1)S(1)}, u32[]{:S(2)}, u32[]{:S(2)}) collective-permute-start(bf16[384,384]{1,0:T(8,128)(2,1)} %get-tuple-element.142), channel_id=1, source_target_pairs={{0,16},{16,0},{1,17},{17,1},{2,18},{18,2},{3,19},{19,3},{4,20},{20... | collective-permute-start | bytes 884744 | tf_op jit(solution)/shard_map/ppermute | solution.py:665
  7.5 3.5 %collective-permute-start.1 = (s32[6]{0:T(128)S(1)}, s32[6]{0:T(128)S(1)}, u32[]{:S(2)}, u32[]{:S(2)}) collective-permute-start(s32[6]{0:T(128)S(1)} %pad_add_fusion.1), channel_id=1, source_target_pairs={{0,2},{1,3},{2,0},{3,1},{4,6},{5,7},{6,4},{7,5},{8,10},{9,11},{10,... | collective-permute-start | bytes 80 | tf_op jit(solution)/shard_map/ppermute | solution.py:473
  10.3 12.4 %collective-permute-start.3 = (bf16[384,384]{1,0:T(8,128)(2,1)}, bf16[384,384]{1,0:T(8,128)(2,1)}, u32[]{:S(2)}, u32[]{:S(2)}) collective-permute-start(bf16[384,384]{1,0:T(8,128)(2,1)} %shard_map.298.refs_0_), channel_id=1, source_target_pairs={{0,16},{16,0},{1,17},{17,1},{2,18},{18,2},{3,19},{19,3},{4,20},{20... | collective-permute-start | bytes 884744 | tf_op jit(solution)/shard_map/ppermute | solution.py:675
  11.1 3.6 %collective-permute-start.4 = (s32[12]{0:T(128)S(1)}, s32[12]{0:T(128)S(1)}, u32[]{:S(2)}, u32[]{:S(2)}) collective-permute-start(s32[12]{0:T(128)S(1)} %pad_add_fusion.2), channel_id=1, source_target_pairs={{0,4},{1,5},{2,6},{3,7},{4,0},{5,1},{6,2},{7,3},{8,12},{9,13},{10,... | collective-permute-start | bytes 152 | tf_op jit(solution)/shard_map/ppermute | solution.py:473
  14.9 16.8 %collective-permute-start.6 = (bf16[592,384]{1,0:T(8,128)(2,1)}, bf16[592,384]{1,0:T(8,128)(2,1)}, u32[]{:S(2)}, u32[]{:S(2)}) collective-permute-start(bf16[592,384]{1,0:T(8,128)(2,1)} %get-tuple-element.157), channel_id=1, source_target_pairs={{0,16},{16,0},{1,17},{17,1},{2,18},{18,2},{3,19},{19,3},{4,20},{20... | collective-permute-start | bytes 1363976 | tf_op jit(solution)/shard_map/ppermute | solution.py:685
  20.1 10.5 %collective-permute-start.5 = (s32[24]{0:T(128)S(1)}, s32[24]{0:T(128)S(1)}, u32[]{:S(2)}, u32[]{:S(2)}) collective-permute-start(s32[24]{0:T(128)S(1)} %pad_add_fusion.3), channel_id=1, source_target_pairs={{0,8},{1,9},{2,10},{3,11},{4,12},{5,13},{6,14},{7,15},{8,0},{9,1},... | collective-permute-start | bytes 296 | tf_op jit(solution)/shard_map/ppermute | solution.py:473
  29.4 19.3 %collective-permute-start.11 = (bf16[608,384]{1,0:T(8,128)(2,1)S(1)}, bf16[608,384]{1,0:T(8,128)(2,1)S(1)}, u32[]{:S(2)}, u32[]{:S(2)}) collective-permute-start(bf16[608,384]{1,0:T(8,128)(2,1)S(1)} %get-tuple-element.192.own_ref), channel_id=1, source_target_pairs={{0,16},{16,0},{1,17},{17,1},{2,18},{18,2},{3,19},{19,3},{4,20},{20... | collective-permute-start | bytes 1400840 | tf_op jit(solution)/shard_map/ppermute | solution.py:720
  41.8 12.6 %collective-permute-start.14 = (bf16[4,336,128]{2,1,0:T(8,128)(2,1)S(1)}, bf16[4,336,128]{2,1,0:T(8,128)(2,1)S(1)}, u32[]{:S(2)}, u32[]{:S(2)}) collective-permute-start(bf16[4,336,128]{2,1,0:T(8,128)(2,1)S(1)} %get-tuple-element.209), channel_id=1, source_target_pairs={{0,16},{1,17},{2,18},{3,19},{4,20},{5,21},{6,22},{7,23},{8,24},{9,... | collective-permute-start | bytes 1032200 | tf_op jit(solution)/shard_map/ppermute | solution.py:481
  43.9 17.1 %collective-permute-start.15 = (bf16[4,336,128]{2,1,0:T(8,128)(2,1)S(1)}, bf16[4,336,128]{2,1,0:T(8,128)(2,1)S(1)}, u32[]{:S(2)}, u32[]{:S(2)}) collective-permute-start(bf16[4,336,128]{2,1,0:T(8,128)(2,1)S(1)} %get-tuple-element.210), channel_id=1, source_target_pairs={{0,2},{1,3},{2,0},{3,1},{4,6},{5,7},{6,4},{7,5},{8,10},{9,11},{10,... | collective-permute-start | bytes 1032200 | tf_op jit(solution)/shard_map/ppermute | solution.py:481
  45.4 15.6 %collective-permute-start.16 = (bf16[4,336,128]{2,1,0:T(8,128)(2,1)S(1)}, bf16[4,336,128]{2,1,0:T(8,128)(2,1)S(1)}, u32[]{:S(2)}, u32[]{:S(2)}) collective-permute-start(bf16[4,336,128]{2,1,0:T(8,128)(2,1)S(1)} %get-tuple-element.211), channel_id=1, source_target_pairs={{0,18},{1,19},{2,16},{3,17},{4,22},{5,23},{6,20},{7,21},{8,26},{9,... | collective-permute-start | bytes 1032200 | tf_op jit(solution)/shard_map/ppermute | solution.py:481
  61.1 5.7 %collective-permute-start.17 = (bf16[4,112,128]{2,1,0:T(8,128)(2,1)S(1)}, bf16[4,112,128]{2,1,0:T(8,128)(2,1)S(1)}, u32[]{:S(2)}, u32[]{:S(2)}) collective-permute-start(bf16[4,112,128]{2,1,0:T(8,128)(2,1)S(1)} %get-tuple-element.217), channel_id=1, source_target_pairs={{0,16},{1,17},{2,18},{3,19},{4,20},{5,21},{6,22},{7,23},{8,24},{9,... | collective-permute-start | bytes 344072 | tf_op jit(solution)/shard_map/ppermute | solution.py:481
  62.3 5.4 %collective-permute-start.18 = (bf16[4,112,128]{2,1,0:T(8,128)(2,1)S(1)}, bf16[4,112,128]{2,1,0:T(8,128)(2,1)S(1)}, u32[]{:S(2)}, u32[]{:S(2)}) collective-permute-start(bf16[4,112,128]{2,1,0:T(8,128)(2,1)S(1)} %get-tuple-element.218), channel_id=1, source_target_pairs={{0,2},{1,3},{2,0},{3,1},{4,6},{5,7},{6,4},{7,5},{8,10},{9,11},{10,... | collective-permute-start | bytes 344072 | tf_op jit(solution)/shard_map/ppermute | solution.py:481
  63.1 5.8 %collective-permute-start.19 = (bf16[4,112,128]{2,1,0:T(8,128)(2,1)S(1)}, bf16[4,112,128]{2,1,0:T(8,128)(2,1)S(1)}, u32[]{:S(2)}, u32[]{:S(2)}) collective-permute-start(bf16[4,112,128]{2,1,0:T(8,128)(2,1)S(1)} %get-tuple-element.219), channel_id=1, source_target_pairs={{0,18},{1,19},{2,16},{3,17},{4,22},{5,23},{6,20},{7,21},{8,26},{9,... | collective-permute-start | bytes 344072 | tf_op jit(solution)/shard_map/ppermute | solution.py:481
  69.1 24.3 %collective-permute-start.26 = (bf16[768,384]{1,0:T(8,128)(2,1)S(1)}, bf16[768,384]{1,0:T(8,128)(2,1)S(1)}, u32[]{:S(2)}, u32[]{:S(2)}) collective-permute-start(bf16[768,384]{1,0:T(8,128)(2,1)S(1)} %get-tuple-element.229.own_ref), channel_id=1, source_target_pairs={{0,16},{16,0},{1,17},{17,1},{2,18},{18,2},{3,19},{19,3},{4,20},{20... | collective-permute-start | bytes 1769480 | tf_op jit(solution)/shard_map/ppermute | solution.py:761
  70.8 6.0 %collective-permute-start.20 = (bf16[1,448,128]{2,1,0:T(8,128)(2,1)S(1)}, bf16[1,448,128]{2,1,0:T(8,128)(2,1)S(1)}, u32[]{:S(2)}, u32[]{:S(2)}) collective-permute-start(bf16[1,448,128]{2,1,0:T(8,128)(2,1)S(1)} %get-tuple-element.226), channel_id=1, source_target_pairs={{0,4},{1,5},{2,6},{3,7},{4,0},{5,1},{6,2},{7,3},{8,12},{9,13},{10,... | collective-permute-start | bytes 344072 | tf_op jit(solution)/shard_map/ppermute | solution.py:473
  72.4 7.4 %collective-permute-start.21 = (bf16[1,448,128]{2,1,0:T(8,128)(2,1)S(1)}, bf16[1,448,128]{2,1,0:T(8,128)(2,1)S(1)}, u32[]{:S(2)}, u32[]{:S(2)}) collective-permute-start(bf16[1,448,128]{2,1,0:T(8,128)(2,1)S(1)} %get-tuple-element.227), channel_id=1, source_target_pairs={{0,8},{1,9},{2,10},{3,11},{4,12},{5,13},{6,14},{7,15},{8,0},{9,1},... | collective-permute-start | bytes 344072 | tf_op jit(solution)/shard_map/ppermute | solution.py:473
  75.0 6.8 %collective-permute-start.22 = (bf16[1,448,128]{2,1,0:T(8,128)(2,1)S(1)}, bf16[1,448,128]{2,1,0:T(8,128)(2,1)S(1)}, u32[]{:S(2)}, u32[]{:S(2)}) collective-permute-start(bf16[1,448,128]{2,1,0:T(8,128)(2,1)S(1)} %get-tuple-element.228), channel_id=1, source_target_pairs={{0,12},{1,13},{2,14},{3,15},{4,8},{5,9},{6,10},{7,11},{8,4},{9,5},... | collective-permute-start | bytes 344072 | tf_op jit(solution)/shard_map/ppermute | solution.py:473
  81.9 10.1 %collective-permute-start.25 = (bf16[1,448,128]{2,1,0:T(8,128)(2,1)S(1)}, bf16[1,448,128]{2,1,0:T(8,128)(2,1)S(1)}, u32[]{:S(2)}, u32[]{:S(2)}) collective-permute-start(bf16[1,448,128]{2,1,0:T(8,128)(2,1)S(1)} %shard_map.310.refs_0_), channel_id=1, source_target_pairs={{0,12},{1,13},{2,14},{3,15},{4,8},{5,9},{6,10},{7,11},{8,4},{9,5},... | collective-permute-start | bytes 344072 | tf_op jit(solution)/shard_map/ppermute | solution.py:473
  86.5 5.7 %collective-permute-start.24 = (bf16[1,448,128]{2,1,0:T(8,128)(2,1)S(1)}, bf16[1,448,128]{2,1,0:T(8,128)(2,1)S(1)}, u32[]{:S(2)}, u32[]{:S(2)}) collective-permute-start(bf16[1,448,128]{2,1,0:T(8,128)(2,1)S(1)} %shard_map.310.refs_0_), channel_id=1, source_target_pairs={{0,8},{1,9},{2,10},{3,11},{4,12},{5,13},{6,14},{7,15},{8,0},{9,1},... | collective-permute-start | bytes 344072 | tf_op jit(solution)/shard_map/ppermute | solution.py:473
  88.1 5.3 %collective-permute-start.23 = (bf16[1,448,128]{2,1,0:T(8,128)(2,1)S(1)}, bf16[1,448,128]{2,1,0:T(8,128)(2,1)S(1)}, u32[]{:S(2)}, u32[]{:S(2)}) collective-permute-start(bf16[1,448,128]{2,1,0:T(8,128)(2,1)S(1)} %shard_map.310.refs_0_), channel_id=1, source_target_pairs={{0,4},{1,5},{2,6},{3,7},{4,0},{5,1},{6,2},{7,3},{8,12},{9,13},{10,... | collective-permute-start | bytes 344072 | tf_op jit(solution)/shard_map/ppermute | solution.py:473
  93.4 13.9 %collective-permute-start.29 = (bf16[4,448,128]{2,1,0:T(8,128)(2,1)S(1)}, bf16[4,448,128]{2,1,0:T(8,128)(2,1)S(1)}, u32[]{:S(2)}, u32[]{:S(2)}) collective-permute-start(bf16[4,448,128]{2,1,0:T(8,128)(2,1)S(1)} %shard_map.311), channel_id=1, source_target_pairs={{0,18},{1,19},{2,16},{3,17},{4,22},{5,23},{6,20},{7,21},{8,26},{9,... | collective-permute-start | bytes 1376264 | tf_op jit(solution)/shard_map/ppermute | solution.py:481
  94.9 17.2 %collective-permute-start.28 = (bf16[4,448,128]{2,1,0:T(8,128)(2,1)S(1)}, bf16[4,448,128]{2,1,0:T(8,128)(2,1)S(1)}, u32[]{:S(2)}, u32[]{:S(2)}) collective-permute-start(bf16[4,448,128]{2,1,0:T(8,128)(2,1)S(1)} %shard_map.311), channel_id=1, source_target_pairs={{0,2},{1,3},{2,0},{3,1},{4,6},{5,7},{6,4},{7,5},{8,10},{9,11},{10,... | collective-permute-start | bytes 1376264 | tf_op jit(solution)/shard_map/ppermute | solution.py:481
  95.4 17.3 %collective-permute-start.27 = (bf16[4,448,128]{2,1,0:T(8,128)(2,1)S(1)}, bf16[4,448,128]{2,1,0:T(8,128)(2,1)S(1)}, u32[]{:S(2)}, u32[]{:S(2)}) collective-permute-start(bf16[4,448,128]{2,1,0:T(8,128)(2,1)S(1)} %shard_map.311), channel_id=1, source_target_pairs={{0,16},{1,17},{2,18},{3,19},{4,20},{5,21},{6,22},{7,23},{8,24},{9,... | collective-permute-start | bytes 1376264 | tf_op jit(solution)/shard_map/ppermute | solution.py:481
  (28 other events, 148.2 us)

commit v7 on v6

--- a/solution.py
+++ b/solution.py
@@ -264,9 +264,12 @@
         rows = pieces[eighth * each : (eighth + 1) * each]
         rows = rows + [jnp.zeros((16 - len(rows), LANES), F32)]
         stage_ref[eighth, base : base + 16, :] = jnp.concatenate(rows, axis=0).astype(BF)
-        rest = stage_ref.shape[1] - base - 16
-        if rest:
-            stage_ref[eighth, base + 16 :, :] = jnp.zeros((rest, LANES), BF)
+    clear_rest(stage_ref, base + 16)
+
+
+def clear_rest(stage_ref, base):
+    if base < stage_ref.shape[1]:
+        stage_ref[:, base:, :] = jnp.zeros((8, stage_ref.shape[1] - base, LANES), BF)
 
 
 def forward_kernel(
@@ -303,13 +306,13 @@
     return scale * (inner - mean - hat * along)
 
 
-def backward_kernel(
-    place_ref, groups_ref, everyone_ref, cot_own, cot_got, middle_ref, normed_ref, active_ref, slope_ref, att_a, att_b,
-    small_ref, w_proj_ref, w_up_ref, w_down_ref,
-    grad_middle_ref, grad_att_ref, keep_ref, *send_refs
+def hidden_back_kernel(
+    place_ref, groups_ref, everyone_ref, cot_own, cot_got, normed_ref, active_ref, slope_ref, w_down_ref,
+    upstream_ref, grad_hidden_ref, sums_ref, keep_ref, *send_refs
 ):
     *send_refs, stage_ref = send_refs
-    rows_a, total = att_a.shape[0], cot_own.shape[0]
+    total = cot_own.shape[0]
+    rows_a = total - cot_got.shape[0] // 3 - EXTRA
     everyone = everyone_ref[...]
 
     def weight_of(group):
@@ -320,35 +323,41 @@
     )
     got = jnp.concatenate([cot_got[...].astype(F32), jnp.zeros((EXTRA, cot_got.shape[1]), F32)], axis=0)
     upstream = (cot_own[...].astype(F32) + got) * weight
+    upstream_ref[...] = upstream
     grad_result = upstream.astype(BF)
     normed = normed_ref[...]
     hidden, step = active_ref.shape[1], 512
-    grad_normed = None
-    sums = []
     slab = hidden // 8 * (grad_result.shape[1] // LANES)
     for first in range(0, hidden, step):
         cols = slice(first, first + step)
         grad_hidden = (dot_last(grad_result, w_down_ref[cols, :]) * slope_ref[:, cols].astype(F32)).astype(BF)
+        grad_hidden_ref[:, cols] = grad_hidden
         stage_rows(stage_ref, 0, dot_rows(active_ref[:, cols], grad_result), hidden, first)
-        part = dot_last(grad_hidden, w_up_ref[:, cols])
-        grad_normed = part if grad_normed is None else grad_normed + part
-        sums.append(column_sums(grad_hidden.astype(F32)))
+        sums_ref[:, cols] = column_sums(grad_hidden.astype(F32))
         stage_columns(stage_ref, slab, dot_rows(normed, grad_hidden), hidden, first)
+    clear_rest(stage_ref, 2 * slab)
+    scatter_chunks(place_ref, stage_ref, keep_ref, send_refs)
+
+
+def middle_back_kernel(
+    place_ref, upstream_ref, grad_hidden_ref, middle_ref, att_a, att_b, small_ref, w_proj_ref, w_up_ref,
+    grad_middle_ref, grad_att_ref, sums_ref, keep_ref, send_a, send_b, stage_ref
+):
+    grad_normed = dot_last(grad_hidden_ref[...], w_up_ref[...])
     hat, scale = normalise(middle_ref[...])
+    upstream = upstream_ref[...]
     grad_middle = upstream + norm_back(grad_normed, hat, scale, small_ref[6:7, :])
     grad_middle_ref[...] = grad_middle
     grad_branch = grad_middle.astype(BF)
     grad_att_ref[...] = dot_last(grad_branch, w_proj_ref[...]).astype(BF)
     width = grad_branch.shape[1]
-    stage_rows(stage_ref, 2 * slab, dot_rows(stacked((att_a, att_b)), grad_branch), width)
-    vectors = sums + [
-        column_sums(grad_normed * hat),
-        column_sums(grad_normed),
-        column_sums(grad_branch.astype(F32)),
-        column_sums(grad_result.astype(F32)),
-    ]
-    stage_vectors(stage_ref, 2 * slab + width // 8 * (width // LANES), vectors)
-    scatter_chunks(place_ref, stage_ref, keep_ref, send_refs)
+    stage_rows(stage_ref, 0, dot_rows(stacked((att_a, att_b)), grad_branch), width)
+    clear_rest(stage_ref, width // 8 * (width // LANES))
+    scatter_chunks(place_ref, stage_ref, keep_ref, (send_a, send_b))
+    sums_ref[0:1, :] = column_sums(grad_normed * hat)
+    sums_ref[1:2, :] = column_sums(grad_normed)
+    sums_ref[2:3, :] = column_sums(grad_branch.astype(F32))
+    sums_ref[3:4, :] = column_sums(upstream.astype(BF).astype(F32))
 
 
 def attention_back_kernel(row_from, g_ref, att_ref, q_ref, k_ref, v_ref, e_ref, inverse_ref, dq_ref, dk_ref, dv_ref):
@@ -376,6 +385,7 @@
 
 def inputs_back_kernel(
     unmasked, place_ref, x_a, x_b, dq_a, dq_b, dk_a, dk_b, dv_a, dv_b, grad_middle_ref, small_ref, w_ref,
+    up_sums_ref, middle_sums_ref,
     grad_ref, keep_ref, *send_refs
 ):
     *send_refs, stage_ref = send_refs
@@ -401,14 +411,17 @@
     grad = grad + jnp.concatenate([grad_middle_ref[:rows], spread(grad_middle_ref[rows:])], axis=0)
     grad_ref[:unmasked] = grad[:unmasked].astype(BF)
     grad_ref[unmasked:] = grad[rows : rows + unmasked].astype(BF)
+    slab = width // 8 * (mixed.shape[1] // LANES)
     vectors = (
+        up_sums_ref[...],
+        *(middle_sums_ref[row : row + 1, :] for row in range(4)),
         column_sums(mixed[:, :width].astype(F32)),
         column_sums(mixed[:, 2 * width :].astype(F32)),
         column_sums(grad_normed * hat),
         column_sums(grad_normed),
         grad[unmasked : unmasked + 1] + grad[rows + unmasked : rows + unmasked + 1],
     )
-    stage_vectors(stage_ref, width // 8 * (mixed.shape[1] // LANES), vectors)
+    stage_vectors(stage_ref, slab, vectors)
     scatter_chunks(place_ref, stage_ref, keep_ref, send_refs)
 
 
@@ -442,12 +455,17 @@
     out_ref[2] = dot(place_back(rank_ref, 2, unmasked, half), whole).astype(BF)
 
 
-def fold_kernel(keep_ref, *refs):
-    got_refs, out_refs = refs[:-4], refs[-4:]
-    each = got_refs[0].shape[0]
-    for step, out_ref in enumerate(out_refs):
-        got = got_refs[step // each][step % each]
-        out_ref[...] = (keep_ref[step].astype(F32) + got.astype(F32)).astype(BF)
+def fold_kernel(parts, *refs):
+    out_refs = refs[-4:]
+    first = 0
+    for count in parts:
+        keep_ref, got_refs, refs = refs[0], refs[1 : 1 + count], refs[1 + count :]
+        each = 4 // count
+        rows = slice(first, first + keep_ref.shape[2])
+        first = rows.stop
+        for step, out_ref in enumerate(out_refs):
+            got = got_refs[step // each][step % each]
+            out_ref[:, rows] = (keep_ref[step].astype(F32) + got.astype(F32)).astype(BF)
 
 
 def fold_four_kernel(units, *refs):
@@ -481,10 +499,16 @@
     return lax.ppermute(values, ("tm", "clip"), pairs)
 
 
-def sum_cores(keep, send, after):
-    _, groups, depth, _ = keep.shape
-    got, after = lax.optimization_barrier(([clip_swap(part, 1) for part in send], after))
-    return plain(fold_kernel, [shape(groups, depth, LANES)] * 4)(keep, *got)
+def swap_cores(send):
+    return [clip_swap(part, 1) for part in send]
+
+
+def fold_cores(units):
+    _, groups, _, _ = units[0][0].shape
+    depth = sum(keep.shape[2] for keep, _ in units)
+    kernel = functools.partial(fold_kernel, [len(got) for _, got in units])
+    refs = [part for keep, got in units for part in (keep, *got)]
+    return plain(kernel, [shape(groups, depth, LANES)] * 4)(*refs)
 
 
 def spread_near(pieces):
@@ -532,14 +556,15 @@
             refs[4][4 * slot + step] = refs[step][slot]
 
 
-def finish_kernel(jobs, first_call, depths, counts, place_ref, *refs):
+def finish_kernel(jobs, first_call, depths, vectors, place_ref, *refs):
     parts = len(jobs) if not first_call else 2 * len(jobs)
     sources, refs = refs[:parts], refs[parts:]
     if not first_call:
         earlier_ref, refs = refs[4], refs[5:]
     outs, refs = refs[:4], refs[4:]
-    vectors, refs = refs[: sum(counts)], refs[sum(counts) :]
-    kept_ref, stage_a, stage_b, done, *wides = refs
+    vectors, refs = refs[:vectors], refs[vectors:]
+    kept_ref, *stage_refs = refs[: 1 + len(depths)]
+    done, *wides = refs[1 + len(depths) :]
     kept_ref[...] = jnp.zeros(kept_ref.shape, F32) if first_call else earlier_ref[...]
     stores = []
     each = parts // len(jobs)
@@ -549,15 +574,16 @@
             start = 0
             for source in sources[job * each : (job + 1) * each]:
                 stop = start + source.shape[1]
-                for stage_ref, low, depth in ((stage_a, 0, depths[0]), (stage_b, depths[0], depths[1])):
+                for unit, (stage_ref, depth) in enumerate(zip(stage_refs, depths)):
+                    low = sum(depths[:unit])
                     top, end = max(start, low), min(stop, low + depth)
                     if top < end:
                         first = pl.multiple_of((far ^ (place_ref[1] >> 3)) * depth + (top - low), 16)
                         stage_ref[pl.ds(first, end - top), :] = source[far, top - start : end - start]
                 start = stop
-        for unit, stage_ref in enumerate((stage_a, stage_b)):
+        for unit, stage_ref in enumerate(stage_refs):
             first = 0
-            for at in ((0, 1, 2), (3,))[unit]:
+            for at in ((0, 1), (3,), (2,))[unit]:
                 wide_ref = wides[at].at[job]
                 depth, width = wide_ref.shape
                 for block in range(width // LANES):
@@ -570,15 +596,13 @@
                     target = outs[at].at[pl.ds(pl.multiple_of(eighth * depth, 16), depth), :]
                 stores.append(pltpu.make_async_copy(wide_ref, target, done.at[len(stores)]))
                 stores[-1].start()
-            kept_ref[eighth, 16 * unit : 16 * unit + 16] = stage_ref[first : first + 16, :].astype(F32)
-    at = 0
-    for unit, count in enumerate(counts):
-        blocks = [(ref, block) for ref in vectors[at : at + count] for block in range(ref.shape[0] // LANES)]
-        at += count
-        each = -(-len(blocks) // 8)
-        for number, (ref, block) in enumerate(blocks):
-            eighth, row = divmod(number, each)
-            ref[block * LANES : (block + 1) * LANES] = kept_ref[eighth, 16 * unit + row]
+            if unit == 1:
+                kept_ref[eighth] = stage_ref[first : first + 16, :].astype(F32)
+    blocks = [(ref, block) for ref in vectors for block in range(ref.shape[0] // LANES)]
+    each = -(-len(blocks) // 8)
+    for number, (ref, block) in enumerate(blocks):
+        eighth, row = divmod(number, each)
+        ref[block * LANES : (block + 1) * LANES] = kept_ref[eighth, row]
     for store in stores:
         store.wait()
 
@@ -640,7 +664,7 @@
         )(*args)
 
     blocks = width // LANES
-    counts = ((2 * hidden + width) // 8 * blocks + 16, 3 * width // 8 * blocks + 16)
+    counts = (2 * hidden // 8 * blocks, 3 * width // 8 * blocks + 16, width // 8 * blocks)
     depths = [chunk_rows(count, devices // 8) for count in counts]
 
     def chunked(unit, parts):
@@ -707,6 +731,7 @@
         distance *= 2
     x_b, q_b, k_b, v_b, e_b, inverse_b, att_b, x_whole = attend((shared,), got_shared, True)
 
+    everyone, att_b = lax.optimization_barrier((everyone, att_b))
     out_rows, middle, normed_two, active, slope = run(
         forward_kernel,
         (att_a, att_b, x_a, x_b, small, bias_up, w_proj, w_up, w_down),
@@ -719,17 +744,25 @@
     )
     out_got = swap(out_rows)
     halves, stage = chunked(0, 4)
-    grad_middle, grad_att, keep, *send = run(
-        backward_kernel,
-        (
-            place, groups, everyone.reshape(1, -1), cot_own, cot_got, middle, normed_two, active, slope, att_a, att_b,
-            small, w_proj, w_up, w_down,
-        ),
-        [shape(total, width, kind=F32), shape(total, width)] + halves,
+    upstream, grad_hidden, up_sums, keep, *send = run(
+        hidden_back_kernel,
+        (place, groups, everyone.reshape(1, -1), cot_own, cot_got, normed_two, active, slope, w_down),
+        [shape(total, width, kind=F32), shape(total, hidden), shape(1, hidden, kind=F32)] + halves,
         stage,
         scalars=2,
         hides=False,
     )
+    halves, stage = chunked(2, 2)
+    grad_middle, grad_att, middle_sums, keep_proj, *send_proj = run(
+        middle_back_kernel,
+        (place, upstream, grad_hidden, middle, att_a, att_b, small, w_proj, w_up),
+        [shape(total, width, kind=F32), shape(total, width), shape(8, width, kind=F32)] + halves,
+        stage,
+        hides=False,
+    )
+    got, grad_att = lax.optimization_barrier((swap_cores(send), grad_att))
+    pieces, grad_att, send_proj = lax.optimization_barrier((fold_cores([(keep, got)]), grad_att, send_proj))
+    first_pieces = spread_near(pieces)
 
     def attend_back(row_from, grads, att, q, k, v, e, inverse):
         return run(
@@ -741,19 +774,19 @@
         )
 
     dq_b, dk_b, dv_b = attend_back(rows, grad_att, att_b, q_b, k_b, v_b, e_b, inverse_b)
-    pieces, grad_att = lax.optimization_barrier((sum_cores(keep, send, dq_b), grad_att))
-    first_pieces = spread_near(pieces)
+    dq_b, out_got = lax.optimization_barrier((dq_b, out_got))
     dq_a, dk_a, dv_a = attend_back(0, grad_att, att_a, q_a, k_a, v_a, e_a, inverse_a)
-    dq_a, out_got = lax.optimization_barrier((dq_a, out_got))
+    dq_a, got_proj = lax.optimization_barrier((dq_a, swap_cores(send_proj)))
     halves, stage = chunked(1, 2)
     grad_rows, keep, *send = run(
         functools.partial(inputs_back_kernel, unmasked),
-        (place, x_a, x_whole, dq_a, dq_b, dk_a, dk_b, dv_a, dv_b, grad_middle, small, w_qkv),
+        (place, x_a, x_whole, dq_a, dq_b, dk_a, dk_b, dv_a, dv_b, grad_middle, small, w_qkv, up_sums, middle_sums),
         [shape(2 * unmasked, width)] + halves,
         stage,
         hides=False,
     )
-    pieces, first_pieces = lax.optimization_barrier((sum_cores(keep, send, ()), first_pieces))
+    pieces = fold_cores([(keep, swap_cores(send)), (keep_proj, got_proj)])
+    pieces, first_pieces = lax.optimization_barrier((pieces, first_pieces))
     second_pieces = spread_near(pieces)
 
     def send_rows(pieces):
@@ -773,9 +806,9 @@
     def finish(jobs, sources, earlier):
         sources = [part for parts in sources for part in parts]
         last = bool(earlier) and jobs[0][1] == 1
-        kept = (8, 32, LANES)
+        kept = (8, 16, LANES)
         return run(
-            functools.partial(finish_kernel, jobs, not earlier, depths, (5, 5) if last else ()),
+            functools.partial(finish_kernel, jobs, not earlier, depths, len(vectors) if last else 0),
             (place, *sources, *earlier),
             [shape(*dims, kind=F32) for dims in weights] + (vectors if last else [shape(*kept, kind=F32)]),
             [pltpu.VMEM(kept, F32)] * last

time: 119 us -> 118 us (level)
  waiting for transfers between devices: 31.8 us -> 35.1 us
  starting transfers between devices: 38.6 us -> 35.4 us
  Pallas kernels: 46.5 us -> 45.1 us
    ppermute x21 -> x23, waiting for transfers between devices: 11.2 us -> 15.3 us  [clip_swap(): lax.ppermute(values, 'clip', [(i, i ^ distance) for i in range(size)])]
    pallas_call x15 -> x16, Pallas kernels: 45.8 us -> 44.1 us  [run(): pl.pallas_call(kernel, out_shape=outs, in_specs=[SMEM if at < scalars els...]
    ppermute x21 -> x23, starting transfers between devices: 20.1 us -> 18.5 us  [clip_swap(): lax.ppermute(values, 'clip', [(i, i ^ distance) for i in range(size)])]
    ppermute x9, waiting for transfers between devices: 19.6 us -> 18.2 us  [near_swap(): return lax.ppermute(values, ('tm', 'clip'), pairs)]
  transfers between devices with their start and end apart: 35 -> 37, of which waited for: 19 -> 17; matrix products, arithmetic and copies ran while one was open for 0% -> 0% of each run, Pallas kernels for 37% -> 36%
where the time goes in v7:
time: 118 us; the launch traced here: 117 us
  Pallas kernels  45.1 us (38%)
  starting transfers between devices  35.4 us (30%)
  waiting for transfers between devices  35.1 us (30%)
  between operations  1.35 us (1%)
    pallas_call x16, Pallas kernels, run(): pl.pallas_call(kernel, out_shape=outs, in_specs=[SMEM if at < scalars els...  44.1 us
    ppermute x23, starting transfers between devices, clip_swap(): lax.ppermute(values, 'clip', [(i, i ^ distance) for i in range(size)])  18.5 us
    ppermute x9, waiting for transfers between devices, near_swap(): return lax.ppermute(values, ('tm', 'clip'), pairs)  18.2 us
    ppermute x23, waiting for transfers between devices, clip_swap(): lax.ppermute(values, 'clip', [(i, i ^ distance) for i in range(size)])  15.3 us
    ppermute x9, starting transfers between devices, near_swap(): return lax.ppermute(values, ('tm', 'clip'), pairs)  10.5 us
    ppermute x1, starting transfers between devices, body(): got_mine = swap(theirs)  2.57 us
  transfers between devices with their start and end apart: 37, of which 17 were waited for; matrix products, arithmetic and copies ran while one was open for 0% of the time, Pallas kernels for 36%

profile of v7, /device:TPU:0, one launch (start us, length us, event | category | flops | bytes accessed | tf_op | source)
XLA Modules:
  0.0 117.5 jit_solution(18066108469972278267)
XLA Ops:
  1.4 2.5 %shard_map.297 = (bf16[384,384]{1,0:T(8,128)(2,1)S(1)}, f32[48,128]{1,0:T(8,128)S(1)}) custom-call(s32[2]{0:T(128)S(1)} %pad_add_fusion.place_ref, s32[3,1152]{1,0:T(4,128)} %masked_ref.1, bf16[3,768,384]{2,1,0:T(8,128)(2,1)} %refs_1_.1), custom_call_target="tpu_custom_call" | custom-call | flops 235929600 | bytes 2102792 | tf_op jit(solution)/shard_map/pallas_call | solution.py:650
  3.9 2.6 %collective-permute-start.2 = (bf16[384,384]{1,0:T(8,128)(2,1)S(1)}, bf16[384,384]{1,0:T(8,128)(2,1)S(1)}, u32[]{:S(2)}, u32[]{:S(2)}) collective-permute-start(bf16[384,384]{1,0:T(8,128)(2,1)S(1)} %get-tuple-element.155), channel_id=1, source_target_pairs={{0,16},{16,0},{1,17},{17,1},{2,18},{18,2},{3,19},{19,3},{4,20},{20... | collective-permute-start | bytes 884744 | tf_op jit(solution)/shard_map/ppermute | solution.py:689
  14.7 3.6 %shard_map.299 = (bf16[400,384]{1,0:T(8,128)(2,1)S(1)}, bf16[400,384]{1,0:T(8,128)(2,1)S(1)}, bf16[400,384]{1,0:T(8,128)(2,1)S(1)}, bf16[400,384]{1,0:T(8,128)(2...) custom-call(s32[2]{0:T(128)S(1)} %pad_add_fusion.place_ref, ...), custom_call_target="tpu_custom_call" | custom-call | flops 599654400 | bytes 7057928 | tf_op jit(solution)/shard_map/pallas_call | solution.py:650
  18.3 2.7 %collective-permute-start.5 = (s32[24]{0:T(128)S(1)}, s32[24]{0:T(128)S(1)}, u32[]{:S(2)}, u32[]{:S(2)}) collective-permute-start(s32[24]{0:T(128)S(1)} %pad_add_fusion.3), channel_id=1, source_target_pairs={{0,8},{1,9},{2,10},{3,11},{4,12},{5,13},{6,14},{7,15},{8,0},{9,1},... | collective-permute-start | bytes 296 | tf_op jit(solution)/shard_map/ppermute | solution.py:491
  21.0 2.4 %shard_map.300 = (bf16[208,384]{1,0:T(8,128)(2,1)S(1)}, bf16[208,384]{1,0:T(8,128)(2,1)S(1)}, bf16[400,384]{1,0:T(8,128)(2,1)S(1)}, bf16[400,384]{1,0:T(8,128)(2...) custom-call(s32[2]{0:T(128)S(1)} %pad_add_fusion.place_ref, ...), custom_call_target="tpu_custom_call" | custom-call | flops 481689600 | bytes 4207112 | tf_op jit(solution)/shard_map/pallas_call | solution.py:650
  23.6 3.7 %shard_map.302 = (bf16[608,384]{1,0:T(8,128)(2,1)S(1)}, f32[608,384]{1,0:T(8,128)S(1)}, bf16[608,384]{1,0:T(8,128)(2,1)S(1)}, bf16[608,1536]{1,0:T(8,128)(2,1)S(1)}, bf16[608,1536]{1,0:T(8,128)(2,1)S(1)}) custom-call(bf16[400,384]{1,0:T(8,128)(2,1)S(1)} %get-tuple-element.173.att_a.att_ref, bf16[208,384]{1,0:T(8,128)(2,1)S(1)} %get-tuple-element.174.att_b.att_ref, ...), custom_call_target="tpu_custom_call" | custom-call | flops 1613758464 | bytes 9211392 | tf_op jit(solution)/shard_map/pallas_call | solution.py:650
  30.4 4.3 %shard_map.303 = (f32[608,384]{1,0:T(8,128)S(1)}, bf16[608,1536]{1,0:T(8,128)(2,1)S(1)}, f32[1,1536]{1,0:T(1,128)S(1)}, bf16[4,4,288,128]{3,2,1,0:T(8,128)(2,1)S...) custom-call(s32[2]{0:T(128)S(1)} %pad_add_fusion.place_ref, ...), custom_call_target="tpu_custom_call" | custom-call | flops 1 | bytes 1 | tf_op jit(solution)/shard_map/pallas_call | solution.py:650
  35.8 2.7 %shard_map.304 = (f32[608,384]{1,0:T(8,128)S(1)}, bf16[608,384]{1,0:T(8,128)(2,1)S(1)}, f32[8,384]{1,0:T(8,128)S(1)}, bf16[4,4,48,128]{3,2,1,0:T(8,128)(2,1)S(1)...) custom-call(s32[2]{0:T(128)S(1)} %pad_add_fusion.place_ref, ...), custom_call_target="tpu_custom_call" | custom-call | flops 1 | bytes 1 | tf_op jit(solution)/shard_map/pallas_call | solution.py:650
  39.4 1.9 %collective-permute-start.16 = (bf16[4,288,128]{2,1,0:T(8,128)(2,1)S(1)}, bf16[4,288,128]{2,1,0:T(8,128)(2,1)S(1)}, u32[]{:S(2)}, u32[]{:S(2)}) collective-permute-start(bf16[4,288,128]{2,1,0:T(8,128)(2,1)S(1)} %get-tuple-element.235), channel_id=1, source_target_pairs={{0,16},{1,17},{2,18},{3,19},{4,20},{5,21},{6,22},{7,23},{8,24},{9,... | collective-permute-start | bytes 884744 | tf_op jit(solution)/shard_map/ppermute | solution.py:499
  42.9 3.2 %shard_map.306 = (bf16[400,384]{1,0:T(8,128)(2,1)S(1)}, bf16[400,384]{1,0:T(8,128)(2,1)S(1)}, bf16[400,384]{1,0:T(8,128)(2,1)S(1)}) custom-call(bf16[608,384]{1,0:T(8,128)(2,1)S(1)} %get-tuple-element.199.g_ref, bf16[400,384]{1,0:T(8,128)(2,1)S(1)} %get-tuple-element.173.att_a.att_ref, bf16[400,384]{1,0:T(8,128)(2,1)S(1)} %get-tuple-element.200.q_ref, ...), custom_call_target="tpu_custom_call" | custom-call | flops 1 | bytes 1 | tf_op jit(solution)/shard_map/pallas_call | solution.py:650
  46.1 2.3 %shard_map.307 = (bf16[208,384]{1,0:T(8,128)(2,1)S(1)}, bf16[400,384]{1,0:T(8,128)(2,1)S(1)}, bf16[400,384]{1,0:T(8,128)(2,1)S(1)}) custom-call(bf16[608,384]{1,0:T(8,128)(2,1)S(1)} %get-tuple-element.199.g_ref, bf16[208,384]{1,0:T(8,128)(2,1)S(1)} %get-tuple-element.174.att_b.att_ref, bf16[208,384]{1,0:T(8,128)(2,1)S(1)} %get-tuple-element.209.q_ref, ...), custom_call_target="tpu_custom_call" | custom-call | flops 1 | bytes 1 | tf_op jit(solution)/shard_map/pallas_call | solution.py:650
  48.5 3.8 %shard_map.308 = (bf16[768,384]{1,0:T(8,128)(2,1)S(1)}, bf16[4,4,112,128]{3,2,1,0:T(8,128)(2,1)S(1)}, bf16[2,4,112,128]{3,2,1,0:T(8,128)(2,1)S(1)}, bf16[2,4,112,128]{3,2,1,0:T(8,128)(2,1)S(1)}) custom-call(s32[2]{0:T(128)S(1)} %pad_add_fusion.place_ref, bf16[400,384]{1,0:T(8,128)(2,1)S(1)} %get-tuple-element.160.x_a, ...), custom_call_target="tpu_custom_call" | custom-call | flops 1 | bytes 1 | tf_op jit(solution)/shard_map/pallas_call | solution.py:650
  59.9 3.3 %collective-permute-done.19.refs_5_ = bf16[4,160,128]{2,1,0:T(8,128)(2,1)S(1)} collective-permute-done((bf16[4,160,128]{2,1,0:T(8,128)(2,1)S(1)}, bf16[4,160,128]{2,1,0:T(8,128)(2,1)S(1)}, u32[]{:S(2)}, u32[]{:S(2)}) %collective-permute-start.19) | collective-permute-done | bytes 163872 | tf_op jit(solution)/shard_map/ppermute | solution.py:499
  63.2 3.3 %collective-permute-done.20.refs_6_ = bf16[4,160,128]{2,1,0:T(8,128)(2,1)S(1)} collective-permute-done((bf16[4,160,128]{2,1,0:T(8,128)(2,1)S(1)}, bf16[4,160,128]{2,1,0:T(8,128)(2,1)S(1)}, u32[]{:S(2)}, u32[]{:S(2)}) %collective-permute-start.20) | collective-permute-done | bytes 163872 | tf_op jit(solution)/shard_map/ppermute | solution.py:499
  69.2 2.6 %collective-permute-start.23 = (bf16[1,448,128]{2,1,0:T(8,128)(2,1)S(1)}, bf16[1,448,128]{2,1,0:T(8,128)(2,1)S(1)}, u32[]{:S(2)}, u32[]{:S(2)}) collective-permute-start(bf16[1,448,128]{2,1,0:T(8,128)(2,1)S(1)} %get-tuple-element.253), channel_id=1, source_target_pairs={{0,8},{1,9},{2,10},{3,11},{4,12},{5,13},{6,14},{7,15},{8,0},{9,1},... | collective-permute-start | bytes 344072 | tf_op jit(solution)/shard_map/ppermute | solution.py:491
  73.4 6.2 %collective-permute-done.23.refs_2_ = bf16[1,448,128]{2,1,0:T(8,128)(2,1)S(1)} collective-permute-done((bf16[1,448,128]{2,1,0:T(8,128)(2,1)S(1)}, bf16[1,448,128]{2,1,0:T(8,128)(2,1)S(1)}, u32[]{:S(2)}, u32[]{:S(2)}) %collective-permute-start.23) | collective-permute-done | bytes 114720 | tf_op jit(solution)/shard_map/ppermute | solution.py:491
  79.7 2.6 %collective-permute-start.27 = (bf16[1,448,128]{2,1,0:T(8,128)(2,1)S(1)}, bf16[1,448,128]{2,1,0:T(8,128)(2,1)S(1)}, u32[]{:S(2)}, u32[]{:S(2)}) collective-permute-start(bf16[1,448,128]{2,1,0:T(8,128)(2,1)S(1)} %shard_map.311.refs_0_), channel_id=1, source_target_pairs={{0,12},{1,13},{2,14},{3,15},{4,8},{5,9},{6,10},{7,11},{8,4},{9,5},... | collective-permute-start | bytes 344072 | tf_op jit(solution)/shard_map/ppermute | solution.py:491
  84.1 3.4 %shard_map.313 = bf16[3,768,384]{2,1,0:T(8,128)(2,1)} custom-call(s32[2]{0:T(128)S(1)} %pad_add_fusion.place_ref, f32[48,128]{1,0:T(8,128)S(1)} %get-tuple-element.159.rank_ref.refs_0_, bf16[608,384]{1,0:T(8,128)(2,1)S(1)} %get-tuple-element.215.own_ref, bf16[608,384]{1,0:T(8,128)(2,1)S(1)} %collective-permute-done.13.got_ref), custom_call_target="tpu_custom_call" | custom-call | flops 1 | bytes 1 | tf_op jit(solution)/shard_map/pallas_call | solution.py:650
  87.6 3.4 %collective-permute-done.26.refs_2_ = bf16[1,448,128]{2,1,0:T(8,128)(2,1)S(1)} collective-permute-done((bf16[1,448,128]{2,1,0:T(8,128)(2,1)S(1)}, bf16[1,448,128]{2,1,0:T(8,128)(2,1)S(1)}, u32[]{:S(2)}, u32[]{:S(2)}) %collective-permute-start.26) | collective-permute-done | bytes 114720 | tf_op jit(solution)/shard_map/ppermute | solution.py:491
  94.6 3.3 %shard_map.314 = bf16[3,768,384]{2,1,0:T(8,128)(2,1)} custom-call(s32[2]{0:T(128)S(1)} %pad_add_fusion.place_ref, f32[48,128]{1,0:T(8,128)S(1)} %get-tuple-element.159.rank_ref.refs_0_, bf16[768,384]{1,0:T(8,128)(2,1)S(1)} %get-tuple-element.255.own_ref, bf16[768,384]{1,0:T(8,128)(2,1)S(1)} %collective-permute-done.28.got_ref), custom_call_target="tpu_custom_call" | custom-call | flops 1 | bytes 1 | tf_op jit(solution)/shard_map/pallas_call | solution.py:650
  101.6 3.8 %collective-permute-done.31.refs_2_ = bf16[4,448,128]{2,1,0:T(8,128)(2,1)S(1)} collective-permute-done((bf16[4,448,128]{2,1,0:T(8,128)(2,1)S(1)}, bf16[4,448,128]{2,1,0:T(8,128)(2,1)S(1)}, u32[]{:S(2)}, u32[]{:S(2)}) %collective-permute-start.31) | collective-permute-done | bytes 458784 | tf_op jit(solution)/shard_map/ppermute | solution.py:499
  105.4 5.9 %collective-permute-done.30.refs_1_ = bf16[4,448,128]{2,1,0:T(8,128)(2,1)S(1)} collective-permute-done((bf16[4,448,128]{2,1,0:T(8,128)(2,1)S(1)}, bf16[4,448,128]{2,1,0:T(8,128)(2,1)S(1)}, u32[]{:S(2)}, u32[]{:S(2)}) %collective-permute-start.30) | collective-permute-done | bytes 458784 | tf_op jit(solution)/shard_map/ppermute | solution.py:499
  111.9 2.2 %shard_map.316 = (f32[1536,384]{1,0:T(8,128)}, f32[384,1536]{1,0:T(8,128)}, f32[384,384]{1,0:T(8,128)}, f32[384,1152]{1,0:T(8,128)}, f32[8,16,128]{2,1,0:T(8,128)S(1)}) custom-call(s32[2]{0:T(128)S(1)} %pad_add_fusion.place_ref, ...), custom_call_target="tpu_custom_call", output_to_operand_aliasing={{0}: (4, {}), {1}: (5, {}), {2}: (6, {}), {3}: (7, {})} | custom-call | flops 1 | bytes 1 | tf_op jit(solution)/shard_map/pallas_call | solution.py:650
  114.5 2.8 %shard_map.317 = (f32[1536,384]{1,0:T(8,128)}, f32[384,1536]{1,0:T(8,128)}, f32[384,384]{1,0:T(8,128)}, f32[384,1152]{1,0:T(8,128)}, f32[1536]{0:T(1024)}, /*ind...) custom-call(s32[2]{0:T(128)S(1)} %pad_add_fusion.place_ref, ...), custom_call_target="tpu_custom_call", output_to_operand_aliasing={{0}: (4, {}), {1}: (5, {}), {2}: (6, {}), {3}: (7, {})} | custom-call | flops 1 | bytes 1 | tf_op jit(solution)/shard_map/pallas_call | solution.py:650
  (123 shorter events, 37.7 us)
Async XLA Ops:
  0.8 6.0 %collective-permute-start = (s32[3]{0:T(128)}, s32[3]{0:T(128)S(1)}, u32[]{:S(2)}, u32[]{:S(2)}) collective-permute-start(s32[3]{0:T(128)} %groups_ref.1), channel_id=1, source_target_pairs={{0,1},{1,0},{2,3},{3,2},{4,5},{5,4},{6,7},{7,6},{8,9},{9,8},{10,11... | collective-permute-start | bytes 44 | tf_op jit(solution)/shard_map/ppermute | solution.py:491
  3.9 10.8 %collective-permute-start.2 = (bf16[384,384]{1,0:T(8,128)(2,1)S(1)}, bf16[384,384]{1,0:T(8,128)(2,1)S(1)}, u32[]{:S(2)}, u32[]{:S(2)}) collective-permute-start(bf16[384,384]{1,0:T(8,128)(2,1)S(1)} %get-tuple-element.155), channel_id=1, source_target_pairs={{0,16},{16,0},{1,17},{17,1},{2,18},{18,2},{3,19},{19,3},{4,20},{20... | collective-permute-start | bytes 884744 | tf_op jit(solution)/shard_map/ppermute | solution.py:689
  8.9 12.1 %collective-permute-start.3 = (bf16[384,384]{1,0:T(8,128)(2,1)S(1)}, bf16[384,384]{1,0:T(8,128)(2,1)S(1)}, u32[]{:S(2)}, u32[]{:S(2)}) collective-permute-start(bf16[384,384]{1,0:T(8,128)(2,1)S(1)} %shard_map.298.refs_0_), channel_id=1, source_target_pairs={{0,16},{16,0},{1,17},{17,1},{2,18},{18,2},{3,19},{19,3},{4,20},{20... | collective-permute-start | bytes 884744 | tf_op jit(solution)/shard_map/ppermute | solution.py:699
  14.1 16.3 %collective-permute-start.6 = (bf16[592,384]{1,0:T(8,128)(2,1)S(1)}, bf16[592,384]{1,0:T(8,128)(2,1)S(1)}, u32[]{:S(2)}, u32[]{:S(2)}) collective-permute-start(bf16[592,384]{1,0:T(8,128)(2,1)S(1)} %get-tuple-element.172), channel_id=1, source_target_pairs={{0,16},{16,0},{1,17},{17,1},{2,18},{18,2},{3,19},{19,3},{4,20},{20... | collective-permute-start | bytes 1363976 | tf_op jit(solution)/shard_map/ppermute | solution.py:709
  18.3 5.2 %collective-permute-start.5 = (s32[24]{0:T(128)S(1)}, s32[24]{0:T(128)S(1)}, u32[]{:S(2)}, u32[]{:S(2)}) collective-permute-start(s32[24]{0:T(128)S(1)} %pad_add_fusion.3), channel_id=1, source_target_pairs={{0,8},{1,9},{2,10},{3,11},{4,12},{5,13},{6,14},{7,15},{8,0},{9,1},... | collective-permute-start | bytes 296 | tf_op jit(solution)/shard_map/ppermute | solution.py:491
  27.2 15.7 %collective-permute-start.13 = (bf16[608,384]{1,0:T(8,128)(2,1)S(1)}, bf16[608,384]{1,0:T(8,128)(2,1)S(1)}, u32[]{:S(2)}, u32[]{:S(2)}) collective-permute-start(bf16[608,384]{1,0:T(8,128)(2,1)S(1)} %get-tuple-element.215.own_ref), channel_id=1, source_target_pairs={{0,16},{16,0},{1,17},{17,1},{2,18},{18,2},{3,19},{19,3},{4,20},{20... | collective-permute-start | bytes 1400840 | tf_op jit(solution)/shard_map/ppermute | solution.py:745
  38.9 9.6 %collective-permute-start.11 = (bf16[2,4,48,128]{3,2,1,0:T(8,128)(2,1)S(1)}, bf16[2,4,48,128]{3,2,1,0:T(8,128)(2,1)S(1)}, u32[]{:S(2)}, u32[]{:S(2)}) collective-permute-start(bf16[2,4,48,128]{3,2,1,0:T(8,128)(2,1)S(1)} %get-tuple-element.206), channel_id=1, source_target_pairs={{0,1},{1,0},{2,3},{3,2},{4,5},{5,4},{6,7},{7,6},{8,9},{9,8},{10,11... | collective-permute-start | bytes 294920 | tf_op jit(solution)/shard_map/ppermute | solution.py:491
  39.0 9.5 %collective-permute-start.12 = (bf16[2,4,48,128]{3,2,1,0:T(8,128)(2,1)S(1)}, bf16[2,4,48,128]{3,2,1,0:T(8,128)(2,1)S(1)}, u32[]{:S(2)}, u32[]{:S(2)}) collective-permute-start(bf16[2,4,48,128]{3,2,1,0:T(8,128)(2,1)S(1)} %get-tuple-element.207), channel_id=1, source_target_pairs={{0,1},{1,0},{2,3},{3,2},{4,5},{5,4},{6,7},{7,6},{8,9},{9,8},{10,11... | collective-permute-start | bytes 294920 | tf_op jit(solution)/shard_map/ppermute | solution.py:491
  39.4 15.1 %collective-permute-start.16 = (bf16[4,288,128]{2,1,0:T(8,128)(2,1)S(1)}, bf16[4,288,128]{2,1,0:T(8,128)(2,1)S(1)}, u32[]{:S(2)}, u32[]{:S(2)}) collective-permute-start(bf16[4,288,128]{2,1,0:T(8,128)(2,1)S(1)} %get-tuple-element.235), channel_id=1, source_target_pairs={{0,16},{1,17},{2,18},{3,19},{4,20},{5,21},{6,22},{7,23},{8,24},{9,... | collective-permute-start | bytes 884744 | tf_op jit(solution)/shard_map/ppermute | solution.py:499
  41.4 15.0 %collective-permute-start.17 = (bf16[4,288,128]{2,1,0:T(8,128)(2,1)S(1)}, bf16[4,288,128]{2,1,0:T(8,128)(2,1)S(1)}, u32[]{:S(2)}, u32[]{:S(2)}) collective-permute-start(bf16[4,288,128]{2,1,0:T(8,128)(2,1)S(1)} %get-tuple-element.236), channel_id=1, source_target_pairs={{0,2},{1,3},{2,0},{3,1},{4,6},{5,7},{6,4},{7,5},{8,10},{9,11},{10,... | collective-permute-start | bytes 884744 | tf_op jit(solution)/shard_map/ppermute | solution.py:499
  42.9 13.5 %collective-permute-start.18 = (bf16[4,288,128]{2,1,0:T(8,128)(2,1)S(1)}, bf16[4,288,128]{2,1,0:T(8,128)(2,1)S(1)}, u32[]{:S(2)}, u32[]{:S(2)}) collective-permute-start(bf16[4,288,128]{2,1,0:T(8,128)(2,1)S(1)} %get-tuple-element.237), channel_id=1, source_target_pairs={{0,18},{1,19},{2,16},{3,17},{4,22},{5,23},{6,20},{7,21},{8,26},{9,... | collective-permute-start | bytes 884744 | tf_op jit(solution)/shard_map/ppermute | solution.py:499
  56.4 6.7 %collective-permute-start.19 = (bf16[4,160,128]{2,1,0:T(8,128)(2,1)S(1)}, bf16[4,160,128]{2,1,0:T(8,128)(2,1)S(1)}, u32[]{:S(2)}, u32[]{:S(2)}) collective-permute-start(bf16[4,160,128]{2,1,0:T(8,128)(2,1)S(1)} %get-tuple-element.243), channel_id=1, source_target_pairs={{0,16},{1,17},{2,18},{3,19},{4,20},{5,21},{6,22},{7,23},{8,24},{9,... | collective-permute-start | bytes 491528 | tf_op jit(solution)/shard_map/ppermute | solution.py:499
  57.6 8.8 %collective-permute-start.20 = (bf16[4,160,128]{2,1,0:T(8,128)(2,1)S(1)}, bf16[4,160,128]{2,1,0:T(8,128)(2,1)S(1)}, u32[]{:S(2)}, u32[]{:S(2)}) collective-permute-start(bf16[4,160,128]{2,1,0:T(8,128)(2,1)S(1)} %get-tuple-element.244), channel_id=1, source_target_pairs={{0,2},{1,3},{2,0},{3,1},{4,6},{5,7},{6,4},{7,5},{8,10},{9,11},{10,... | collective-permute-start | bytes 491528 | tf_op jit(solution)/shard_map/ppermute | solution.py:499
  58.5 8.0 %collective-permute-start.21 = (bf16[4,160,128]{2,1,0:T(8,128)(2,1)S(1)}, bf16[4,160,128]{2,1,0:T(8,128)(2,1)S(1)}, u32[]{:S(2)}, u32[]{:S(2)}) collective-permute-start(bf16[4,160,128]{2,1,0:T(8,128)(2,1)S(1)} %get-tuple-element.245), channel_id=1, source_target_pairs={{0,18},{1,19},{2,16},{3,17},{4,22},{5,23},{6,20},{7,21},{8,26},{9,... | collective-permute-start | bytes 491528 | tf_op jit(solution)/shard_map/ppermute | solution.py:499
  66.7 24.3 %collective-permute-start.28 = (bf16[768,384]{1,0:T(8,128)(2,1)S(1)}, bf16[768,384]{1,0:T(8,128)(2,1)S(1)}, u32[]{:S(2)}, u32[]{:S(2)}) collective-permute-start(bf16[768,384]{1,0:T(8,128)(2,1)S(1)} %get-tuple-element.255.own_ref), channel_id=1, source_target_pairs={{0,16},{16,0},{1,17},{17,1},{2,18},{18,2},{3,19},{19,3},{4,20},{20... | collective-permute-start | bytes 1769480 | tf_op jit(solution)/shard_map/ppermute | solution.py:794
  67.6 5.8 %collective-permute-start.22 = (bf16[1,448,128]{2,1,0:T(8,128)(2,1)S(1)}, bf16[1,448,128]{2,1,0:T(8,128)(2,1)S(1)}, u32[]{:S(2)}, u32[]{:S(2)}) collective-permute-start(bf16[1,448,128]{2,1,0:T(8,128)(2,1)S(1)} %get-tuple-element.252), channel_id=1, source_target_pairs={{0,4},{1,5},{2,6},{3,7},{4,0},{5,1},{6,2},{7,3},{8,12},{9,13},{10,... | collective-permute-start | bytes 344072 | tf_op jit(solution)/shard_map/ppermute | solution.py:491
  69.2 10.4 %collective-permute-start.23 = (bf16[1,448,128]{2,1,0:T(8,128)(2,1)S(1)}, bf16[1,448,128]{2,1,0:T(8,128)(2,1)S(1)}, u32[]{:S(2)}, u32[]{:S(2)}) collective-permute-start(bf16[1,448,128]{2,1,0:T(8,128)(2,1)S(1)} %get-tuple-element.253), channel_id=1, source_target_pairs={{0,8},{1,9},{2,10},{3,11},{4,12},{5,13},{6,14},{7,15},{8,0},{9,1},... | collective-permute-start | bytes 344072 | tf_op jit(solution)/shard_map/ppermute | solution.py:491
  71.8 7.8 %collective-permute-start.24 = (bf16[1,448,128]{2,1,0:T(8,128)(2,1)S(1)}, bf16[1,448,128]{2,1,0:T(8,128)(2,1)S(1)}, u32[]{:S(2)}, u32[]{:S(2)}) collective-permute-start(bf16[1,448,128]{2,1,0:T(8,128)(2,1)S(1)} %get-tuple-element.254), channel_id=1, source_target_pairs={{0,12},{1,13},{2,14},{3,15},{4,8},{5,9},{6,10},{7,11},{8,4},{9,5},... | collective-permute-start | bytes 344072 | tf_op jit(solution)/shard_map/ppermute | solution.py:491
  79.7 7.9 %collective-permute-start.27 = (bf16[1,448,128]{2,1,0:T(8,128)(2,1)S(1)}, bf16[1,448,128]{2,1,0:T(8,128)(2,1)S(1)}, u32[]{:S(2)}, u32[]{:S(2)}) collective-permute-start(bf16[1,448,128]{2,1,0:T(8,128)(2,1)S(1)} %shard_map.311.refs_0_), channel_id=1, source_target_pairs={{0,12},{1,13},{2,14},{3,15},{4,8},{5,9},{6,10},{7,11},{8,4},{9,5},... | collective-permute-start | bytes 344072 | tf_op jit(solution)/shard_map/ppermute | solution.py:491
  82.3 8.7 %collective-permute-start.26 = (bf16[1,448,128]{2,1,0:T(8,128)(2,1)S(1)}, bf16[1,448,128]{2,1,0:T(8,128)(2,1)S(1)}, u32[]{:S(2)}, u32[]{:S(2)}) collective-permute-start(bf16[1,448,128]{2,1,0:T(8,128)(2,1)S(1)} %shard_map.311.refs_0_), channel_id=1, source_target_pairs={{0,8},{1,9},{2,10},{3,11},{4,12},{5,13},{6,14},{7,15},{8,0},{9,1},... | collective-permute-start | bytes 344072 | tf_op jit(solution)/shard_map/ppermute | solution.py:491
  83.0 8.0 %collective-permute-start.25 = (bf16[1,448,128]{2,1,0:T(8,128)(2,1)S(1)}, bf16[1,448,128]{2,1,0:T(8,128)(2,1)S(1)}, u32[]{:S(2)}, u32[]{:S(2)}) collective-permute-start(bf16[1,448,128]{2,1,0:T(8,128)(2,1)S(1)} %shard_map.311.refs_0_), channel_id=1, source_target_pairs={{0,4},{1,5},{2,6},{3,7},{4,0},{5,1},{6,2},{7,3},{8,12},{9,13},{10,... | collective-permute-start | bytes 344072 | tf_op jit(solution)/shard_map/ppermute | solution.py:491
  91.0 14.4 %collective-permute-start.31 = (bf16[4,448,128]{2,1,0:T(8,128)(2,1)S(1)}, bf16[4,448,128]{2,1,0:T(8,128)(2,1)S(1)}, u32[]{:S(2)}, u32[]{:S(2)}) collective-permute-start(bf16[4,448,128]{2,1,0:T(8,128)(2,1)S(1)} %shard_map.312), channel_id=1, source_target_pairs={{0,18},{1,19},{2,16},{3,17},{4,22},{5,23},{6,20},{7,21},{8,26},{9,... | collective-permute-start | bytes 1376264 | tf_op jit(solution)/shard_map/ppermute | solution.py:499
  91.5 19.8 %collective-permute-start.30 = (bf16[4,448,128]{2,1,0:T(8,128)(2,1)S(1)}, bf16[4,448,128]{2,1,0:T(8,128)(2,1)S(1)}, u32[]{:S(2)}, u32[]{:S(2)}) collective-permute-start(bf16[4,448,128]{2,1,0:T(8,128)(2,1)S(1)} %shard_map.312), channel_id=1, source_target_pairs={{0,2},{1,3},{2,0},{3,1},{4,6},{5,7},{6,4},{7,5},{8,10},{9,11},{10,... | collective-permute-start | bytes 1376264 | tf_op jit(solution)/shard_map/ppermute | solution.py:499
  93.0 18.4 %collective-permute-start.29 = (bf16[4,448,128]{2,1,0:T(8,128)(2,1)S(1)}, bf16[4,448,128]{2,1,0:T(8,128)(2,1)S(1)}, u32[]{:S(2)}, u32[]{:S(2)}) collective-permute-start(bf16[4,448,128]{2,1,0:T(8,128)(2,1)S(1)} %shard_map.312), channel_id=1, source_target_pairs={{0,16},{1,17},{2,18},{3,19},{4,20},{5,21},{6,22},{7,23},{8,24},{9,... | collective-permute-start | bytes 1376264 | tf_op jit(solution)/shard_map/ppermute | solution.py:499
  (30 other events, 147.7 us)

commit v8 on v7

--- a/solution.py
+++ b/solution.py
@@ -54,12 +54,11 @@
     return pl.pallas_call(kernel, out_shape=outs, compiler_params=pltpu.CompilerParams(vmem_limit_bytes=8 << 20))
 
 
-def all_ranks(masked_ref, tm, half, unmasked):
-    copies, hide = masked_ref.shape
+def ranks(rows, tm, half, unmasked):
+    copies, hide = len(rows), rows[0].shape[1]
     blocks = half // LANES
     marks = []
-    for copy in range(copies):
-        row = masked_ref[copy : copy + 1, :]
+    for row in rows:
         low = ones_where(iota((LANES, hide), 0) == (row & (LANES - 1)))
         high = ones_where(iota((16, hide), 0) == (row >> 7))
         marks.append(dot_last(high, low))
@@ -86,8 +85,8 @@
     return jnp.concatenate([ones_where(wide == rank[b : b + 1, :]) for b in range(rank.shape[0])], axis=1)
 
 
-def ranks_of(rank_ref, copy, half):
-    return rank_ref[pl.ds(pl.multiple_of(16 * copy, 16), 16), :][: half // LANES]
+def ranks_of(rank_ref, at, half):
+    return rank_ref[16 * at : 16 * at + half // LANES, :]
 
 
 def prep_theirs_kernel(
@@ -100,18 +99,22 @@
     load = pltpu.make_async_copy(tokens_ref.at[1 - tm], half_ref, arrived.at[1])
     load.start()
     load_marks.wait()
-    rank_ref[...] = all_ranks(marks_ref, tm, half, unmasked)
-    chosen = picks(ranks_of(rank_ref, 1 - tm, half), iota((unmasked, 1), 0))
+    rank = ranks([marks_ref[pl.ds(1 - tm, 1), :]], tm, half, unmasked)
+    rank_ref[...] = rank
+    chosen = picks(rank[: half // LANES], iota((unmasked, 1), 0))
     load.wait()
     theirs_ref[...] = dot(chosen, half_ref[...]).astype(BF)
 
 
-def prep_shared_kernel(unmasked, rank_ref, tokens_ref, shared_ref):
-    chosen = picks(ranks_of(rank_ref, 2, tokens_ref.shape[1]), iota((unmasked, 1), 0))
-    shared_ref[...] = dot(chosen, tokens_ref[2]).astype(BF)
-
-
-def prep_grads_kernel(unmasked, place_ref, rank_ref, cotangent_ref, keep_ref, send_ref):
+def prep_shared_kernel(unmasked, place_ref, masked_ref, tokens_ref, shared_ref, rank_ref):
+    tm = place_ref[0]
+    half = tokens_ref.shape[1]
+    rank = ranks([masked_ref[2:3, :], masked_ref[pl.ds(tm, 1), :]], tm, half, unmasked)
+    rank_ref[...] = rank
+    shared_ref[...] = dot(picks(rank[: half // LANES], iota((unmasked, 1), 0)), tokens_ref[2]).astype(BF)
+
+
+def prep_grads_kernel(unmasked, place_ref, theirs_ref, rank_ref, cotangent_ref, keep_ref, send_ref):
     tm = place_ref[0]
     half = cotangent_ref.shape[1]
     rows = unmasked + EXTRA
@@ -120,12 +123,12 @@
     small = iota((part + EXTRA, 1), 0)
     theirs = iota((part, 1), 0) + part * (1 - tm)
     own = jnp.where(small < part, small + part * tm, small + part)
-    send_ref[:rows, :] = dot(picks(ranks_of(rank_ref, 1 - tm, half), labels), cotangent_ref[1 - tm]).astype(BF)
-    chosen = picks(ranks_of(rank_ref, 2, half), jnp.concatenate([theirs, own], axis=0))
+    send_ref[:rows, :] = dot(picks(ranks_of(theirs_ref, 0, half), labels), cotangent_ref[1 - tm]).astype(BF)
+    chosen = picks(ranks_of(rank_ref, 0, half), jnp.concatenate([theirs, own], axis=0))
     both = dot(chosen, cotangent_ref[2]).astype(BF)
     send_ref[rows:, :] = both[:part]
     keep_ref[rows:, :] = both[part:]
-    keep_ref[:rows, :] = dot(picks(ranks_of(rank_ref, tm, half), labels), cotangent_ref[tm]).astype(BF)
+    keep_ref[:rows, :] = dot(picks(ranks_of(rank_ref, 1, half), labels), cotangent_ref[tm]).astype(BF)
 
 
 def normalise(values):
@@ -149,7 +152,7 @@
         own = own_ref[...].astype(F32)
     else:
         rank_ref, tokens_ref, got_ref, small_ref, w_ref, x_ref, q_ref, k_ref, v_ref, e_ref, inverse_ref, att_ref = refs
-        chosen = picks(ranks_of(rank_ref, tm, tokens_ref.shape[1]), iota((unmasked, 1), 0))
+        chosen = picks(ranks_of(rank_ref, 1, tokens_ref.shape[1]), iota((unmasked, 1), 0))
         own = dot(chosen, tokens_ref[tm])
     rows, width = k_ref.shape
     extra = jnp.where(iota((EXTRA, width), 0) == 0, small_ref[0:1, :], 0.0)
@@ -425,34 +428,34 @@
     scatter_chunks(place_ref, stage_ref, keep_ref, send_refs)
 
 
-def place_back(rank_ref, copy, rows, half):
-    down = jnp.transpose(ranks_of(rank_ref, copy, 16 * LANES))
+def place_back(rank_ref, at, rows, half):
+    down = jnp.transpose(ranks_of(rank_ref, at, 16 * LANES))
     labels = jnp.broadcast_to(iota((1, rows), 1).astype(F32), (LANES, rows))
     return jnp.concatenate([ones_where(labels == down[:, b : b + 1]) for b in range(half // LANES)], axis=0)
 
 
-def outputs_kernel(unmasked, place_ref, rank_ref, own_ref, got_ref, out_ref):
+def outputs_kernel(unmasked, place_ref, theirs_ref, rank_ref, own_ref, got_ref, out_ref):
     tm = place_ref[0]
     half = out_ref.shape[1]
     rows = unmasked + EXTRA
     part = unmasked // 2
-    out_ref[tm] = dot(place_back(rank_ref, tm, rows, half), own_ref[:rows]).astype(BF)
-    out_ref[1 - tm] = dot(place_back(rank_ref, 1 - tm, rows, half), got_ref[:rows]).astype(BF)
+    out_ref[tm] = dot(place_back(rank_ref, 1, rows, half), own_ref[:rows]).astype(BF)
+    out_ref[1 - tm] = dot(place_back(theirs_ref, 0, rows, half), got_ref[:rows]).astype(BF)
     own = own_ref[rows:].astype(F32)
     got = got_ref[rows:].astype(F32)
     left = jnp.where(tm == 0, own[:part], got[:part])
     right = jnp.where(tm == 0, got[:part], own[:part])
     whole = jnp.concatenate([left, right, own[part:]], axis=0).astype(BF)
-    out_ref[2] = dot(place_back(rank_ref, 2, rows, half), whole).astype(BF)
-
-
-def grads_out_kernel(unmasked, place_ref, rank_ref, own_ref, got_ref, out_ref):
+    out_ref[2] = dot(place_back(rank_ref, 0, rows, half), whole).astype(BF)
+
+
+def grads_out_kernel(unmasked, place_ref, theirs_ref, rank_ref, own_ref, got_ref, out_ref):
     tm = place_ref[0]
     half = out_ref.shape[1]
-    out_ref[tm] = dot(place_back(rank_ref, tm, unmasked, half), own_ref[:unmasked]).astype(BF)
-    out_ref[1 - tm] = dot(place_back(rank_ref, 1 - tm, unmasked, half), got_ref[:unmasked]).astype(BF)
+    out_ref[tm] = dot(place_back(rank_ref, 1, unmasked, half), own_ref[:unmasked]).astype(BF)
+    out_ref[1 - tm] = dot(place_back(theirs_ref, 0, unmasked, half), got_ref[:unmasked]).astype(BF)
     whole = (own_ref[unmasked:].astype(F32) + got_ref[unmasked:].astype(F32)).astype(BF)
-    out_ref[2] = dot(place_back(rank_ref, 2, unmasked, half), whole).astype(BF)
+    out_ref[2] = dot(place_back(rank_ref, 0, unmasked, half), whole).astype(BF)
 
 
 def fold_kernel(parts, *refs):
@@ -532,7 +535,7 @@
         pieces = plain(fold, [shape(left, depth, LANES)] * 4)(*pieces)
         if sent is None:
             sent, pieces = send_far(pieces)
-        pieces = [pieces[0]] + [clip_swap(pieces[step], step * distance) for step in (1, 2, 3)]
+        pieces = [pieces[0]] + [clip_swap(pieces[step], step * distance) for step in (3, 2, 1)]
     total = plain(functools.partial(fold_four_kernel, 1), shape(left, depth, LANES))(*pieces)
     for distance in reversed(far):
         pieces = [total] + [clip_swap(total, step * distance) for step in (1, 2, 3)]
@@ -678,22 +681,21 @@
 
     block = shape(rows, width)
     everyone = jnp.concatenate([groups, clip_swap(groups, 1)])
-    theirs, rank = run(
+    theirs, rank_theirs = run(
         functools.partial(prep_theirs_kernel, unmasked),
         (place, *(pltpu.with_memory_space_constraint(each, pltpu.HBM) for each in (masked, tokens))),
-        [shape(unmasked, width), shape(16 * copies, LANES, kind=F32)],
+        [shape(unmasked, width), shape(16, LANES, kind=F32)],
         [pltpu.VMEM(masked.shape, jnp.int32), pltpu.VMEM((half, width), BF), pltpu.SemaphoreType.DMA((2,))],
         flops=2 * rows * half * width,
         in_hbm=(1, 2),
     )
     got_mine = swap(theirs)
-    everyone, theirs, rank = lax.optimization_barrier((everyone, theirs, rank))
+    everyone, theirs, rank_theirs, masked = lax.optimization_barrier((everyone, theirs, rank_theirs, masked))
     everyone = jnp.concatenate([everyone, clip_swap(everyone, 2)])
-    shared = run(
+    shared, rank = run(
         functools.partial(prep_shared_kernel, unmasked),
-        (rank, tokens),
-        shape(unmasked, width),
-        scalars=0,
+        (place, masked, tokens),
+        [shape(unmasked, width), shape(32, LANES, kind=F32)],
         flops=2 * rows * half * width,
     )
     got_shared = swap(shared)
@@ -701,7 +703,7 @@
     everyone = jnp.concatenate([everyone, clip_swap(everyone, 4)])
     cot_own, cot_send = run(
         functools.partial(prep_grads_kernel, unmasked),
-        (place, rank, cotangent),
+        (place, rank_theirs, rank, cotangent),
         [shape(total, width), shape(total - EXTRA, width)],
         flops=2 * copies * rows * half * width,
     )
@@ -795,8 +797,8 @@
 
     def place_rows(got):
         return (
-            run(functools.partial(outputs_kernel, unmasked), (place, rank, out_rows, out_got), shape(*tokens.shape), hides=False),
-            run(functools.partial(grads_out_kernel, unmasked), (place, rank, grad_rows, got), shape(*tokens.shape), hides=False),
+            run(functools.partial(outputs_kernel, unmasked), (place, rank_theirs, rank, out_rows, out_got), shape(*tokens.shape), hides=False),
+            run(functools.partial(grads_out_kernel, unmasked), (place, rank_theirs, rank, grad_rows, got), shape(*tokens.shape), hides=False),
         )
 
     weights = [(hidden, width), (width, hidden), (width, width), (width, 3 * width)]

time: 118 us -> 117 us (level)
  waiting for transfers between devices: 35.1 us -> 33.6 us
  transfers between devices with their start and end apart: 37 -> 37, of which waited for: 17 -> 16; matrix products, arithmetic and copies ran while one was open for 0% -> 0% of each run, Pallas kernels for 36% -> 37%
where the time goes in v8:
time: 117 us
  Pallas kernels  46 us (39%)
  starting transfers between devices  35.2 us (30%)
  waiting for transfers between devices  33.6 us (29%)
  between operations  1.35 us (1%)
    pallas_call x16, Pallas kernels, run(): pl.pallas_call(kernel, out_shape=outs, in_specs=[SMEM if at < scalars els...  45 us
    ppermute x23, starting transfers between devices, clip_swap(): lax.ppermute(values, 'clip', [(i, i ^ distance) for i in range(size)])  18.4 us
    ppermute x9, waiting for transfers between devices, near_swap(): return lax.ppermute(values, ('tm', 'clip'), pairs)  17.6 us
    ppermute x23, waiting for transfers between devices, clip_swap(): lax.ppermute(values, 'clip', [(i, i ^ distance) for i in range(size)])  14.5 us
    ppermute x9, starting transfers between devices, near_swap(): return lax.ppermute(values, ('tm', 'clip'), pairs)  10.5 us
    ppermute x1, starting transfers between devices, body(): got_mine = swap(theirs)  2.57 us
  transfers between devices with their start and end apart: 37, of which 16 were waited for; matrix products, arithmetic and copies ran while one was open for 0% of the time, Pallas kernels for 37%

profile of v8, /device:TPU:0, one launch (start us, length us, event | category | flops | bytes accessed | tf_op | source)
XLA Modules:
  0.0 116.8 jit_solution(16424918866571694172)
XLA Ops:
  1.4 2.4 %shard_map.297 = (bf16[384,384]{1,0:T(8,128)(2,1)S(1)}, f32[16,128]{1,0:T(8,128)S(1)}) custom-call(s32[2]{0:T(128)S(1)} %pad_add_fusion.place_ref, s32[3,1152]{1,0:T(4,128)} %masked_ref.2, bf16[3,768,384]{2,1,0:T(8,128)(2,1)} %refs_1_.1), custom_call_target="tpu_custom_call" | custom-call | flops 235929600 | bytes 2086408 | tf_op jit(solution)/shard_map/pallas_call | solution.py:653
  3.8 2.6 %collective-permute-start.2 = (bf16[384,384]{1,0:T(8,128)(2,1)S(1)}, bf16[384,384]{1,0:T(8,128)(2,1)S(1)}, u32[]{:S(2)}, u32[]{:S(2)}) collective-permute-start(bf16[384,384]{1,0:T(8,128)(2,1)S(1)} %get-tuple-element.158), channel_id=1, source_target_pairs={{0,16},{16,0},{1,17},{17,1},{2,18},{18,2},{3,19},{19,3},{4,20},{20... | collective-permute-start | bytes 884744 | tf_op jit(solution)/shard_map/ppermute | solution.py:692
  15.6 3.6 %shard_map.299 = (bf16[400,384]{1,0:T(8,128)(2,1)S(1)}, bf16[400,384]{1,0:T(8,128)(2,1)S(1)}, bf16[400,384]{1,0:T(8,128)(2,1)S(1)}, bf16[400,384]{1,0:T(8,128)(2...) custom-call(s32[2]{0:T(128)S(1)} %pad_add_fusion.place_ref, ...), custom_call_target="tpu_custom_call" | custom-call | flops 599654400 | bytes 7049736 | tf_op jit(solution)/shard_map/pallas_call | solution.py:653
  19.2 2.7 %collective-permute-start.5 = (s32[24]{0:T(128)S(1)}, s32[24]{0:T(128)S(1)}, u32[]{:S(2)}, u32[]{:S(2)}) collective-permute-start(s32[24]{0:T(128)S(1)} %pad_add_fusion.3), channel_id=1, source_target_pairs={{0,8},{1,9},{2,10},{3,11},{4,12},{5,13},{6,14},{7,15},{8,0},{9,1},... | collective-permute-start | bytes 296 | tf_op jit(solution)/shard_map/ppermute | solution.py:494
  21.8 2.5 %shard_map.300 = (bf16[208,384]{1,0:T(8,128)(2,1)S(1)}, bf16[208,384]{1,0:T(8,128)(2,1)S(1)}, bf16[400,384]{1,0:T(8,128)(2,1)S(1)}, bf16[400,384]{1,0:T(8,128)(2...) custom-call(s32[2]{0:T(128)S(1)} %pad_add_fusion.place_ref, ...), custom_call_target="tpu_custom_call" | custom-call | flops 481689600 | bytes 4207112 | tf_op jit(solution)/shard_map/pallas_call | solution.py:653
  24.4 3.7 %shard_map.302 = (bf16[608,384]{1,0:T(8,128)(2,1)S(1)}, f32[608,384]{1,0:T(8,128)S(1)}, bf16[608,384]{1,0:T(8,128)(2,1)S(1)}, bf16[608,1536]{1,0:T(8,128)(2,1)S(1)}, bf16[608,1536]{1,0:T(8,128)(2,1)S(1)}) custom-call(bf16[400,384]{1,0:T(8,128)(2,1)S(1)} %get-tuple-element.179.att_a.att_ref, bf16[208,384]{1,0:T(8,128)(2,1)S(1)} %get-tuple-element.180.att_b.att_ref, ...), custom_call_target="tpu_custom_call" | custom-call | flops 1613758464 | bytes 9211392 | tf_op jit(solution)/shard_map/pallas_call | solution.py:653
  30.3 4.3 %shard_map.303 = (f32[608,384]{1,0:T(8,128)S(1)}, bf16[608,1536]{1,0:T(8,128)(2,1)S(1)}, f32[1,1536]{1,0:T(1,128)S(1)}, bf16[4,4,288,128]{3,2,1,0:T(8,128)(2,1)S...) custom-call(s32[2]{0:T(128)S(1)} %pad_add_fusion.place_ref, ...), custom_call_target="tpu_custom_call" | custom-call | flops 1 | bytes 1 | tf_op jit(solution)/shard_map/pallas_call | solution.py:653
  35.7 2.7 %shard_map.304 = (f32[608,384]{1,0:T(8,128)S(1)}, bf16[608,384]{1,0:T(8,128)(2,1)S(1)}, f32[8,384]{1,0:T(8,128)S(1)}, bf16[4,4,48,128]{3,2,1,0:T(8,128)(2,1)S(1)...) custom-call(s32[2]{0:T(128)S(1)} %pad_add_fusion.place_ref, ...), custom_call_target="tpu_custom_call" | custom-call | flops 1 | bytes 1 | tf_op jit(solution)/shard_map/pallas_call | solution.py:653
  42.8 3.2 %shard_map.306 = (bf16[400,384]{1,0:T(8,128)(2,1)S(1)}, bf16[400,384]{1,0:T(8,128)(2,1)S(1)}, bf16[400,384]{1,0:T(8,128)(2,1)S(1)}) custom-call(bf16[608,384]{1,0:T(8,128)(2,1)S(1)} %get-tuple-element.205.g_ref, bf16[400,384]{1,0:T(8,128)(2,1)S(1)} %get-tuple-element.179.att_a.att_ref, bf16[400,384]{1,0:T(8,128)(2,1)S(1)} %get-tuple-element.206.q_ref, ...), custom_call_target="tpu_custom_call" | custom-call | flops 1 | bytes 1 | tf_op jit(solution)/shard_map/pallas_call | solution.py:653
  46.0 2.3 %shard_map.307 = (bf16[208,384]{1,0:T(8,128)(2,1)S(1)}, bf16[400,384]{1,0:T(8,128)(2,1)S(1)}, bf16[400,384]{1,0:T(8,128)(2,1)S(1)}) custom-call(bf16[608,384]{1,0:T(8,128)(2,1)S(1)} %get-tuple-element.205.g_ref, bf16[208,384]{1,0:T(8,128)(2,1)S(1)} %get-tuple-element.180.att_b.att_ref, bf16[208,384]{1,0:T(8,128)(2,1)S(1)} %get-tuple-element.215.q_ref, ...), custom_call_target="tpu_custom_call" | custom-call | flops 1 | bytes 1 | tf_op jit(solution)/shard_map/pallas_call | solution.py:653
  48.3 3.8 %shard_map.308 = (bf16[768,384]{1,0:T(8,128)(2,1)S(1)}, bf16[4,4,112,128]{3,2,1,0:T(8,128)(2,1)S(1)}, bf16[2,4,112,128]{3,2,1,0:T(8,128)(2,1)S(1)}, bf16[2,4,112,128]{3,2,1,0:T(8,128)(2,1)S(1)}) custom-call(s32[2]{0:T(128)S(1)} %pad_add_fusion.place_ref, bf16[400,384]{1,0:T(8,128)(2,1)S(1)} %get-tuple-element.165.x_a, ...), custom_call_target="tpu_custom_call" | custom-call | flops 1 | bytes 1 | tf_op jit(solution)/shard_map/pallas_call | solution.py:653
  59.8 3.3 %collective-permute-done.19.refs_5_ = bf16[4,160,128]{2,1,0:T(8,128)(2,1)S(1)} collective-permute-done((bf16[4,160,128]{2,1,0:T(8,128)(2,1)S(1)}, bf16[4,160,128]{2,1,0:T(8,128)(2,1)S(1)}, u32[]{:S(2)}, u32[]{:S(2)}) %collective-permute-start.19) | collective-permute-done | bytes 163872 | tf_op jit(solution)/shard_map/ppermute | solution.py:502
  63.0 3.3 %collective-permute-done.20.refs_6_ = bf16[4,160,128]{2,1,0:T(8,128)(2,1)S(1)} collective-permute-done((bf16[4,160,128]{2,1,0:T(8,128)(2,1)S(1)}, bf16[4,160,128]{2,1,0:T(8,128)(2,1)S(1)}, u32[]{:S(2)}, u32[]{:S(2)}) %collective-permute-start.20) | collective-permute-done | bytes 163872 | tf_op jit(solution)/shard_map/ppermute | solution.py:502
  67.5 3.6 %collective-permute-start.22 = (bf16[1,448,128]{2,1,0:T(8,128)(2,1)S(1)}, bf16[1,448,128]{2,1,0:T(8,128)(2,1)S(1)}, u32[]{:S(2)}, u32[]{:S(2)}) collective-permute-start(bf16[1,448,128]{2,1,0:T(8,128)(2,1)S(1)} %get-tuple-element.258), channel_id=1, source_target_pairs={{0,12},{1,13},{2,14},{3,15},{4,8},{5,9},{6,10},{7,11},{8,4},{9,5},... | collective-permute-start | bytes 344072 | tf_op jit(solution)/shard_map/ppermute | solution.py:494
  71.9 2.8 %collective-permute-done.22.refs_1_ = bf16[1,448,128]{2,1,0:T(8,128)(2,1)S(1)} collective-permute-done((bf16[1,448,128]{2,1,0:T(8,128)(2,1)S(1)}, bf16[1,448,128]{2,1,0:T(8,128)(2,1)S(1)}, u32[]{:S(2)}, u32[]{:S(2)}) %collective-permute-start.22) | collective-permute-done | bytes 114720 | tf_op jit(solution)/shard_map/ppermute | solution.py:494
  74.7 4.9 %collective-permute-done.23.refs_2_ = bf16[1,448,128]{2,1,0:T(8,128)(2,1)S(1)} collective-permute-done((bf16[1,448,128]{2,1,0:T(8,128)(2,1)S(1)}, bf16[1,448,128]{2,1,0:T(8,128)(2,1)S(1)}, u32[]{:S(2)}, u32[]{:S(2)}) %collective-permute-start.23) | collective-permute-done | bytes 114720 | tf_op jit(solution)/shard_map/ppermute | solution.py:494
  79.6 2.7 %collective-permute-start.27 = (bf16[1,448,128]{2,1,0:T(8,128)(2,1)S(1)}, bf16[1,448,128]{2,1,0:T(8,128)(2,1)S(1)}, u32[]{:S(2)}, u32[]{:S(2)}) collective-permute-start(bf16[1,448,128]{2,1,0:T(8,128)(2,1)S(1)} %shard_map.311.refs_0_), channel_id=1, source_target_pairs={{0,12},{1,13},{2,14},{3,15},{4,8},{5,9},{6,10},{7,11},{8,4},{9,5},... | collective-permute-start | bytes 344072 | tf_op jit(solution)/shard_map/ppermute | solution.py:494
  84.1 3.4 %shard_map.313 = bf16[3,768,384]{2,1,0:T(8,128)(2,1)} custom-call(s32[2]{0:T(128)S(1)} %pad_add_fusion.place_ref, f32[16,128]{1,0:T(8,128)S(1)} %get-tuple-element.169.theirs_ref, f32[32,128]{1,0:T(8,128)S(1)} %get-tuple-element.164.refs_0_.rank_ref, bf16[608,384]{1,0:T(8,128)(2,1)S(1)} %get-tuple-element.221.own_ref, ...), custom_call_target="tpu_custom_call" | custom-call | flops 1 | bytes 1 | tf_op jit(solution)/shard_map/pallas_call | solution.py:653
  87.5 3.4 %collective-permute-done.26.refs_2_ = bf16[1,448,128]{2,1,0:T(8,128)(2,1)S(1)} collective-permute-done((bf16[1,448,128]{2,1,0:T(8,128)(2,1)S(1)}, bf16[1,448,128]{2,1,0:T(8,128)(2,1)S(1)}, u32[]{:S(2)}, u32[]{:S(2)}) %collective-permute-start.26) | collective-permute-done | bytes 114720 | tf_op jit(solution)/shard_map/ppermute | solution.py:494
  94.5 3.2 %shard_map.314 = bf16[3,768,384]{2,1,0:T(8,128)(2,1)} custom-call(s32[2]{0:T(128)S(1)} %pad_add_fusion.place_ref, f32[16,128]{1,0:T(8,128)S(1)} %get-tuple-element.169.theirs_ref, f32[32,128]{1,0:T(8,128)S(1)} %get-tuple-element.164.refs_0_.rank_ref, bf16[768,384]{1,0:T(8,128)(2,1)S(1)} %get-tuple-element.261.own_ref, ...), custom_call_target="tpu_custom_call" | custom-call | flops 1 | bytes 1 | tf_op jit(solution)/shard_map/pallas_call | solution.py:653
  101.5 3.8 %collective-permute-done.31.refs_2_ = bf16[4,448,128]{2,1,0:T(8,128)(2,1)S(1)} collective-permute-done((bf16[4,448,128]{2,1,0:T(8,128)(2,1)S(1)}, bf16[4,448,128]{2,1,0:T(8,128)(2,1)S(1)}, u32[]{:S(2)}, u32[]{:S(2)}) %collective-permute-start.31) | collective-permute-done | bytes 458784 | tf_op jit(solution)/shard_map/ppermute | solution.py:502
  105.4 5.3 %collective-permute-done.30.refs_1_ = bf16[4,448,128]{2,1,0:T(8,128)(2,1)S(1)} collective-permute-done((bf16[4,448,128]{2,1,0:T(8,128)(2,1)S(1)}, bf16[4,448,128]{2,1,0:T(8,128)(2,1)S(1)}, u32[]{:S(2)}, u32[]{:S(2)}) %collective-permute-start.30) | collective-permute-done | bytes 458784 | tf_op jit(solution)/shard_map/ppermute | solution.py:502
  111.2 2.2 %shard_map.316 = (f32[1536,384]{1,0:T(8,128)}, f32[384,1536]{1,0:T(8,128)}, f32[384,384]{1,0:T(8,128)}, f32[384,1152]{1,0:T(8,128)}, f32[8,16,128]{2,1,0:T(8,128)S(1)}) custom-call(s32[2]{0:T(128)S(1)} %pad_add_fusion.place_ref, ...), custom_call_target="tpu_custom_call", output_to_operand_aliasing={{0}: (4, {}), {1}: (5, {}), {2}: (6, {}), {3}: (7, {})} | custom-call | flops 1 | bytes 1 | tf_op jit(solution)/shard_map/pallas_call | solution.py:653
  113.8 2.8 %shard_map.317 = (f32[1536,384]{1,0:T(8,128)}, f32[384,1536]{1,0:T(8,128)}, f32[384,384]{1,0:T(8,128)}, f32[384,1152]{1,0:T(8,128)}, f32[1536]{0:T(1024)}, /*ind...) custom-call(s32[2]{0:T(128)S(1)} %pad_add_fusion.place_ref, ...), custom_call_target="tpu_custom_call", output_to_operand_aliasing={{0}: (4, {}), {1}: (5, {}), {2}: (6, {}), {3}: (7, {})} | custom-call | flops 1 | bytes 1 | tf_op jit(solution)/shard_map/pallas_call | solution.py:653
  (125 shorter events, 37.2 us)
Async XLA Ops:
  0.8 5.8 %collective-permute-start = (s32[3]{0:T(128)}, s32[3]{0:T(128)S(1)}, u32[]{:S(2)}, u32[]{:S(2)}) collective-permute-start(s32[3]{0:T(128)} %groups_ref.1), channel_id=1, source_target_pairs={{0,1},{1,0},{2,3},{3,2},{4,5},{5,4},{6,7},{7,6},{8,9},{9,8},{10,11... | collective-permute-start | bytes 44 | tf_op jit(solution)/shard_map/ppermute | solution.py:494
  3.8 11.9 %collective-permute-start.2 = (bf16[384,384]{1,0:T(8,128)(2,1)S(1)}, bf16[384,384]{1,0:T(8,128)(2,1)S(1)}, u32[]{:S(2)}, u32[]{:S(2)}) collective-permute-start(bf16[384,384]{1,0:T(8,128)(2,1)S(1)} %get-tuple-element.158), channel_id=1, source_target_pairs={{0,16},{16,0},{1,17},{17,1},{2,18},{18,2},{3,19},{19,3},{4,20},{20... | collective-permute-start | bytes 884744 | tf_op jit(solution)/shard_map/ppermute | solution.py:692
  9.8 12.1 %collective-permute-start.3 = (bf16[384,384]{1,0:T(8,128)(2,1)S(1)}, bf16[384,384]{1,0:T(8,128)(2,1)S(1)}, u32[]{:S(2)}, u32[]{:S(2)}) collective-permute-start(bf16[384,384]{1,0:T(8,128)(2,1)S(1)} %get-tuple-element.166.refs_0_), channel_id=1, source_target_pairs={{0,16},{16,0},{1,17},{17,1},{2,18},{18,2},{3,19},{19,3},{4,20},{20... | collective-permute-start | bytes 884744 | tf_op jit(solution)/shard_map/ppermute | solution.py:701
  14.1 16.2 %collective-permute-start.6 = (bf16[592,384]{1,0:T(8,128)(2,1)S(1)}, bf16[592,384]{1,0:T(8,128)(2,1)S(1)}, u32[]{:S(2)}, u32[]{:S(2)}) collective-permute-start(bf16[592,384]{1,0:T(8,128)(2,1)S(1)} %get-tuple-element.178), channel_id=1, source_target_pairs={{0,16},{16,0},{1,17},{17,1},{2,18},{18,2},{3,19},{19,3},{4,20},{20... | collective-permute-start | bytes 1363976 | tf_op jit(solution)/shard_map/ppermute | solution.py:711
  19.2 5.1 %collective-permute-start.5 = (s32[24]{0:T(128)S(1)}, s32[24]{0:T(128)S(1)}, u32[]{:S(2)}, u32[]{:S(2)}) collective-permute-start(s32[24]{0:T(128)S(1)} %pad_add_fusion.3), channel_id=1, source_target_pairs={{0,8},{1,9},{2,10},{3,11},{4,12},{5,13},{6,14},{7,15},{8,0},{9,1},... | collective-permute-start | bytes 296 | tf_op jit(solution)/shard_map/ppermute | solution.py:494
  28.1 14.7 %collective-permute-start.13 = (bf16[608,384]{1,0:T(8,128)(2,1)S(1)}, bf16[608,384]{1,0:T(8,128)(2,1)S(1)}, u32[]{:S(2)}, u32[]{:S(2)}) collective-permute-start(bf16[608,384]{1,0:T(8,128)(2,1)S(1)} %get-tuple-element.221.own_ref), channel_id=1, source_target_pairs={{0,16},{16,0},{1,17},{17,1},{2,18},{18,2},{3,19},{19,3},{4,20},{20... | collective-permute-start | bytes 1400840 | tf_op jit(solution)/shard_map/ppermute | solution.py:747
  38.7 9.6 %collective-permute-start.11 = (bf16[2,4,48,128]{3,2,1,0:T(8,128)(2,1)S(1)}, bf16[2,4,48,128]{3,2,1,0:T(8,128)(2,1)S(1)}, u32[]{:S(2)}, u32[]{:S(2)}) collective-permute-start(bf16[2,4,48,128]{3,2,1,0:T(8,128)(2,1)S(1)} %get-tuple-element.212), channel_id=1, source_target_pairs={{0,1},{1,0},{2,3},{3,2},{4,5},{5,4},{6,7},{7,6},{8,9},{9,8},{10,11... | collective-permute-start | bytes 294920 | tf_op jit(solution)/shard_map/ppermute | solution.py:494
  38.9 9.5 %collective-permute-start.12 = (bf16[2,4,48,128]{3,2,1,0:T(8,128)(2,1)S(1)}, bf16[2,4,48,128]{3,2,1,0:T(8,128)(2,1)S(1)}, u32[]{:S(2)}, u32[]{:S(2)}) collective-permute-start(bf16[2,4,48,128]{3,2,1,0:T(8,128)(2,1)S(1)} %get-tuple-element.213), channel_id=1, source_target_pairs={{0,1},{1,0},{2,3},{3,2},{4,5},{5,4},{6,7},{7,6},{8,9},{9,8},{10,11... | collective-permute-start | bytes 294920 | tf_op jit(solution)/shard_map/ppermute | solution.py:494
  39.3 15.1 %collective-permute-start.16 = (bf16[4,288,128]{2,1,0:T(8,128)(2,1)S(1)}, bf16[4,288,128]{2,1,0:T(8,128)(2,1)S(1)}, u32[]{:S(2)}, u32[]{:S(2)}) collective-permute-start(bf16[4,288,128]{2,1,0:T(8,128)(2,1)S(1)} %get-tuple-element.241), channel_id=1, source_target_pairs={{0,16},{1,17},{2,18},{3,19},{4,20},{5,21},{6,22},{7,23},{8,24},{9,... | collective-permute-start | bytes 884744 | tf_op jit(solution)/shard_map/ppermute | solution.py:502
  41.2 15.0 %collective-permute-start.17 = (bf16[4,288,128]{2,1,0:T(8,128)(2,1)S(1)}, bf16[4,288,128]{2,1,0:T(8,128)(2,1)S(1)}, u32[]{:S(2)}, u32[]{:S(2)}) collective-permute-start(bf16[4,288,128]{2,1,0:T(8,128)(2,1)S(1)} %get-tuple-element.242), channel_id=1, source_target_pairs={{0,2},{1,3},{2,0},{3,1},{4,6},{5,7},{6,4},{7,5},{8,10},{9,11},{10,... | collective-permute-start | bytes 884744 | tf_op jit(solution)/shard_map/ppermute | solution.py:502
  42.7 13.5 %collective-permute-start.18 = (bf16[4,288,128]{2,1,0:T(8,128)(2,1)S(1)}, bf16[4,288,128]{2,1,0:T(8,128)(2,1)S(1)}, u32[]{:S(2)}, u32[]{:S(2)}) collective-permute-start(bf16[4,288,128]{2,1,0:T(8,128)(2,1)S(1)} %get-tuple-element.243), channel_id=1, source_target_pairs={{0,18},{1,19},{2,16},{3,17},{4,22},{5,23},{6,20},{7,21},{8,26},{9,... | collective-permute-start | bytes 884744 | tf_op jit(solution)/shard_map/ppermute | solution.py:502
  56.3 6.8 %collective-permute-start.19 = (bf16[4,160,128]{2,1,0:T(8,128)(2,1)S(1)}, bf16[4,160,128]{2,1,0:T(8,128)(2,1)S(1)}, u32[]{:S(2)}, u32[]{:S(2)}) collective-permute-start(bf16[4,160,128]{2,1,0:T(8,128)(2,1)S(1)} %get-tuple-element.249), channel_id=1, source_target_pairs={{0,16},{1,17},{2,18},{3,19},{4,20},{5,21},{6,22},{7,23},{8,24},{9,... | collective-permute-start | bytes 491528 | tf_op jit(solution)/shard_map/ppermute | solution.py:502
  57.5 8.8 %collective-permute-start.20 = (bf16[4,160,128]{2,1,0:T(8,128)(2,1)S(1)}, bf16[4,160,128]{2,1,0:T(8,128)(2,1)S(1)}, u32[]{:S(2)}, u32[]{:S(2)}) collective-permute-start(bf16[4,160,128]{2,1,0:T(8,128)(2,1)S(1)} %get-tuple-element.250), channel_id=1, source_target_pairs={{0,2},{1,3},{2,0},{3,1},{4,6},{5,7},{6,4},{7,5},{8,10},{9,11},{10,... | collective-permute-start | bytes 491528 | tf_op jit(solution)/shard_map/ppermute | solution.py:502
  58.3 8.0 %collective-permute-start.21 = (bf16[4,160,128]{2,1,0:T(8,128)(2,1)S(1)}, bf16[4,160,128]{2,1,0:T(8,128)(2,1)S(1)}, u32[]{:S(2)}, u32[]{:S(2)}) collective-permute-start(bf16[4,160,128]{2,1,0:T(8,128)(2,1)S(1)} %get-tuple-element.251), channel_id=1, source_target_pairs={{0,18},{1,19},{2,16},{3,17},{4,22},{5,23},{6,20},{7,21},{8,26},{9,... | collective-permute-start | bytes 491528 | tf_op jit(solution)/shard_map/ppermute | solution.py:502
  66.6 24.4 %collective-permute-start.28 = (bf16[768,384]{1,0:T(8,128)(2,1)S(1)}, bf16[768,384]{1,0:T(8,128)(2,1)S(1)}, u32[]{:S(2)}, u32[]{:S(2)}) collective-permute-start(bf16[768,384]{1,0:T(8,128)(2,1)S(1)} %get-tuple-element.261.own_ref), channel_id=1, source_target_pairs={{0,16},{16,0},{1,17},{17,1},{2,18},{18,2},{3,19},{19,3},{4,20},{20... | collective-permute-start | bytes 1769480 | tf_op jit(solution)/shard_map/ppermute | solution.py:796
  67.5 7.2 %collective-permute-start.22 = (bf16[1,448,128]{2,1,0:T(8,128)(2,1)S(1)}, bf16[1,448,128]{2,1,0:T(8,128)(2,1)S(1)}, u32[]{:S(2)}, u32[]{:S(2)}) collective-permute-start(bf16[1,448,128]{2,1,0:T(8,128)(2,1)S(1)} %get-tuple-element.258), channel_id=1, source_target_pairs={{0,12},{1,13},{2,14},{3,15},{4,8},{5,9},{6,10},{7,11},{8,4},{9,5},... | collective-permute-start | bytes 344072 | tf_op jit(solution)/shard_map/ppermute | solution.py:494
  71.1 8.5 %collective-permute-start.23 = (bf16[1,448,128]{2,1,0:T(8,128)(2,1)S(1)}, bf16[1,448,128]{2,1,0:T(8,128)(2,1)S(1)}, u32[]{:S(2)}, u32[]{:S(2)}) collective-permute-start(bf16[1,448,128]{2,1,0:T(8,128)(2,1)S(1)} %get-tuple-element.259), channel_id=1, source_target_pairs={{0,8},{1,9},{2,10},{3,11},{4,12},{5,13},{6,14},{7,15},{8,0},{9,1},... | collective-permute-start | bytes 344072 | tf_op jit(solution)/shard_map/ppermute | solution.py:494
  71.1 8.5 %collective-permute-start.24 = (bf16[1,448,128]{2,1,0:T(8,128)(2,1)S(1)}, bf16[1,448,128]{2,1,0:T(8,128)(2,1)S(1)}, u32[]{:S(2)}, u32[]{:S(2)}) collective-permute-start(bf16[1,448,128]{2,1,0:T(8,128)(2,1)S(1)} %get-tuple-element.260), channel_id=1, source_target_pairs={{0,4},{1,5},{2,6},{3,7},{4,0},{5,1},{6,2},{7,3},{8,12},{9,13},{10,... | collective-permute-start | bytes 344072 | tf_op jit(solution)/shard_map/ppermute | solution.py:494
  79.6 7.9 %collective-permute-start.27 = (bf16[1,448,128]{2,1,0:T(8,128)(2,1)S(1)}, bf16[1,448,128]{2,1,0:T(8,128)(2,1)S(1)}, u32[]{:S(2)}, u32[]{:S(2)}) collective-permute-start(bf16[1,448,128]{2,1,0:T(8,128)(2,1)S(1)} %shard_map.311.refs_0_), channel_id=1, source_target_pairs={{0,12},{1,13},{2,14},{3,15},{4,8},{5,9},{6,10},{7,11},{8,4},{9,5},... | collective-permute-start | bytes 344072 | tf_op jit(solution)/shard_map/ppermute | solution.py:494
  82.3 8.6 %collective-permute-start.26 = (bf16[1,448,128]{2,1,0:T(8,128)(2,1)S(1)}, bf16[1,448,128]{2,1,0:T(8,128)(2,1)S(1)}, u32[]{:S(2)}, u32[]{:S(2)}) collective-permute-start(bf16[1,448,128]{2,1,0:T(8,128)(2,1)S(1)} %shard_map.311.refs_0_), channel_id=1, source_target_pairs={{0,8},{1,9},{2,10},{3,11},{4,12},{5,13},{6,14},{7,15},{8,0},{9,1},... | collective-permute-start | bytes 344072 | tf_op jit(solution)/shard_map/ppermute | solution.py:494
  82.3 8.6 %collective-permute-start.25 = (bf16[1,448,128]{2,1,0:T(8,128)(2,1)S(1)}, bf16[1,448,128]{2,1,0:T(8,128)(2,1)S(1)}, u32[]{:S(2)}, u32[]{:S(2)}) collective-permute-start(bf16[1,448,128]{2,1,0:T(8,128)(2,1)S(1)} %shard_map.311.refs_0_), channel_id=1, source_target_pairs={{0,4},{1,5},{2,6},{3,7},{4,0},{5,1},{6,2},{7,3},{8,12},{9,13},{10,... | collective-permute-start | bytes 344072 | tf_op jit(solution)/shard_map/ppermute | solution.py:494
  91.0 14.4 %collective-permute-start.31 = (bf16[4,448,128]{2,1,0:T(8,128)(2,1)S(1)}, bf16[4,448,128]{2,1,0:T(8,128)(2,1)S(1)}, u32[]{:S(2)}, u32[]{:S(2)}) collective-permute-start(bf16[4,448,128]{2,1,0:T(8,128)(2,1)S(1)} %shard_map.312), channel_id=1, source_target_pairs={{0,18},{1,19},{2,16},{3,17},{4,22},{5,23},{6,20},{7,21},{8,26},{9,... | collective-permute-start | bytes 1376264 | tf_op jit(solution)/shard_map/ppermute | solution.py:502
  91.6 19.1 %collective-permute-start.30 = (bf16[4,448,128]{2,1,0:T(8,128)(2,1)S(1)}, bf16[4,448,128]{2,1,0:T(8,128)(2,1)S(1)}, u32[]{:S(2)}, u32[]{:S(2)}) collective-permute-start(bf16[4,448,128]{2,1,0:T(8,128)(2,1)S(1)} %shard_map.312), channel_id=1, source_target_pairs={{0,2},{1,3},{2,0},{3,1},{4,6},{5,7},{6,4},{7,5},{8,10},{9,11},{10,... | collective-permute-start | bytes 1376264 | tf_op jit(solution)/shard_map/ppermute | solution.py:502
  93.1 17.6 %collective-permute-start.29 = (bf16[4,448,128]{2,1,0:T(8,128)(2,1)S(1)}, bf16[4,448,128]{2,1,0:T(8,128)(2,1)S(1)}, u32[]{:S(2)}, u32[]{:S(2)}) collective-permute-start(bf16[4,448,128]{2,1,0:T(8,128)(2,1)S(1)} %shard_map.312), channel_id=1, source_target_pairs={{0,16},{1,17},{2,18},{3,19},{4,20},{5,21},{6,22},{7,23},{8,24},{9,... | collective-permute-start | bytes 1376264 | tf_op jit(solution)/shard_map/ppermute | solution.py:502
  (31 other events, 159.2 us)

commit v9 on v8

--- a/solution.py
+++ b/solution.py
@@ -546,11 +546,13 @@
     early, last = lax.optimization_barrier((total, last))
     middle = total.shape[1] // 32 * 16
     parts = [early[:, :middle], early[:, middle:]]
-    done = finish(((0, 0), (0, 1)), [parts, [clip_swap(part, 1) for part in parts]], ())
+    got_parts = [clip_swap(part, 1) for part in parts]
+    done = finish(((0, 0), (0, 1)), [parts, got_parts], (), ())
     *pieces, done = lax.optimization_barrier((*pieces, done))
-    got = [clip_swap(piece, 1) for piece in pieces[1:]]
-    done = finish(((1, 0), (2, 0), (3, 0)), [[piece] for piece in pieces[1:]], done)
-    return finish(((1, 1), (2, 1), (3, 1)), [[piece] for piece in got], done), last
+    own = [[piece] for piece in pieces[1:]]
+    got = [[clip_swap(piece, 1)] for piece in pieces[1:]]
+    done = finish(((1, 0), (2, 0), (3, 0)), own, done, ())
+    return finish(((1, 1), (2, 1), (3, 1)), got, done, [parts, got_parts, *own]), last
 
 
 def join_kernel(*refs):
@@ -559,30 +561,56 @@
             refs[4][4 * slot + step] = refs[step][slot]
 
 
-def finish_kernel(jobs, first_call, depths, vectors, place_ref, *refs):
-    parts = len(jobs) if not first_call else 2 * len(jobs)
-    sources, refs = refs[:parts], refs[parts:]
+def finish_kernel(jobs, counts, extra_jobs, extra_counts, first_call, depths, base, vectors, place_ref, *refs):
+    def take(counts):
+        nonlocal refs
+        taken = []
+        for count in counts:
+            taken.append(refs[:count])
+            refs = refs[count:]
+        return taken
+
+    sources, extra_sources = take(counts), take(extra_counts)
     if not first_call:
-        earlier_ref, refs = refs[4], refs[5:]
-    outs, refs = refs[:4], refs[4:]
-    vectors, refs = refs[:vectors], refs[vectors:]
-    kept_ref, *stage_refs = refs[: 1 + len(depths)]
-    done, *wides = refs[1 + len(depths) :]
-    kept_ref[...] = jnp.zeros(kept_ref.shape, F32) if first_call else earlier_ref[...]
+        take((4,))
+    outs, vector_outs, stage_refs, (done,), wides, (kept_ref,), flat_refs = take(
+        (4, vectors, len(depths), 1, 4, 1, vectors)
+    )
     stores = []
-    each = parts // len(jobs)
-    for job, (near, side) in enumerate(jobs):
+
+    def store(source, target):
+        stores.append(pltpu.make_async_copy(source, target, done.at[len(stores)]))
+        stores[-1].start()
+
+    if vectors:
+        number, offset = divmod(base, depths[1])
+        for (near, side), parts in zip(jobs + extra_jobs, sources + extra_sources):
+            start = 0
+            for part in parts:
+                row = depths[0] + offset - start
+                if 0 <= row < part.shape[1]:
+                    rows = part[number ^ (place_ref[1] >> 3), row : row + 16]
+                    kept_ref[eighth_at(place_ref, near, side)] = rows.astype(F32)
+                start += part.shape[1]
+        blocks = [(ref, block) for ref in flat_refs for block in range(ref.shape[0] // LANES)]
+        each = -(-len(blocks) // 8)
+        for at, (ref, block) in enumerate(blocks):
+            eighth, row = divmod(at, each)
+            ref[block * LANES : (block + 1) * LANES] = kept_ref[eighth, row]
+        for flat_ref, out_ref in zip(flat_refs, vector_outs):
+            store(flat_ref, out_ref)
+    for job, ((near, side), parts) in enumerate(zip(jobs, sources)):
         eighth = eighth_at(place_ref, near, side)
-        for far in range(sources[0].shape[0]):
+        for far in range(parts[0].shape[0]):
             start = 0
-            for source in sources[job * each : (job + 1) * each]:
-                stop = start + source.shape[1]
+            for part in parts:
+                stop = start + part.shape[1]
                 for unit, (stage_ref, depth) in enumerate(zip(stage_refs, depths)):
                     low = sum(depths[:unit])
                     top, end = max(start, low), min(stop, low + depth)
                     if top < end:
                         first = pl.multiple_of((far ^ (place_ref[1] >> 3)) * depth + (top - low), 16)
-                        stage_ref[pl.ds(first, end - top), :] = source[far, top - start : end - start]
+                        stage_ref[pl.ds(first, end - top), :] = part[far, top - start : end - start]
                 start = stop
         for unit, stage_ref in enumerate(stage_refs):
             first = 0
@@ -597,17 +625,9 @@
                     target = outs[at].at[rows, pl.ds(pl.multiple_of((eighth >> 1) * width, LANES), width)]
                 else:
                     target = outs[at].at[pl.ds(pl.multiple_of(eighth * depth, 16), depth), :]
-                stores.append(pltpu.make_async_copy(wide_ref, target, done.at[len(stores)]))
-                stores[-1].start()
-            if unit == 1:
-                kept_ref[eighth] = stage_ref[first : first + 16, :].astype(F32)
-    blocks = [(ref, block) for ref in vectors for block in range(ref.shape[0] // LANES)]
-    each = -(-len(blocks) // 8)
-    for number, (ref, block) in enumerate(blocks):
-        eighth, row = divmod(number, each)
-        ref[block * LANES : (block + 1) * LANES] = kept_ref[eighth, row]
-    for store in stores:
-        store.wait()
+                store(wide_ref, target)
+    for each in stores:
+        each.wait()
 
 
 def chunk_rows(count, devices):
@@ -805,21 +825,33 @@
     slabs = [(hidden // 8, width), (width // 2, hidden // 4), (width // 8, width), (width // 8, 3 * width)]
     vectors = [shape(dim, kind=F32) for dim in [hidden] + [width] * 9]
 
-    def finish(jobs, sources, earlier):
-        sources = [part for parts in sources for part in parts]
-        last = bool(earlier) and jobs[0][1] == 1
-        kept = (8, 16, LANES)
+    def finish(jobs, sources, earlier, extra_sources):
+        extra_jobs = ((0, 0), (0, 1), (1, 0), (2, 0), (3, 0)) if extra_sources else ()
+        refs = [part for parts in [*sources, *extra_sources] for part in parts]
+        flat = vectors if extra_sources else []
+        kernel = functools.partial(
+            finish_kernel,
+            jobs,
+            [len(parts) for parts in sources],
+            extra_jobs,
+            [len(parts) for parts in extra_sources],
+            not earlier,
+            depths,
+            counts[1] - 16,
+            len(flat),
+        )
         return run(
-            functools.partial(finish_kernel, jobs, not earlier, depths, len(vectors) if last else 0),
-            (place, *sources, *earlier),
-            [shape(*dims, kind=F32) for dims in weights] + (vectors if last else [shape(*kept, kind=F32)]),
-            [pltpu.VMEM(kept, F32)] * last
-            + [pltpu.VMEM((devices // 8 * depth, LANES), BF) for depth in depths]
-            + [pltpu.SemaphoreType.DMA((4 * len(jobs),))]
-            + [pltpu.VMEM((len(jobs), *dims), F32) for dims in slabs],
-            in_hbm=range(1 + len(sources), 5 + len(sources)) if earlier else (),
-            out_hbm=range(4),
-            aliases={1 + len(sources) + at: at for at in range(4)} if earlier else {},
+            kernel,
+            (place, *refs, *earlier),
+            [shape(*dims, kind=F32) for dims in weights] + flat,
+            [pltpu.VMEM((devices // 8 * depth, LANES), BF) for depth in depths]
+            + [pltpu.SemaphoreType.DMA((4 * len(jobs) + len(flat),))]
+            + [pltpu.VMEM((len(jobs), *dims), F32) for dims in slabs]
+            + [pltpu.VMEM((8, 16, LANES), F32)]
+            + [pltpu.VMEM(each.shape, F32) for each in flat],
+            in_hbm=range(1 + len(refs), 5 + len(refs)) if earlier else (),
+            out_hbm=range(4 + len(flat)),
+            aliases={1 + len(refs) + at: at for at in range(4)} if earlier else {},
             hides=False,
         )
 

time: 117 us -> 116 us (level)
  no operation moved by 1% of the time
where the time goes in v9:
time: 116 us
  Pallas kernels  45.5 us (39%)
  starting transfers between devices  35.2 us (30%)
  waiting for transfers between devices  33.6 us (29%)
  between operations  1.35 us (1%)
    pallas_call x16, Pallas kernels, run(): pl.pallas_call(kernel, out_shape=outs, in_specs=[SMEM if at < scalars els...  44.5 us
    ppermute x23, starting transfers between devices, clip_swap(): lax.ppermute(values, 'clip', [(i, i ^ distance) for i in range(size)])  18.4 us
    ppermute x9, waiting for transfers between devices, near_swap(): return lax.ppermute(values, ('tm', 'clip'), pairs)  17.6 us
    ppermute x23, waiting for transfers between devices, clip_swap(): lax.ppermute(values, 'clip', [(i, i ^ distance) for i in range(size)])  14.5 us
    ppermute x9, starting transfers between devices, near_swap(): return lax.ppermute(values, ('tm', 'clip'), pairs)  10.5 us
    ppermute x1, starting transfers between devices, body(): got_mine = swap(theirs)  2.57 us
  transfers between devices with their start and end apart: 37, of which 16 were waited for; matrix products, arithmetic and copies ran while one was open for 0% of the time, Pallas kernels for 37%

profile of v9, /device:TPU:0, one launch (start us, length us, event | category | flops | bytes accessed | tf_op | source)
XLA Modules:
  0.0 116.3 jit_solution(2364954269250384370)
XLA Ops:
  1.4 2.4 %shard_map.297 = (bf16[384,384]{1,0:T(8,128)(2,1)S(1)}, f32[16,128]{1,0:T(8,128)S(1)}) custom-call(s32[2]{0:T(128)S(1)} %pad_add_fusion.place_ref, s32[3,1152]{1,0:T(4,128)} %masked_ref.2, bf16[3,768,384]{2,1,0:T(8,128)(2,1)} %refs_1_.1), custom_call_target="tpu_custom_call" | custom-call | flops 235929600 | bytes 2086408 | tf_op jit(solution)/shard_map/pallas_call | solution.py:673
  3.8 2.6 %collective-permute-start.2 = (bf16[384,384]{1,0:T(8,128)(2,1)S(1)}, bf16[384,384]{1,0:T(8,128)(2,1)S(1)}, u32[]{:S(2)}, u32[]{:S(2)}) collective-permute-start(bf16[384,384]{1,0:T(8,128)(2,1)S(1)} %get-tuple-element.155), channel_id=1, source_target_pairs={{0,16},{16,0},{1,17},{17,1},{2,18},{18,2},{3,19},{19,3},{4,20},{20... | collective-permute-start | bytes 884744 | tf_op jit(solution)/shard_map/ppermute | solution.py:712
  15.6 3.6 %shard_map.299 = (bf16[400,384]{1,0:T(8,128)(2,1)S(1)}, bf16[400,384]{1,0:T(8,128)(2,1)S(1)}, bf16[400,384]{1,0:T(8,128)(2,1)S(1)}, bf16[400,384]{1,0:T(8,128)(2...) custom-call(s32[2]{0:T(128)S(1)} %pad_add_fusion.place_ref, ...), custom_call_target="tpu_custom_call" | custom-call | flops 599654400 | bytes 7049736 | tf_op jit(solution)/shard_map/pallas_call | solution.py:673
  19.2 2.7 %collective-permute-start.5 = (s32[24]{0:T(128)S(1)}, s32[24]{0:T(128)S(1)}, u32[]{:S(2)}, u32[]{:S(2)}) collective-permute-start(s32[24]{0:T(128)S(1)} %pad_add_fusion.3), channel_id=1, source_target_pairs={{0,8},{1,9},{2,10},{3,11},{4,12},{5,13},{6,14},{7,15},{8,0},{9,1},... | collective-permute-start | bytes 296 | tf_op jit(solution)/shard_map/ppermute | solution.py:494
  21.8 2.5 %shard_map.300 = (bf16[208,384]{1,0:T(8,128)(2,1)S(1)}, bf16[208,384]{1,0:T(8,128)(2,1)S(1)}, bf16[400,384]{1,0:T(8,128)(2,1)S(1)}, bf16[400,384]{1,0:T(8,128)(2...) custom-call(s32[2]{0:T(128)S(1)} %pad_add_fusion.place_ref, ...), custom_call_target="tpu_custom_call" | custom-call | flops 481689600 | bytes 4207112 | tf_op jit(solution)/shard_map/pallas_call | solution.py:673
  24.4 3.7 %shard_map.302 = (bf16[608,384]{1,0:T(8,128)(2,1)S(1)}, f32[608,384]{1,0:T(8,128)S(1)}, bf16[608,384]{1,0:T(8,128)(2,1)S(1)}, bf16[608,1536]{1,0:T(8,128)(2,1)S(1)}, bf16[608,1536]{1,0:T(8,128)(2,1)S(1)}) custom-call(bf16[400,384]{1,0:T(8,128)(2,1)S(1)} %get-tuple-element.176.att_a.att_ref, bf16[208,384]{1,0:T(8,128)(2,1)S(1)} %get-tuple-element.177.att_b.att_ref, ...), custom_call_target="tpu_custom_call" | custom-call | flops 1613758464 | bytes 9211392 | tf_op jit(solution)/shard_map/pallas_call | solution.py:673
  30.3 4.3 %shard_map.303 = (f32[608,384]{1,0:T(8,128)S(1)}, bf16[608,1536]{1,0:T(8,128)(2,1)S(1)}, f32[1,1536]{1,0:T(1,128)S(1)}, bf16[4,4,288,128]{3,2,1,0:T(8,128)(2,1)S...) custom-call(s32[2]{0:T(128)S(1)} %pad_add_fusion.place_ref, ...), custom_call_target="tpu_custom_call" | custom-call | flops 1 | bytes 1 | tf_op jit(solution)/shard_map/pallas_call | solution.py:673
  35.7 2.7 %shard_map.304 = (f32[608,384]{1,0:T(8,128)S(1)}, bf16[608,384]{1,0:T(8,128)(2,1)S(1)}, f32[8,384]{1,0:T(8,128)S(1)}, bf16[4,4,48,128]{3,2,1,0:T(8,128)(2,1)S(1)...) custom-call(s32[2]{0:T(128)S(1)} %pad_add_fusion.place_ref, ...), custom_call_target="tpu_custom_call" | custom-call | flops 1 | bytes 1 | tf_op jit(solution)/shard_map/pallas_call | solution.py:673
  42.8 3.2 %shard_map.306 = (bf16[400,384]{1,0:T(8,128)(2,1)S(1)}, bf16[400,384]{1,0:T(8,128)(2,1)S(1)}, bf16[400,384]{1,0:T(8,128)(2,1)S(1)}) custom-call(bf16[608,384]{1,0:T(8,128)(2,1)S(1)} %get-tuple-element.202.g_ref, bf16[400,384]{1,0:T(8,128)(2,1)S(1)} %get-tuple-element.176.att_a.att_ref, bf16[400,384]{1,0:T(8,128)(2,1)S(1)} %get-tuple-element.203.q_ref, ...), custom_call_target="tpu_custom_call" | custom-call | flops 1 | bytes 1 | tf_op jit(solution)/shard_map/pallas_call | solution.py:673
  46.0 2.3 %shard_map.307 = (bf16[208,384]{1,0:T(8,128)(2,1)S(1)}, bf16[400,384]{1,0:T(8,128)(2,1)S(1)}, bf16[400,384]{1,0:T(8,128)(2,1)S(1)}) custom-call(bf16[608,384]{1,0:T(8,128)(2,1)S(1)} %get-tuple-element.202.g_ref, bf16[208,384]{1,0:T(8,128)(2,1)S(1)} %get-tuple-element.177.att_b.att_ref, bf16[208,384]{1,0:T(8,128)(2,1)S(1)} %get-tuple-element.212.q_ref, ...), custom_call_target="tpu_custom_call" | custom-call | flops 1 | bytes 1 | tf_op jit(solution)/shard_map/pallas_call | solution.py:673
  48.3 3.8 %shard_map.308 = (bf16[768,384]{1,0:T(8,128)(2,1)S(1)}, bf16[4,4,112,128]{3,2,1,0:T(8,128)(2,1)S(1)}, bf16[2,4,112,128]{3,2,1,0:T(8,128)(2,1)S(1)}, bf16[2,4,112,128]{3,2,1,0:T(8,128)(2,1)S(1)}) custom-call(s32[2]{0:T(128)S(1)} %pad_add_fusion.place_ref, bf16[400,384]{1,0:T(8,128)(2,1)S(1)} %get-tuple-element.162.x_a, ...), custom_call_target="tpu_custom_call" | custom-call | flops 1 | bytes 1 | tf_op jit(solution)/shard_map/pallas_call | solution.py:673
  59.8 3.2 %collective-permute-done.19.refs_5_ = bf16[4,160,128]{2,1,0:T(8,128)(2,1)S(1)} collective-permute-done((bf16[4,160,128]{2,1,0:T(8,128)(2,1)S(1)}, bf16[4,160,128]{2,1,0:T(8,128)(2,1)S(1)}, u32[]{:S(2)}, u32[]{:S(2)}) %collective-permute-start.19) | collective-permute-done | bytes 163872 | tf_op jit(solution)/shard_map/ppermute | solution.py:502
  63.0 3.3 %collective-permute-done.20.refs_6_ = bf16[4,160,128]{2,1,0:T(8,128)(2,1)S(1)} collective-permute-done((bf16[4,160,128]{2,1,0:T(8,128)(2,1)S(1)}, bf16[4,160,128]{2,1,0:T(8,128)(2,1)S(1)}, u32[]{:S(2)}, u32[]{:S(2)}) %collective-permute-start.20) | collective-permute-done | bytes 163872 | tf_op jit(solution)/shard_map/ppermute | solution.py:502
  67.5 3.6 %collective-permute-start.22 = (bf16[1,448,128]{2,1,0:T(8,128)(2,1)S(1)}, bf16[1,448,128]{2,1,0:T(8,128)(2,1)S(1)}, u32[]{:S(2)}, u32[]{:S(2)}) collective-permute-start(bf16[1,448,128]{2,1,0:T(8,128)(2,1)S(1)} %get-tuple-element.255), channel_id=1, source_target_pairs={{0,12},{1,13},{2,14},{3,15},{4,8},{5,9},{6,10},{7,11},{8,4},{9,5},... | collective-permute-start | bytes 344072 | tf_op jit(solution)/shard_map/ppermute | solution.py:494
  71.9 2.8 %collective-permute-done.22.refs_1_ = bf16[1,448,128]{2,1,0:T(8,128)(2,1)S(1)} collective-permute-done((bf16[1,448,128]{2,1,0:T(8,128)(2,1)S(1)}, bf16[1,448,128]{2,1,0:T(8,128)(2,1)S(1)}, u32[]{:S(2)}, u32[]{:S(2)}) %collective-permute-start.22) | collective-permute-done | bytes 114720 | tf_op jit(solution)/shard_map/ppermute | solution.py:494
  74.7 4.9 %collective-permute-done.23.refs_2_ = bf16[1,448,128]{2,1,0:T(8,128)(2,1)S(1)} collective-permute-done((bf16[1,448,128]{2,1,0:T(8,128)(2,1)S(1)}, bf16[1,448,128]{2,1,0:T(8,128)(2,1)S(1)}, u32[]{:S(2)}, u32[]{:S(2)}) %collective-permute-start.23) | collective-permute-done | bytes 114720 | tf_op jit(solution)/shard_map/ppermute | solution.py:494
  79.6 2.7 %collective-permute-start.27 = (bf16[1,448,128]{2,1,0:T(8,128)(2,1)S(1)}, bf16[1,448,128]{2,1,0:T(8,128)(2,1)S(1)}, u32[]{:S(2)}, u32[]{:S(2)}) collective-permute-start(bf16[1,448,128]{2,1,0:T(8,128)(2,1)S(1)} %shard_map.311.refs_0_), channel_id=1, source_target_pairs={{0,12},{1,13},{2,14},{3,15},{4,8},{5,9},{6,10},{7,11},{8,4},{9,5},... | collective-permute-start | bytes 344072 | tf_op jit(solution)/shard_map/ppermute | solution.py:494
  84.1 3.4 %shard_map.313 = bf16[3,768,384]{2,1,0:T(8,128)(2,1)} custom-call(s32[2]{0:T(128)S(1)} %pad_add_fusion.place_ref, f32[16,128]{1,0:T(8,128)S(1)} %get-tuple-element.166.theirs_ref, f32[32,128]{1,0:T(8,128)S(1)} %get-tuple-element.161.refs_0_.rank_ref, bf16[608,384]{1,0:T(8,128)(2,1)S(1)} %get-tuple-element.218.own_ref, ...), custom_call_target="tpu_custom_call" | custom-call | flops 1 | bytes 1 | tf_op jit(solution)/shard_map/pallas_call | solution.py:673
  87.5 3.4 %collective-permute-done.26.refs_2_ = bf16[1,448,128]{2,1,0:T(8,128)(2,1)S(1)} collective-permute-done((bf16[1,448,128]{2,1,0:T(8,128)(2,1)S(1)}, bf16[1,448,128]{2,1,0:T(8,128)(2,1)S(1)}, u32[]{:S(2)}, u32[]{:S(2)}) %collective-permute-start.26) | collective-permute-done | bytes 114720 | tf_op jit(solution)/shard_map/ppermute | solution.py:494
  94.5 3.3 %shard_map.314 = bf16[3,768,384]{2,1,0:T(8,128)(2,1)} custom-call(s32[2]{0:T(128)S(1)} %pad_add_fusion.place_ref, f32[16,128]{1,0:T(8,128)S(1)} %get-tuple-element.166.theirs_ref, f32[32,128]{1,0:T(8,128)S(1)} %get-tuple-element.161.refs_0_.rank_ref, bf16[768,384]{1,0:T(8,128)(2,1)S(1)} %get-tuple-element.258.own_ref, ...), custom_call_target="tpu_custom_call" | custom-call | flops 1 | bytes 1 | tf_op jit(solution)/shard_map/pallas_call | solution.py:673
  101.5 3.8 %collective-permute-done.31.refs_2_.refs_9_ = bf16[4,448,128]{2,1,0:T(8,128)(2,1)S(1)} collective-permute-done((bf16[4,448,128]{2,1,0:T(8,128)(2,1)S(1)}, bf16[4,448,128]{2,1,0:T(8,128)(2,1)S(1)}, u32[]{:S(2)}, u32[]{:S(2)}) %collective-permute-start.31) | collective-permute-done | bytes 458784 | tf_op jit(solution)/shard_map/ppermute | solution.py:502
  105.4 5.3 %collective-permute-done.30.refs_1_.refs_8_ = bf16[4,448,128]{2,1,0:T(8,128)(2,1)S(1)} collective-permute-done((bf16[4,448,128]{2,1,0:T(8,128)(2,1)S(1)}, bf16[4,448,128]{2,1,0:T(8,128)(2,1)S(1)}, u32[]{:S(2)}, u32[]{:S(2)}) %collective-permute-start.30) | collective-permute-done | bytes 458784 | tf_op jit(solution)/shard_map/ppermute | solution.py:502
  111.2 2.2 %shard_map.316 = (f32[1536,384]{1,0:T(8,128)}, f32[384,1536]{1,0:T(8,128)}, f32[384,384]{1,0:T(8,128)}, f32[384,1152]{1,0:T(8,128)}) custom-call(s32[2]{0:T(128)S(1)} %pad_add_fusion.place_ref, bf16[4,448,128]{2,1,0:T(8,128)(2,1)S(1)} %collective-permute-done.29.refs_0_.refs_7_, ...), custom_call_target="tpu_custom_call", output_to_operand_aliasing={{0}: (4, {}), {1}: (5, {}), {2}: (6, {}), {3}: (7, {})} | custom-call | flops 1 | bytes 1 | tf_op jit(solution)/shard_map/pallas_call | solution.py:673
  113.8 2.3 %shard_map.317 = (f32[1536,384]{1,0:T(8,128)}, f32[384,1536]{1,0:T(8,128)}, f32[384,384]{1,0:T(8,128)}, f32[384,1152]{1,0:T(8,128)}, f32[1536]{0:T(1024)}, /*ind...) custom-call(s32[2]{0:T(128)S(1)} %pad_add_fusion.place_ref, ...), custom_call_target="tpu_custom_call", output_to_operand_aliasing={{0}: (11, {}), {1}: (12, {}), {2}: (13, {}), {3}: (14, {})} | custom-call | flops 1 | bytes 1 | tf_op jit(solution)/shard_map/pallas_call | solution.py:673
  (125 shorter events, 37.2 us)
Async XLA Ops:
  0.8 5.8 %collective-permute-start = (s32[3]{0:T(128)}, s32[3]{0:T(128)S(1)}, u32[]{:S(2)}, u32[]{:S(2)}) collective-permute-start(s32[3]{0:T(128)} %groups_ref.1), channel_id=1, source_target_pairs={{0,1},{1,0},{2,3},{3,2},{4,5},{5,4},{6,7},{7,6},{8,9},{9,8},{10,11... | collective-permute-start | bytes 44 | tf_op jit(solution)/shard_map/ppermute | solution.py:494
  3.8 11.9 %collective-permute-start.2 = (bf16[384,384]{1,0:T(8,128)(2,1)S(1)}, bf16[384,384]{1,0:T(8,128)(2,1)S(1)}, u32[]{:S(2)}, u32[]{:S(2)}) collective-permute-start(bf16[384,384]{1,0:T(8,128)(2,1)S(1)} %get-tuple-element.155), channel_id=1, source_target_pairs={{0,16},{16,0},{1,17},{17,1},{2,18},{18,2},{3,19},{19,3},{4,20},{20... | collective-permute-start | bytes 884744 | tf_op jit(solution)/shard_map/ppermute | solution.py:712
  9.8 12.1 %collective-permute-start.3 = (bf16[384,384]{1,0:T(8,128)(2,1)S(1)}, bf16[384,384]{1,0:T(8,128)(2,1)S(1)}, u32[]{:S(2)}, u32[]{:S(2)}) collective-permute-start(bf16[384,384]{1,0:T(8,128)(2,1)S(1)} %get-tuple-element.163.refs_0_), channel_id=1, source_target_pairs={{0,16},{16,0},{1,17},{17,1},{2,18},{18,2},{3,19},{19,3},{4,20},{20... | collective-permute-start | bytes 884744 | tf_op jit(solution)/shard_map/ppermute | solution.py:721
  14.1 16.2 %collective-permute-start.6 = (bf16[592,384]{1,0:T(8,128)(2,1)S(1)}, bf16[592,384]{1,0:T(8,128)(2,1)S(1)}, u32[]{:S(2)}, u32[]{:S(2)}) collective-permute-start(bf16[592,384]{1,0:T(8,128)(2,1)S(1)} %get-tuple-element.175), channel_id=1, source_target_pairs={{0,16},{16,0},{1,17},{17,1},{2,18},{18,2},{3,19},{19,3},{4,20},{20... | collective-permute-start | bytes 1363976 | tf_op jit(solution)/shard_map/ppermute | solution.py:731
  19.2 5.1 %collective-permute-start.5 = (s32[24]{0:T(128)S(1)}, s32[24]{0:T(128)S(1)}, u32[]{:S(2)}, u32[]{:S(2)}) collective-permute-start(s32[24]{0:T(128)S(1)} %pad_add_fusion.3), channel_id=1, source_target_pairs={{0,8},{1,9},{2,10},{3,11},{4,12},{5,13},{6,14},{7,15},{8,0},{9,1},... | collective-permute-start | bytes 296 | tf_op jit(solution)/shard_map/ppermute | solution.py:494
  28.1 14.7 %collective-permute-start.13 = (bf16[608,384]{1,0:T(8,128)(2,1)S(1)}, bf16[608,384]{1,0:T(8,128)(2,1)S(1)}, u32[]{:S(2)}, u32[]{:S(2)}) collective-permute-start(bf16[608,384]{1,0:T(8,128)(2,1)S(1)} %get-tuple-element.218.own_ref), channel_id=1, source_target_pairs={{0,16},{16,0},{1,17},{17,1},{2,18},{18,2},{3,19},{19,3},{4,20},{20... | collective-permute-start | bytes 1400840 | tf_op jit(solution)/shard_map/ppermute | solution.py:767
  38.7 9.6 %collective-permute-start.11 = (bf16[2,4,48,128]{3,2,1,0:T(8,128)(2,1)S(1)}, bf16[2,4,48,128]{3,2,1,0:T(8,128)(2,1)S(1)}, u32[]{:S(2)}, u32[]{:S(2)}) collective-permute-start(bf16[2,4,48,128]{3,2,1,0:T(8,128)(2,1)S(1)} %get-tuple-element.209), channel_id=1, source_target_pairs={{0,1},{1,0},{2,3},{3,2},{4,5},{5,4},{6,7},{7,6},{8,9},{9,8},{10,11... | collective-permute-start | bytes 294920 | tf_op jit(solution)/shard_map/ppermute | solution.py:494
  38.9 9.5 %collective-permute-start.12 = (bf16[2,4,48,128]{3,2,1,0:T(8,128)(2,1)S(1)}, bf16[2,4,48,128]{3,2,1,0:T(8,128)(2,1)S(1)}, u32[]{:S(2)}, u32[]{:S(2)}) collective-permute-start(bf16[2,4,48,128]{3,2,1,0:T(8,128)(2,1)S(1)} %get-tuple-element.210), channel_id=1, source_target_pairs={{0,1},{1,0},{2,3},{3,2},{4,5},{5,4},{6,7},{7,6},{8,9},{9,8},{10,11... | collective-permute-start | bytes 294920 | tf_op jit(solution)/shard_map/ppermute | solution.py:494
  39.3 15.1 %collective-permute-start.16 = (bf16[4,288,128]{2,1,0:T(8,128)(2,1)S(1)}, bf16[4,288,128]{2,1,0:T(8,128)(2,1)S(1)}, u32[]{:S(2)}, u32[]{:S(2)}) collective-permute-start(bf16[4,288,128]{2,1,0:T(8,128)(2,1)S(1)} %get-tuple-element.238), channel_id=1, source_target_pairs={{0,16},{1,17},{2,18},{3,19},{4,20},{5,21},{6,22},{7,23},{8,24},{9,... | collective-permute-start | bytes 884744 | tf_op jit(solution)/shard_map/ppermute | solution.py:502
  41.2 15.0 %collective-permute-start.17 = (bf16[4,288,128]{2,1,0:T(8,128)(2,1)S(1)}, bf16[4,288,128]{2,1,0:T(8,128)(2,1)S(1)}, u32[]{:S(2)}, u32[]{:S(2)}) collective-permute-start(bf16[4,288,128]{2,1,0:T(8,128)(2,1)S(1)} %get-tuple-element.239), channel_id=1, source_target_pairs={{0,2},{1,3},{2,0},{3,1},{4,6},{5,7},{6,4},{7,5},{8,10},{9,11},{10,... | collective-permute-start | bytes 884744 | tf_op jit(solution)/shard_map/ppermute | solution.py:502
  42.8 13.5 %collective-permute-start.18 = (bf16[4,288,128]{2,1,0:T(8,128)(2,1)S(1)}, bf16[4,288,128]{2,1,0:T(8,128)(2,1)S(1)}, u32[]{:S(2)}, u32[]{:S(2)}) collective-permute-start(bf16[4,288,128]{2,1,0:T(8,128)(2,1)S(1)} %get-tuple-element.240), channel_id=1, source_target_pairs={{0,18},{1,19},{2,16},{3,17},{4,22},{5,23},{6,20},{7,21},{8,26},{9,... | collective-permute-start | bytes 884744 | tf_op jit(solution)/shard_map/ppermute | solution.py:502
  56.3 6.7 %collective-permute-start.19 = (bf16[4,160,128]{2,1,0:T(8,128)(2,1)S(1)}, bf16[4,160,128]{2,1,0:T(8,128)(2,1)S(1)}, u32[]{:S(2)}, u32[]{:S(2)}) collective-permute-start(bf16[4,160,128]{2,1,0:T(8,128)(2,1)S(1)} %get-tuple-element.246), channel_id=1, source_target_pairs={{0,16},{1,17},{2,18},{3,19},{4,20},{5,21},{6,22},{7,23},{8,24},{9,... | collective-permute-start | bytes 491528 | tf_op jit(solution)/shard_map/ppermute | solution.py:502
  57.5 8.8 %collective-permute-start.20 = (bf16[4,160,128]{2,1,0:T(8,128)(2,1)S(1)}, bf16[4,160,128]{2,1,0:T(8,128)(2,1)S(1)}, u32[]{:S(2)}, u32[]{:S(2)}) collective-permute-start(bf16[4,160,128]{2,1,0:T(8,128)(2,1)S(1)} %get-tuple-element.247), channel_id=1, source_target_pairs={{0,2},{1,3},{2,0},{3,1},{4,6},{5,7},{6,4},{7,5},{8,10},{9,11},{10,... | collective-permute-start | bytes 491528 | tf_op jit(solution)/shard_map/ppermute | solution.py:502
  58.3 8.0 %collective-permute-start.21 = (bf16[4,160,128]{2,1,0:T(8,128)(2,1)S(1)}, bf16[4,160,128]{2,1,0:T(8,128)(2,1)S(1)}, u32[]{:S(2)}, u32[]{:S(2)}) collective-permute-start(bf16[4,160,128]{2,1,0:T(8,128)(2,1)S(1)} %get-tuple-element.248), channel_id=1, source_target_pairs={{0,18},{1,19},{2,16},{3,17},{4,22},{5,23},{6,20},{7,21},{8,26},{9,... | collective-permute-start | bytes 491528 | tf_op jit(solution)/shard_map/ppermute | solution.py:502
  66.6 24.4 %collective-permute-start.28 = (bf16[768,384]{1,0:T(8,128)(2,1)S(1)}, bf16[768,384]{1,0:T(8,128)(2,1)S(1)}, u32[]{:S(2)}, u32[]{:S(2)}) collective-permute-start(bf16[768,384]{1,0:T(8,128)(2,1)S(1)} %get-tuple-element.258.own_ref), channel_id=1, source_target_pairs={{0,16},{16,0},{1,17},{17,1},{2,18},{18,2},{3,19},{19,3},{4,20},{20... | collective-permute-start | bytes 1769480 | tf_op jit(solution)/shard_map/ppermute | solution.py:816
  67.5 7.2 %collective-permute-start.22 = (bf16[1,448,128]{2,1,0:T(8,128)(2,1)S(1)}, bf16[1,448,128]{2,1,0:T(8,128)(2,1)S(1)}, u32[]{:S(2)}, u32[]{:S(2)}) collective-permute-start(bf16[1,448,128]{2,1,0:T(8,128)(2,1)S(1)} %get-tuple-element.255), channel_id=1, source_target_pairs={{0,12},{1,13},{2,14},{3,15},{4,8},{5,9},{6,10},{7,11},{8,4},{9,5},... | collective-permute-start | bytes 344072 | tf_op jit(solution)/shard_map/ppermute | solution.py:494
  71.1 8.5 %collective-permute-start.23 = (bf16[1,448,128]{2,1,0:T(8,128)(2,1)S(1)}, bf16[1,448,128]{2,1,0:T(8,128)(2,1)S(1)}, u32[]{:S(2)}, u32[]{:S(2)}) collective-permute-start(bf16[1,448,128]{2,1,0:T(8,128)(2,1)S(1)} %get-tuple-element.256), channel_id=1, source_target_pairs={{0,8},{1,9},{2,10},{3,11},{4,12},{5,13},{6,14},{7,15},{8,0},{9,1},... | collective-permute-start | bytes 344072 | tf_op jit(solution)/shard_map/ppermute | solution.py:494
  71.1 8.5 %collective-permute-start.24 = (bf16[1,448,128]{2,1,0:T(8,128)(2,1)S(1)}, bf16[1,448,128]{2,1,0:T(8,128)(2,1)S(1)}, u32[]{:S(2)}, u32[]{:S(2)}) collective-permute-start(bf16[1,448,128]{2,1,0:T(8,128)(2,1)S(1)} %get-tuple-element.257), channel_id=1, source_target_pairs={{0,4},{1,5},{2,6},{3,7},{4,0},{5,1},{6,2},{7,3},{8,12},{9,13},{10,... | collective-permute-start | bytes 344072 | tf_op jit(solution)/shard_map/ppermute | solution.py:494
  79.6 7.9 %collective-permute-start.27 = (bf16[1,448,128]{2,1,0:T(8,128)(2,1)S(1)}, bf16[1,448,128]{2,1,0:T(8,128)(2,1)S(1)}, u32[]{:S(2)}, u32[]{:S(2)}) collective-permute-start(bf16[1,448,128]{2,1,0:T(8,128)(2,1)S(1)} %shard_map.311.refs_0_), channel_id=1, source_target_pairs={{0,12},{1,13},{2,14},{3,15},{4,8},{5,9},{6,10},{7,11},{8,4},{9,5},... | collective-permute-start | bytes 344072 | tf_op jit(solution)/shard_map/ppermute | solution.py:494
  82.3 8.6 %collective-permute-start.26 = (bf16[1,448,128]{2,1,0:T(8,128)(2,1)S(1)}, bf16[1,448,128]{2,1,0:T(8,128)(2,1)S(1)}, u32[]{:S(2)}, u32[]{:S(2)}) collective-permute-start(bf16[1,448,128]{2,1,0:T(8,128)(2,1)S(1)} %shard_map.311.refs_0_), channel_id=1, source_target_pairs={{0,8},{1,9},{2,10},{3,11},{4,12},{5,13},{6,14},{7,15},{8,0},{9,1},... | collective-permute-start | bytes 344072 | tf_op jit(solution)/shard_map/ppermute | solution.py:494
  82.3 8.6 %collective-permute-start.25 = (bf16[1,448,128]{2,1,0:T(8,128)(2,1)S(1)}, bf16[1,448,128]{2,1,0:T(8,128)(2,1)S(1)}, u32[]{:S(2)}, u32[]{:S(2)}) collective-permute-start(bf16[1,448,128]{2,1,0:T(8,128)(2,1)S(1)} %shard_map.311.refs_0_), channel_id=1, source_target_pairs={{0,4},{1,5},{2,6},{3,7},{4,0},{5,1},{6,2},{7,3},{8,12},{9,13},{10,... | collective-permute-start | bytes 344072 | tf_op jit(solution)/shard_map/ppermute | solution.py:494
  91.0 14.4 %collective-permute-start.31 = (bf16[4,448,128]{2,1,0:T(8,128)(2,1)S(1)}, bf16[4,448,128]{2,1,0:T(8,128)(2,1)S(1)}, u32[]{:S(2)}, u32[]{:S(2)}) collective-permute-start(bf16[4,448,128]{2,1,0:T(8,128)(2,1)S(1)} %shard_map.312), channel_id=1, source_target_pairs={{0,18},{1,19},{2,16},{3,17},{4,22},{5,23},{6,20},{7,21},{8,26},{9,... | collective-permute-start | bytes 1376264 | tf_op jit(solution)/shard_map/ppermute | solution.py:502
  91.6 19.1 %collective-permute-start.30 = (bf16[4,448,128]{2,1,0:T(8,128)(2,1)S(1)}, bf16[4,448,128]{2,1,0:T(8,128)(2,1)S(1)}, u32[]{:S(2)}, u32[]{:S(2)}) collective-permute-start(bf16[4,448,128]{2,1,0:T(8,128)(2,1)S(1)} %shard_map.312), channel_id=1, source_target_pairs={{0,2},{1,3},{2,0},{3,1},{4,6},{5,7},{6,4},{7,5},{8,10},{9,11},{10,... | collective-permute-start | bytes 1376264 | tf_op jit(solution)/shard_map/ppermute | solution.py:502
  93.1 17.6 %collective-permute-start.29 = (bf16[4,448,128]{2,1,0:T(8,128)(2,1)S(1)}, bf16[4,448,128]{2,1,0:T(8,128)(2,1)S(1)}, u32[]{:S(2)}, u32[]{:S(2)}) collective-permute-start(bf16[4,448,128]{2,1,0:T(8,128)(2,1)S(1)} %shard_map.312), channel_id=1, source_target_pairs={{0,16},{1,17},{2,18},{3,19},{4,20},{5,21},{6,22},{7,23},{8,24},{9,... | collective-permute-start | bytes 1376264 | tf_op jit(solution)/shard_map/ppermute | solution.py:502
  (31 other events, 159.3 us)

commit v10 on v9

--- a/solution.py
+++ b/solution.py
@@ -514,8 +514,8 @@
     return plain(kernel, [shape(groups, depth, LANES)] * 4)(*refs)
 
 
-def spread_near(pieces):
-    return [pieces[0]] + [near_swap(pieces[step], step) for step in (1, 2, 3)]
+def spread_near(pieces, steps=(1, 2, 3)):
+    return [pieces[0]] + [near_swap(pieces[step], step) for step in steps]
 
 
 def sum_over_devices(first_pieces, second_pieces, send_far, beside_last, finish):
@@ -784,7 +784,7 @@
     )
     got, grad_att = lax.optimization_barrier((swap_cores(send), grad_att))
     pieces, grad_att, send_proj = lax.optimization_barrier((fold_cores([(keep, got)]), grad_att, send_proj))
-    first_pieces = spread_near(pieces)
+    first_pieces = spread_near(pieces, (2, 1, 3))
 
     def attend_back(row_from, grads, att, q, k, v, e, inverse):
         return run(
@@ -809,7 +809,7 @@
     )
     pieces = fold_cores([(keep, swap_cores(send)), (keep_proj, got_proj)])
     pieces, first_pieces = lax.optimization_barrier((pieces, first_pieces))
-    second_pieces = spread_near(pieces)
+    second_pieces = spread_near(pieces, (2, 1, 3))
 
     def send_rows(pieces):
         *pieces, grads = lax.optimization_barrier((*pieces, grad_rows))

time: 116 us -> 113 us (0.974)
  waiting for transfers between devices: 33.6 us -> 28.6 us
  starting transfers between devices: 35.2 us -> 36.9 us
    ppermute x9, waiting for transfers between devices: 17.6 us -> 14.4 us  [near_swap(): return lax.ppermute(values, ('tm', 'clip'), pairs)]
    ppermute x23, waiting for transfers between devices: 14.5 us -> 12.7 us  [clip_swap(): lax.ppermute(values, 'clip', [(i, i ^ distance) for i in range(size)])]
    ppermute x23, starting transfers between devices: 18.4 us -> 19.8 us  [clip_swap(): lax.ppermute(values, 'clip', [(i, i ^ distance) for i in range(size)])]
  transfers between devices with their start and end apart: 37 -> 37, of which waited for: 16 -> 18; matrix products, arithmetic and copies ran while one was open for 0% -> 0% of each run, Pallas kernels for 37% -> 38%
where the time goes in v10:
time: 113 us
  Pallas kernels  45.5 us (40%)
  starting transfers between devices  36.9 us (33%)
  waiting for transfers between devices  28.6 us (25%)
  between operations  1.36 us (1%)
    pallas_call x16, Pallas kernels, run(): pl.pallas_call(kernel, out_shape=outs, in_specs=[SMEM if at < scalars els...  44.5 us
    ppermute x23, starting transfers between devices, clip_swap(): lax.ppermute(values, 'clip', [(i, i ^ distance) for i in range(size)])  19.8 us
    ppermute x9, waiting for transfers between devices, near_swap(): return lax.ppermute(values, ('tm', 'clip'), pairs)  14.4 us
    ppermute x23, waiting for transfers between devices, clip_swap(): lax.ppermute(values, 'clip', [(i, i ^ distance) for i in range(size)])  12.7 us
    ppermute x9, starting transfers between devices, near_swap(): return lax.ppermute(values, ('tm', 'clip'), pairs)  10.5 us
    ppermute x1, starting transfers between devices, body(): got_mine = swap(theirs)  2.57 us
  transfers between devices with their start and end apart: 37, of which 18 were waited for; matrix products, arithmetic and copies ran while one was open for 0% of the time, Pallas kernels for 38%

profile of v10, /device:TPU:0, one launch (start us, length us, event | category | flops | bytes accessed | tf_op | source)
XLA Modules:
  0.0 113.0 jit_solution(2947473383784846095)
XLA Ops:
  1.4 2.4 %shard_map.297 = (bf16[384,384]{1,0:T(8,128)(2,1)S(1)}, f32[16,128]{1,0:T(8,128)S(1)}) custom-call(s32[2]{0:T(128)S(1)} %pad_add_fusion.place_ref, s32[3,1152]{1,0:T(4,128)} %masked_ref.2, bf16[3,768,384]{2,1,0:T(8,128)(2,1)} %refs_1_.1), custom_call_target="tpu_custom_call" | custom-call | flops 235929600 | bytes 2086408 | tf_op jit(solution)/shard_map/pallas_call | solution.py:673
  3.8 2.6 %collective-permute-start.2 = (bf16[384,384]{1,0:T(8,128)(2,1)S(1)}, bf16[384,384]{1,0:T(8,128)(2,1)S(1)}, u32[]{:S(2)}, u32[]{:S(2)}) collective-permute-start(bf16[384,384]{1,0:T(8,128)(2,1)S(1)} %get-tuple-element.155), channel_id=1, source_target_pairs={{0,16},{16,0},{1,17},{17,1},{2,18},{18,2},{3,19},{19,3},{4,20},{20... | collective-permute-start | bytes 884744 | tf_op jit(solution)/shard_map/ppermute | solution.py:712
  15.6 3.6 %shard_map.299 = (bf16[400,384]{1,0:T(8,128)(2,1)S(1)}, bf16[400,384]{1,0:T(8,128)(2,1)S(1)}, bf16[400,384]{1,0:T(8,128)(2,1)S(1)}, bf16[400,384]{1,0:T(8,128)(2...) custom-call(s32[2]{0:T(128)S(1)} %pad_add_fusion.place_ref, ...), custom_call_target="tpu_custom_call" | custom-call | flops 599654400 | bytes 7049736 | tf_op jit(solution)/shard_map/pallas_call | solution.py:673
  19.2 2.7 %collective-permute-start.5 = (s32[24]{0:T(128)S(1)}, s32[24]{0:T(128)S(1)}, u32[]{:S(2)}, u32[]{:S(2)}) collective-permute-start(s32[24]{0:T(128)S(1)} %pad_add_fusion.3), channel_id=1, source_target_pairs={{0,8},{1,9},{2,10},{3,11},{4,12},{5,13},{6,14},{7,15},{8,0},{9,1},... | collective-permute-start | bytes 296 | tf_op jit(solution)/shard_map/ppermute | solution.py:494
  21.8 2.5 %shard_map.300 = (bf16[208,384]{1,0:T(8,128)(2,1)S(1)}, bf16[208,384]{1,0:T(8,128)(2,1)S(1)}, bf16[400,384]{1,0:T(8,128)(2,1)S(1)}, bf16[400,384]{1,0:T(8,128)(2...) custom-call(s32[2]{0:T(128)S(1)} %pad_add_fusion.place_ref, ...), custom_call_target="tpu_custom_call" | custom-call | flops 481689600 | bytes 4207112 | tf_op jit(solution)/shard_map/pallas_call | solution.py:673
  24.4 3.7 %shard_map.302 = (bf16[608,384]{1,0:T(8,128)(2,1)S(1)}, f32[608,384]{1,0:T(8,128)S(1)}, bf16[608,384]{1,0:T(8,128)(2,1)S(1)}, bf16[608,1536]{1,0:T(8,128)(2,1)S(1)}, bf16[608,1536]{1,0:T(8,128)(2,1)S(1)}) custom-call(bf16[400,384]{1,0:T(8,128)(2,1)S(1)} %get-tuple-element.176.att_a.att_ref, bf16[208,384]{1,0:T(8,128)(2,1)S(1)} %get-tuple-element.177.att_b.att_ref, ...), custom_call_target="tpu_custom_call" | custom-call | flops 1613758464 | bytes 9211392 | tf_op jit(solution)/shard_map/pallas_call | solution.py:673
  30.3 4.3 %shard_map.303 = (f32[608,384]{1,0:T(8,128)S(1)}, bf16[608,1536]{1,0:T(8,128)(2,1)S(1)}, f32[1,1536]{1,0:T(1,128)S(1)}, bf16[4,4,288,128]{3,2,1,0:T(8,128)(2,1)S...) custom-call(s32[2]{0:T(128)S(1)} %pad_add_fusion.place_ref, ...), custom_call_target="tpu_custom_call" | custom-call | flops 1 | bytes 1 | tf_op jit(solution)/shard_map/pallas_call | solution.py:673
  35.7 2.7 %shard_map.304 = (f32[608,384]{1,0:T(8,128)S(1)}, bf16[608,384]{1,0:T(8,128)(2,1)S(1)}, f32[8,384]{1,0:T(8,128)S(1)}, bf16[4,4,48,128]{3,2,1,0:T(8,128)(2,1)S(1)...) custom-call(s32[2]{0:T(128)S(1)} %pad_add_fusion.place_ref, ...), custom_call_target="tpu_custom_call" | custom-call | flops 1 | bytes 1 | tf_op jit(solution)/shard_map/pallas_call | solution.py:673
  39.3 2.0 %collective-permute-start.16 = (bf16[4,288,128]{2,1,0:T(8,128)(2,1)S(1)}, bf16[4,288,128]{2,1,0:T(8,128)(2,1)S(1)}, u32[]{:S(2)}, u32[]{:S(2)}) collective-permute-start(bf16[4,288,128]{2,1,0:T(8,128)(2,1)S(1)} %get-tuple-element.238), channel_id=1, source_target_pairs={{0,2},{1,3},{2,0},{3,1},{4,6},{5,7},{6,4},{7,5},{8,10},{9,11},{10,... | collective-permute-start | bytes 884744 | tf_op jit(solution)/shard_map/ppermute | solution.py:502
  42.8 3.2 %shard_map.306 = (bf16[400,384]{1,0:T(8,128)(2,1)S(1)}, bf16[400,384]{1,0:T(8,128)(2,1)S(1)}, bf16[400,384]{1,0:T(8,128)(2,1)S(1)}) custom-call(bf16[608,384]{1,0:T(8,128)(2,1)S(1)} %get-tuple-element.202.g_ref, bf16[400,384]{1,0:T(8,128)(2,1)S(1)} %get-tuple-element.176.att_a.att_ref, bf16[400,384]{1,0:T(8,128)(2,1)S(1)} %get-tuple-element.203.q_ref, ...), custom_call_target="tpu_custom_call" | custom-call | flops 1 | bytes 1 | tf_op jit(solution)/shard_map/pallas_call | solution.py:673
  46.0 2.3 %shard_map.307 = (bf16[208,384]{1,0:T(8,128)(2,1)S(1)}, bf16[400,384]{1,0:T(8,128)(2,1)S(1)}, bf16[400,384]{1,0:T(8,128)(2,1)S(1)}) custom-call(bf16[608,384]{1,0:T(8,128)(2,1)S(1)} %get-tuple-element.202.g_ref, bf16[208,384]{1,0:T(8,128)(2,1)S(1)} %get-tuple-element.177.att_b.att_ref, bf16[208,384]{1,0:T(8,128)(2,1)S(1)} %get-tuple-element.212.q_ref, ...), custom_call_target="tpu_custom_call" | custom-call | flops 1 | bytes 1 | tf_op jit(solution)/shard_map/pallas_call | solution.py:673
  48.3 3.8 %shard_map.308 = (bf16[768,384]{1,0:T(8,128)(2,1)S(1)}, bf16[4,4,112,128]{3,2,1,0:T(8,128)(2,1)S(1)}, bf16[2,4,112,128]{3,2,1,0:T(8,128)(2,1)S(1)}, bf16[2,4,112,128]{3,2,1,0:T(8,128)(2,1)S(1)}) custom-call(s32[2]{0:T(128)S(1)} %pad_add_fusion.place_ref, bf16[400,384]{1,0:T(8,128)(2,1)S(1)} %get-tuple-element.162.x_a, ...), custom_call_target="tpu_custom_call" | custom-call | flops 1 | bytes 1 | tf_op jit(solution)/shard_map/pallas_call | solution.py:673
  59.5 2.4 %collective-permute-done.19.refs_5_ = bf16[4,160,128]{2,1,0:T(8,128)(2,1)S(1)} collective-permute-done((bf16[4,160,128]{2,1,0:T(8,128)(2,1)S(1)}, bf16[4,160,128]{2,1,0:T(8,128)(2,1)S(1)}, u32[]{:S(2)}, u32[]{:S(2)}) %collective-permute-start.19) | collective-permute-done | bytes 163872 | tf_op jit(solution)/shard_map/ppermute | solution.py:502
  61.9 2.3 %collective-permute-done.20.refs_6_ = bf16[4,160,128]{2,1,0:T(8,128)(2,1)S(1)} collective-permute-done((bf16[4,160,128]{2,1,0:T(8,128)(2,1)S(1)}, bf16[4,160,128]{2,1,0:T(8,128)(2,1)S(1)}, u32[]{:S(2)}, u32[]{:S(2)}) %collective-permute-start.20) | collective-permute-done | bytes 163872 | tf_op jit(solution)/shard_map/ppermute | solution.py:502
  64.3 2.0 %collective-permute-done.21.refs_7_ = bf16[4,160,128]{2,1,0:T(8,128)(2,1)S(1)} collective-permute-done((bf16[4,160,128]{2,1,0:T(8,128)(2,1)S(1)}, bf16[4,160,128]{2,1,0:T(8,128)(2,1)S(1)}, u32[]{:S(2)}, u32[]{:S(2)}) %collective-permute-start.21) | collective-permute-done | bytes 163872 | tf_op jit(solution)/shard_map/ppermute | solution.py:502
  67.7 3.6 %collective-permute-start.22 = (bf16[1,448,128]{2,1,0:T(8,128)(2,1)S(1)}, bf16[1,448,128]{2,1,0:T(8,128)(2,1)S(1)}, u32[]{:S(2)}, u32[]{:S(2)}) collective-permute-start(bf16[1,448,128]{2,1,0:T(8,128)(2,1)S(1)} %get-tuple-element.255), channel_id=1, source_target_pairs={{0,12},{1,13},{2,14},{3,15},{4,8},{5,9},{6,10},{7,11},{8,4},{9,5},... | collective-permute-start | bytes 344072 | tf_op jit(solution)/shard_map/ppermute | solution.py:494
  72.1 3.3 %collective-permute-done.22.refs_1_ = bf16[1,448,128]{2,1,0:T(8,128)(2,1)S(1)} collective-permute-done((bf16[1,448,128]{2,1,0:T(8,128)(2,1)S(1)}, bf16[1,448,128]{2,1,0:T(8,128)(2,1)S(1)}, u32[]{:S(2)}, u32[]{:S(2)}) %collective-permute-start.22) | collective-permute-done | bytes 114720 | tf_op jit(solution)/shard_map/ppermute | solution.py:494
  75.5 4.0 %collective-permute-done.23.refs_2_ = bf16[1,448,128]{2,1,0:T(8,128)(2,1)S(1)} collective-permute-done((bf16[1,448,128]{2,1,0:T(8,128)(2,1)S(1)}, bf16[1,448,128]{2,1,0:T(8,128)(2,1)S(1)}, u32[]{:S(2)}, u32[]{:S(2)}) %collective-permute-start.23) | collective-permute-done | bytes 114720 | tf_op jit(solution)/shard_map/ppermute | solution.py:494
  79.6 5.1 %collective-permute-start.27 = (bf16[1,448,128]{2,1,0:T(8,128)(2,1)S(1)}, bf16[1,448,128]{2,1,0:T(8,128)(2,1)S(1)}, u32[]{:S(2)}, u32[]{:S(2)}) collective-permute-start(bf16[1,448,128]{2,1,0:T(8,128)(2,1)S(1)} %shard_map.311.refs_0_), channel_id=1, source_target_pairs={{0,12},{1,13},{2,14},{3,15},{4,8},{5,9},{6,10},{7,11},{8,4},{9,5},... | collective-permute-start | bytes 344072 | tf_op jit(solution)/shard_map/ppermute | solution.py:494
  85.4 3.4 %shard_map.313 = bf16[3,768,384]{2,1,0:T(8,128)(2,1)} custom-call(s32[2]{0:T(128)S(1)} %pad_add_fusion.place_ref, f32[16,128]{1,0:T(8,128)S(1)} %get-tuple-element.166.theirs_ref, f32[32,128]{1,0:T(8,128)S(1)} %get-tuple-element.161.refs_0_.rank_ref, bf16[608,384]{1,0:T(8,128)(2,1)S(1)} %get-tuple-element.218.own_ref, ...), custom_call_target="tpu_custom_call" | custom-call | flops 1 | bytes 1 | tf_op jit(solution)/shard_map/pallas_call | solution.py:673
  94.3 3.3 %shard_map.314 = bf16[3,768,384]{2,1,0:T(8,128)(2,1)} custom-call(s32[2]{0:T(128)S(1)} %pad_add_fusion.place_ref, f32[16,128]{1,0:T(8,128)S(1)} %get-tuple-element.166.theirs_ref, f32[32,128]{1,0:T(8,128)S(1)} %get-tuple-element.161.refs_0_.rank_ref, bf16[768,384]{1,0:T(8,128)(2,1)S(1)} %get-tuple-element.258.own_ref, ...), custom_call_target="tpu_custom_call" | custom-call | flops 1 | bytes 1 | tf_op jit(solution)/shard_map/pallas_call | solution.py:673
  102.4 4.8 %collective-permute-done.30.refs_1_.refs_8_ = bf16[4,448,128]{2,1,0:T(8,128)(2,1)S(1)} collective-permute-done((bf16[4,448,128]{2,1,0:T(8,128)(2,1)S(1)}, bf16[4,448,128]{2,1,0:T(8,128)(2,1)S(1)}, u32[]{:S(2)}, u32[]{:S(2)}) %collective-permute-start.30) | collective-permute-done | bytes 458784 | tf_op jit(solution)/shard_map/ppermute | solution.py:502
  107.9 2.2 %shard_map.316 = (f32[1536,384]{1,0:T(8,128)}, f32[384,1536]{1,0:T(8,128)}, f32[384,384]{1,0:T(8,128)}, f32[384,1152]{1,0:T(8,128)}) custom-call(s32[2]{0:T(128)S(1)} %pad_add_fusion.place_ref, bf16[4,448,128]{2,1,0:T(8,128)(2,1)S(1)} %collective-permute-done.29.refs_0_.refs_7_, ...), custom_call_target="tpu_custom_call", output_to_operand_aliasing={{0}: (4, {}), {1}: (5, {}), {2}: (6, {}), {3}: (7, {})} | custom-call | flops 1 | bytes 1 | tf_op jit(solution)/shard_map/pallas_call | solution.py:673
  110.5 2.3 %shard_map.317 = (f32[1536,384]{1,0:T(8,128)}, f32[384,1536]{1,0:T(8,128)}, f32[384,384]{1,0:T(8,128)}, f32[384,1152]{1,0:T(8,128)}, f32[1536]{0:T(1024)}, /*ind...) custom-call(s32[2]{0:T(128)S(1)} %pad_add_fusion.place_ref, ...), custom_call_target="tpu_custom_call", output_to_operand_aliasing={{0}: (11, {}), {1}: (12, {}), {2}: (13, {}), {3}: (14, {})} | custom-call | flops 1 | bytes 1 | tf_op jit(solution)/shard_map/pallas_call | solution.py:673
  (125 shorter events, 37.3 us)
Async XLA Ops:
  0.8 5.8 %collective-permute-start = (s32[3]{0:T(128)}, s32[3]{0:T(128)S(1)}, u32[]{:S(2)}, u32[]{:S(2)}) collective-permute-start(s32[3]{0:T(128)} %groups_ref.1), channel_id=1, source_target_pairs={{0,1},{1,0},{2,3},{3,2},{4,5},{5,4},{6,7},{7,6},{8,9},{9,8},{10,11... | collective-permute-start | bytes 44 | tf_op jit(solution)/shard_map/ppermute | solution.py:494
  3.8 11.9 %collective-permute-start.2 = (bf16[384,384]{1,0:T(8,128)(2,1)S(1)}, bf16[384,384]{1,0:T(8,128)(2,1)S(1)}, u32[]{:S(2)}, u32[]{:S(2)}) collective-permute-start(bf16[384,384]{1,0:T(8,128)(2,1)S(1)} %get-tuple-element.155), channel_id=1, source_target_pairs={{0,16},{16,0},{1,17},{17,1},{2,18},{18,2},{3,19},{19,3},{4,20},{20... | collective-permute-start | bytes 884744 | tf_op jit(solution)/shard_map/ppermute | solution.py:712
  9.8 12.1 %collective-permute-start.3 = (bf16[384,384]{1,0:T(8,128)(2,1)S(1)}, bf16[384,384]{1,0:T(8,128)(2,1)S(1)}, u32[]{:S(2)}, u32[]{:S(2)}) collective-permute-start(bf16[384,384]{1,0:T(8,128)(2,1)S(1)} %get-tuple-element.163.refs_0_), channel_id=1, source_target_pairs={{0,16},{16,0},{1,17},{17,1},{2,18},{18,2},{3,19},{19,3},{4,20},{20... | collective-permute-start | bytes 884744 | tf_op jit(solution)/shard_map/ppermute | solution.py:721
  14.1 16.2 %collective-permute-start.6 = (bf16[592,384]{1,0:T(8,128)(2,1)S(1)}, bf16[592,384]{1,0:T(8,128)(2,1)S(1)}, u32[]{:S(2)}, u32[]{:S(2)}) collective-permute-start(bf16[592,384]{1,0:T(8,128)(2,1)S(1)} %get-tuple-element.175), channel_id=1, source_target_pairs={{0,16},{16,0},{1,17},{17,1},{2,18},{18,2},{3,19},{19,3},{4,20},{20... | collective-permute-start | bytes 1363976 | tf_op jit(solution)/shard_map/ppermute | solution.py:731
  19.2 5.1 %collective-permute-start.5 = (s32[24]{0:T(128)S(1)}, s32[24]{0:T(128)S(1)}, u32[]{:S(2)}, u32[]{:S(2)}) collective-permute-start(s32[24]{0:T(128)S(1)} %pad_add_fusion.3), channel_id=1, source_target_pairs={{0,8},{1,9},{2,10},{3,11},{4,12},{5,13},{6,14},{7,15},{8,0},{9,1},... | collective-permute-start | bytes 296 | tf_op jit(solution)/shard_map/ppermute | solution.py:494
  28.1 14.7 %collective-permute-start.13 = (bf16[608,384]{1,0:T(8,128)(2,1)S(1)}, bf16[608,384]{1,0:T(8,128)(2,1)S(1)}, u32[]{:S(2)}, u32[]{:S(2)}) collective-permute-start(bf16[608,384]{1,0:T(8,128)(2,1)S(1)} %get-tuple-element.218.own_ref), channel_id=1, source_target_pairs={{0,16},{16,0},{1,17},{17,1},{2,18},{18,2},{3,19},{19,3},{4,20},{20... | collective-permute-start | bytes 1400840 | tf_op jit(solution)/shard_map/ppermute | solution.py:767
  38.7 9.6 %collective-permute-start.11 = (bf16[2,4,48,128]{3,2,1,0:T(8,128)(2,1)S(1)}, bf16[2,4,48,128]{3,2,1,0:T(8,128)(2,1)S(1)}, u32[]{:S(2)}, u32[]{:S(2)}) collective-permute-start(bf16[2,4,48,128]{3,2,1,0:T(8,128)(2,1)S(1)} %get-tuple-element.209), channel_id=1, source_target_pairs={{0,1},{1,0},{2,3},{3,2},{4,5},{5,4},{6,7},{7,6},{8,9},{9,8},{10,11... | collective-permute-start | bytes 294920 | tf_op jit(solution)/shard_map/ppermute | solution.py:494
  38.9 9.5 %collective-permute-start.12 = (bf16[2,4,48,128]{3,2,1,0:T(8,128)(2,1)S(1)}, bf16[2,4,48,128]{3,2,1,0:T(8,128)(2,1)S(1)}, u32[]{:S(2)}, u32[]{:S(2)}) collective-permute-start(bf16[2,4,48,128]{3,2,1,0:T(8,128)(2,1)S(1)} %get-tuple-element.210), channel_id=1, source_target_pairs={{0,1},{1,0},{2,3},{3,2},{4,5},{5,4},{6,7},{7,6},{8,9},{9,8},{10,11... | collective-permute-start | bytes 294920 | tf_op jit(solution)/shard_map/ppermute | solution.py:494
  39.3 15.1 %collective-permute-start.16 = (bf16[4,288,128]{2,1,0:T(8,128)(2,1)S(1)}, bf16[4,288,128]{2,1,0:T(8,128)(2,1)S(1)}, u32[]{:S(2)}, u32[]{:S(2)}) collective-permute-start(bf16[4,288,128]{2,1,0:T(8,128)(2,1)S(1)} %get-tuple-element.238), channel_id=1, source_target_pairs={{0,2},{1,3},{2,0},{3,1},{4,6},{5,7},{6,4},{7,5},{8,10},{9,11},{10,... | collective-permute-start | bytes 884744 | tf_op jit(solution)/shard_map/ppermute | solution.py:502
  41.3 13.1 %collective-permute-start.17 = (bf16[4,288,128]{2,1,0:T(8,128)(2,1)S(1)}, bf16[4,288,128]{2,1,0:T(8,128)(2,1)S(1)}, u32[]{:S(2)}, u32[]{:S(2)}) collective-permute-start(bf16[4,288,128]{2,1,0:T(8,128)(2,1)S(1)} %get-tuple-element.239), channel_id=1, source_target_pairs={{0,16},{1,17},{2,18},{3,19},{4,20},{5,21},{6,22},{7,23},{8,24},{9,... | collective-permute-start | bytes 884744 | tf_op jit(solution)/shard_map/ppermute | solution.py:502
  42.8 13.3 %collective-permute-start.18 = (bf16[4,288,128]{2,1,0:T(8,128)(2,1)S(1)}, bf16[4,288,128]{2,1,0:T(8,128)(2,1)S(1)}, u32[]{:S(2)}, u32[]{:S(2)}) collective-permute-start(bf16[4,288,128]{2,1,0:T(8,128)(2,1)S(1)} %get-tuple-element.240), channel_id=1, source_target_pairs={{0,18},{1,19},{2,16},{3,17},{4,22},{5,23},{6,20},{7,21},{8,26},{9,... | collective-permute-start | bytes 884744 | tf_op jit(solution)/shard_map/ppermute | solution.py:502
  56.0 5.9 %collective-permute-start.19 = (bf16[4,160,128]{2,1,0:T(8,128)(2,1)S(1)}, bf16[4,160,128]{2,1,0:T(8,128)(2,1)S(1)}, u32[]{:S(2)}, u32[]{:S(2)}) collective-permute-start(bf16[4,160,128]{2,1,0:T(8,128)(2,1)S(1)} %get-tuple-element.246), channel_id=1, source_target_pairs={{0,2},{1,3},{2,0},{3,1},{4,6},{5,7},{6,4},{7,5},{8,10},{9,11},{10,... | collective-permute-start | bytes 491528 | tf_op jit(solution)/shard_map/ppermute | solution.py:502
  57.8 6.5 %collective-permute-start.20 = (bf16[4,160,128]{2,1,0:T(8,128)(2,1)S(1)}, bf16[4,160,128]{2,1,0:T(8,128)(2,1)S(1)}, u32[]{:S(2)}, u32[]{:S(2)}) collective-permute-start(bf16[4,160,128]{2,1,0:T(8,128)(2,1)S(1)} %get-tuple-element.247), channel_id=1, source_target_pairs={{0,16},{1,17},{2,18},{3,19},{4,20},{5,21},{6,22},{7,23},{8,24},{9,... | collective-permute-start | bytes 491528 | tf_op jit(solution)/shard_map/ppermute | solution.py:502
  59.3 7.0 %collective-permute-start.21 = (bf16[4,160,128]{2,1,0:T(8,128)(2,1)S(1)}, bf16[4,160,128]{2,1,0:T(8,128)(2,1)S(1)}, u32[]{:S(2)}, u32[]{:S(2)}) collective-permute-start(bf16[4,160,128]{2,1,0:T(8,128)(2,1)S(1)} %get-tuple-element.248), channel_id=1, source_target_pairs={{0,18},{1,19},{2,16},{3,17},{4,22},{5,23},{6,20},{7,21},{8,26},{9,... | collective-permute-start | bytes 491528 | tf_op jit(solution)/shard_map/ppermute | solution.py:502
  66.5 24.3 %collective-permute-start.28 = (bf16[768,384]{1,0:T(8,128)(2,1)S(1)}, bf16[768,384]{1,0:T(8,128)(2,1)S(1)}, u32[]{:S(2)}, u32[]{:S(2)}) collective-permute-start(bf16[768,384]{1,0:T(8,128)(2,1)S(1)} %get-tuple-element.258.own_ref), channel_id=1, source_target_pairs={{0,16},{16,0},{1,17},{17,1},{2,18},{18,2},{3,19},{19,3},{4,20},{20... | collective-permute-start | bytes 1769480 | tf_op jit(solution)/shard_map/ppermute | solution.py:816
  67.7 7.7 %collective-permute-start.22 = (bf16[1,448,128]{2,1,0:T(8,128)(2,1)S(1)}, bf16[1,448,128]{2,1,0:T(8,128)(2,1)S(1)}, u32[]{:S(2)}, u32[]{:S(2)}) collective-permute-start(bf16[1,448,128]{2,1,0:T(8,128)(2,1)S(1)} %get-tuple-element.255), channel_id=1, source_target_pairs={{0,12},{1,13},{2,14},{3,15},{4,8},{5,9},{6,10},{7,11},{8,4},{9,5},... | collective-permute-start | bytes 344072 | tf_op jit(solution)/shard_map/ppermute | solution.py:494
  71.3 8.2 %collective-permute-start.23 = (bf16[1,448,128]{2,1,0:T(8,128)(2,1)S(1)}, bf16[1,448,128]{2,1,0:T(8,128)(2,1)S(1)}, u32[]{:S(2)}, u32[]{:S(2)}) collective-permute-start(bf16[1,448,128]{2,1,0:T(8,128)(2,1)S(1)} %get-tuple-element.256), channel_id=1, source_target_pairs={{0,8},{1,9},{2,10},{3,11},{4,12},{5,13},{6,14},{7,15},{8,0},{9,1},... | collective-permute-start | bytes 344072 | tf_op jit(solution)/shard_map/ppermute | solution.py:494
  71.3 8.2 %collective-permute-start.24 = (bf16[1,448,128]{2,1,0:T(8,128)(2,1)S(1)}, bf16[1,448,128]{2,1,0:T(8,128)(2,1)S(1)}, u32[]{:S(2)}, u32[]{:S(2)}) collective-permute-start(bf16[1,448,128]{2,1,0:T(8,128)(2,1)S(1)} %get-tuple-element.257), channel_id=1, source_target_pairs={{0,4},{1,5},{2,6},{3,7},{4,0},{5,1},{6,2},{7,3},{8,12},{9,13},{10,... | collective-permute-start | bytes 344072 | tf_op jit(solution)/shard_map/ppermute | solution.py:494
  79.6 9.1 %collective-permute-start.27 = (bf16[1,448,128]{2,1,0:T(8,128)(2,1)S(1)}, bf16[1,448,128]{2,1,0:T(8,128)(2,1)S(1)}, u32[]{:S(2)}, u32[]{:S(2)}) collective-permute-start(bf16[1,448,128]{2,1,0:T(8,128)(2,1)S(1)} %shard_map.311.refs_0_), channel_id=1, source_target_pairs={{0,12},{1,13},{2,14},{3,15},{4,8},{5,9},{6,10},{7,11},{8,4},{9,5},... | collective-permute-start | bytes 344072 | tf_op jit(solution)/shard_map/ppermute | solution.py:494
  84.7 5.8 %collective-permute-start.26 = (bf16[1,448,128]{2,1,0:T(8,128)(2,1)S(1)}, bf16[1,448,128]{2,1,0:T(8,128)(2,1)S(1)}, u32[]{:S(2)}, u32[]{:S(2)}) collective-permute-start(bf16[1,448,128]{2,1,0:T(8,128)(2,1)S(1)} %shard_map.311.refs_0_), channel_id=1, source_target_pairs={{0,8},{1,9},{2,10},{3,11},{4,12},{5,13},{6,14},{7,15},{8,0},{9,1},... | collective-permute-start | bytes 344072 | tf_op jit(solution)/shard_map/ppermute | solution.py:494
  84.7 6.0 %collective-permute-start.25 = (bf16[1,448,128]{2,1,0:T(8,128)(2,1)S(1)}, bf16[1,448,128]{2,1,0:T(8,128)(2,1)S(1)}, u32[]{:S(2)}, u32[]{:S(2)}) collective-permute-start(bf16[1,448,128]{2,1,0:T(8,128)(2,1)S(1)} %shard_map.311.refs_0_), channel_id=1, source_target_pairs={{0,4},{1,5},{2,6},{3,7},{4,0},{5,1},{6,2},{7,3},{8,12},{9,13},{10,... | collective-permute-start | bytes 344072 | tf_op jit(solution)/shard_map/ppermute | solution.py:494
  90.8 11.6 %collective-permute-start.31 = (bf16[4,448,128]{2,1,0:T(8,128)(2,1)S(1)}, bf16[4,448,128]{2,1,0:T(8,128)(2,1)S(1)}, u32[]{:S(2)}, u32[]{:S(2)}) collective-permute-start(bf16[4,448,128]{2,1,0:T(8,128)(2,1)S(1)} %shard_map.312), channel_id=1, source_target_pairs={{0,18},{1,19},{2,16},{3,17},{4,22},{5,23},{6,20},{7,21},{8,26},{9,... | collective-permute-start | bytes 1376264 | tf_op jit(solution)/shard_map/ppermute | solution.py:502
  92.3 14.9 %collective-permute-start.30 = (bf16[4,448,128]{2,1,0:T(8,128)(2,1)S(1)}, bf16[4,448,128]{2,1,0:T(8,128)(2,1)S(1)}, u32[]{:S(2)}, u32[]{:S(2)}) collective-permute-start(bf16[4,448,128]{2,1,0:T(8,128)(2,1)S(1)} %shard_map.312), channel_id=1, source_target_pairs={{0,2},{1,3},{2,0},{3,1},{4,6},{5,7},{6,4},{7,5},{8,10},{9,11},{10,... | collective-permute-start | bytes 1376264 | tf_op jit(solution)/shard_map/ppermute | solution.py:502
  92.4 14.9 %collective-permute-start.29 = (bf16[4,448,128]{2,1,0:T(8,128)(2,1)S(1)}, bf16[4,448,128]{2,1,0:T(8,128)(2,1)S(1)}, u32[]{:S(2)}, u32[]{:S(2)}) collective-permute-start(bf16[4,448,128]{2,1,0:T(8,128)(2,1)S(1)} %shard_map.312), channel_id=1, source_target_pairs={{0,16},{1,17},{2,18},{3,19},{4,20},{5,21},{6,22},{7,23},{8,24},{9,... | collective-permute-start | bytes 1376264 | tf_op jit(solution)/shard_map/ppermute | solution.py:502
  (31 other events, 159.3 us)

commit v11 on v10

--- a/solution.py
+++ b/solution.py
@@ -96,14 +96,28 @@
     half = tokens_ref.shape[1]
     load_marks = pltpu.make_async_copy(masked_ref, marks_ref, arrived.at[0])
     load_marks.start()
-    load = pltpu.make_async_copy(tokens_ref.at[1 - tm], half_ref, arrived.at[1])
-    load.start()
+    step = half // 3
+    loads = [
+        pltpu.make_async_copy(
+            tokens_ref.at[1 - tm, block * step : (block + 1) * step],
+            half_ref.at[block * step : (block + 1) * step],
+            arrived.at[1 + block],
+        )
+        for block in range(3)
+    ]
+    for load in loads:
+        load.start()
     load_marks.wait()
     rank = ranks([marks_ref[pl.ds(1 - tm, 1), :]], tm, half, unmasked)
     rank_ref[...] = rank
     chosen = picks(rank[: half // LANES], iota((unmasked, 1), 0))
-    load.wait()
-    theirs_ref[...] = dot(chosen, half_ref[...]).astype(BF)
+    total = None
+    for block, load in enumerate(loads):
+        load.wait()
+        rows = slice(block * step, (block + 1) * step)
+        part = dot(chosen[:, rows], half_ref[rows, :])
+        total = part if total is None else total + part
+    theirs_ref[...] = total.astype(BF)
 
 
 def prep_shared_kernel(unmasked, place_ref, masked_ref, tokens_ref, shared_ref, rank_ref):
@@ -705,7 +719,7 @@
         functools.partial(prep_theirs_kernel, unmasked),
         (place, *(pltpu.with_memory_space_constraint(each, pltpu.HBM) for each in (masked, tokens))),
         [shape(unmasked, width), shape(16, LANES, kind=F32)],
-        [pltpu.VMEM(masked.shape, jnp.int32), pltpu.VMEM((half, width), BF), pltpu.SemaphoreType.DMA((2,))],
+        [pltpu.VMEM(masked.shape, jnp.int32), pltpu.VMEM((half, width), BF), pltpu.SemaphoreType.DMA((4,))],
         flops=2 * rows * half * width,
         in_hbm=(1, 2),
     )

time: 113 us -> 113 us (level)
  no operation moved by 1% of the time
where the time goes in v11:
time: 113 us
  Pallas kernels  45.5 us (40%)
  starting transfers between devices  36.9 us (33%)
  waiting for transfers between devices  28.9 us (26%)
  between operations  1.35 us (1%)
    pallas_call x16, Pallas kernels, run(): pl.pallas_call(kernel, out_shape=outs, in_specs=[SMEM if at < scalars els...  44.8 us
    ppermute x23, starting transfers between devices, clip_swap(): lax.ppermute(values, 'clip', [(i, i ^ distance) for i in range(size)])  19.8 us
    ppermute x9, waiting for transfers between devices, near_swap(): return lax.ppermute(values, ('tm', 'clip'), pairs)  14.6 us
    ppermute x23, waiting for transfers between devices, clip_swap(): lax.ppermute(values, 'clip', [(i, i ^ distance) for i in range(size)])  12.7 us
    ppermute x9, starting transfers between devices, near_swap(): return lax.ppermute(values, ('tm', 'clip'), pairs)  10.5 us
    ppermute x1, starting transfers between devices, body(): got_mine = swap(theirs)  2.57 us
  transfers between devices with their start and end apart: 37, of which 18 were waited for; matrix products, arithmetic and copies ran while one was open for 0% of the time, Pallas kernels for 38%

profile of v11, /device:TPU:0, one launch (start us, length us, event | category | flops | bytes accessed | tf_op | source)
XLA Modules:
  0.0 113.2 jit_solution(14477948472323245833)
XLA Ops:
  1.4 2.6 %shard_map.297 = (bf16[384,384]{1,0:T(8,128)(2,1)S(1)}, f32[16,128]{1,0:T(8,128)S(1)}) custom-call(s32[2]{0:T(128)S(1)} %pad_add_fusion.place_ref, s32[3,1152]{1,0:T(4,128)} %masked_ref.2, bf16[3,768,384]{2,1,0:T(8,128)(2,1)} %refs_1_.1), custom_call_target="tpu_custom_call" | custom-call | flops 235929600 | bytes 2086408 | tf_op jit(solution)/shard_map/pallas_call | solution.py:687
  4.0 2.6 %collective-permute-start.2 = (bf16[384,384]{1,0:T(8,128)(2,1)S(1)}, bf16[384,384]{1,0:T(8,128)(2,1)S(1)}, u32[]{:S(2)}, u32[]{:S(2)}) collective-permute-start(bf16[384,384]{1,0:T(8,128)(2,1)S(1)} %get-tuple-element.155), channel_id=1, source_target_pairs={{0,16},{16,0},{1,17},{17,1},{2,18},{18,2},{3,19},{19,3},{4,20},{20... | collective-permute-start | bytes 884744 | tf_op jit(solution)/shard_map/ppermute | solution.py:726
  15.9 3.5 %shard_map.299 = (bf16[400,384]{1,0:T(8,128)(2,1)S(1)}, bf16[400,384]{1,0:T(8,128)(2,1)S(1)}, bf16[400,384]{1,0:T(8,128)(2,1)S(1)}, bf16[400,384]{1,0:T(8,128)(2...) custom-call(s32[2]{0:T(128)S(1)} %pad_add_fusion.place_ref, ...), custom_call_target="tpu_custom_call" | custom-call | flops 599654400 | bytes 7049736 | tf_op jit(solution)/shard_map/pallas_call | solution.py:687
  19.4 2.7 %collective-permute-start.5 = (s32[24]{0:T(128)S(1)}, s32[24]{0:T(128)S(1)}, u32[]{:S(2)}, u32[]{:S(2)}) collective-permute-start(s32[24]{0:T(128)S(1)} %pad_add_fusion.3), channel_id=1, source_target_pairs={{0,8},{1,9},{2,10},{3,11},{4,12},{5,13},{6,14},{7,15},{8,0},{9,1},... | collective-permute-start | bytes 296 | tf_op jit(solution)/shard_map/ppermute | solution.py:508
  22.1 2.5 %shard_map.300 = (bf16[208,384]{1,0:T(8,128)(2,1)S(1)}, bf16[208,384]{1,0:T(8,128)(2,1)S(1)}, bf16[400,384]{1,0:T(8,128)(2,1)S(1)}, bf16[400,384]{1,0:T(8,128)(2...) custom-call(s32[2]{0:T(128)S(1)} %pad_add_fusion.place_ref, ...), custom_call_target="tpu_custom_call" | custom-call | flops 481689600 | bytes 4207112 | tf_op jit(solution)/shard_map/pallas_call | solution.py:687
  24.6 3.7 %shard_map.302 = (bf16[608,384]{1,0:T(8,128)(2,1)S(1)}, f32[608,384]{1,0:T(8,128)S(1)}, bf16[608,384]{1,0:T(8,128)(2,1)S(1)}, bf16[608,1536]{1,0:T(8,128)(2,1)S(1)}, bf16[608,1536]{1,0:T(8,128)(2,1)S(1)}) custom-call(bf16[400,384]{1,0:T(8,128)(2,1)S(1)} %get-tuple-element.176.att_a.att_ref, bf16[208,384]{1,0:T(8,128)(2,1)S(1)} %get-tuple-element.177.att_b.att_ref, ...), custom_call_target="tpu_custom_call" | custom-call | flops 1613758464 | bytes 9211392 | tf_op jit(solution)/shard_map/pallas_call | solution.py:687
  30.5 4.3 %shard_map.303 = (f32[608,384]{1,0:T(8,128)S(1)}, bf16[608,1536]{1,0:T(8,128)(2,1)S(1)}, f32[1,1536]{1,0:T(1,128)S(1)}, bf16[4,4,288,128]{3,2,1,0:T(8,128)(2,1)S...) custom-call(s32[2]{0:T(128)S(1)} %pad_add_fusion.place_ref, ...), custom_call_target="tpu_custom_call" | custom-call | flops 1 | bytes 1 | tf_op jit(solution)/shard_map/pallas_call | solution.py:687
  35.9 2.7 %shard_map.304 = (f32[608,384]{1,0:T(8,128)S(1)}, bf16[608,384]{1,0:T(8,128)(2,1)S(1)}, f32[8,384]{1,0:T(8,128)S(1)}, bf16[4,4,48,128]{3,2,1,0:T(8,128)(2,1)S(1)...) custom-call(s32[2]{0:T(128)S(1)} %pad_add_fusion.place_ref, ...), custom_call_target="tpu_custom_call" | custom-call | flops 1 | bytes 1 | tf_op jit(solution)/shard_map/pallas_call | solution.py:687
  39.5 2.0 %collective-permute-start.16 = (bf16[4,288,128]{2,1,0:T(8,128)(2,1)S(1)}, bf16[4,288,128]{2,1,0:T(8,128)(2,1)S(1)}, u32[]{:S(2)}, u32[]{:S(2)}) collective-permute-start(bf16[4,288,128]{2,1,0:T(8,128)(2,1)S(1)} %get-tuple-element.238), channel_id=1, source_target_pairs={{0,2},{1,3},{2,0},{3,1},{4,6},{5,7},{6,4},{7,5},{8,10},{9,11},{10,... | collective-permute-start | bytes 884744 | tf_op jit(solution)/shard_map/ppermute | solution.py:516
  43.0 3.2 %shard_map.306 = (bf16[400,384]{1,0:T(8,128)(2,1)S(1)}, bf16[400,384]{1,0:T(8,128)(2,1)S(1)}, bf16[400,384]{1,0:T(8,128)(2,1)S(1)}) custom-call(bf16[608,384]{1,0:T(8,128)(2,1)S(1)} %get-tuple-element.202.g_ref, bf16[400,384]{1,0:T(8,128)(2,1)S(1)} %get-tuple-element.176.att_a.att_ref, bf16[400,384]{1,0:T(8,128)(2,1)S(1)} %get-tuple-element.203.q_ref, ...), custom_call_target="tpu_custom_call" | custom-call | flops 1 | bytes 1 | tf_op jit(solution)/shard_map/pallas_call | solution.py:687
  46.2 2.3 %shard_map.307 = (bf16[208,384]{1,0:T(8,128)(2,1)S(1)}, bf16[400,384]{1,0:T(8,128)(2,1)S(1)}, bf16[400,384]{1,0:T(8,128)(2,1)S(1)}) custom-call(bf16[608,384]{1,0:T(8,128)(2,1)S(1)} %get-tuple-element.202.g_ref, bf16[208,384]{1,0:T(8,128)(2,1)S(1)} %get-tuple-element.177.att_b.att_ref, bf16[208,384]{1,0:T(8,128)(2,1)S(1)} %get-tuple-element.212.q_ref, ...), custom_call_target="tpu_custom_call" | custom-call | flops 1 | bytes 1 | tf_op jit(solution)/shard_map/pallas_call | solution.py:687
  48.5 3.8 %shard_map.308 = (bf16[768,384]{1,0:T(8,128)(2,1)S(1)}, bf16[4,4,112,128]{3,2,1,0:T(8,128)(2,1)S(1)}, bf16[2,4,112,128]{3,2,1,0:T(8,128)(2,1)S(1)}, bf16[2,4,112,128]{3,2,1,0:T(8,128)(2,1)S(1)}) custom-call(s32[2]{0:T(128)S(1)} %pad_add_fusion.place_ref, bf16[400,384]{1,0:T(8,128)(2,1)S(1)} %get-tuple-element.162.x_a, ...), custom_call_target="tpu_custom_call" | custom-call | flops 1 | bytes 1 | tf_op jit(solution)/shard_map/pallas_call | solution.py:687
  59.7 2.5 %collective-permute-done.19.refs_5_ = bf16[4,160,128]{2,1,0:T(8,128)(2,1)S(1)} collective-permute-done((bf16[4,160,128]{2,1,0:T(8,128)(2,1)S(1)}, bf16[4,160,128]{2,1,0:T(8,128)(2,1)S(1)}, u32[]{:S(2)}, u32[]{:S(2)}) %collective-permute-start.19) | collective-permute-done | bytes 163872 | tf_op jit(solution)/shard_map/ppermute | solution.py:516
  62.2 2.3 %collective-permute-done.20.refs_6_ = bf16[4,160,128]{2,1,0:T(8,128)(2,1)S(1)} collective-permute-done((bf16[4,160,128]{2,1,0:T(8,128)(2,1)S(1)}, bf16[4,160,128]{2,1,0:T(8,128)(2,1)S(1)}, u32[]{:S(2)}, u32[]{:S(2)}) %collective-permute-start.20) | collective-permute-done | bytes 163872 | tf_op jit(solution)/shard_map/ppermute | solution.py:516
  64.5 2.0 %collective-permute-done.21.refs_7_ = bf16[4,160,128]{2,1,0:T(8,128)(2,1)S(1)} collective-permute-done((bf16[4,160,128]{2,1,0:T(8,128)(2,1)S(1)}, bf16[4,160,128]{2,1,0:T(8,128)(2,1)S(1)}, u32[]{:S(2)}, u32[]{:S(2)}) %collective-permute-start.21) | collective-permute-done | bytes 163872 | tf_op jit(solution)/shard_map/ppermute | solution.py:516
  68.0 3.6 %collective-permute-start.22 = (bf16[1,448,128]{2,1,0:T(8,128)(2,1)S(1)}, bf16[1,448,128]{2,1,0:T(8,128)(2,1)S(1)}, u32[]{:S(2)}, u32[]{:S(2)}) collective-permute-start(bf16[1,448,128]{2,1,0:T(8,128)(2,1)S(1)} %get-tuple-element.255), channel_id=1, source_target_pairs={{0,12},{1,13},{2,14},{3,15},{4,8},{5,9},{6,10},{7,11},{8,4},{9,5},... | collective-permute-start | bytes 344072 | tf_op jit(solution)/shard_map/ppermute | solution.py:508
  72.4 3.3 %collective-permute-done.22.refs_1_ = bf16[1,448,128]{2,1,0:T(8,128)(2,1)S(1)} collective-permute-done((bf16[1,448,128]{2,1,0:T(8,128)(2,1)S(1)}, bf16[1,448,128]{2,1,0:T(8,128)(2,1)S(1)}, u32[]{:S(2)}, u32[]{:S(2)}) %collective-permute-start.22) | collective-permute-done | bytes 114720 | tf_op jit(solution)/shard_map/ppermute | solution.py:508
  75.7 4.0 %collective-permute-done.23.refs_2_ = bf16[1,448,128]{2,1,0:T(8,128)(2,1)S(1)} collective-permute-done((bf16[1,448,128]{2,1,0:T(8,128)(2,1)S(1)}, bf16[1,448,128]{2,1,0:T(8,128)(2,1)S(1)}, u32[]{:S(2)}, u32[]{:S(2)}) %collective-permute-start.23) | collective-permute-done | bytes 114720 | tf_op jit(solution)/shard_map/ppermute | solution.py:508
  79.8 5.1 %collective-permute-start.27 = (bf16[1,448,128]{2,1,0:T(8,128)(2,1)S(1)}, bf16[1,448,128]{2,1,0:T(8,128)(2,1)S(1)}, u32[]{:S(2)}, u32[]{:S(2)}) collective-permute-start(bf16[1,448,128]{2,1,0:T(8,128)(2,1)S(1)} %shard_map.311.refs_0_), channel_id=1, source_target_pairs={{0,12},{1,13},{2,14},{3,15},{4,8},{5,9},{6,10},{7,11},{8,4},{9,5},... | collective-permute-start | bytes 344072 | tf_op jit(solution)/shard_map/ppermute | solution.py:508
  85.6 3.4 %shard_map.313 = bf16[3,768,384]{2,1,0:T(8,128)(2,1)} custom-call(s32[2]{0:T(128)S(1)} %pad_add_fusion.place_ref, f32[16,128]{1,0:T(8,128)S(1)} %get-tuple-element.166.theirs_ref, f32[32,128]{1,0:T(8,128)S(1)} %get-tuple-element.161.refs_0_.rank_ref, bf16[608,384]{1,0:T(8,128)(2,1)S(1)} %get-tuple-element.218.own_ref, ...), custom_call_target="tpu_custom_call" | custom-call | flops 1 | bytes 1 | tf_op jit(solution)/shard_map/pallas_call | solution.py:687
  94.5 3.2 %shard_map.314 = bf16[3,768,384]{2,1,0:T(8,128)(2,1)} custom-call(s32[2]{0:T(128)S(1)} %pad_add_fusion.place_ref, f32[16,128]{1,0:T(8,128)S(1)} %get-tuple-element.166.theirs_ref, f32[32,128]{1,0:T(8,128)S(1)} %get-tuple-element.161.refs_0_.rank_ref, bf16[768,384]{1,0:T(8,128)(2,1)S(1)} %get-tuple-element.258.own_ref, ...), custom_call_target="tpu_custom_call" | custom-call | flops 1 | bytes 1 | tf_op jit(solution)/shard_map/pallas_call | solution.py:687
  102.6 4.8 %collective-permute-done.30.refs_1_.refs_8_ = bf16[4,448,128]{2,1,0:T(8,128)(2,1)S(1)} collective-permute-done((bf16[4,448,128]{2,1,0:T(8,128)(2,1)S(1)}, bf16[4,448,128]{2,1,0:T(8,128)(2,1)S(1)}, u32[]{:S(2)}, u32[]{:S(2)}) %collective-permute-start.30) | collective-permute-done | bytes 458784 | tf_op jit(solution)/shard_map/ppermute | solution.py:516
  108.1 2.2 %shard_map.316 = (f32[1536,384]{1,0:T(8,128)}, f32[384,1536]{1,0:T(8,128)}, f32[384,384]{1,0:T(8,128)}, f32[384,1152]{1,0:T(8,128)}) custom-call(s32[2]{0:T(128)S(1)} %pad_add_fusion.place_ref, bf16[4,448,128]{2,1,0:T(8,128)(2,1)S(1)} %collective-permute-done.29.refs_0_.refs_7_, ...), custom_call_target="tpu_custom_call", output_to_operand_aliasing={{0}: (4, {}), {1}: (5, {}), {2}: (6, {}), {3}: (7, {})} | custom-call | flops 1 | bytes 1 | tf_op jit(solution)/shard_map/pallas_call | solution.py:687
  110.7 2.3 %shard_map.317 = (f32[1536,384]{1,0:T(8,128)}, f32[384,1536]{1,0:T(8,128)}, f32[384,384]{1,0:T(8,128)}, f32[384,1152]{1,0:T(8,128)}, f32[1536]{0:T(1024)}, /*ind...) custom-call(s32[2]{0:T(128)S(1)} %pad_add_fusion.place_ref, ...), custom_call_target="tpu_custom_call", output_to_operand_aliasing={{0}: (11, {}), {1}: (12, {}), {2}: (13, {}), {3}: (14, {})} | custom-call | flops 1 | bytes 1 | tf_op jit(solution)/shard_map/pallas_call | solution.py:687
  (125 shorter events, 37.3 us)
Async XLA Ops:
  0.8 6.1 %collective-permute-start = (s32[3]{0:T(128)}, s32[3]{0:T(128)S(1)}, u32[]{:S(2)}, u32[]{:S(2)}) collective-permute-start(s32[3]{0:T(128)} %groups_ref.1), channel_id=1, source_target_pairs={{0,1},{1,0},{2,3},{3,2},{4,5},{5,4},{6,7},{7,6},{8,9},{9,8},{10,11... | collective-permute-start | bytes 44 | tf_op jit(solution)/shard_map/ppermute | solution.py:508
  4.0 11.9 %collective-permute-start.2 = (bf16[384,384]{1,0:T(8,128)(2,1)S(1)}, bf16[384,384]{1,0:T(8,128)(2,1)S(1)}, u32[]{:S(2)}, u32[]{:S(2)}) collective-permute-start(bf16[384,384]{1,0:T(8,128)(2,1)S(1)} %get-tuple-element.155), channel_id=1, source_target_pairs={{0,16},{16,0},{1,17},{17,1},{2,18},{18,2},{3,19},{19,3},{4,20},{20... | collective-permute-start | bytes 884744 | tf_op jit(solution)/shard_map/ppermute | solution.py:726
  10.0 12.0 %collective-permute-start.3 = (bf16[384,384]{1,0:T(8,128)(2,1)S(1)}, bf16[384,384]{1,0:T(8,128)(2,1)S(1)}, u32[]{:S(2)}, u32[]{:S(2)}) collective-permute-start(bf16[384,384]{1,0:T(8,128)(2,1)S(1)} %get-tuple-element.163.refs_0_), channel_id=1, source_target_pairs={{0,16},{16,0},{1,17},{17,1},{2,18},{18,2},{3,19},{19,3},{4,20},{20... | collective-permute-start | bytes 884744 | tf_op jit(solution)/shard_map/ppermute | solution.py:735
  14.3 16.2 %collective-permute-start.6 = (bf16[592,384]{1,0:T(8,128)(2,1)S(1)}, bf16[592,384]{1,0:T(8,128)(2,1)S(1)}, u32[]{:S(2)}, u32[]{:S(2)}) collective-permute-start(bf16[592,384]{1,0:T(8,128)(2,1)S(1)} %get-tuple-element.175), channel_id=1, source_target_pairs={{0,16},{16,0},{1,17},{17,1},{2,18},{18,2},{3,19},{19,3},{4,20},{20... | collective-permute-start | bytes 1363976 | tf_op jit(solution)/shard_map/ppermute | solution.py:745
  19.4 5.1 %collective-permute-start.5 = (s32[24]{0:T(128)S(1)}, s32[24]{0:T(128)S(1)}, u32[]{:S(2)}, u32[]{:S(2)}) collective-permute-start(s32[24]{0:T(128)S(1)} %pad_add_fusion.3), channel_id=1, source_target_pairs={{0,8},{1,9},{2,10},{3,11},{4,12},{5,13},{6,14},{7,15},{8,0},{9,1},... | collective-permute-start | bytes 296 | tf_op jit(solution)/shard_map/ppermute | solution.py:508
  28.3 14.7 %collective-permute-start.13 = (bf16[608,384]{1,0:T(8,128)(2,1)S(1)}, bf16[608,384]{1,0:T(8,128)(2,1)S(1)}, u32[]{:S(2)}, u32[]{:S(2)}) collective-permute-start(bf16[608,384]{1,0:T(8,128)(2,1)S(1)} %get-tuple-element.218.own_ref), channel_id=1, source_target_pairs={{0,16},{16,0},{1,17},{17,1},{2,18},{18,2},{3,19},{19,3},{4,20},{20... | collective-permute-start | bytes 1400840 | tf_op jit(solution)/shard_map/ppermute | solution.py:781
  38.9 9.6 %collective-permute-start.11 = (bf16[2,4,48,128]{3,2,1,0:T(8,128)(2,1)S(1)}, bf16[2,4,48,128]{3,2,1,0:T(8,128)(2,1)S(1)}, u32[]{:S(2)}, u32[]{:S(2)}) collective-permute-start(bf16[2,4,48,128]{3,2,1,0:T(8,128)(2,1)S(1)} %get-tuple-element.209), channel_id=1, source_target_pairs={{0,1},{1,0},{2,3},{3,2},{4,5},{5,4},{6,7},{7,6},{8,9},{9,8},{10,11... | collective-permute-start | bytes 294920 | tf_op jit(solution)/shard_map/ppermute | solution.py:508
  39.1 9.5 %collective-permute-start.12 = (bf16[2,4,48,128]{3,2,1,0:T(8,128)(2,1)S(1)}, bf16[2,4,48,128]{3,2,1,0:T(8,128)(2,1)S(1)}, u32[]{:S(2)}, u32[]{:S(2)}) collective-permute-start(bf16[2,4,48,128]{3,2,1,0:T(8,128)(2,1)S(1)} %get-tuple-element.210), channel_id=1, source_target_pairs={{0,1},{1,0},{2,3},{3,2},{4,5},{5,4},{6,7},{7,6},{8,9},{9,8},{10,11... | collective-permute-start | bytes 294920 | tf_op jit(solution)/shard_map/ppermute | solution.py:508
  39.5 14.9 %collective-permute-start.16 = (bf16[4,288,128]{2,1,0:T(8,128)(2,1)S(1)}, bf16[4,288,128]{2,1,0:T(8,128)(2,1)S(1)}, u32[]{:S(2)}, u32[]{:S(2)}) collective-permute-start(bf16[4,288,128]{2,1,0:T(8,128)(2,1)S(1)} %get-tuple-element.238), channel_id=1, source_target_pairs={{0,2},{1,3},{2,0},{3,1},{4,6},{5,7},{6,4},{7,5},{8,10},{9,11},{10,... | collective-permute-start | bytes 884744 | tf_op jit(solution)/shard_map/ppermute | solution.py:516
  41.5 12.9 %collective-permute-start.17 = (bf16[4,288,128]{2,1,0:T(8,128)(2,1)S(1)}, bf16[4,288,128]{2,1,0:T(8,128)(2,1)S(1)}, u32[]{:S(2)}, u32[]{:S(2)}) collective-permute-start(bf16[4,288,128]{2,1,0:T(8,128)(2,1)S(1)} %get-tuple-element.239), channel_id=1, source_target_pairs={{0,16},{1,17},{2,18},{3,19},{4,20},{5,21},{6,22},{7,23},{8,24},{9,... | collective-permute-start | bytes 884744 | tf_op jit(solution)/shard_map/ppermute | solution.py:516
  43.0 13.3 %collective-permute-start.18 = (bf16[4,288,128]{2,1,0:T(8,128)(2,1)S(1)}, bf16[4,288,128]{2,1,0:T(8,128)(2,1)S(1)}, u32[]{:S(2)}, u32[]{:S(2)}) collective-permute-start(bf16[4,288,128]{2,1,0:T(8,128)(2,1)S(1)} %get-tuple-element.240), channel_id=1, source_target_pairs={{0,18},{1,19},{2,16},{3,17},{4,22},{5,23},{6,20},{7,21},{8,26},{9,... | collective-permute-start | bytes 884744 | tf_op jit(solution)/shard_map/ppermute | solution.py:516
  56.2 5.9 %collective-permute-start.19 = (bf16[4,160,128]{2,1,0:T(8,128)(2,1)S(1)}, bf16[4,160,128]{2,1,0:T(8,128)(2,1)S(1)}, u32[]{:S(2)}, u32[]{:S(2)}) collective-permute-start(bf16[4,160,128]{2,1,0:T(8,128)(2,1)S(1)} %get-tuple-element.246), channel_id=1, source_target_pairs={{0,2},{1,3},{2,0},{3,1},{4,6},{5,7},{6,4},{7,5},{8,10},{9,11},{10,... | collective-permute-start | bytes 491528 | tf_op jit(solution)/shard_map/ppermute | solution.py:516
  58.0 6.5 %collective-permute-start.20 = (bf16[4,160,128]{2,1,0:T(8,128)(2,1)S(1)}, bf16[4,160,128]{2,1,0:T(8,128)(2,1)S(1)}, u32[]{:S(2)}, u32[]{:S(2)}) collective-permute-start(bf16[4,160,128]{2,1,0:T(8,128)(2,1)S(1)} %get-tuple-element.247), channel_id=1, source_target_pairs={{0,16},{1,17},{2,18},{3,19},{4,20},{5,21},{6,22},{7,23},{8,24},{9,... | collective-permute-start | bytes 491528 | tf_op jit(solution)/shard_map/ppermute | solution.py:516
  59.5 7.1 %collective-permute-start.21 = (bf16[4,160,128]{2,1,0:T(8,128)(2,1)S(1)}, bf16[4,160,128]{2,1,0:T(8,128)(2,1)S(1)}, u32[]{:S(2)}, u32[]{:S(2)}) collective-permute-start(bf16[4,160,128]{2,1,0:T(8,128)(2,1)S(1)} %get-tuple-element.248), channel_id=1, source_target_pairs={{0,18},{1,19},{2,16},{3,17},{4,22},{5,23},{6,20},{7,21},{8,26},{9,... | collective-permute-start | bytes 491528 | tf_op jit(solution)/shard_map/ppermute | solution.py:516
  66.8 24.2 %collective-permute-start.28 = (bf16[768,384]{1,0:T(8,128)(2,1)S(1)}, bf16[768,384]{1,0:T(8,128)(2,1)S(1)}, u32[]{:S(2)}, u32[]{:S(2)}) collective-permute-start(bf16[768,384]{1,0:T(8,128)(2,1)S(1)} %get-tuple-element.258.own_ref), channel_id=1, source_target_pairs={{0,16},{16,0},{1,17},{17,1},{2,18},{18,2},{3,19},{19,3},{4,20},{20... | collective-permute-start | bytes 1769480 | tf_op jit(solution)/shard_map/ppermute | solution.py:830
  68.0 7.7 %collective-permute-start.22 = (bf16[1,448,128]{2,1,0:T(8,128)(2,1)S(1)}, bf16[1,448,128]{2,1,0:T(8,128)(2,1)S(1)}, u32[]{:S(2)}, u32[]{:S(2)}) collective-permute-start(bf16[1,448,128]{2,1,0:T(8,128)(2,1)S(1)} %get-tuple-element.255), channel_id=1, source_target_pairs={{0,12},{1,13},{2,14},{3,15},{4,8},{5,9},{6,10},{7,11},{8,4},{9,5},... | collective-permute-start | bytes 344072 | tf_op jit(solution)/shard_map/ppermute | solution.py:508
  71.6 8.1 %collective-permute-start.23 = (bf16[1,448,128]{2,1,0:T(8,128)(2,1)S(1)}, bf16[1,448,128]{2,1,0:T(8,128)(2,1)S(1)}, u32[]{:S(2)}, u32[]{:S(2)}) collective-permute-start(bf16[1,448,128]{2,1,0:T(8,128)(2,1)S(1)} %get-tuple-element.256), channel_id=1, source_target_pairs={{0,8},{1,9},{2,10},{3,11},{4,12},{5,13},{6,14},{7,15},{8,0},{9,1},... | collective-permute-start | bytes 344072 | tf_op jit(solution)/shard_map/ppermute | solution.py:508
  71.6 8.1 %collective-permute-start.24 = (bf16[1,448,128]{2,1,0:T(8,128)(2,1)S(1)}, bf16[1,448,128]{2,1,0:T(8,128)(2,1)S(1)}, u32[]{:S(2)}, u32[]{:S(2)}) collective-permute-start(bf16[1,448,128]{2,1,0:T(8,128)(2,1)S(1)} %get-tuple-element.257), channel_id=1, source_target_pairs={{0,4},{1,5},{2,6},{3,7},{4,0},{5,1},{6,2},{7,3},{8,12},{9,13},{10,... | collective-permute-start | bytes 344072 | tf_op jit(solution)/shard_map/ppermute | solution.py:508
  79.8 9.1 %collective-permute-start.27 = (bf16[1,448,128]{2,1,0:T(8,128)(2,1)S(1)}, bf16[1,448,128]{2,1,0:T(8,128)(2,1)S(1)}, u32[]{:S(2)}, u32[]{:S(2)}) collective-permute-start(bf16[1,448,128]{2,1,0:T(8,128)(2,1)S(1)} %shard_map.311.refs_0_), channel_id=1, source_target_pairs={{0,12},{1,13},{2,14},{3,15},{4,8},{5,9},{6,10},{7,11},{8,4},{9,5},... | collective-permute-start | bytes 344072 | tf_op jit(solution)/shard_map/ppermute | solution.py:508
  84.9 5.8 %collective-permute-start.26 = (bf16[1,448,128]{2,1,0:T(8,128)(2,1)S(1)}, bf16[1,448,128]{2,1,0:T(8,128)(2,1)S(1)}, u32[]{:S(2)}, u32[]{:S(2)}) collective-permute-start(bf16[1,448,128]{2,1,0:T(8,128)(2,1)S(1)} %shard_map.311.refs_0_), channel_id=1, source_target_pairs={{0,8},{1,9},{2,10},{3,11},{4,12},{5,13},{6,14},{7,15},{8,0},{9,1},... | collective-permute-start | bytes 344072 | tf_op jit(solution)/shard_map/ppermute | solution.py:508
  84.9 6.0 %collective-permute-start.25 = (bf16[1,448,128]{2,1,0:T(8,128)(2,1)S(1)}, bf16[1,448,128]{2,1,0:T(8,128)(2,1)S(1)}, u32[]{:S(2)}, u32[]{:S(2)}) collective-permute-start(bf16[1,448,128]{2,1,0:T(8,128)(2,1)S(1)} %shard_map.311.refs_0_), channel_id=1, source_target_pairs={{0,4},{1,5},{2,6},{3,7},{4,0},{5,1},{6,2},{7,3},{8,12},{9,13},{10,... | collective-permute-start | bytes 344072 | tf_op jit(solution)/shard_map/ppermute | solution.py:508
  91.0 11.7 %collective-permute-start.31 = (bf16[4,448,128]{2,1,0:T(8,128)(2,1)S(1)}, bf16[4,448,128]{2,1,0:T(8,128)(2,1)S(1)}, u32[]{:S(2)}, u32[]{:S(2)}) collective-permute-start(bf16[4,448,128]{2,1,0:T(8,128)(2,1)S(1)} %shard_map.312), channel_id=1, source_target_pairs={{0,18},{1,19},{2,16},{3,17},{4,22},{5,23},{6,20},{7,21},{8,26},{9,... | collective-permute-start | bytes 1376264 | tf_op jit(solution)/shard_map/ppermute | solution.py:516
  92.5 14.9 %collective-permute-start.30 = (bf16[4,448,128]{2,1,0:T(8,128)(2,1)S(1)}, bf16[4,448,128]{2,1,0:T(8,128)(2,1)S(1)}, u32[]{:S(2)}, u32[]{:S(2)}) collective-permute-start(bf16[4,448,128]{2,1,0:T(8,128)(2,1)S(1)} %shard_map.312), channel_id=1, source_target_pairs={{0,2},{1,3},{2,0},{3,1},{4,6},{5,7},{6,4},{7,5},{8,10},{9,11},{10,... | collective-permute-start | bytes 1376264 | tf_op jit(solution)/shard_map/ppermute | solution.py:516
  92.7 14.9 %collective-permute-start.29 = (bf16[4,448,128]{2,1,0:T(8,128)(2,1)S(1)}, bf16[4,448,128]{2,1,0:T(8,128)(2,1)S(1)}, u32[]{:S(2)}, u32[]{:S(2)}) collective-permute-start(bf16[4,448,128]{2,1,0:T(8,128)(2,1)S(1)} %shard_map.312), channel_id=1, source_target_pairs={{0,16},{1,17},{2,18},{3,19},{4,20},{5,21},{6,22},{7,23},{8,24},{9,... | collective-permute-start | bytes 1376264 | tf_op jit(solution)/shard_map/ppermute | solution.py:516
  (31 other events, 162.3 us)
